TPU v7x, 256 devices: a whole 4x4x8 slice. The times are simulated.
256 devices in a mesh: ctx: 64 (over x, z, core), tp: 4 (over y).
Axes of the slice: x: 4, y: 4, z: 8, core: 2. Of those that a mesh axis runs over, the one named last changes fastest.
Arguments:
- queries: bfloat16 [64, 2, 256, 2048], P('ctx', None, None, 'tp'), may hold values from -6 to 6
- keys: bfloat16 [64, 2, 256, 512], P('ctx', None, None, 'tp'), may hold values from -6 to 6
- values: bfloat16 [64, 2, 256, 512], P('ctx', None, None, 'tp'), may hold values from -24 to 24
- column_block_table: int32 [4, 64], P('tp'), may hold values from 0 to 255, as said below
- slash_offsets: int32 [16, 64], P('tp'), may hold values from 1 to 256, as said below
- out_weight: bfloat16 [2048, 4096], P('tp'), may hold values from -0.125 to 0.125
Outputs:
- mixed: bfloat16 [64, 2, 256, 4096], P('ctx', None, None, 'tp')
Inputs may be any that keep to these rules, and one draw needn't show every extreme that they name: `column_block_table`: each row holds 64 distinct block numbers below 256, block b holding positions b * 128 to b * 128 + 127 and lying on the ctx device that holds its stretch. For each row, a quarter of the ctx devices hold exactly 2 of its blocks, half hold exactly one, the rest none. `slash_offsets`: each row holds 64 distinct offsets, and 1 and 256 are in every row.
All inputs are finite; a program needn't handle non-finite values.
Results may differ from a plain program's by a relative error of at most 0.00185.
The roundings to bfloat16 on the way count: a program that leaves them out, or rounds other values in their place, can miss the bound.
Values may be sent and summed in bfloat16 or wider, within the bound.
No kernel may reach another device: no remote copies, remote signals or barrier semaphores. Data moves between devices by JAX's collectives and lax.ppermute only.
A program may use at most 128 MiB of HBM per device.

v0:
```python
import jax
import jax.numpy as jnp
from jax import lax
from jax.sharding import PartitionSpec as P

HEAD_SIZE = 128
KEY_BLOCK_TOKENS = 128
CAP = 2


def passed_along(block, axis, distance):
    devices = range(lax.axis_size(axis))
    route = [(i - distance, i) for i in devices if i - distance in devices]
    return lax.ppermute(block, axis, route)


def owner_place(blocks, stretch_blocks, ctx_count):
    stretch_index = blocks // stretch_blocks
    first_half = stretch_index < ctx_count
    owner_device = jnp.where(first_half, stretch_index, 2 * ctx_count - 1 - stretch_index)
    local_index = jnp.where(first_half, 0, stretch_blocks) + blocks % stretch_blocks
    return (owner_device, local_index)


def slash_masks(offsets, stretch_len):
    span = 3 * stretch_len - 1
    relative = 2 * stretch_len - 1 - jnp.arange(span, dtype=jnp.int32)
    table = (
        jnp.any(relative[None, None, :] == offsets[:, :, None], axis=1) | (relative == 0)[None, :]
    )
    padded = jnp.concatenate([table, jnp.zeros((offsets.shape[0], 1), jnp.bool_)], axis=1)
    tiled = jnp.tile(padded, (1, stretch_len))[:, : stretch_len * span]
    rolled = tiled.reshape(offsets.shape[0], stretch_len, span)
    return rolled[:, :, stretch_len - 1 : 3 * stretch_len - 1]


def per_device(queries, keys, values, column_block_table, slash_offsets, out_weight):
    ctx_count = lax.axis_size("ctx")
    ctx_index = lax.axis_index("ctx")
    stretch_len = keys.shape[2]
    groups = keys.shape[3] // HEAD_SIZE
    heads = queries.shape[3] // HEAD_SIZE
    heads_per_group = heads // groups
    stretch_blocks = stretch_len // KEY_BLOCK_TOKENS
    listed = column_block_table.shape[1]
    scale = HEAD_SIZE ** (-0.5)
    kv_halves = jnp.stack([keys[0], values[0]], axis=1)
    local_blocks = kv_halves.reshape(2, 2, stretch_blocks, KEY_BLOCK_TOKENS, groups, HEAD_SIZE)
    local_blocks = local_blocks.transpose(4, 1, 0, 2, 3, 5).reshape(
        groups, 2, 2 * stretch_blocks, KEY_BLOCK_TOKENS, HEAD_SIZE
    )
    owner_device, local_index = owner_place(column_block_table, stretch_blocks, ctx_count)
    owned_here = owner_device == ctx_index
    same_owner = owner_device[:, :, None] == owner_device[:, None, :]
    position = jnp.arange(listed, dtype=jnp.int32)
    earlier = position[None, :] < position[:, None]
    owner_rank = jnp.sum(same_owner & earlier[None], axis=2)
    chosen_local = []
    chosen_valid = []
    for slot_rank in range(CAP):
        slot_hit = owned_here & (owner_rank == slot_rank)
        chosen_local.append(jnp.sum(jnp.where(slot_hit, local_index, 0), axis=1))
        chosen_valid.append(jnp.any(slot_hit, axis=1))
    chosen_local = jnp.stack(chosen_local, axis=1)
    chosen_valid = jnp.stack(chosen_valid, axis=1)
    outgoing = jnp.take_along_axis(local_blocks, chosen_local[:, None, :, None, None], axis=2)
    outgoing = jnp.where(
        chosen_valid[:, None, :, None, None], outgoing, jnp.zeros((), local_blocks.dtype)
    )
    arrived = lax.all_gather(outgoing, "ctx", axis=2, tiled=True)
    slot_index = owner_device * CAP + owner_rank
    column_kv = jnp.take_along_axis(arrived, slot_index[:, None, :, None, None], axis=2)
    before = passed_along(kv_halves[0], "ctx", 1)
    after = passed_along(kv_halves[1], "ctx", -1)
    after = jnp.where(ctx_index == ctx_count - 1, kv_halves[0], after)
    band_kv = jnp.concatenate([jnp.stack([before, after]), kv_halves], axis=2)
    stretch_ids = jnp.stack([ctx_index, 2 * ctx_count - 1 - ctx_index])
    query_pos = (
        stretch_ids[:, None] * stretch_len + jnp.arange(stretch_len, dtype=jnp.int32)[None, :]
    )
    flat_pos = query_pos.reshape(2 * stretch_len)
    band_pos = (stretch_ids[:, None] - 1) * stretch_len + jnp.arange(
        2 * stretch_len, dtype=jnp.int32
    )[None, :]
    band_listed = jnp.any(
        (band_pos // KEY_BLOCK_TOKENS)[None, :, :, None] == column_block_table[:, None, None, :],
        axis=3,
    )
    band_open = (band_pos >= 0)[None] & jnp.logical_not(band_listed)
    column_position = (
        column_block_table[:, :, None] * KEY_BLOCK_TOKENS
        + jnp.arange(KEY_BLOCK_TOKENS, dtype=jnp.int32)[None, None, :]
    ).reshape(groups, listed * KEY_BLOCK_TOKENS)
    slash_ok = slash_masks(slash_offsets, stretch_len)
    head_query = queries[0].reshape(2, stretch_len, heads, HEAD_SIZE).transpose(2, 0, 1, 3)
    column_keys = column_kv[:, 0].reshape(groups, listed * KEY_BLOCK_TOKENS, HEAD_SIZE)
    column_vals = column_kv[:, 1].reshape(groups, listed * KEY_BLOCK_TOKENS, HEAD_SIZE)
    band_keys = band_kv[:, 0].reshape(2, 2 * stretch_len, groups, HEAD_SIZE)
    band_vals = band_kv[:, 1].reshape(2, 2 * stretch_len, groups, HEAD_SIZE)

    def attend_head(inputs):
        one_query, one_slash, head_number = inputs
        group_number = head_number // heads_per_group
        keys_col = lax.dynamic_index_in_dim(column_keys, group_number, 0, keepdims=False)
        vals_col = lax.dynamic_index_in_dim(column_vals, group_number, 0, keepdims=False)
        keys_band = lax.dynamic_index_in_dim(band_keys, group_number, 2, keepdims=False)
        vals_band = lax.dynamic_index_in_dim(band_vals, group_number, 2, keepdims=False)
        open_band = lax.dynamic_index_in_dim(band_open, group_number, 0, keepdims=False)
        pos_col = lax.dynamic_index_in_dim(column_position, group_number, 0, keepdims=False)
        flat_query = one_query.reshape(2 * stretch_len, HEAD_SIZE)
        col_scores = (
            jnp.einsum("id,jd->ij", flat_query, keys_col, preferred_element_type=jnp.float32)
            * scale
        )
        col_mask = pos_col[None, :] <= flat_pos[:, None]
        band_scores = (
            jnp.einsum("hid,hjd->hij", one_query, keys_band, preferred_element_type=jnp.float32)
            * scale
        )
        band_mask = one_slash[None] & open_band[:, None, :]
        col_max = jnp.max(jnp.where(col_mask, col_scores, -jnp.inf), axis=1).reshape(2, stretch_len)
        band_max = jnp.max(jnp.where(band_mask, band_scores, -jnp.inf), axis=2)
        row_max = jnp.maximum(col_max, band_max)
        col_exp = jnp.where(
            col_mask, jnp.exp(col_scores - row_max.reshape(2 * stretch_len)[:, None]), 0.0
        )
        band_exp = jnp.where(band_mask, jnp.exp(band_scores - row_max[:, :, None]), 0.0)
        row_total = jnp.sum(col_exp, axis=1).reshape(2, stretch_len) + jnp.sum(band_exp, axis=2)
        weighted = jnp.dot(
            col_exp.astype(jnp.bfloat16), vals_col, preferred_element_type=jnp.float32
        ).reshape(2, stretch_len, HEAD_SIZE)
        weighted = weighted + jnp.einsum(
            "hij,hjd->hid",
            band_exp.astype(jnp.bfloat16),
            vals_band,
            preferred_element_type=jnp.float32,
        )
        return (weighted / row_total[:, :, None]).astype(jnp.bfloat16)

    head_out = lax.map(attend_head, (head_query, slash_ok, jnp.arange(heads, dtype=jnp.int32)))
    attended = head_out.transpose(1, 2, 0, 3).reshape(2, stretch_len, heads * HEAD_SIZE)
    partial_out = jnp.einsum(
        "hic,cd->hid", attended, out_weight, preferred_element_type=jnp.float32
    )
    mixed = lax.psum_scatter(partial_out, "tp", scatter_dimension=2, tiled=True).astype(
        jnp.bfloat16
    )
    return mixed[None]


def solution(mesh):
    in_specs = (
        P("ctx", None, None, "tp"),
        P("ctx", None, None, "tp"),
        P("ctx", None, None, "tp"),
        P("tp", None),
        P("tp", None),
        P("tp", None),
    )
    out_specs = P("ctx", None, None, "tp")
    return jax.shard_map(
        per_device, mesh=mesh, in_specs=in_specs, out_specs=out_specs, check_vma=False
    )
```

profile of v0, /device:TPU:96, one launch (start us, length us, event | category | flops | bytes accessed | tf_op | source)
XLA Modules:
  0.0 332.6 jit_solution(4886587028446778955)
XLA Ops:
  8.8 1.3 fusion.35
  10.1 1.3 compare_and_fusion
  11.4 1.0 pad_maximum_fusion
  13.0 1.4 add_bitcast_fusion.1
  16.1 1.9 collective-permute-start.1
  21.3 0.9 select_bitcast_fusion
  22.2 4.5 %collective-permute-start = (bf16[2,256,128]{2,1,0:T(8,128)(2,1)S(1)}, bf16[2,256,128]{2,1,0:T(8,128)(2,1)}, u32[]{:S(2)}, u32[]{:S(2)}) collective-permute-start(bf16[2,256,128]{2,1,0:T(8,128)(2,1)S(1)} %get-tuple-element.185), channel_id=1, source_target_pairs={{0,4},{4,8},{8,12},{12,16},{16,20},{20,24},{24,28},{28,32},{32,36}... | collective-permute-start | bytes 393224 | tf_op jit(solution)/shard_map/ppermute | solution.py:14
  27.3 1.0 copy.51
  29.9 3.7 %reshape.503 = pred[4,256,767]{2,1,0:T(8,128)(4,1)S(1)} reshape(pred[785408]{0:T(1024)(128)(4,1)S(1)} %reshape.531) | data formatting | bytes 1570816 | tf_op jit(solution)/shard_map/reshape | solution.py:33
  34.3 1.3 copy.34
  36.2 0.9 maximum_maximum_fusion
  37.2 62.7 %all-gather.2.cloned.1.call-done = bf16[1,2,128,128,128]{4,3,1,0,2:T(8,128)(2,1)} async-done(((bf16[1,2,2,128,128]{4,3,1,0,2:T(8,128)(2,1)}), bf16[1,2,128,128,128]{4,3,1,0,2:T(8,128)(2,1)}) %all-gather.2.cloned.1.call-update) | async-done | bytes 8388624 | tf_op jit(solution)/shard_map/all_gather | solution.py:70
  99.9 10.3 %copy.55 = bf16[1,2,128,128,128]{4,3,2,1,0:T(8,128)(2,1)} copy(bf16[1,2,128,128,128]{4,3,1,0,2:T(8,128)(2,1)} %all-gather.2.cloned.1.call-done) | data formatting | bytes 16777216 | tf_op jit(solution)/shard_map/all_gather | solution.py:70
  110.2 6.4 %gather_fusion.1 = bf16[64,2,128,128]{3,2,1,0:T(8,128)(2,1)} fusion(bf16[2,128,128,128]{3,2,1,0:T(8,128)(2,1)} %bitcast.175, s32[1024]{0:T(1024)S(1)} %pad_clamp_fusion), kind=kCustom, calls=%fused_computation.1 | custom fusion | bytes 8388864 | tf_op jit(solution)/shard_map/jit(take_along_axis)/gather | solution.py:72
  116.6 2.6 bitcast_select_fusion
  119.3 2.5 fusion.41
  121.7 112.7 %while.12 = (s32[]{:T(128)}, bf16[4,2,256,128]{2,3,0,1:T(8,128)(2,1)S(1)}, bf16[4,2,256,128]{2,3,0,1:T(8,128)(2,1)S(1)}, bf16[1,8192,128]{2,1,0:T(8,128)(2,1)}, ...) while((s32[]{:T(128)}, ...), condition=%wide.region_12.13_spmd.clone, body=%wide.region_7.12_spmd.clone.sunk | while | flops 2326994944 | bytes 61042056 | solution.py:140
  122.6 8.7 %fusion.62 = (f32[512]{0:T(512)S(1)}, f32[512,8192]{1,0:T(8,128)}) fusion(s32[8192]{0:T(1024)S(1)} %bitcast.176, s32[512]{0:T(512)S(1)} %bitcast.194, bf16[512,128]{1,0:T(8,128)(2,1)S(1)} %bitcast.178, bf16[1,8192,128]{2,1,0:T(8,128)(2,1)} %get-tuple-element.312), kind=kOutput, calls=%fused_computation.6.clone.1 | convolution fusion | flops 1090518528 | bytes 19042304 | tf_op jit(solution)/shard_map/while/body/eval_jaxpr/id,jd->ij/dot_general | solution.py:112
  131.8 11.2 %fusion.64 = (f32[512]{0:T(512)S(1)}, bf16[512,8192]{1,0:T(8,128)(2,1)}) fusion(f32[512,8192]{1,0:T(8,128)} %get-tuple-element.279, f32[512]{0:T(512)S(1)} %max.19, s32[8192]{0:T(1024)S(1)} %bitcast.177, s32[512]{0:T(512)S(1)} %bitcast.195), kind=kLoop, calls=%fused_computation.7.clone.1 | loop fusion | flops 25165312 | bytes 25204736 | tf_op jit(solution)/shard_map/while/body/eval_jaxpr/reduce_sum | solution.py:128
  143.0 6.3 %fusion.65 = f32[2,256,128]{2,1,0:T(8,128)S(1)} fusion(bf16[2,256,8192]{2,1,0:T(8,128)(2,1)} %bitcast.174, bf16[1,8192,128]{2,1,0:T(8,128)(2,1)} %get-tuple-element.316), kind=kOutput, calls=%fused_computation.9.clone.1 | convolution fusion | flops 1073741824 | bytes 10747904 | tf_op jit(solution)/shard_map/while/body/eval_jaxpr/dot_general | solution.py:129
  150.8 8.7 %fusion.62 = (f32[512]{0:T(512)S(1)}, f32[512,8192]{1,0:T(8,128)}) fusion(s32[8192]{0:T(1024)S(1)} %bitcast.176, s32[512]{0:T(512)S(1)} %bitcast.194, bf16[512,128]{1,0:T(8,128)(2,1)S(1)} %bitcast.178, bf16[1,8192,128]{2,1,0:T(8,128)(2,1)} %get-tuple-element.312), kind=kOutput, calls=%fused_computation.6.clone.1 | convolution fusion | flops 1090518528 | bytes 19042304 | tf_op jit(solution)/shard_map/while/body/eval_jaxpr/id,jd->ij/dot_general | solution.py:112
  159.9 11.2 %fusion.64 = (f32[512]{0:T(512)S(1)}, bf16[512,8192]{1,0:T(8,128)(2,1)}) fusion(f32[512,8192]{1,0:T(8,128)} %get-tuple-element.279, f32[512]{0:T(512)S(1)} %max.19, s32[8192]{0:T(1024)S(1)} %bitcast.177, s32[512]{0:T(512)S(1)} %bitcast.195), kind=kLoop, calls=%fused_computation.7.clone.1 | loop fusion | flops 25165312 | bytes 25204736 | tf_op jit(solution)/shard_map/while/body/eval_jaxpr/reduce_sum | solution.py:128
  171.2 6.3 %fusion.65 = f32[2,256,128]{2,1,0:T(8,128)S(1)} fusion(bf16[2,256,8192]{2,1,0:T(8,128)(2,1)} %bitcast.174, bf16[1,8192,128]{2,1,0:T(8,128)(2,1)} %get-tuple-element.316), kind=kOutput, calls=%fused_computation.9.clone.1 | convolution fusion | flops 1073741824 | bytes 10747904 | tf_op jit(solution)/shard_map/while/body/eval_jaxpr/dot_general | solution.py:129
  179.0 8.7 %fusion.62 = (f32[512]{0:T(512)S(1)}, f32[512,8192]{1,0:T(8,128)}) fusion(s32[8192]{0:T(1024)S(1)} %bitcast.176, s32[512]{0:T(512)S(1)} %bitcast.194, bf16[512,128]{1,0:T(8,128)(2,1)S(1)} %bitcast.178, bf16[1,8192,128]{2,1,0:T(8,128)(2,1)} %get-tuple-element.312), kind=kOutput, calls=%fused_computation.6.clone.1 | convolution fusion | flops 1090518528 | bytes 19042304 | tf_op jit(solution)/shard_map/while/body/eval_jaxpr/id,jd->ij/dot_general | solution.py:112
  188.1 11.2 %fusion.64 = (f32[512]{0:T(512)S(1)}, bf16[512,8192]{1,0:T(8,128)(2,1)}) fusion(f32[512,8192]{1,0:T(8,128)} %get-tuple-element.279, f32[512]{0:T(512)S(1)} %max.19, s32[8192]{0:T(1024)S(1)} %bitcast.177, s32[512]{0:T(512)S(1)} %bitcast.195), kind=kLoop, calls=%fused_computation.7.clone.1 | loop fusion | flops 25165312 | bytes 25204736 | tf_op jit(solution)/shard_map/while/body/eval_jaxpr/reduce_sum | solution.py:128
  199.4 6.3 %fusion.65 = f32[2,256,128]{2,1,0:T(8,128)S(1)} fusion(bf16[2,256,8192]{2,1,0:T(8,128)(2,1)} %bitcast.174, bf16[1,8192,128]{2,1,0:T(8,128)(2,1)} %get-tuple-element.316), kind=kOutput, calls=%fused_computation.9.clone.1 | convolution fusion | flops 1073741824 | bytes 10747904 | tf_op jit(solution)/shard_map/while/body/eval_jaxpr/dot_general | solution.py:129
  207.2 8.7 %fusion.62 = (f32[512]{0:T(512)S(1)}, f32[512,8192]{1,0:T(8,128)}) fusion(s32[8192]{0:T(1024)S(1)} %bitcast.176, s32[512]{0:T(512)S(1)} %bitcast.194, bf16[512,128]{1,0:T(8,128)(2,1)S(1)} %bitcast.178, bf16[1,8192,128]{2,1,0:T(8,128)(2,1)} %get-tuple-element.312), kind=kOutput, calls=%fused_computation.6.clone.1 | convolution fusion | flops 1090518528 | bytes 19042304 | tf_op jit(solution)/shard_map/while/body/eval_jaxpr/id,jd->ij/dot_general | solution.py:112
  216.3 11.2 %fusion.64 = (f32[512]{0:T(512)S(1)}, bf16[512,8192]{1,0:T(8,128)(2,1)}) fusion(f32[512,8192]{1,0:T(8,128)} %get-tuple-element.279, f32[512]{0:T(512)S(1)} %max.19, s32[8192]{0:T(1024)S(1)} %bitcast.177, s32[512]{0:T(512)S(1)} %bitcast.195), kind=kLoop, calls=%fused_computation.7.clone.1 | loop fusion | flops 25165312 | bytes 25204736 | tf_op jit(solution)/shard_map/while/body/eval_jaxpr/reduce_sum | solution.py:128
  227.6 6.3 %fusion.65 = f32[2,256,128]{2,1,0:T(8,128)S(1)} fusion(bf16[2,256,8192]{2,1,0:T(8,128)(2,1)} %bitcast.174, bf16[1,8192,128]{2,1,0:T(8,128)(2,1)} %get-tuple-element.316), kind=kOutput, calls=%fused_computation.9.clone.1 | convolution fusion | flops 1073741824 | bytes 10747904 | tf_op jit(solution)/shard_map/while/body/eval_jaxpr/dot_general | solution.py:129
  234.4 7.8 %fusion.26 = f32[2,256,4096]{2,1,0:T(8,128)} fusion(bf16[2,256,512]{1,2,0:T(8,128)(2,1)S(1)} %bitcast.193, bf16[512,4096]{1,0:T(8,128)(2,1)} %param.13), kind=kOutput, calls=%fused_computation.38 | convolution fusion | flops 2147483648 | bytes 13107200 | tf_op jit(solution)/shard_map/hic,cd->hid/dot_general | solution.py:142
  242.2 80.8 %reduce-scatter.2.cloned.1.call-done = f32[2,256,1024]{2,1,0:T(8,128)} async-done(((f32[2,256,4096]{2,1,0:T(8,128)}), f32[2,256,1024]{2,1,0:T(8,128)}) %reduce-scatter.2.cloned.1.call-update) | async-done | bytes 2097168 | tf_op jit(solution)/shard_map/reduce_scatter | solution.py:145
  323.1 2.7 convert_bitcast_fusion
  (112 shorter events, 18.8 us)
Async XLA Ops:
  6.5 29.7 %copy-start.1 = (bf16[1,2,256,128]{3,2,1,0:T(8,128)(2,1)S(1)}, bf16[1,2,256,128]{3,2,1,0:T(8,128)(2,1)}, u32[]{:S(2)}) copy-start(bf16[1,2,256,128]{3,2,1,0:T(8,128)(2,1)} %param.9) | copy-start | bytes 393220
  6.5 29.7 %copy-start = (bf16[1,2,256,128]{3,2,1,0:T(8,128)(2,1)S(1)}, bf16[1,2,256,128]{3,2,1,0:T(8,128)(2,1)}, u32[]{:S(2)}) copy-start(bf16[1,2,256,128]{3,2,1,0:T(8,128)(2,1)} %param.10) | copy-start | bytes 393220
  6.5 93.4 %all-gather.2.cloned.1.call-start = ((), (), s32[]{:S(2)}) async-start(), calls=%async_computation.1 | async-start | bytes 8519680 | tf_op jit(solution)/shard_map/all_gather | solution.py:70
  15.1 307.9 %reduce-scatter.2.cloned.1.call-start = ((), (), s32[]{:S(2)}) async-start(), calls=%async_computation.2 | async-start | bytes 10485760 | tf_op jit(solution)/shard_map/reduce_scatter | solution.py:145
  16.1 5.2 %collective-permute-start.1 = (bf16[2,256,128]{2,1,0:T(8,128)(2,1)S(1)}, bf16[2,256,128]{2,1,0:T(8,128)(2,1)S(1)}, u32[]{:S(2)}, u32[]{:S(2)}) collective-permute-start(bf16[2,256,128]{2,1,0:T(8,128)(2,1)S(1)} %fusion.30), channel_id=1, source_target_pairs={{4,0},{8,4},{12,8},{16,12},{20,16},{24,20},{28,24},{32,28},{36,32}... | collective-permute-start | bytes 393224 | tf_op jit(solution)/shard_map/ppermute | solution.py:14
  22.2 14.0 %collective-permute-start = (bf16[2,256,128]{2,1,0:T(8,128)(2,1)S(1)}, bf16[2,256,128]{2,1,0:T(8,128)(2,1)}, u32[]{:S(2)}, u32[]{:S(2)}) collective-permute-start(bf16[2,256,128]{2,1,0:T(8,128)(2,1)S(1)} %get-tuple-element.185), channel_id=1, source_target_pairs={{0,4},{4,8},{8,12},{12,16},{16,20},{20,24},{24,28},{28,32},{32,36}... | collective-permute-start | bytes 393224 | tf_op jit(solution)/shard_map/ppermute | solution.py:14
  110.2 6.4 %copy-start.2 = (pred[64]{0:T(512)(128)(4,1)S(1)}, pred[64]{0:T(512)(128)(4,1)}, u32[]{:S(2)}) copy-start(pred[64]{0:T(512)(128)(4,1)} %compare_and_fusion.3) | copy-start | bytes 196
Sparse Core Ops, SparseCore 0:
  15.3 84.6 all-gather.1
  242.4 80.6 reduce-scatter.1
where the time goes:
time: 335 us; the launch traced here: 333 us
  waiting for transfers between devices  144 us (43%)
  matrix products  71.3 us (21%)
  other arithmetic  67.9 us (20%)
  local copies, waits for them, and re-layouts  29.5 us (9%)
  between operations  13.6 us (4%)
  starting transfers between devices  6.49 us (2%)
    reduce_scatter x1, waiting for transfers between devices, per_device(): lax.psum_scatter(partial_out, 'tp', scatter_dimension=2, tiled=True)  80.8 us
    all_gather x1, waiting for transfers between devices, per_device(): arrived = lax.all_gather(outgoing, 'ctx', axis=2, tiled=True)  62.7 us
    reduce_sum x4, other arithmetic, attend_head(): jnp.sum(col_exp, axis=1).reshape(2, stretch_len) + jnp.sum(band_exp, axis=2)  45 us
    dot_general x4, matrix products, attend_head(): jnp.einsum('id,jd->ij', flat_query, keys_col, preferred_element_type=jnp....  34.7 us
    dot_general x4, matrix products, attend_head(): jnp.dot(col_exp.astype(jnp.bfloat16), vals_col, preferred_element_type=jn...  25.2 us
    all_gather x1, local copies, waits for them, and re-layouts, per_device(): arrived = lax.all_gather(outgoing, 'ctx', axis=2, tiled=True)  10.3 us
    dot_general x1, matrix products, per_device(): jnp.einsum('hic,cd->hid', attended, out_weight, preferred_element_type=jn...  7.79 us
  transfers between devices with their start and end apart: 4, of which 2 were waited for; matrix products, arithmetic and copies ran while one was open for 5% of the time, Pallas kernels for 0%

commit v1 on v0

v1 whole, which is shorter than its diff:
```python
import functools
import math

import jax
import jax.numpy as jnp
from jax import lax
from jax.experimental import pallas as pl
from jax.experimental.pallas import tpu as pltpu
from jax.sharding import PartitionSpec as P

HEAD = 128
BLOCK = 128
STRETCH = 256
CAP = 2
GROUP = 4
SPAN = GROUP * BLOCK
LISTED = 64
HEADS = 4
EXP_SCALE = math.log2(math.e) * HEAD ** (-0.5)
VMEM_LIMIT = 48 * 1024 * 1024

SMEM = functools.partial(pl.BlockSpec, memory_space=pltpu.SMEM)
VMEM = functools.partial(pl.BlockSpec, memory_space=pltpu.VMEM)
ANY = functools.partial(pl.BlockSpec, memory_space=pl.ANY)
PARAMS = pltpu.CompilerParams(vmem_limit_bytes=VMEM_LIMIT)
F32 = jnp.float32
BF16 = jnp.bfloat16


def dot_t(a, b):
    return lax.dot_general(a, b, (((1,), (1,)), ((), ())), preferred_element_type=F32)


def plan_kernel(ctx_count, me_ref, table_ref, k_ref, v_ref, pay_ref, ahead_ref, back_ref, blk_ref, ent_ref, meta_ref, count, place):
    me = me_ref[0]
    stretches = 2 * ctx_count
    near, far = me, stretches - 1 - me

    def clear(i, _):
        place[4 * i] = -1
        place[4 * i + 1] = -1
        place[4 * i + 2] = -1
        place[4 * i + 3] = -1
        count[i] = 0
        return 0

    lax.fori_loop(0, ctx_count, clear, 0)

    def assign(j, carry):
        loc0, loc1 = carry
        b = table_ref[0, j]
        stretch = b // 2
        first = stretch < ctx_count
        owner = jnp.where(first, stretch, stretches - 1 - stretch)
        local = jnp.where(first, 0, 2) + b % 2
        rank = count[owner]
        count[owner] = rank + 1
        place[b] = owner * CAP + rank
        mine = owner == me
        loc0 = jnp.where(mine & (rank == 0), local, loc0)
        loc1 = jnp.where(mine & (rank == 1), local, loc1)
        return loc0, loc1

    loc0, loc1 = lax.fori_loop(0, LISTED, assign, (jnp.int32(0), jnp.int32(0)))
    for slot, loc in enumerate((loc0, loc1)):
        pay_ref[slot, 0] = k_ref[loc]
        pay_ref[slot, 1] = v_ref[loc]
    for half, ref in ((0, ahead_ref), (1, back_ref)):
        for part in range(2):
            ref[0, part * BLOCK : (part + 1) * BLOCK] = k_ref[2 * half + part]
            ref[1, part * BLOCK : (part + 1) * BLOCK] = v_ref[2 * half + part]

    def order(b, carry):
        at, full0, seen0, full1, seen1 = carry
        e = place[b]
        blk_ref[at] = b
        ent_ref[at] = e
        hit = jnp.where(e >= 0, 1, 0)
        one = lambda test: jnp.where(test, hit, 0)
        return (
            at + hit,
            full0 + one(b < 2 * near),
            seen0 + one(b <= 2 * near + 1),
            full1 + one(b < 2 * far),
            seen1 + one(b <= 2 * far + 1),
        )

    zero = jnp.int32(0)
    _, full0, seen0, full1, seen1 = lax.fori_loop(0, 4 * ctx_count, order, (zero,) * 5)
    for st, (s, full, seen) in enumerate(((near, full0, seen0), (far, full1, seen1))):
        meta_ref[8 * st] = full
        meta_ref[8 * st + 1] = seen
        meta_ref[8 * st + 2] = s
        meta_ref[8 * st + 3] = me
        for n in range(4):
            b = 2 * (s - 1) + n
            free = place[jnp.maximum(b, 0)] < 0
            meta_ref[8 * st + 4 + n] = jnp.where((b >= 0) & free, 1, 0)


def band_halves(own_ref, ahead_ref, back_ref, which, st, me, ctx_count):
    if st == 0:
        return ahead_ref[which]
    return jnp.where(me == ctx_count - 1, own_ref[0], back_ref[which])


def band_kernel(ctx_count, meta_ref, slash_ref, q_ref, k_ref, ahead_ref, back_ref, mask_ref, top_ref):
    behind = STRETCH - lax.broadcasted_iota(jnp.int32, (8, 2 * STRETCH), 1)
    for h in range(HEADS):
        def listed(n, hit):
            return hit | (behind == slash_ref[h, n])

        hit = behind == 0
        for n in range(LISTED):
            hit = listed(n, hit)
        row = jnp.where(hit, 1.0, 0.0).astype(F32)[:1]
        spread = jnp.broadcast_to(row, (STRETCH, 2 * STRETCH))
        mask_ref[h] = pltpu.roll(spread, 0, 1, stride=1, stride_axis=0)
    me = meta_ref[3]
    for st in range(2):
        before = band_halves(k_ref, ahead_ref, back_ref, 0, st, me, ctx_count)
        for h in range(HEADS):
            q = q_ref[st, :, h * HEAD : (h + 1) * HEAD]
            top = jnp.full((STRETCH, BLOCK), -jnp.inf, F32)
            for n in range(4):
                part = before if n < 2 else k_ref[st]
                s = dot_t(q, part[(n % 2) * BLOCK : (n % 2 + 1) * BLOCK])
                ok = (mask_ref[h, :, n * BLOCK : (n + 1) * BLOCK] > 0.5) & (meta_ref[8 * st + 4 + n] > 0)
                top = jnp.maximum(top, jnp.where(ok, s, -jnp.inf))
            top_ref[st, h] = top


def fetch(ent_ref, source_ref, which, target_ref, sems, groups):
    def start(j, _):
        e = ent_ref[j]
        pltpu.make_async_copy(source_ref.at[e // CAP, e % CAP, which], target_ref.at[j], sems.at[j // GROUP]).start()
        return 0

    lax.fori_loop(0, groups * GROUP, start, 0)


def arrived(target_ref, sems, g):
    part = target_ref.at[pl.ds(g * GROUP, GROUP)]
    pltpu.make_async_copy(part, part, sems.at[g]).wait()


def causal(blk_ref, s, g):
    lead = lax.broadcasted_iota(jnp.int32, (STRETCH, BLOCK), 1) - lax.broadcasted_iota(jnp.int32, (STRETCH, BLOCK), 0)
    return [lead <= s * STRETCH - blk_ref[g * GROUP + n] * BLOCK for n in range(GROUP)]


def top_kernel(meta_ref, blk_ref, ent_ref, q_ref, top_in_ref, source_ref, keys_ref, top_ref, sems):
    fetch(ent_ref, source_ref, 0, keys_ref, sems, LISTED // GROUP)

    def ready(g, _):
        arrived(keys_ref, sems, g)
        return 0

    lax.fori_loop(0, LISTED // GROUP, ready, 0)
    for st in range(2):
        full, seen, s = meta_ref[8 * st], meta_ref[8 * st + 1], meta_ref[8 * st + 2]
        plain, groups = full // GROUP, (seen + GROUP - 1) // GROUP
        for h in range(HEADS):
            top_ref[st, h] = top_in_ref[st, h]

        def step(masked, g, _):
            keys = keys_ref[pl.ds(g * GROUP, GROUP)].reshape(SPAN, HEAD)
            ok = causal(blk_ref, s, g) if masked else None
            for h in range(HEADS):
                scores = dot_t(q_ref[st, :, h * HEAD : (h + 1) * HEAD], keys)
                tops = []
                for n in range(GROUP):
                    part = scores[:, n * BLOCK : (n + 1) * BLOCK]
                    tops.append(jnp.where(ok[n], part, -jnp.inf) if masked else part)
                top = functools.reduce(jnp.maximum, tops)
                top_ref[st, h] = jnp.maximum(top_ref[st, h], top)
            return 0

        lax.fori_loop(0, plain, functools.partial(step, False), 0)
        lax.fori_loop(plain, groups, functools.partial(step, True), 0)
        for h in range(HEADS):
            row = jnp.max(top_ref[st, h], axis=1, keepdims=True)
            top_ref[st, h] = jnp.broadcast_to(row, (STRETCH, BLOCK))


def out_kernel(ctx_count, st, meta_ref, blk_ref, ent_ref, q_ref, keys_ref, top_ref, mask_ref, k_ref, v_ref, ahead_ref, back_ref, source_ref, out_ref, vals, total, acc, sems):
    full, seen, s = meta_ref[8 * st], meta_ref[8 * st + 1], meta_ref[8 * st + 2]
    me = meta_ref[8 * st + 3]
    plain, groups = full // GROUP, (seen + GROUP - 1) // GROUP
    fetch(ent_ref, source_ref, 1, vals, sems, groups)
    k_before = band_halves(k_ref, ahead_ref, back_ref, 0, st, me, ctx_count)
    v_before = band_halves(v_ref, ahead_ref, back_ref, 1, st, me, ctx_count)

    for h in range(HEADS):
        q = q_ref[0, :, h * HEAD : (h + 1) * HEAD]
        scores = [dot_t(q, k_before), dot_t(q, k_ref[st])]
        expos = []
        for n in range(4):
            part = scores[n // 2][:, (n % 2) * BLOCK : (n % 2 + 1) * BLOCK]
            ok = (mask_ref[h, :, n * BLOCK : (n + 1) * BLOCK] > 0.5) & (meta_ref[8 * st + 4 + n] > 0)
            expos.append(jnp.where(ok, jnp.exp2((part - top_ref[0, h]) * EXP_SCALE), 0.0))
        total[h] = (expos[0] + expos[1]) + (expos[2] + expos[3])
        weights = [e.astype(BF16) for e in expos]
        acc[h] = jnp.dot(
            jnp.concatenate(weights[:2], axis=1), v_before, preferred_element_type=F32
        ) + jnp.dot(jnp.concatenate(weights[2:], axis=1), v_ref[st], preferred_element_type=F32)

    def step(masked, g, _):
        arrived(vals, sems, g)
        keys = keys_ref[pl.ds(g * GROUP, GROUP)].reshape(SPAN, HEAD)
        values = vals[pl.ds(g * GROUP, GROUP)].reshape(SPAN, HEAD)
        ok = causal(blk_ref, s, g) if masked else None
        for h in range(HEADS):
            scores = dot_t(q_ref[0, :, h * HEAD : (h + 1) * HEAD], keys)
            expos = []
            for n in range(GROUP):
                part = jnp.exp2((scores[:, n * BLOCK : (n + 1) * BLOCK] - top_ref[0, h]) * EXP_SCALE)
                expos.append(jnp.where(ok[n], part, 0.0) if masked else part)
            total[h] += (expos[0] + expos[1]) + (expos[2] + expos[3])
            weights = jnp.concatenate([e.astype(BF16) for e in expos], axis=1)
            acc[h] += jnp.dot(weights, values, preferred_element_type=F32)
        return 0

    lax.fori_loop(0, plain, functools.partial(step, False), 0)
    lax.fori_loop(plain, groups, functools.partial(step, True), 0)
    for h in range(HEADS):
        row = jnp.sum(total[h], axis=1, keepdims=True)
        out_ref[:, h * HEAD : (h + 1) * HEAD] = (acc[h] / row).astype(BF16)


def mix_kernel(a0, a1, a2, a3, w0, w1, w2, w3, *refs):
    out_ref = refs[-1]
    sums = [jnp.dot(a[...], w[...], preferred_element_type=F32) for a, w in ((a0, w0), (a1, w1), (a2, w2), (a3, w3))]
    out_ref[0] = ((sums[0] + sums[1]) + (sums[2] + sums[3])).astype(BF16)


def from_ahead(x, axis, shift):
    n = lax.axis_size(axis)
    return lax.ppermute(x, axis, [((i + shift) % n, i) for i in range(n)])


def per_device(queries, keys, values, column_block_table, slash_offsets, out_weight):
    ctx_count = lax.axis_size("ctx")
    tp = lax.axis_size("tp")
    me = lax.axis_index("ctx")
    tp_index = lax.axis_index("tp")
    q, k, v = queries[0], keys[0], values[0]
    shape = jax.ShapeDtypeStruct
    i32 = jnp.int32

    pay, ahead, back, blk, ent, meta = pl.pallas_call(
        functools.partial(plan_kernel, ctx_count),
        out_shape=[
            shape((CAP, 2, BLOCK, HEAD), BF16),
            shape((2, STRETCH, HEAD), BF16),
            shape((2, STRETCH, HEAD), BF16),
            shape((128,), i32),
            shape((128,), i32),
            shape((16,), i32),
        ],
        in_specs=[SMEM(), SMEM(), VMEM(), VMEM()],
        out_specs=[VMEM(), VMEM(), VMEM(), SMEM(), SMEM(), SMEM()],
        scratch_shapes=[pltpu.SMEM((ctx_count,), i32), pltpu.SMEM((4 * ctx_count,), i32)],
        compiler_params=PARAMS,
        name="plan",
    )(me.reshape(1).astype(i32), column_block_table, k.reshape(4, BLOCK, HEAD), v.reshape(4, BLOCK, HEAD))

    source = lax.all_gather(pay, "ctx", axis=0)

    steps = range(ctx_count - 1)
    before = lax.ppermute(ahead, "ctx", [(i, i + 1) for i in steps])
    after = lax.ppermute(back, "ctx", [(i + 1, i) for i in steps])

    width = out_weight.shape[1] // tp
    slabs = []
    for shift in range(tp):
        target = lax.rem(tp_index + tp - shift, tp)
        slab = lax.dynamic_slice(out_weight, (0, target * width), (out_weight.shape[0], width))
        slabs.append(slab if shift == 0 else from_ahead(slab, "tp", shift))

    mask, top = pl.pallas_call(
        functools.partial(band_kernel, ctx_count),
        out_shape=[shape((HEADS, STRETCH, 2 * STRETCH), F32), shape((2, HEADS, STRETCH, BLOCK), F32)],
        in_specs=[SMEM(), SMEM(), VMEM(), VMEM(), VMEM(), VMEM()],
        out_specs=[VMEM(), VMEM()],
        compiler_params=PARAMS,
        name="band",
    )(meta, slash_offsets, q, k, before, after)

    columns, top = pl.pallas_call(
        top_kernel,
        out_shape=[shape((LISTED, BLOCK, HEAD), BF16), shape((2, HEADS, STRETCH, BLOCK), F32)],
        in_specs=[SMEM(), SMEM(), SMEM(), VMEM(), VMEM(), ANY()],
        out_specs=[VMEM(), VMEM()],
        scratch_shapes=[pltpu.SemaphoreType.DMA((LISTED // GROUP,))],
        compiler_params=PARAMS,
        name="top",
    )(meta, blk, ent, q, top, source)

    mixed = None
    for st in range(2):
        head_out = pl.pallas_call(
            functools.partial(out_kernel, ctx_count, st),
            grid=(1,),
            out_shape=shape((STRETCH, HEADS * HEAD), BF16),
            in_specs=[
                SMEM(), SMEM(), SMEM(),
                pl.BlockSpec((1, STRETCH, HEADS * HEAD), lambda i, st=st: (st, 0, 0)),
                VMEM(),
                pl.BlockSpec((1, HEADS, STRETCH, BLOCK), lambda i, st=st: (st, 0, 0, 0)),
                VMEM(), VMEM(), VMEM(), VMEM(), VMEM(), ANY(),
            ],
            out_specs=VMEM(),
            scratch_shapes=[
                pltpu.VMEM((LISTED, BLOCK, HEAD), BF16),
                pltpu.VMEM((HEADS, STRETCH, BLOCK), F32),
                pltpu.VMEM((HEADS, STRETCH, HEAD), F32),
                pltpu.SemaphoreType.DMA((LISTED // GROUP,)),
            ],
            compiler_params=PARAMS,
            name=f"attend{st}",
        )(meta, blk, ent, q, columns, top, mask, k, v, before, after, source)
        parts = [head_out] + [from_ahead(head_out, "tp", shift) for shift in range(1, tp)]
        mixed = pl.pallas_call(
            mix_kernel,
            grid=(1,),
            out_shape=shape((2, STRETCH, width), BF16),
            in_specs=[VMEM()] * 8 + ([ANY()] if st else []),
            out_specs=pl.BlockSpec((1, STRETCH, width), lambda i, st=st: (st, 0, 0)),
            input_output_aliases={8: 0} if st else {},
            compiler_params=PARAMS,
            name=f"mix{st}",
        )(*parts, *slabs, *([mixed] if st else []))
    return mixed[None]


def solution(mesh):
    in_specs = (
        P("ctx", None, None, "tp"),
        P("ctx", None, None, "tp"),
        P("ctx", None, None, "tp"),
        P("tp", None),
        P("tp", None),
        P("tp", None),
    )
    out_specs = P("ctx", None, None, "tp")
    return jax.shard_map(
        per_device, mesh=mesh, in_specs=in_specs, out_specs=out_specs, check_vma=False
    )
```

time: 335 us -> 175 us (0.52)
  matrix products: 71.3 us -> 0 us
  other arithmetic: 67.9 us -> 0 us
  waiting for transfers between devices: 144 us -> 76.4 us
  Pallas kernels: 0 us -> 53.5 us
  local copies, waits for them, and re-layouts: 29.5 us -> 10.2 us
  starting transfers between devices: 6.49 us -> 19.9 us
    reduce_scatter x1 -> x0, waiting for transfers between devices: 80.8 us -> none  [per_device(): lax.psum_scatter(partial_out, 'tp', scatter_dimension=2, tiled=True)]
    dot_general x17 -> x0, matrix products: 71.3 us -> none  [the longest x4 34.7 us: attend_head(): jnp.einsum('id,jd->ij', flat_query, keys_col, preferred_element_type=jnp....]
    pallas_call x0 -> x7, Pallas kernels: none -> 53.5 us  [the longest x2 27.2 us: per_device(): pl.pallas_call(functools.partial(out_kernel, ctx_count, st), grid=(1,), o...]
    reduce_sum x10 -> x0, other arithmetic: 47.5 us -> none  [the longest x4 45 us: attend_head(): jnp.sum(col_exp, axis=1).reshape(2, stretch_len) + jnp.sum(band_exp, axis=2)]
    ppermute x2 -> x11, starting transfers between devices: 6.44 us -> 19.9 us  [the longest x9 14.4 us: from_ahead(): return lax.ppermute(x, axis, [((i + shift) % n, i) for i in range(n)])]
    ppermute x2 -> x11, waiting for transfers between devices: 0.01 us -> 13.3 us  [the longest x9 10.8 us: from_ahead(): return lax.ppermute(x, axis, [((i + shift) % n, i) for i in range(n)])]
    all_gather x1 -> x0, local copies, waits for them, and re-layouts: 10.3 us -> none  [per_device(): arrived = lax.all_gather(outgoing, 'ctx', axis=2, tiled=True)]
    gather x2 -> x0, local copies, waits for them, and re-layouts: 6.96 us -> none  [the longest x1 6.39 us: per_device(): jnp.take_along_axis(arrived, slot_index[:, None, :, None, None], axis=2)]
  transfers between devices with their start and end apart: 4 -> 12, of which waited for: 2 -> 5; matrix products, arithmetic and copies ran while one was open for 5% -> 2% of each run, Pallas kernels for 0% -> 25%
where the time goes in v1:
time: 175 us; the launch traced here: 173 us
  waiting for transfers between devices  76.4 us (44%)
  Pallas kernels  53.5 us (31%)
  starting transfers between devices  19.9 us (11%)
  between operations  13.5 us (8%)
  local copies, waits for them, and re-layouts  10.2 us (6%)
    all_gather x1, waiting for transfers between devices, per_device(): source = lax.all_gather(pay, 'ctx', axis=0)  63.1 us
    pallas_call x2, Pallas kernels, per_device(): pl.pallas_call(functools.partial(out_kernel, ctx_count, st), grid=(1,), o...  27.2 us
    ppermute x9, starting transfers between devices, from_ahead(): return lax.ppermute(x, axis, [((i + shift) % n, i) for i in range(n)])  14.4 us
    pallas_call x1, Pallas kernels, per_device(): pl.pallas_call(top_kernel, out_shape=[shape((LISTED, BLOCK, HEAD), BF16),...  11 us
    ppermute x9, waiting for transfers between devices, from_ahead(): return lax.ppermute(x, axis, [((i + shift) % n, i) for i in range(n)])  10.8 us
    pallas_call x2, Pallas kernels, per_device(): pl.pallas_call(mix_kernel, grid=(1,), out_shape=shape((2, STRETCH, width)...  7.21 us
    pallas_call x1, Pallas kernels, per_device(): pl.pallas_call(functools.partial(plan_kernel, ctx_count), out_shape=[shap...  6.17 us
    unnamed x20, local copies, waits for them, and re-layouts  6.06 us
  transfers between devices with their start and end apart: 12, of which 5 were waited for; matrix products, arithmetic and copies ran while one was open for 2% of the time, Pallas kernels for 25%

profile of v1, /device:TPU:96, one launch (start us, length us, event | category | flops | bytes accessed | tf_op | source)
XLA Modules:
  0.0 173.5 jit_solution(12907326893015333971)
XLA Ops:
  6.5 0.9 copy-done.2
  7.4 0.9 copy-done.4
  8.3 0.7 copy-done.9
  9.0 6.2 %plan.1 = (bf16[2,2,128,128]{3,2,1,0:T(8,128)(2,1)}, bf16[2,256,128]{2,1,0:T(8,128)(2,1)S(1)}, bf16[2,256,128]{2,1,0:T(8,128)(2,1)S(1)}, s32[128]{0:T(128)S(1)}, s32[128]{0:T(128)S(1)}, /*index=5*/s32[16]{0:T(128)S(1)}) custom-call(s32[1]{0:T(128)} %bitcast.me_ref, s32[1,64]{1,0:T(1,128)S(1)} %copy-done.9, bf16[4,128,128]{2,1,0:T(8,128)(2,1)S(1)} %bitcast.12, ...), custom_call_target="tpu_custom_call" | custom-call | tf_op jit(solution)/shard_map/plan/pallas_call | solution.py:251
  15.2 0.0 all-gather.3.cloned.1.call-update
  15.2 0.0 copy-start.1
  15.3 4.1 %constant_dynamic-slice_fusion = (bf16[512,1024]{1,0:T(8,128)(2,1)}, bf16[512,1024]{1,0:T(8,128)(2,1)}, bf16[512,1024]{1,0:T(8,128)(2,1)S(1)}, bf16[512,1024]{1,0:T(8,128)(2,1)}) fusion(bf16[512,4096]{1,0:T(8,128)(2,1)} %param.11, s32[]{:T(128)S(6)} %select_n.15, s32[]{:T(128)S(6)} %select_n.13, s32[]{:T(128)S(6)} %select_n.12, s32[]{:T(128)S(6)} %select_n.14), kind=kLoop, calls=%fused_computation | loop fusion | bytes 8388624 | tf_op jit(solution)/shard_map/dynamic_slice | solution.py:278
  19.4 1.6 collective-permute-start.7
  20.9 1.7 collective-permute-start.5
  22.6 2.0 %collective-permute-start.6 = (bf16[512,1024]{1,0:T(8,128)(2,1)}, bf16[512,1024]{1,0:T(8,128)(2,1)}, u32[]{:S(2)}, u32[]{:S(2)}) collective-permute-start(bf16[512,1024]{1,0:T(8,128)(2,1)} %get-tuple-element.28), channel_id=1, source_target_pairs={{2,0},{3,1},{0,2},{1,3},{6,4},{7,5},{4,6},{5,7},{10,8},{11,9},{8,1... | collective-permute-start | bytes 3145736 | tf_op jit(solution)/shard_map/ppermute | solution.py:239
  24.6 1.9 %collective-permute-start = (bf16[2,256,128]{2,1,0:T(8,128)(2,1)S(1)}, bf16[2,256,128]{2,1,0:T(8,128)(2,1)S(1)}, u32[]{:S(2)}, u32[]{:S(2)}) collective-permute-start(bf16[2,256,128]{2,1,0:T(8,128)(2,1)S(1)} %get-tuple-element.18), channel_id=1, source_target_pairs={{0,4},{4,8},{8,12},{12,16},{16,20},{20,24},{24,28},{28,32},{32,36}... | collective-permute-start | bytes 393224 | tf_op jit(solution)/shard_map/ppermute | solution.py:271
  26.5 3.6 %collective-permute-start.1 = (bf16[2,256,128]{2,1,0:T(8,128)(2,1)S(1)}, bf16[2,256,128]{2,1,0:T(8,128)(2,1)S(1)}, u32[]{:S(2)}, u32[]{:S(2)}) collective-permute-start(bf16[2,256,128]{2,1,0:T(8,128)(2,1)S(1)} %get-tuple-element.19), channel_id=1, source_target_pairs={{4,0},{8,4},{12,8},{16,12},{20,16},{24,20},{28,24},{32,28},{36,32}... | collective-permute-start | bytes 393224 | tf_op jit(solution)/shard_map/ppermute | solution.py:272
  30.1 0.7 collective-permute-done.ahead_ref
  30.9 1.8 %collective-permute-done.1.back_ref = bf16[2,256,128]{2,1,0:T(8,128)(2,1)S(1)} collective-permute-done((bf16[2,256,128]{2,1,0:T(8,128)(2,1)S(1)}, bf16[2,256,128]{2,1,0:T(8,128)(2,1)S(1)}, u32[]{:S(2)}, u32[]{:S(2)}) %collective-permute-start.1) | collective-permute-done | bytes 131104 | tf_op jit(solution)/shard_map/ppermute | solution.py:272
  32.7 1.9 %band.1 = (f32[4,256,512]{2,1,0:T(8,128)S(1)}, f32[2,4,256,128]{3,2,1,0:T(8,128)S(1)}) custom-call(s32[16]{0:T(128)S(1)} %get-tuple-element.15.meta_ref, s32[4,64]{1,0:T(4,128)S(1)} %copy-done.8, bf16[2,256,512]{2,1,0:T(8,128)(2,1)S(1)} %bitcast.8, bf16[2,256,128]{2,1,0:T(8,128)(2,1)S(1)} %bitcast.13, ...), custom_call_target="tpu_custom_call" | custom-call | tf_op jit(solution)/shard_map/band/pallas_call | solution.py:281
  34.6 1.4 copy-done
  35.9 1.0 copy-done.6
  36.9 63.1 %all-gather.3.cloned.1.call-done = bf16[128,2,128,128]{3,2,1,0:T(8,128)(2,1)} async-done(((bf16[2,2,128,128]{3,2,1,0:T(8,128)(2,1)}), bf16[128,2,128,128]{3,2,1,0:T(8,128)(2,1)}) %all-gather.3.cloned.1.call-update) | async-done | bytes 8388624 | tf_op jit(solution)/shard_map/all_gather | solution.py:268
  100.0 1.2 copy-done.7
  101.2 11.0 %top.1 = (bf16[64,128,128]{2,1,0:T(8,128)(2,1)S(1)}, f32[2,4,256,128]{3,2,1,0:T(8,128)S(1)}) custom-call(s32[16]{0:T(128)S(1)} %get-tuple-element.15.meta_ref, s32[128]{0:T(128)S(1)} %get-tuple-element.16.blk_ref, s32[128]{0:T(128)S(1)} %get-tuple-element.17.ent_ref, bf16[2,256,512]{2,1,0:T(8,128)(2,1)S(1)} %bitcast.9, f32[2,4,256,128]{3,2,1,0:T(8,128)S(1)} %copy-done.7, ...), custom_call_target="tpu_custom_call" | custom-call | tf_op jit(solution)/shard_map/top/pallas_call | solution.py:290
  112.2 5.6 %attend0.1.a0 = bf16[256,512]{1,0:T(8,128)(2,1)S(1)} custom-call(s32[16]{0:T(128)S(1)} %get-tuple-element.15.meta_ref, s32[128]{0:T(128)S(1)} %get-tuple-element.16.blk_ref, s32[128]{0:T(128)S(1)} %get-tuple-element.17.ent_ref, bf16[2,256,512]{2,1,0:T(8,128)(2,1)S(1)} %bitcast.10, bf16[64,128,128]{2,1,0:T(8,128)(2,1)S(1)} %get-tuple-element.22.keys_ref, ...), custom_call_target="tpu_custom_call" | custom-call | tf_op jit(solution)/shard_map/attend0/pallas_call | solution.py:302
  117.8 1.4 collective-permute-start.10
  119.2 2.9 %collective-permute-start.9 = (bf16[256,512]{1,0:T(8,128)(2,1)S(1)}, bf16[256,512]{1,0:T(8,128)(2,1)S(1)}, u32[]{:S(2)}, u32[]{:S(2)}) collective-permute-start(bf16[256,512]{1,0:T(8,128)(2,1)S(1)} %attend0.1.a0), channel_id=1, source_target_pairs={{2,0},{3,1},{0,2},{1,3},{6,4},{7,5},{4,6},{5,7},{10,8},{11,9},{8,1... | collective-permute-start | bytes 786440 | tf_op jit(solution)/shard_map/ppermute | solution.py:239
  122.1 21.6 %attend1.1.a0 = bf16[256,512]{1,0:T(8,128)(2,1)S(1)} custom-call(s32[16]{0:T(128)S(1)} %get-tuple-element.15.meta_ref, s32[128]{0:T(128)S(1)} %get-tuple-element.16.blk_ref, s32[128]{0:T(128)S(1)} %get-tuple-element.17.ent_ref, bf16[2,256,512]{2,1,0:T(8,128)(2,1)S(1)} %bitcast.11, bf16[64,128,128]{2,1,0:T(8,128)(2,1)S(1)} %get-tuple-element.22.keys_ref, ...), custom_call_target="tpu_custom_call" | custom-call | tf_op jit(solution)/shard_map/attend1/pallas_call | solution.py:302
  143.7 1.5 collective-permute-start.8
  145.2 0.6 collective-permute-start.4
  145.9 0.9 collective-permute-start.3
  146.8 1.8 %collective-permute-start.2 = (bf16[256,512]{1,0:T(8,128)(2,1)S(1)}, bf16[256,512]{1,0:T(8,128)(2,1)S(1)}, u32[]{:S(2)}, u32[]{:S(2)}) collective-permute-start(bf16[256,512]{1,0:T(8,128)(2,1)S(1)} %attend1.1.a0), channel_id=1, source_target_pairs={{1,0},{2,1},{3,2},{0,3},{5,4},{6,5},{7,6},{4,7},{9,8},{10,9},{11,1... | collective-permute-start | bytes 786440 | tf_op jit(solution)/shard_map/ppermute | solution.py:239
  148.6 8.3 %collective-permute-done.8.a1 = bf16[256,512]{1,0:T(8,128)(2,1)S(1)} collective-permute-done((bf16[256,512]{1,0:T(8,128)(2,1)S(1)}, bf16[256,512]{1,0:T(8,128)(2,1)S(1)}, u32[]{:S(2)}, u32[]{:S(2)}) %collective-permute-start.8) | collective-permute-done | bytes 262176 | tf_op jit(solution)/shard_map/ppermute | solution.py:239
  156.9 3.6 %mix0.1.refs_0_ = bf16[2,256,1024]{2,1,0:T(8,128)(2,1)} custom-call(bf16[256,512]{1,0:T(8,128)(2,1)S(1)} %attend0.1.a0, bf16[256,512]{1,0:T(8,128)(2,1)S(1)} %collective-permute-done.8.a1, bf16[256,512]{1,0:T(8,128)(2,1)S(1)} %collective-permute-done.9.a2, bf16[256,512]{1,0:T(8,128)(2,1)S(1)} %collective-permute-done.10.a3, ...), custom_call_target="tpu_custom_call" | custom-call | tf_op jit(solution)/shard_map/mix0/pallas_call | solution.py:324
  160.5 2.5 %collective-permute-done.2.a1 = bf16[256,512]{1,0:T(8,128)(2,1)S(1)} collective-permute-done((bf16[256,512]{1,0:T(8,128)(2,1)S(1)}, bf16[256,512]{1,0:T(8,128)(2,1)S(1)}, u32[]{:S(2)}, u32[]{:S(2)}) %collective-permute-start.2) | collective-permute-done | bytes 262176 | tf_op jit(solution)/shard_map/ppermute | solution.py:239
  163.0 3.6 %mix1.1 = bf16[2,256,1024]{2,1,0:T(8,128)(2,1)} custom-call(bf16[256,512]{1,0:T(8,128)(2,1)S(1)} %attend1.1.a0, bf16[256,512]{1,0:T(8,128)(2,1)S(1)} %collective-permute-done.2.a1, bf16[256,512]{1,0:T(8,128)(2,1)S(1)} %collective-permute-done.3.a2, bf16[256,512]{1,0:T(8,128)(2,1)S(1)} %collective-permute-done.4.a3, ...), custom_call_target="tpu_custom_call", output_to_operand_aliasing={{}: (8, {})} | custom-call | tf_op jit(solution)/shard_map/mix1/pallas_call | solution.py:324
  (21 shorter events, 0.0 us)
Async XLA Ops:
  6.5 93.4 %all-gather.3.cloned.1.call-start = ((), (), s32[]{:S(2)}) async-start(), calls=%async_computation | async-start | bytes 8519680 | tf_op jit(solution)/shard_map/all_gather | solution.py:268
  6.5 0.9 copy-start.2
  7.4 0.9 copy-start.4
  8.3 0.7 copy-start.9
  15.2 17.4 %copy-start.1 = (bf16[1,2,256,512]{3,2,1,0:T(8,128)(2,1)S(1)}, bf16[1,2,256,512]{3,2,1,0:T(8,128)(2,1)}, u32[]{:S(2)}) copy-start(bf16[1,2,256,512]{3,2,1,0:T(8,128)(2,1)} %param.6) | copy-start | bytes 1572868
  15.2 17.4 %copy-start.3 = (bf16[1,2,256,128]{3,2,1,0:T(8,128)(2,1)S(1)}, bf16[1,2,256,128]{3,2,1,0:T(8,128)(2,1)}, u32[]{:S(2)}) copy-start(bf16[1,2,256,128]{3,2,1,0:T(8,128)(2,1)} %param.7) | copy-start | bytes 393220
  15.3 17.4 %copy-start.8 = (s32[4,64]{1,0:T(4,128)S(1)}, s32[4,64]{1,0:T(4,128)}, u32[]{:S(2)}) copy-start(s32[4,64]{1,0:T(4,128)} %slash_ref.1) | copy-start | bytes 3076
  19.4 124.4 %collective-permute-start.7 = (bf16[512,1024]{1,0:T(8,128)(2,1)}, bf16[512,1024]{1,0:T(8,128)(2,1)S(1)}, u32[]{:S(2)}, u32[]{:S(2)}) collective-permute-start(bf16[512,1024]{1,0:T(8,128)(2,1)} %get-tuple-element.25), channel_id=1, source_target_pairs={{3,0},{0,1},{1,2},{2,3},{7,4},{4,5},{5,6},{6,7},{11,8},{8,9},{9,10... | collective-permute-start | bytes 3145736 | tf_op jit(solution)/shard_map/ppermute | solution.py:239
  20.9 124.3 %collective-permute-start.5 = (bf16[512,1024]{1,0:T(8,128)(2,1)}, bf16[512,1024]{1,0:T(8,128)(2,1)}, u32[]{:S(2)}, u32[]{:S(2)}) collective-permute-start(bf16[512,1024]{1,0:T(8,128)(2,1)} %get-tuple-element.26), channel_id=1, source_target_pairs={{1,0},{2,1},{3,2},{0,3},{5,4},{6,5},{7,6},{4,7},{9,8},{10,9},{11,1... | collective-permute-start | bytes 3145736 | tf_op jit(solution)/shard_map/ppermute | solution.py:239
  22.6 123.3 %collective-permute-start.6 = (bf16[512,1024]{1,0:T(8,128)(2,1)}, bf16[512,1024]{1,0:T(8,128)(2,1)}, u32[]{:S(2)}, u32[]{:S(2)}) collective-permute-start(bf16[512,1024]{1,0:T(8,128)(2,1)} %get-tuple-element.28), channel_id=1, source_target_pairs={{2,0},{3,1},{0,2},{1,3},{6,4},{7,5},{4,6},{5,7},{10,8},{11,9},{8,1... | collective-permute-start | bytes 3145736 | tf_op jit(solution)/shard_map/ppermute | solution.py:239
  24.6 6.3 %collective-permute-start = (bf16[2,256,128]{2,1,0:T(8,128)(2,1)S(1)}, bf16[2,256,128]{2,1,0:T(8,128)(2,1)S(1)}, u32[]{:S(2)}, u32[]{:S(2)}) collective-permute-start(bf16[2,256,128]{2,1,0:T(8,128)(2,1)S(1)} %get-tuple-element.18), channel_id=1, source_target_pairs={{0,4},{4,8},{8,12},{12,16},{16,20},{20,24},{24,28},{28,32},{32,36}... | collective-permute-start | bytes 393224 | tf_op jit(solution)/shard_map/ppermute | solution.py:271
  26.5 6.2 %collective-permute-start.1 = (bf16[2,256,128]{2,1,0:T(8,128)(2,1)S(1)}, bf16[2,256,128]{2,1,0:T(8,128)(2,1)S(1)}, u32[]{:S(2)}, u32[]{:S(2)}) collective-permute-start(bf16[2,256,128]{2,1,0:T(8,128)(2,1)S(1)} %get-tuple-element.19), channel_id=1, source_target_pairs={{4,0},{8,4},{12,8},{16,12},{20,16},{24,20},{28,24},{32,28},{36,32}... | collective-permute-start | bytes 393224 | tf_op jit(solution)/shard_map/ppermute | solution.py:272
  34.5 1.4 copy-start
  35.9 1.0 copy-start.6
  100.0 1.2 copy-start.7
  101.2 11.0 %copy-start.5 = (bf16[1,2,256,128]{3,2,1,0:T(8,128)(2,1)S(1)}, bf16[1,2,256,128]{3,2,1,0:T(8,128)(2,1)}, u32[]{:S(2)}) copy-start(bf16[1,2,256,128]{3,2,1,0:T(8,128)(2,1)} %param.8) | copy-start | bytes 393220
  117.8 29.0 %collective-permute-start.10 = (bf16[256,512]{1,0:T(8,128)(2,1)S(1)}, bf16[256,512]{1,0:T(8,128)(2,1)S(1)}, u32[]{:S(2)}, u32[]{:S(2)}) collective-permute-start(bf16[256,512]{1,0:T(8,128)(2,1)S(1)} %attend0.1.a0), channel_id=1, source_target_pairs={{3,0},{0,1},{1,2},{2,3},{7,4},{4,5},{5,6},{6,7},{11,8},{8,9},{9,10... | collective-permute-start | bytes 786440 | tf_op jit(solution)/shard_map/ppermute | solution.py:239
  119.2 29.4 %collective-permute-start.9 = (bf16[256,512]{1,0:T(8,128)(2,1)S(1)}, bf16[256,512]{1,0:T(8,128)(2,1)S(1)}, u32[]{:S(2)}, u32[]{:S(2)}) collective-permute-start(bf16[256,512]{1,0:T(8,128)(2,1)S(1)} %attend0.1.a0), channel_id=1, source_target_pairs={{2,0},{3,1},{0,2},{1,3},{6,4},{7,5},{4,6},{5,7},{10,8},{11,9},{8,1... | collective-permute-start | bytes 786440 | tf_op jit(solution)/shard_map/ppermute | solution.py:239
  143.7 13.2 %collective-permute-start.8 = (bf16[256,512]{1,0:T(8,128)(2,1)S(1)}, bf16[256,512]{1,0:T(8,128)(2,1)S(1)}, u32[]{:S(2)}, u32[]{:S(2)}) collective-permute-start(bf16[256,512]{1,0:T(8,128)(2,1)S(1)} %attend0.1.a0), channel_id=1, source_target_pairs={{1,0},{2,1},{3,2},{0,3},{5,4},{6,5},{7,6},{4,7},{9,8},{10,9},{11,1... | collective-permute-start | bytes 786440 | tf_op jit(solution)/shard_map/ppermute | solution.py:239
  145.2 15.3 %collective-permute-start.4 = (bf16[256,512]{1,0:T(8,128)(2,1)S(1)}, bf16[256,512]{1,0:T(8,128)(2,1)S(1)}, u32[]{:S(2)}, u32[]{:S(2)}) collective-permute-start(bf16[256,512]{1,0:T(8,128)(2,1)S(1)} %attend1.1.a0), channel_id=1, source_target_pairs={{3,0},{0,1},{1,2},{2,3},{7,4},{4,5},{5,6},{6,7},{11,8},{8,9},{9,10... | collective-permute-start | bytes 786440 | tf_op jit(solution)/shard_map/ppermute | solution.py:239
  145.9 14.7 %collective-permute-start.3 = (bf16[256,512]{1,0:T(8,128)(2,1)S(1)}, bf16[256,512]{1,0:T(8,128)(2,1)S(1)}, u32[]{:S(2)}, u32[]{:S(2)}) collective-permute-start(bf16[256,512]{1,0:T(8,128)(2,1)S(1)} %attend1.1.a0), channel_id=1, source_target_pairs={{2,0},{3,1},{0,2},{1,3},{6,4},{7,5},{4,6},{5,7},{10,8},{11,9},{8,1... | collective-permute-start | bytes 786440 | tf_op jit(solution)/shard_map/ppermute | solution.py:239
  146.8 16.2 %collective-permute-start.2 = (bf16[256,512]{1,0:T(8,128)(2,1)S(1)}, bf16[256,512]{1,0:T(8,128)(2,1)S(1)}, u32[]{:S(2)}, u32[]{:S(2)}) collective-permute-start(bf16[256,512]{1,0:T(8,128)(2,1)S(1)} %attend1.1.a0), channel_id=1, source_target_pairs={{1,0},{2,1},{3,2},{0,3},{5,4},{6,5},{7,6},{4,7},{9,8},{10,9},{11,1... | collective-permute-start | bytes 786440 | tf_op jit(solution)/shard_map/ppermute | solution.py:239
Sparse Core Ops, SparseCore 0:
  15.3 84.6 all-gather.2

commit v2 on v1

--- a/solution.py
+++ b/solution.py
@@ -12,9 +12,10 @@
 BLOCK = 128
 STRETCH = 256
 CAP = 2
-GROUP = 4
+GROUP = 8
 SPAN = GROUP * BLOCK
 LISTED = 64
+X_CHIPS = 4
 HEADS = 4
 EXP_SCALE = math.log2(math.e) * HEAD ** (-0.5)
 VMEM_LIMIT = 48 * 1024 * 1024
@@ -31,50 +32,58 @@
     return lax.dot_general(a, b, (((1,), (1,)), ((), ())), preferred_element_type=F32)
 
 
-def plan_kernel(ctx_count, me_ref, table_ref, k_ref, v_ref, pay_ref, ahead_ref, back_ref, blk_ref, ent_ref, meta_ref, count, place):
+def pack_kernel(ctx_count, me_ref, table_ref, k_ref, v_ref, keys_ref, vals_ref, ahead_ref, back_ref):
     me = me_ref[0]
-    stretches = 2 * ctx_count
-    near, far = me, stretches - 1 - me
-
-    def clear(i, _):
-        place[4 * i] = -1
-        place[4 * i + 1] = -1
-        place[4 * i + 2] = -1
-        place[4 * i + 3] = -1
-        count[i] = 0
-        return 0
-
-    lax.fori_loop(0, ctx_count, clear, 0)
-
-    def assign(j, carry):
-        loc0, loc1 = carry
-        b = table_ref[0, j]
-        stretch = b // 2
-        first = stretch < ctx_count
-        owner = jnp.where(first, stretch, stretches - 1 - stretch)
-        local = jnp.where(first, 0, 2) + b % 2
-        rank = count[owner]
-        count[owner] = rank + 1
-        place[b] = owner * CAP + rank
-        mine = owner == me
-        loc0 = jnp.where(mine & (rank == 0), local, loc0)
-        loc1 = jnp.where(mine & (rank == 1), local, loc1)
-        return loc0, loc1
-
-    loc0, loc1 = lax.fori_loop(0, LISTED, assign, (jnp.int32(0), jnp.int32(0)))
-    for slot, loc in enumerate((loc0, loc1)):
-        pay_ref[slot, 0] = k_ref[loc]
-        pay_ref[slot, 1] = v_ref[loc]
+    table = table_ref[...]
+    stretch = table // 2
+    first = stretch < ctx_count
+    owner = jnp.where(first, stretch, 2 * ctx_count - 1 - stretch)
+    local = jnp.where(first, 0, 2) + table % 2
+    at = lax.broadcasted_iota(jnp.int32, table.shape, 1)
+    mine = owner == me
+    for slot in range(CAP):
+        found = jnp.min(jnp.where(mine, at, LISTED))
+        loc = jnp.sum(jnp.where(at == found, local, 0))
+        mine = mine & (at > found)
+        keys_ref[slot] = k_ref[loc]
+        vals_ref[slot] = v_ref[loc]
     for half, ref in ((0, ahead_ref), (1, back_ref)):
         for part in range(2):
             ref[0, part * BLOCK : (part + 1) * BLOCK] = k_ref[2 * half + part]
             ref[1, part * BLOCK : (part + 1) * BLOCK] = v_ref[2 * half + part]
 
+
+def plan_kernel(ctx_count, me_ref, table_ref, blk_ref, inv_ref, meta_ref, count, place):
+    me = me_ref[0]
+    stretches = 2 * ctx_count
+    near, far = me, stretches - 1 - me
+
+    def clear(i, _):
+        for n in range(4):
+            place[4 * i + n] = -1
+        for n in range(CAP):
+            inv_ref[CAP * i + n] = -1
+        count[i] = 0
+        return 0
+
+    lax.fori_loop(0, ctx_count, clear, 0)
+
+    def assign(j, _):
+        b = table_ref[0, j]
+        stretch = b // 2
+        owner = jnp.where(stretch < ctx_count, stretch, stretches - 1 - stretch)
+        rank = count[owner]
+        count[owner] = rank + 1
+        place[b] = owner * CAP + rank
+        return 0
+
+    lax.fori_loop(0, LISTED, assign, 0)
+
     def order(b, carry):
         at, full0, seen0, full1, seen1 = carry
         e = place[b]
         blk_ref[at] = b
-        ent_ref[at] = e
+        inv_ref[jnp.where(e >= 0, e, CAP * ctx_count)] = at
         hit = jnp.where(e >= 0, 1, 0)
         one = lambda test: jnp.where(test, hit, 0)
         return (
@@ -130,13 +139,18 @@
             top_ref[st, h] = top
 
 
-def fetch(ent_ref, source_ref, which, target_ref, sems, groups):
-    def start(j, _):
-        e = ent_ref[j]
-        pltpu.make_async_copy(source_ref.at[e // CAP, e % CAP, which], target_ref.at[j], sems.at[j // GROUP]).start()
-        return 0
-
-    lax.fori_loop(0, groups * GROUP, start, 0)
+def fetch(inv_ref, me, pieces, origins, target_ref, sems):
+    for ref, origin in zip(pieces, origins):
+        def start(i, _, ref=ref, origin=origin):
+            at = inv_ref[origin(me, i)]
+
+            @pl.when(at >= 0)
+            def _():
+                pltpu.make_async_copy(ref.at[i], target_ref.at[at], sems.at[at // GROUP]).start()
+
+            return 0
+
+        lax.fori_loop(0, ref.shape[0], start, 0)
 
 
 def arrived(target_ref, sems, g):
@@ -149,8 +163,9 @@
     return [lead <= s * STRETCH - blk_ref[g * GROUP + n] * BLOCK for n in range(GROUP)]
 
 
-def top_kernel(meta_ref, blk_ref, ent_ref, q_ref, top_in_ref, source_ref, keys_ref, top_ref, sems):
-    fetch(ent_ref, source_ref, 0, keys_ref, sems, LISTED // GROUP)
+def top_kernel(origins, meta_ref, blk_ref, inv_ref, q_ref, top_in_ref, *refs):
+    pieces, (keys_ref, top_ref, sems) = refs[:-3], refs[-3:]
+    fetch(inv_ref, meta_ref[3], pieces, origins, keys_ref, sems)
 
     def ready(g, _):
         arrived(keys_ref, sems, g)
@@ -183,11 +198,15 @@
             top_ref[st, h] = jnp.broadcast_to(row, (STRETCH, BLOCK))
 
 
-def out_kernel(ctx_count, st, meta_ref, blk_ref, ent_ref, q_ref, keys_ref, top_ref, mask_ref, k_ref, v_ref, ahead_ref, back_ref, source_ref, out_ref, vals, total, acc, sems):
+def out_kernel(ctx_count, st, origins, meta_ref, blk_ref, inv_ref, q_ref, keys_ref, top_ref, mask_ref, k_ref, v_ref, ahead_ref, back_ref, *refs):
     full, seen, s = meta_ref[8 * st], meta_ref[8 * st + 1], meta_ref[8 * st + 2]
     me = meta_ref[8 * st + 3]
     plain, groups = full // GROUP, (seen + GROUP - 1) // GROUP
-    fetch(ent_ref, source_ref, 1, vals, sems, groups)
+    if origins:
+        pieces, (out_ref, vals, total, acc, sems) = refs[:-5], refs[-5:]
+        fetch(inv_ref, me, pieces, origins, vals, sems)
+    else:
+        vals, out_ref, total, acc = refs
     k_before = band_halves(k_ref, ahead_ref, back_ref, 0, st, me, ctx_count)
     v_before = band_halves(v_ref, ahead_ref, back_ref, 1, st, me, ctx_count)
 
@@ -206,7 +225,8 @@
         ) + jnp.dot(jnp.concatenate(weights[2:], axis=1), v_ref[st], preferred_element_type=F32)
 
     def step(masked, g, _):
-        arrived(vals, sems, g)
+        if origins:
+            arrived(vals, sems, g)
         keys = keys_ref[pl.ds(g * GROUP, GROUP)].reshape(SPAN, HEAD)
         values = vals[pl.ds(g * GROUP, GROUP)].reshape(SPAN, HEAD)
         ok = causal(blk_ref, s, g) if masked else None
@@ -216,13 +236,19 @@
             for n in range(GROUP):
                 part = jnp.exp2((scores[:, n * BLOCK : (n + 1) * BLOCK] - top_ref[0, h]) * EXP_SCALE)
                 expos.append(jnp.where(ok[n], part, 0.0) if masked else part)
-            total[h] += (expos[0] + expos[1]) + (expos[2] + expos[3])
+            total[h] += functools.reduce(jnp.add, expos)
             weights = jnp.concatenate([e.astype(BF16) for e in expos], axis=1)
             acc[h] += jnp.dot(weights, values, preferred_element_type=F32)
         return 0
 
     lax.fori_loop(0, plain, functools.partial(step, False), 0)
     lax.fori_loop(plain, groups, functools.partial(step, True), 0)
+    if origins:
+        def ready(g, _):
+            arrived(vals, sems, g)
+            return 0
+
+        lax.fori_loop(groups, LISTED // GROUP, ready, 0)
     for h in range(HEADS):
         row = jnp.sum(total[h], axis=1, keepdims=True)
         out_ref[:, h * HEAD : (h + 1) * HEAD] = (acc[h] / row).astype(BF16)
@@ -239,33 +265,110 @@
     return lax.ppermute(x, axis, [((i + shift) % n, i) for i in range(n)])
 
 
+def gather_columns(mesh_sizes, keys, vals):
+    nx, nz = mesh_sizes
+    place = lambda x, z, c: ((x % nx) * nz + z % nz) * 2 + c
+    every = [(x, z, c) for x in range(nx) for z in range(nz) for c in range(2)]
+    route = lambda f: [(place(*d), place(*f(*d))) for d in every]
+    across = route(lambda x, z, c: (x, z, 1 - c))
+    along_x = route(lambda x, z, c: (x + 1 - 2 * c, z, c))
+    along_z = route(lambda x, z, c: (x, z + 1 - 2 * c, c))
+    send = lambda a, r: lax.ppermute(a, "ctx", r)
+    lines = [[place(x, z, c) for z in range(nz)] for x in range(nx) for c in range(2)]
+
+    line = [vals] + [send(vals, route(lambda x, z, c, n=n: (x - n, z, c))) for n in range(1, nx)]
+    own = jnp.stack(line)
+    chip = jnp.stack([own, send(own, across)])
+    v_pieces = [chip]
+    own_k = lax.all_to_all(jnp.broadcast_to(keys[None], (nz,) + keys.shape), "ctx", 0, 0, axis_index_groups=lines)
+    moving = chip
+    for n in range(1, nz // 2):
+        moving = send(moving, along_z)
+        v_pieces += [moving, send(moving, across)]
+    last = send(moving[0], along_z)
+    v_pieces += [last, send(last, across)]
+
+    chip_k = jnp.stack([own_k, send(own_k, across)])
+    one = send(chip_k, along_x)
+    two = send(one[0], along_x)
+    k_pieces = [chip_k, one, send(one, across), two, send(two, across)]
+
+    def where(me):
+        return me // (2 * nz), (me // 2) % nz, me % 2
+
+    def entry(x, z, c, slot):
+        return (((x + nx) % nx * nz + (z + nz) % nz) * 2 + c) * CAP + slot
+
+    def k_origin(hops, mirrored, half):
+        def origin(me, i):
+            x, z, c = where(me)
+            side = (2 * c - 1) * hops
+            h = half if half is not None else i // (nz * CAP)
+            core = jnp.where(h == 0, c, 1 - c)
+            i = i % (nz * CAP)
+            if mirrored:
+                side, core = -side, 1 - core
+            return entry(x + side, i // CAP, core, i % CAP)
+
+        return origin
+
+    def v_origin(hops, mirrored, half):
+        def origin(me, i):
+            x, z, c = where(me)
+            side = (2 * c - 1) * hops
+            h = half if half is not None else i // (nx * CAP)
+            core = jnp.where(h == 0, c, 1 - c)
+            i = i % (nx * CAP)
+            if mirrored:
+                side, core = -side, 1 - core
+            return entry(x + i // CAP, z + side, core, i % CAP)
+
+        return origin
+
+    k_origins = [
+        k_origin(0, False, None),
+        k_origin(1, False, None),
+        k_origin(1, True, None),
+        k_origin(2, False, 0),
+        k_origin(2, True, 0),
+    ]
+    v_origins = [v_origin(0, False, None)]
+    for n in range(1, nz // 2):
+        v_origins += [v_origin(n, False, None), v_origin(n, True, None)]
+    v_origins += [v_origin(nz // 2, False, 0), v_origin(nz // 2, True, 0)]
+    flat = lambda pieces: [p.reshape(-1, BLOCK, HEAD) for p in pieces]
+    return flat(k_pieces), tuple(k_origins), flat(v_pieces), tuple(v_origins)
+
+
 def per_device(queries, keys, values, column_block_table, slash_offsets, out_weight):
     ctx_count = lax.axis_size("ctx")
     tp = lax.axis_size("tp")
-    me = lax.axis_index("ctx")
+    me = lax.axis_index("ctx").reshape(1).astype(jnp.int32)
     tp_index = lax.axis_index("tp")
     q, k, v = queries[0], keys[0], values[0]
     shape = jax.ShapeDtypeStruct
     i32 = jnp.int32
 
-    pay, ahead, back, blk, ent, meta = pl.pallas_call(
+    send_keys, send_vals, ahead, back = pl.pallas_call(
+        functools.partial(pack_kernel, ctx_count),
+        out_shape=[shape((CAP, BLOCK, HEAD), BF16)] * 2 + [shape((2, STRETCH, HEAD), BF16)] * 2,
+        in_specs=[SMEM(), VMEM(), VMEM(), VMEM()],
+        out_specs=[VMEM()] * 4,
+        compiler_params=PARAMS,
+        name="pack",
+    )(me, column_block_table, k.reshape(4, BLOCK, HEAD), v.reshape(4, BLOCK, HEAD))
+
+    k_pieces, k_origins, v_pieces, v_origins = gather_columns((X_CHIPS, ctx_count // (2 * X_CHIPS)), send_keys, send_vals)
+
+    blk, inv, meta = pl.pallas_call(
         functools.partial(plan_kernel, ctx_count),
-        out_shape=[
-            shape((CAP, 2, BLOCK, HEAD), BF16),
-            shape((2, STRETCH, HEAD), BF16),
-            shape((2, STRETCH, HEAD), BF16),
-            shape((128,), i32),
-            shape((128,), i32),
-            shape((16,), i32),
-        ],
-        in_specs=[SMEM(), SMEM(), VMEM(), VMEM()],
-        out_specs=[VMEM(), VMEM(), VMEM(), SMEM(), SMEM(), SMEM()],
+        out_shape=[shape((128,), i32), shape((256,), i32), shape((16,), i32)],
+        in_specs=[SMEM(), SMEM()],
+        out_specs=[SMEM()] * 3,
         scratch_shapes=[pltpu.SMEM((ctx_count,), i32), pltpu.SMEM((4 * ctx_count,), i32)],
         compiler_params=PARAMS,
         name="plan",
-    )(me.reshape(1).astype(i32), column_block_table, k.reshape(4, BLOCK, HEAD), v.reshape(4, BLOCK, HEAD))
-
-    source = lax.all_gather(pay, "ctx", axis=0)
+    )(me, column_block_table)
 
     steps = range(ctx_count - 1)
     before = lax.ppermute(ahead, "ctx", [(i, i + 1) for i in steps])
@@ -288,45 +391,50 @@
     )(meta, slash_offsets, q, k, before, after)
 
     columns, top = pl.pallas_call(
-        top_kernel,
+        functools.partial(top_kernel, k_origins),
         out_shape=[shape((LISTED, BLOCK, HEAD), BF16), shape((2, HEADS, STRETCH, BLOCK), F32)],
-        in_specs=[SMEM(), SMEM(), SMEM(), VMEM(), VMEM(), ANY()],
+        in_specs=[SMEM(), SMEM(), SMEM(), VMEM(), VMEM()] + [ANY()] * len(k_pieces),
         out_specs=[VMEM(), VMEM()],
         scratch_shapes=[pltpu.SemaphoreType.DMA((LISTED // GROUP,))],
         compiler_params=PARAMS,
         name="top",
-    )(meta, blk, ent, q, top, source)
-
-    mixed = None
+    )(meta, blk, inv, q, top, *k_pieces)
+
+    mixed = column_vals = None
     for st in range(2):
-        head_out = pl.pallas_call(
-            functools.partial(out_kernel, ctx_count, st),
+        arriving = st == 0
+        result = pl.pallas_call(
+            functools.partial(out_kernel, ctx_count, st, v_origins if arriving else ()),
             grid=(1,),
-            out_shape=shape((STRETCH, HEADS * HEAD), BF16),
+            out_shape=[shape((STRETCH, HEADS * HEAD), BF16)] + [shape((LISTED, BLOCK, HEAD), BF16)] * arriving,
             in_specs=[
                 SMEM(), SMEM(), SMEM(),
                 pl.BlockSpec((1, STRETCH, HEADS * HEAD), lambda i, st=st: (st, 0, 0)),
                 VMEM(),
                 pl.BlockSpec((1, HEADS, STRETCH, BLOCK), lambda i, st=st: (st, 0, 0, 0)),
-                VMEM(), VMEM(), VMEM(), VMEM(), VMEM(), ANY(),
-            ],
-            out_specs=VMEM(),
+                VMEM(), VMEM(), VMEM(), VMEM(), VMEM(),
+            ] + ([ANY()] * len(v_pieces) if arriving else [VMEM()]),
+            out_specs=[VMEM()] * (1 + arriving),
             scratch_shapes=[
-                pltpu.VMEM((LISTED, BLOCK, HEAD), BF16),
                 pltpu.VMEM((HEADS, STRETCH, BLOCK), F32),
                 pltpu.VMEM((HEADS, STRETCH, HEAD), F32),
-                pltpu.SemaphoreType.DMA((LISTED // GROUP,)),
-            ],
+            ] + [pltpu.SemaphoreType.DMA((LISTED // GROUP,))] * arriving,
             compiler_params=PARAMS,
             name=f"attend{st}",
-        )(meta, blk, ent, q, columns, top, mask, k, v, before, after, source)
+        )(meta, blk, inv, q, columns, top, mask, k, v, before, after, *(v_pieces if arriving else [column_vals]))
+        head_out = result[0]
+        if arriving:
+            column_vals = result[1]
         parts = [head_out] + [from_ahead(head_out, "tp", shift) for shift in range(1, tp)]
+        tile = width // 4
         mixed = pl.pallas_call(
             mix_kernel,
-            grid=(1,),
+            grid=(width // tile,),
             out_shape=shape((2, STRETCH, width), BF16),
-            in_specs=[VMEM()] * 8 + ([ANY()] if st else []),
-            out_specs=pl.BlockSpec((1, STRETCH, width), lambda i, st=st: (st, 0, 0)),
+            in_specs=[VMEM()] * 4
+            + [pl.BlockSpec((HEADS * HEAD, tile), lambda i: (0, i))] * 4
+            + ([ANY()] if st else []),
+            out_specs=pl.BlockSpec((1, STRETCH, tile), lambda i, st=st: (st, 0, i)),
             input_output_aliases={8: 0} if st else {},
             compiler_params=PARAMS,
             name=f"mix{st}",

time: 175 us -> 165 us (0.943)
  the two profiles are of different devices: /device:TPU:96 before, /device:TPU:1 now
where the time goes in v2:
time: 165 us
  Pallas kernels  56.7 us (34%)
  starting transfers between devices  50 us (30%)
  waiting for transfers between devices  44.4 us (27%)
  local copies, waits for them, and re-layouts  13.1 us (8%)
    pallas_call x2, Pallas kernels, per_device(): pl.pallas_call(functools.partial(out_kernel, ctx_count, st, v_origins if...  27.4 us
    ppermute x17, starting transfers between devices, gather_columns(): send = lambda a, r: lax.ppermute(a, 'ctx', r)  23.2 us
    ppermute x17, waiting for transfers between devices, gather_columns(): send = lambda a, r: lax.ppermute(a, 'ctx', r)  15.1 us
    pallas_call x1, Pallas kernels, per_device(): pl.pallas_call(functools.partial(top_kernel, k_origins), out_shape=[shape...  14.9 us
    all_to_all x1, waiting for transfers between devices, gather_columns(): lax.all_to_all(jnp.broadcast_to(keys[None], (nz,) + keys.shape), 'ctx', 0...  13.1 us
    ppermute x9, waiting for transfers between devices, from_ahead(): return lax.ppermute(x, axis, [((i + shift) % n, i) for i in range(n)])  13.1 us
    ppermute x9, starting transfers between devices, from_ahead(): return lax.ppermute(x, axis, [((i + shift) % n, i) for i in range(n)])  10.6 us
    all_to_all x1, starting transfers between devices, gather_columns(): lax.all_to_all(jnp.broadcast_to(keys[None], (nz,) + keys.shape), 'ctx', 0...  9.01 us
  transfers between devices with their start and end apart: 29, of which 9 were waited for; matrix products, arithmetic and copies ran while one was open for 3% of the time, Pallas kernels for 32%

profile of v2, /device:TPU:1, one launch (start us, length us, event | category | flops | bytes accessed | tf_op | source)
XLA Modules:
  0.0 164.6 jit_solution(3949635581597179889)
XLA Ops:
  3.9 9.0 %all-to-all-start = ((bf16[8,2,128,128]{3,2,1,0:T(8,128)(2,1)}), bf16[8,2,128,128]{3,2,1,0:T(8,128)(2,1)S(1)}, u32[]{:S(2)}, u32[]{:S(2)}) async-start(bf16[8,2,128,128]{3,2,1,0:T(8,128)(2,1)} %broadcast_in_dim.4), calls=%async_computation | async-start | bytes 1048576 | tf_op jit(solution)/shard_map/all_to_all | solution.py:283
  12.9 1.2 collective-permute-start.9
  14.1 2.5 %collective-permute-start.8 = (bf16[2,128,128]{2,1,0:T(8,128)(2,1)S(1)}, bf16[2,128,128]{2,1,0:T(8,128)(2,1)S(1)}, u32[]{:S(2)}, u32[]{:S(2)}) collective-permute-start(bf16[2,128,128]{2,1,0:T(8,128)(2,1)S(1)} %get-tuple-element.28), channel_id=1, source_target_pairs={{0,128},{4,132},{8,136},{12,140},{16,144},{20,148},{24,152},{28,15... | collective-permute-start | bytes 196616 | tf_op jit(solution)/shard_map/ppermute | solution.py:276
  16.6 1.2 collective-permute-start.7
  17.7 13.1 %all-to-all-done = bf16[8,2,128,128]{3,2,1,0:T(8,128)(2,1)S(1)} async-done(((bf16[8,2,128,128]{3,2,1,0:T(8,128)(2,1)}), bf16[8,2,128,128]{3,2,1,0:T(8,128)(2,1)S(1)}, u32[]{:S(2)}, u32[]{:S(2)}) %all-to-all-start) | async-done | bytes 524320 | tf_op jit(solution)/shard_map/all_to_all | solution.py:283
  31.5 1.7 %collective-permute-done.10 = bf16[4,2,128,128]{3,2,1,0:T(8,128)(2,1)S(1)} collective-permute-done((bf16[4,2,128,128]{3,2,1,0:T(8,128)(2,1)S(1)}, bf16[4,2,128,128]{3,2,1,0:T(8,128)(2,1)S(1)}, u32[]{:S(2)}, u32[]{:S(2)}) %collective-permute-start.10) | collective-permute-done | bytes 262176 | tf_op jit(solution)/shard_map/ppermute | solution.py:276
  33.5 2.6 %collective-permute-start.3 = (bf16[2,8,2,128,128]{4,3,2,1,0:T(8,128)(2,1)S(1)}, bf16[2,8,2,128,128]{4,3,2,1,0:T(8,128)(2,1)S(1)}, u32[]{:S(2)}, u32[]{:S(2)}) collective-permute-start(bf16[2,8,2,128,128]{4,3,2,1,0:T(8,128)(2,1)S(1)} %pad_maximum_fusion), channel_id=1, source_target_pairs={{0,64},{4,196},{8,72},{12,204},{16,80},{20,212},{24,88},{28,220},{... | collective-permute-start | bytes 3145736 | tf_op jit(solution)/shard_map/ppermute | solution.py:276
  36.1 5.7 %collective-permute-done.11 = bf16[2,4,2,128,128]{4,3,2,1,0:T(8,128)(2,1)} collective-permute-done((bf16[2,4,2,128,128]{4,3,2,1,0:T(8,128)(2,1)S(1)}, bf16[2,4,2,128,128]{4,3,2,1,0:T(8,128)(2,1)}, u32[]{:S(2)}, u32[]{:S(2)}) %collective-permute-start.11) | collective-permute-done | bytes 524320 | tf_op jit(solution)/shard_map/ppermute | solution.py:276
  43.0 7.5 %collective-permute-done.13 = bf16[2,4,2,128,128]{4,3,2,1,0:T(8,128)(2,1)} collective-permute-done((bf16[2,4,2,128,128]{4,3,2,1,0:T(8,128)(2,1)}, bf16[2,4,2,128,128]{4,3,2,1,0:T(8,128)(2,1)}, u32[]{:S(2)}, u32[]{:S(2)}) %collective-permute-start.13) | collective-permute-done | bytes 524320 | tf_op jit(solution)/shard_map/ppermute | solution.py:276
  50.5 2.1 %collective-permute-start.15 = (bf16[2,4,2,128,128]{4,3,2,1,0:T(8,128)(2,1)}, bf16[2,4,2,128,128]{4,3,2,1,0:T(8,128)(2,1)S(1)}, u32[]{:S(2)}, u32[]{:S(2)}) collective-permute-start(bf16[2,4,2,128,128]{4,3,2,1,0:T(8,128)(2,1)} %collective-permute-done.13), channel_id=1, source_target_pairs={{0,8},{4,60},{8,16},{12,4},{16,24},{20,12},{24,32},{28,20},{32,40}... | collective-permute-start | bytes 1572872 | tf_op jit(solution)/shard_map/ppermute | solution.py:276
  52.5 2.5 %collective-permute-start.4 = (bf16[2,8,2,128,128]{4,3,2,1,0:T(8,128)(2,1)S(1)}, bf16[2,8,2,128,128]{4,3,2,1,0:T(8,128)(2,1)}, u32[]{:S(2)}, u32[]{:S(2)}) collective-permute-start(bf16[2,8,2,128,128]{4,3,2,1,0:T(8,128)(2,1)S(1)} %collective-permute-done.3), channel_id=1, source_target_pairs={{0,4},{4,0},{8,12},{12,8},{16,20},{20,16},{24,28},{28,24},{32,36},... | collective-permute-start | bytes 3145736 | tf_op jit(solution)/shard_map/ppermute | solution.py:276
  55.8 2.5 %collective-permute-start.5 = (bf16[8,2,128,128]{3,2,1,0:T(8,128)(2,1)}, bf16[8,2,128,128]{3,2,1,0:T(8,128)(2,1)}, u32[]{:S(2)}, u32[]{:S(2)}) collective-permute-start(bf16[8,2,128,128]{3,2,1,0:T(8,128)(2,1)} %slice_bitcast_fusion), channel_id=1, source_target_pairs={{0,64},{4,196},{8,72},{12,204},{16,80},{20,212},{24,88},{28,220},{... | collective-permute-start | bytes 1572872 | tf_op jit(solution)/shard_map/ppermute | solution.py:276
  58.3 1.9 %collective-permute-start = (bf16[2,256,128]{2,1,0:T(8,128)(2,1)S(1)}, bf16[2,256,128]{2,1,0:T(8,128)(2,1)S(1)}, u32[]{:S(2)}, u32[]{:S(2)}) collective-permute-start(bf16[2,256,128]{2,1,0:T(8,128)(2,1)S(1)} %get-tuple-element.21), channel_id=1, source_target_pairs={{0,4},{4,8},{8,12},{12,16},{16,20},{20,24},{24,28},{28,32},{32,36}... | collective-permute-start | bytes 393224 | tf_op jit(solution)/shard_map/ppermute | solution.py:374
  60.8 2.1 %collective-permute-done.ahead_ref = bf16[2,256,128]{2,1,0:T(8,128)(2,1)S(1)} collective-permute-done((bf16[2,256,128]{2,1,0:T(8,128)(2,1)S(1)}, bf16[2,256,128]{2,1,0:T(8,128)(2,1)S(1)}, u32[]{:S(2)}, u32[]{:S(2)}) %collective-permute-start) | collective-permute-done | bytes 131104 | tf_op jit(solution)/shard_map/ppermute | solution.py:374
  62.9 5.3 %collective-permute-start.1 = (bf16[2,256,128]{2,1,0:T(8,128)(2,1)S(1)}, bf16[2,256,128]{2,1,0:T(8,128)(2,1)S(1)}, u32[]{:S(2)}, u32[]{:S(2)}) collective-permute-start(bf16[2,256,128]{2,1,0:T(8,128)(2,1)S(1)} %get-tuple-element.22), channel_id=1, source_target_pairs={{4,0},{8,4},{12,8},{16,12},{20,16},{24,20},{28,24},{32,28},{36,32}... | collective-permute-start | bytes 393224 | tf_op jit(solution)/shard_map/ppermute | solution.py:375
  69.9 5.1 %collective-permute-start.17 = (bf16[4,2,128,128]{3,2,1,0:T(8,128)(2,1)}, bf16[4,2,128,128]{3,2,1,0:T(8,128)(2,1)}, u32[]{:S(2)}, u32[]{:S(2)}) collective-permute-start(bf16[4,2,128,128]{3,2,1,0:T(8,128)(2,1)} %slice_bitcast_fusion.1), channel_id=1, source_target_pairs={{0,8},{4,60},{8,16},{12,4},{16,24},{20,12},{24,32},{28,20},{32,40}... | collective-permute-start | bytes 786440 | tf_op jit(solution)/shard_map/ppermute | solution.py:276
  75.1 4.0 %constant_dynamic-slice_fusion = (bf16[512,1024]{1,0:T(8,128)(2,1)}, bf16[512,1024]{1,0:T(8,128)(2,1)}, bf16[512,1024]{1,0:T(8,128)(2,1)S(1)}, bf16[512,1024]{1,0:T(8,128)(2,1)}) fusion(bf16[512,4096]{1,0:T(8,128)(2,1)} %param.11, s32[]{:T(128)S(6)} %select_n.15, s32[]{:T(128)S(6)} %select_n.13, s32[]{:T(128)S(6)} %select_n.12, s32[]{:T(128)S(6)} %select_n.14), kind=kLoop, calls=%fused_computation.5 | loop fusion | bytes 8388624 | tf_op jit(solution)/shard_map/dynamic_slice | solution.py:381
  79.2 2.7 %collective-permute-start.22 = (bf16[512,1024]{1,0:T(8,128)(2,1)}, bf16[512,1024]{1,0:T(8,128)(2,1)S(1)}, u32[]{:S(2)}, u32[]{:S(2)}) collective-permute-start(bf16[512,1024]{1,0:T(8,128)(2,1)} %get-tuple-element.32), channel_id=1, source_target_pairs={{1,0},{2,1},{3,2},{0,3},{5,4},{6,5},{7,6},{4,7},{9,8},{10,9},{11,1... | collective-permute-start | bytes 3145736 | tf_op jit(solution)/shard_map/ppermute | solution.py:265
  82.9 1.2 collective-permute-start.16
  84.3 5.7 %plan.1 = (s32[128]{0:T(128)S(1)}, s32[256]{0:T(256)S(1)}, s32[16]{0:T(128)S(1)}) custom-call(s32[1]{0:T(128)} %bitcast.me_ref, s32[1,64]{1,0:T(1,128)S(1)} %copy-done.13), custom_call_target="tpu_custom_call" | custom-call | tf_op jit(solution)/shard_map/plan/pallas_call | solution.py:363
  90.1 1.9 %band.1 = (f32[4,256,512]{2,1,0:T(8,128)S(1)}, f32[2,4,256,128]{3,2,1,0:T(8,128)S(1)}) custom-call(s32[16]{0:T(128)S(1)} %get-tuple-element.18.meta_ref, s32[4,64]{1,0:T(4,128)S(1)} %copy-done.11, bf16[2,256,512]{2,1,0:T(8,128)(2,1)S(1)} %bitcast.34, bf16[2,256,128]{2,1,0:T(8,128)(2,1)S(1)} %bitcast.41, ...), custom_call_target="tpu_custom_call" | custom-call | tf_op jit(solution)/shard_map/band/pallas_call | solution.py:384
  92.0 1.3 copy-done
  93.3 14.9 %top.1 = (bf16[64,128,128]{2,1,0:T(8,128)(2,1)}, f32[2,4,256,128]{3,2,1,0:T(8,128)S(1)}) custom-call(s32[16]{0:T(128)S(1)} %get-tuple-element.18.meta_ref, s32[128]{0:T(128)S(1)} %get-tuple-element.19.blk_ref, s32[256]{0:T(256)S(1)} %get-tuple-element.20.inv_ref, bf16[2,256,512]{2,1,0:T(8,128)(2,1)S(1)} %bitcast.35, ...), custom_call_target="tpu_custom_call" | custom-call | tf_op jit(solution)/shard_map/top/pallas_call | solution.py:393
  111.1 12.7 %attend0.1 = (bf16[256,512]{1,0:T(8,128)(2,1)S(1)}, bf16[64,128,128]{2,1,0:T(8,128)(2,1)}) custom-call(s32[16]{0:T(128)S(1)} %get-tuple-element.18.meta_ref, s32[128]{0:T(128)S(1)} %get-tuple-element.19.blk_ref, s32[256]{0:T(256)S(1)} %get-tuple-element.20.inv_ref, bf16[2,256,512]{2,1,0:T(8,128)(2,1)S(1)} %bitcast.36, ...), custom_call_target="tpu_custom_call" | custom-call | tf_op jit(solution)/shard_map/attend0/pallas_call | solution.py:406
  123.8 2.2 %collective-permute-start.25 = (bf16[256,512]{1,0:T(8,128)(2,1)S(1)}, bf16[256,512]{1,0:T(8,128)(2,1)S(1)}, u32[]{:S(2)}, u32[]{:S(2)}) collective-permute-start(bf16[256,512]{1,0:T(8,128)(2,1)S(1)} %get-tuple-element.30.a0), channel_id=1, source_target_pairs={{1,0},{2,1},{3,2},{0,3},{5,4},{6,5},{7,6},{4,7},{9,8},{10,9},{11,1... | collective-permute-start | bytes 786440 | tf_op jit(solution)/shard_map/ppermute | solution.py:265
  126.1 1.1 collective-permute-start.26
  127.2 14.7 %attend1.1.a0 = bf16[256,512]{1,0:T(8,128)(2,1)S(1)} custom-call(s32[16]{0:T(128)S(1)} %get-tuple-element.18.meta_ref, s32[128]{0:T(128)S(1)} %get-tuple-element.19.blk_ref, s32[256]{0:T(256)S(1)} %get-tuple-element.20.inv_ref, bf16[2,256,512]{2,1,0:T(8,128)(2,1)S(1)} %bitcast.37, bf16[64,128,128]{2,1,0:T(8,128)(2,1)S(1)} %copy-done.1, ...), custom_call_target="tpu_custom_call" | custom-call | tf_op jit(solution)/shard_map/attend1/pallas_call | solution.py:406
  142.0 2.7 %collective-permute-start.19 = (bf16[256,512]{1,0:T(8,128)(2,1)S(1)}, bf16[256,512]{1,0:T(8,128)(2,1)S(1)}, u32[]{:S(2)}, u32[]{:S(2)}) collective-permute-start(bf16[256,512]{1,0:T(8,128)(2,1)S(1)} %attend1.1.a0), channel_id=1, source_target_pairs={{1,0},{2,1},{3,2},{0,3},{5,4},{6,5},{7,6},{4,7},{9,8},{10,9},{11,1... | collective-permute-start | bytes 786440 | tf_op jit(solution)/shard_map/ppermute | solution.py:265
  145.4 5.7 %collective-permute-done.27.a3 = bf16[256,512]{1,0:T(8,128)(2,1)S(1)} collective-permute-done((bf16[256,512]{1,0:T(8,128)(2,1)S(1)}, bf16[256,512]{1,0:T(8,128)(2,1)S(1)}, u32[]{:S(2)}, u32[]{:S(2)}) %collective-permute-start.27) | collective-permute-done | bytes 262176 | tf_op jit(solution)/shard_map/ppermute | solution.py:265
  151.1 3.1 %mix0.1.refs_0_ = bf16[2,256,1024]{2,1,0:T(8,128)(2,1)} custom-call(bf16[256,512]{1,0:T(8,128)(2,1)S(1)} %get-tuple-element.30.a0, bf16[256,512]{1,0:T(8,128)(2,1)S(1)} %collective-permute-done.25.a1, bf16[256,512]{1,0:T(8,128)(2,1)S(1)} %collective-permute-done.26.a2, bf16[256,512]{1,0:T(8,128)(2,1)S(1)} %collective-permute-done.27.a3, ...), custom_call_target="tpu_custom_call" | custom-call | tf_op jit(solution)/shard_map/mix0/pallas_call | solution.py:430
  155.2 6.3 %collective-permute-done.21.a3 = bf16[256,512]{1,0:T(8,128)(2,1)S(1)} collective-permute-done((bf16[256,512]{1,0:T(8,128)(2,1)S(1)}, bf16[256,512]{1,0:T(8,128)(2,1)S(1)}, u32[]{:S(2)}, u32[]{:S(2)}) %collective-permute-start.21) | collective-permute-done | bytes 262176 | tf_op jit(solution)/shard_map/ppermute | solution.py:265
  161.6 3.1 %mix1.1 = bf16[2,256,1024]{2,1,0:T(8,128)(2,1)} custom-call(bf16[256,512]{1,0:T(8,128)(2,1)S(1)} %attend1.1.a0, bf16[256,512]{1,0:T(8,128)(2,1)S(1)} %collective-permute-done.19.a1, bf16[256,512]{1,0:T(8,128)(2,1)S(1)} %collective-permute-done.20.a2, bf16[256,512]{1,0:T(8,128)(2,1)S(1)} %collective-permute-done.21.a3, ...), custom_call_target="tpu_custom_call", output_to_operand_aliasing={{}: (8, {})} | custom-call | tf_op jit(solution)/shard_map/mix1/pallas_call | solution.py:430
  (69 shorter events, 15.0 us)
Async XLA Ops:
  3.9 27.0 %all-to-all-start = ((bf16[8,2,128,128]{3,2,1,0:T(8,128)(2,1)}), bf16[8,2,128,128]{3,2,1,0:T(8,128)(2,1)S(1)}, u32[]{:S(2)}, u32[]{:S(2)}) async-start(bf16[8,2,128,128]{3,2,1,0:T(8,128)(2,1)} %broadcast_in_dim.4), calls=%async_computation | async-start | bytes 1048576 | tf_op jit(solution)/shard_map/all_to_all | solution.py:283
  12.9 18.5 %collective-permute-start.9 = (bf16[2,128,128]{2,1,0:T(8,128)(2,1)S(1)}, bf16[2,128,128]{2,1,0:T(8,128)(2,1)S(1)}, u32[]{:S(2)}, u32[]{:S(2)}) collective-permute-start(bf16[2,128,128]{2,1,0:T(8,128)(2,1)S(1)} %get-tuple-element.28), channel_id=1, source_target_pairs={{0,64},{4,68},{8,72},{12,76},{16,80},{20,84},{24,88},{28,92},{32,9... | collective-permute-start | bytes 196616 | tf_op jit(solution)/shard_map/ppermute | solution.py:276
  14.1 17.2 %collective-permute-start.8 = (bf16[2,128,128]{2,1,0:T(8,128)(2,1)S(1)}, bf16[2,128,128]{2,1,0:T(8,128)(2,1)S(1)}, u32[]{:S(2)}, u32[]{:S(2)}) collective-permute-start(bf16[2,128,128]{2,1,0:T(8,128)(2,1)S(1)} %get-tuple-element.28), channel_id=1, source_target_pairs={{0,128},{4,132},{8,136},{12,140},{16,144},{20,148},{24,152},{28,15... | collective-permute-start | bytes 196616 | tf_op jit(solution)/shard_map/ppermute | solution.py:276
  16.6 14.8 %collective-permute-start.7 = (bf16[2,128,128]{2,1,0:T(8,128)(2,1)S(1)}, bf16[2,128,128]{2,1,0:T(8,128)(2,1)S(1)}, u32[]{:S(2)}, u32[]{:S(2)}) collective-permute-start(bf16[2,128,128]{2,1,0:T(8,128)(2,1)S(1)} %get-tuple-element.28), channel_id=1, source_target_pairs={{0,192},{4,196},{8,200},{12,204},{16,208},{20,212},{24,216},{28,22... | collective-permute-start | bytes 196616 | tf_op jit(solution)/shard_map/ppermute | solution.py:276
  30.9 2.6 %collective-permute-start.2 = (bf16[8,2,128,128]{3,2,1,0:T(8,128)(2,1)S(1)}, bf16[8,2,128,128]{3,2,1,0:T(8,128)(2,1)S(1)}, u32[]{:S(2)}, u32[]{:S(2)}) collective-permute-start(bf16[8,2,128,128]{3,2,1,0:T(8,128)(2,1)S(1)} %all-to-all-done), channel_id=1, source_target_pairs={{0,4},{4,0},{8,12},{12,8},{16,20},{20,16},{24,28},{28,24},{32,36},... | collective-permute-start | bytes 1572872 | tf_op jit(solution)/shard_map/ppermute | solution.py:276
  31.4 1.8 %collective-permute-start.10 = (bf16[4,2,128,128]{3,2,1,0:T(8,128)(2,1)S(1)}, bf16[4,2,128,128]{3,2,1,0:T(8,128)(2,1)S(1)}, u32[]{:S(2)}, u32[]{:S(2)}) collective-permute-start(bf16[4,2,128,128]{3,2,1,0:T(8,128)(2,1)S(1)} %get-tuple-element.36), channel_id=1, source_target_pairs={{0,4},{4,0},{8,12},{12,8},{16,20},{20,16},{24,28},{28,24},{32,36},... | collective-permute-start | bytes 786440 | tf_op jit(solution)/shard_map/ppermute | solution.py:276
  33.3 8.5 %collective-permute-start.11 = (bf16[2,4,2,128,128]{4,3,2,1,0:T(8,128)(2,1)S(1)}, bf16[2,4,2,128,128]{4,3,2,1,0:T(8,128)(2,1)}, u32[]{:S(2)}, u32[]{:S(2)}) collective-permute-start(bf16[2,4,2,128,128]{4,3,2,1,0:T(8,128)(2,1)S(1)} %pad_maximum_fusion.1), channel_id=1, source_target_pairs={{0,8},{4,60},{8,16},{12,4},{16,24},{20,12},{24,32},{28,20},{32,40}... | collective-permute-start | bytes 1572872 | tf_op jit(solution)/shard_map/ppermute | solution.py:276
  33.5 19.0 %collective-permute-start.3 = (bf16[2,8,2,128,128]{4,3,2,1,0:T(8,128)(2,1)S(1)}, bf16[2,8,2,128,128]{4,3,2,1,0:T(8,128)(2,1)S(1)}, u32[]{:S(2)}, u32[]{:S(2)}) collective-permute-start(bf16[2,8,2,128,128]{4,3,2,1,0:T(8,128)(2,1)S(1)} %pad_maximum_fusion), channel_id=1, source_target_pairs={{0,64},{4,196},{8,72},{12,204},{16,80},{20,212},{24,88},{28,220},{... | collective-permute-start | bytes 3145736 | tf_op jit(solution)/shard_map/ppermute | solution.py:276
  41.8 8.6 %collective-permute-start.13 = (bf16[2,4,2,128,128]{4,3,2,1,0:T(8,128)(2,1)}, bf16[2,4,2,128,128]{4,3,2,1,0:T(8,128)(2,1)}, u32[]{:S(2)}, u32[]{:S(2)}) collective-permute-start(bf16[2,4,2,128,128]{4,3,2,1,0:T(8,128)(2,1)} %collective-permute-done.11), channel_id=1, source_target_pairs={{0,8},{4,60},{8,16},{12,4},{16,24},{20,12},{24,32},{28,20},{32,40}... | collective-permute-start | bytes 1572872 | tf_op jit(solution)/shard_map/ppermute | solution.py:276
  50.5 12.4 %collective-permute-start.15 = (bf16[2,4,2,128,128]{4,3,2,1,0:T(8,128)(2,1)}, bf16[2,4,2,128,128]{4,3,2,1,0:T(8,128)(2,1)S(1)}, u32[]{:S(2)}, u32[]{:S(2)}) collective-permute-start(bf16[2,4,2,128,128]{4,3,2,1,0:T(8,128)(2,1)} %collective-permute-done.13), channel_id=1, source_target_pairs={{0,8},{4,60},{8,16},{12,4},{16,24},{20,12},{24,32},{28,20},{32,40}... | collective-permute-start | bytes 1572872 | tf_op jit(solution)/shard_map/ppermute | solution.py:276
  52.5 30.4 %collective-permute-start.4 = (bf16[2,8,2,128,128]{4,3,2,1,0:T(8,128)(2,1)S(1)}, bf16[2,8,2,128,128]{4,3,2,1,0:T(8,128)(2,1)}, u32[]{:S(2)}, u32[]{:S(2)}) collective-permute-start(bf16[2,8,2,128,128]{4,3,2,1,0:T(8,128)(2,1)S(1)} %collective-permute-done.3), channel_id=1, source_target_pairs={{0,4},{4,0},{8,12},{12,8},{16,20},{20,16},{24,28},{28,24},{32,36},... | collective-permute-start | bytes 3145736 | tf_op jit(solution)/shard_map/ppermute | solution.py:276
  55.8 19.2 %collective-permute-start.5 = (bf16[8,2,128,128]{3,2,1,0:T(8,128)(2,1)}, bf16[8,2,128,128]{3,2,1,0:T(8,128)(2,1)}, u32[]{:S(2)}, u32[]{:S(2)}) collective-permute-start(bf16[8,2,128,128]{3,2,1,0:T(8,128)(2,1)} %slice_bitcast_fusion), channel_id=1, source_target_pairs={{0,64},{4,196},{8,72},{12,204},{16,80},{20,212},{24,88},{28,220},{... | collective-permute-start | bytes 1572872 | tf_op jit(solution)/shard_map/ppermute | solution.py:276
  58.3 4.6 %collective-permute-start = (bf16[2,256,128]{2,1,0:T(8,128)(2,1)S(1)}, bf16[2,256,128]{2,1,0:T(8,128)(2,1)S(1)}, u32[]{:S(2)}, u32[]{:S(2)}) collective-permute-start(bf16[2,256,128]{2,1,0:T(8,128)(2,1)S(1)} %get-tuple-element.21), channel_id=1, source_target_pairs={{0,4},{4,8},{8,12},{12,16},{16,20},{20,24},{24,28},{28,32},{32,36}... | collective-permute-start | bytes 393224 | tf_op jit(solution)/shard_map/ppermute | solution.py:374
  60.2 18.9 %collective-permute-start.12 = (bf16[2,4,2,128,128]{4,3,2,1,0:T(8,128)(2,1)}, bf16[2,4,2,128,128]{4,3,2,1,0:T(8,128)(2,1)}, u32[]{:S(2)}, u32[]{:S(2)}) collective-permute-start(bf16[2,4,2,128,128]{4,3,2,1,0:T(8,128)(2,1)} %collective-permute-done.11), channel_id=1, source_target_pairs={{0,4},{4,0},{8,12},{12,8},{16,20},{20,16},{24,28},{28,24},{32,36},... | collective-permute-start | bytes 1572872 | tf_op jit(solution)/shard_map/ppermute | solution.py:276
  62.9 19.0 %collective-permute-start.14 = (bf16[2,4,2,128,128]{4,3,2,1,0:T(8,128)(2,1)}, bf16[2,4,2,128,128]{4,3,2,1,0:T(8,128)(2,1)}, u32[]{:S(2)}, u32[]{:S(2)}) collective-permute-start(bf16[2,4,2,128,128]{4,3,2,1,0:T(8,128)(2,1)} %collective-permute-done.13), channel_id=1, source_target_pairs={{0,4},{4,0},{8,12},{12,8},{16,20},{20,16},{24,28},{28,24},{32,36},... | collective-permute-start | bytes 1572872 | tf_op jit(solution)/shard_map/ppermute | solution.py:276
  62.9 7.0 %collective-permute-start.1 = (bf16[2,256,128]{2,1,0:T(8,128)(2,1)S(1)}, bf16[2,256,128]{2,1,0:T(8,128)(2,1)S(1)}, u32[]{:S(2)}, u32[]{:S(2)}) collective-permute-start(bf16[2,256,128]{2,1,0:T(8,128)(2,1)S(1)} %get-tuple-element.22), channel_id=1, source_target_pairs={{4,0},{8,4},{12,8},{16,12},{20,16},{24,20},{28,24},{32,28},{36,32}... | collective-permute-start | bytes 393224 | tf_op jit(solution)/shard_map/ppermute | solution.py:375
  69.9 12.4 %collective-permute-start.17 = (bf16[4,2,128,128]{3,2,1,0:T(8,128)(2,1)}, bf16[4,2,128,128]{3,2,1,0:T(8,128)(2,1)}, u32[]{:S(2)}, u32[]{:S(2)}) collective-permute-start(bf16[4,2,128,128]{3,2,1,0:T(8,128)(2,1)} %slice_bitcast_fusion.1), channel_id=1, source_target_pairs={{0,8},{4,60},{8,16},{12,4},{16,24},{20,12},{24,32},{28,20},{32,40}... | collective-permute-start | bytes 786440 | tf_op jit(solution)/shard_map/ppermute | solution.py:276
  75.0 9.1 %collective-permute-start.6 = (bf16[8,2,128,128]{3,2,1,0:T(8,128)(2,1)}, bf16[8,2,128,128]{3,2,1,0:T(8,128)(2,1)S(1)}, u32[]{:S(2)}, u32[]{:S(2)}) collective-permute-start(bf16[8,2,128,128]{3,2,1,0:T(8,128)(2,1)} %collective-permute-done.5), channel_id=1, source_target_pairs={{0,4},{4,0},{8,12},{12,8},{16,20},{20,16},{24,28},{28,24},{32,36},... | collective-permute-start | bytes 1572872 | tf_op jit(solution)/shard_map/ppermute | solution.py:276
  79.2 62.8 %collective-permute-start.22 = (bf16[512,1024]{1,0:T(8,128)(2,1)}, bf16[512,1024]{1,0:T(8,128)(2,1)S(1)}, u32[]{:S(2)}, u32[]{:S(2)}) collective-permute-start(bf16[512,1024]{1,0:T(8,128)(2,1)} %get-tuple-element.32), channel_id=1, source_target_pairs={{1,0},{2,1},{3,2},{0,3},{5,4},{6,5},{7,6},{4,7},{9,8},{10,9},{11,1... | collective-permute-start | bytes 3145736 | tf_op jit(solution)/shard_map/ppermute | solution.py:265
  81.9 60.1 %collective-permute-start.23 = (bf16[512,1024]{1,0:T(8,128)(2,1)}, bf16[512,1024]{1,0:T(8,128)(2,1)S(1)}, u32[]{:S(2)}, u32[]{:S(2)}) collective-permute-start(bf16[512,1024]{1,0:T(8,128)(2,1)} %get-tuple-element.34), channel_id=1, source_target_pairs={{2,0},{3,1},{0,2},{1,3},{6,4},{7,5},{4,6},{5,7},{10,8},{11,9},{8,1... | collective-permute-start | bytes 3145736 | tf_op jit(solution)/shard_map/ppermute | solution.py:265
  82.4 62.4 %collective-permute-start.24 = (bf16[512,1024]{1,0:T(8,128)(2,1)}, bf16[512,1024]{1,0:T(8,128)(2,1)S(1)}, u32[]{:S(2)}, u32[]{:S(2)}) collective-permute-start(bf16[512,1024]{1,0:T(8,128)(2,1)} %get-tuple-element.31), channel_id=1, source_target_pairs={{3,0},{0,1},{1,2},{2,3},{7,4},{4,5},{5,6},{6,7},{11,8},{8,9},{9,10... | collective-permute-start | bytes 3145736 | tf_op jit(solution)/shard_map/ppermute | solution.py:265
  82.9 26.3 %collective-permute-start.16 = (bf16[2,4,2,128,128]{4,3,2,1,0:T(8,128)(2,1)S(1)}, bf16[2,4,2,128,128]{4,3,2,1,0:T(8,128)(2,1)S(1)}, u32[]{:S(2)}, u32[]{:S(2)}) collective-permute-start(bf16[2,4,2,128,128]{4,3,2,1,0:T(8,128)(2,1)S(1)} %collective-permute-done.15), channel_id=1, source_target_pairs={{0,4},{4,0},{8,12},{12,8},{16,20},{20,16},{24,28},{28,24},{32,36},... | collective-permute-start | bytes 1572872 | tf_op jit(solution)/shard_map/ppermute | solution.py:276
  84.2 25.1 %collective-permute-start.18 = (bf16[4,2,128,128]{3,2,1,0:T(8,128)(2,1)}, bf16[4,2,128,128]{3,2,1,0:T(8,128)(2,1)S(1)}, u32[]{:S(2)}, u32[]{:S(2)}) collective-permute-start(bf16[4,2,128,128]{3,2,1,0:T(8,128)(2,1)} %collective-permute-done.17), channel_id=1, source_target_pairs={{0,4},{4,0},{8,12},{12,8},{16,20},{20,16},{24,28},{28,24},{32,36},... | collective-permute-start | bytes 786440 | tf_op jit(solution)/shard_map/ppermute | solution.py:276
  93.3 16.7 %copy-start.8 = (bf16[1,2,256,128]{3,2,1,0:T(8,128)(2,1)S(1)}, bf16[1,2,256,128]{3,2,1,0:T(8,128)(2,1)}, u32[]{:S(2)}) copy-start(bf16[1,2,256,128]{3,2,1,0:T(8,128)(2,1)} %param.8) | copy-start | bytes 393220
  111.1 16.1 %copy-start.1 = (bf16[64,128,128]{2,1,0:T(8,128)(2,1)S(1)}, bf16[64,128,128]{2,1,0:T(8,128)(2,1)}, u32[]{:S(2)}) copy-start(bf16[64,128,128]{2,1,0:T(8,128)(2,1)} %get-tuple-element.25.keys_ref) | copy-start | bytes 6291460
  111.1 16.1 %copy-start.4 = (f32[2,4,256,128]{3,2,1,0:T(8,128)S(1)}, f32[2,4,256,128]{3,2,1,0:T(8,128)}, u32[]{:S(2)}) copy-start(f32[2,4,256,128]{3,2,1,0:T(8,128)} %copy-done.3) | copy-start | bytes 3145732
  123.8 21.5 %collective-permute-start.25 = (bf16[256,512]{1,0:T(8,128)(2,1)S(1)}, bf16[256,512]{1,0:T(8,128)(2,1)S(1)}, u32[]{:S(2)}, u32[]{:S(2)}) collective-permute-start(bf16[256,512]{1,0:T(8,128)(2,1)S(1)} %get-tuple-element.30.a0), channel_id=1, source_target_pairs={{1,0},{2,1},{3,2},{0,3},{5,4},{6,5},{7,6},{4,7},{9,8},{10,9},{11,1... | collective-permute-start | bytes 786440 | tf_op jit(solution)/shard_map/ppermute | solution.py:265
  126.1 19.3 %collective-permute-start.26 = (bf16[256,512]{1,0:T(8,128)(2,1)S(1)}, bf16[256,512]{1,0:T(8,128)(2,1)S(1)}, u32[]{:S(2)}, u32[]{:S(2)}) collective-permute-start(bf16[256,512]{1,0:T(8,128)(2,1)S(1)} %get-tuple-element.30.a0), channel_id=1, source_target_pairs={{2,0},{3,1},{0,2},{1,3},{6,4},{7,5},{4,6},{5,7},{10,8},{11,9},{8,1... | collective-permute-start | bytes 786440 | tf_op jit(solution)/shard_map/ppermute | solution.py:265
  141.9 9.1 %collective-permute-start.27 = (bf16[256,512]{1,0:T(8,128)(2,1)S(1)}, bf16[256,512]{1,0:T(8,128)(2,1)S(1)}, u32[]{:S(2)}, u32[]{:S(2)}) collective-permute-start(bf16[256,512]{1,0:T(8,128)(2,1)S(1)} %get-tuple-element.30.a0), channel_id=1, source_target_pairs={{3,0},{0,1},{1,2},{2,3},{7,4},{4,5},{5,6},{6,7},{11,8},{8,9},{9,10... | collective-permute-start | bytes 786440 | tf_op jit(solution)/shard_map/ppermute | solution.py:265
  142.0 12.1 %collective-permute-start.19 = (bf16[256,512]{1,0:T(8,128)(2,1)S(1)}, bf16[256,512]{1,0:T(8,128)(2,1)S(1)}, u32[]{:S(2)}, u32[]{:S(2)}) collective-permute-start(bf16[256,512]{1,0:T(8,128)(2,1)S(1)} %attend1.1.a0), channel_id=1, source_target_pairs={{1,0},{2,1},{3,2},{0,3},{5,4},{6,5},{7,6},{4,7},{9,8},{10,9},{11,1... | collective-permute-start | bytes 786440 | tf_op jit(solution)/shard_map/ppermute | solution.py:265
  144.7 10.5 %collective-permute-start.20 = (bf16[256,512]{1,0:T(8,128)(2,1)S(1)}, bf16[256,512]{1,0:T(8,128)(2,1)S(1)}, u32[]{:S(2)}, u32[]{:S(2)}) collective-permute-start(bf16[256,512]{1,0:T(8,128)(2,1)S(1)} %attend1.1.a0), channel_id=1, source_target_pairs={{2,0},{3,1},{0,2},{1,3},{6,4},{7,5},{4,6},{5,7},{10,8},{11,9},{8,1... | collective-permute-start | bytes 786440 | tf_op jit(solution)/shard_map/ppermute | solution.py:265
  145.4 16.2 %collective-permute-start.21 = (bf16[256,512]{1,0:T(8,128)(2,1)S(1)}, bf16[256,512]{1,0:T(8,128)(2,1)S(1)}, u32[]{:S(2)}, u32[]{:S(2)}) collective-permute-start(bf16[256,512]{1,0:T(8,128)(2,1)S(1)} %attend1.1.a0), channel_id=1, source_target_pairs={{3,0},{0,1},{1,2},{2,3},{7,4},{4,5},{5,6},{6,7},{11,8},{8,9},{9,10... | collective-permute-start | bytes 786440 | tf_op jit(solution)/shard_map/ppermute | solution.py:265
  (11 other events, 60.9 us)

commit v3 on v2

--- a/solution.py
+++ b/solution.py
@@ -15,6 +15,7 @@
 GROUP = 8
 SPAN = GROUP * BLOCK
 LISTED = 64
+UNROLL = 4
 X_CHIPS = 4
 HEADS = 4
 EXP_SCALE = math.log2(math.e) * HEAD ** (-0.5)
@@ -32,7 +33,7 @@
     return lax.dot_general(a, b, (((1,), (1,)), ((), ())), preferred_element_type=F32)
 
 
-def pack_kernel(ctx_count, me_ref, table_ref, k_ref, v_ref, keys_ref, vals_ref, ahead_ref, back_ref):
+def pack_kernel(ctx_count, me_ref, table_ref, k_ref, v_ref, pay_ref, ahead_ref, back_ref):
     me = me_ref[0]
     table = table_ref[...]
     stretch = table // 2
@@ -45,15 +46,15 @@
         found = jnp.min(jnp.where(mine, at, LISTED))
         loc = jnp.sum(jnp.where(at == found, local, 0))
         mine = mine & (at > found)
-        keys_ref[slot] = k_ref[loc]
-        vals_ref[slot] = v_ref[loc]
+        pay_ref[0, slot] = k_ref[loc]
+        pay_ref[1, slot] = v_ref[loc]
     for half, ref in ((0, ahead_ref), (1, back_ref)):
         for part in range(2):
             ref[0, part * BLOCK : (part + 1) * BLOCK] = k_ref[2 * half + part]
             ref[1, part * BLOCK : (part + 1) * BLOCK] = v_ref[2 * half + part]
 
 
-def plan_kernel(ctx_count, me_ref, table_ref, blk_ref, inv_ref, meta_ref, count, place):
+def plan_kernel(ctx_count, arrivals, me_ref, table_ref, blk_ref, at_ref, meta_ref, count, place, inv_ref):
     me = me_ref[0]
     stretches = 2 * ctx_count
     near, far = me, stretches - 1 - me
@@ -70,7 +71,7 @@
 
     def assign(j, _):
         b = table_ref[0, j]
-        stretch = b // 2
+        stretch = lax.div(b, 2)
         owner = jnp.where(stretch < ctx_count, stretch, stretches - 1 - stretch)
         rank = count[owner]
         count[owner] = rank + 1
@@ -96,6 +97,8 @@
 
     zero = jnp.int32(0)
     _, full0, seen0, full1, seen1 = lax.fori_loop(0, 4 * ctx_count, order, (zero,) * 5)
+    for i, (owner, slot) in enumerate(arrivals(me)):
+        at_ref[i] = inv_ref[owner * CAP + slot]
     for st, (s, full, seen) in enumerate(((near, full0, seen0), (far, full1, seen1))):
         meta_ref[8 * st] = full
         meta_ref[8 * st + 1] = seen
@@ -139,18 +142,23 @@
             top_ref[st, h] = top
 
 
-def fetch(inv_ref, me, pieces, origins, target_ref, sems):
-    for ref, origin in zip(pieces, origins):
-        def start(i, _, ref=ref, origin=origin):
-            at = inv_ref[origin(me, i)]
-
-            @pl.when(at >= 0)
-            def _():
-                pltpu.make_async_copy(ref.at[i], target_ref.at[at], sems.at[at // GROUP]).start()
+def fetch(at_ref, pieces, target_ref, sems):
+    base = 0
+    for ref in pieces:
+        def start(i, _, ref=ref, base=base):
+            for n in range(UNROLL):
+                at = at_ref[base + i * UNROLL + n]
+
+                @pl.when(at >= 0)
+                def _(n=n, at=at):
+                    pltpu.make_async_copy(
+                        ref.at[i * UNROLL + n], target_ref.at[at], sems.at[lax.div(at, GROUP)]
+                    ).start()
 
             return 0
 
-        lax.fori_loop(0, ref.shape[0], start, 0)
+        lax.fori_loop(0, ref.shape[0] // UNROLL, start, 0)
+        base += ref.shape[0]
 
 
 def arrived(target_ref, sems, g):
@@ -163,9 +171,9 @@
     return [lead <= s * STRETCH - blk_ref[g * GROUP + n] * BLOCK for n in range(GROUP)]
 
 
-def top_kernel(origins, meta_ref, blk_ref, inv_ref, q_ref, top_in_ref, *refs):
+def top_kernel(meta_ref, blk_ref, at_ref, q_ref, top_in_ref, *refs):
     pieces, (keys_ref, top_ref, sems) = refs[:-3], refs[-3:]
-    fetch(inv_ref, meta_ref[3], pieces, origins, keys_ref, sems)
+    fetch(at_ref, pieces, keys_ref, sems)
 
     def ready(g, _):
         arrived(keys_ref, sems, g)
@@ -198,13 +206,13 @@
             top_ref[st, h] = jnp.broadcast_to(row, (STRETCH, BLOCK))
 
 
-def out_kernel(ctx_count, st, origins, meta_ref, blk_ref, inv_ref, q_ref, keys_ref, top_ref, mask_ref, k_ref, v_ref, ahead_ref, back_ref, *refs):
+def out_kernel(ctx_count, st, arriving, meta_ref, blk_ref, at_ref, q_ref, keys_ref, top_ref, mask_ref, k_ref, v_ref, ahead_ref, back_ref, *refs):
     full, seen, s = meta_ref[8 * st], meta_ref[8 * st + 1], meta_ref[8 * st + 2]
     me = meta_ref[8 * st + 3]
     plain, groups = full // GROUP, (seen + GROUP - 1) // GROUP
-    if origins:
-        pieces, (out_ref, vals, total, acc, sems) = refs[:-5], refs[-5:]
-        fetch(inv_ref, me, pieces, origins, vals, sems)
+    if arriving:
+        pieces, (out_ref, vals, total, acc, sems) = refs[:arriving], refs[-5:]
+        fetch(at_ref, pieces, vals, sems)
     else:
         vals, out_ref, total, acc = refs
     k_before = band_halves(k_ref, ahead_ref, back_ref, 0, st, me, ctx_count)
@@ -225,7 +233,7 @@
         ) + jnp.dot(jnp.concatenate(weights[2:], axis=1), v_ref[st], preferred_element_type=F32)
 
     def step(masked, g, _):
-        if origins:
+        if arriving:
             arrived(vals, sems, g)
         keys = keys_ref[pl.ds(g * GROUP, GROUP)].reshape(SPAN, HEAD)
         values = vals[pl.ds(g * GROUP, GROUP)].reshape(SPAN, HEAD)
@@ -243,7 +251,7 @@
 
     lax.fori_loop(0, plain, functools.partial(step, False), 0)
     lax.fori_loop(plain, groups, functools.partial(step, True), 0)
-    if origins:
+    if arriving:
         def ready(g, _):
             arrived(vals, sems, g)
             return 0
@@ -265,79 +273,91 @@
     return lax.ppermute(x, axis, [((i + shift) % n, i) for i in range(n)])
 
 
-def gather_columns(mesh_sizes, keys, vals):
-    nx, nz = mesh_sizes
+def line_kernel(*refs):
+    pieces, out_ref = refs[:-1], refs[-1]
+    for n, ref in enumerate(pieces):
+        for which in range(2):
+            out_ref[which, n * CAP : (n + 1) * CAP] = ref[which]
+
+
+def chip_kernel(own_ref, other_ref, keys_ref, vals_ref):
+    count = own_ref.shape[1]
+    for which, ref in ((0, keys_ref), (1, vals_ref)):
+        ref[:count] = own_ref[which]
+        ref[count:] = other_ref[which]
+
+
+def half_kernel(keys_ref, vals_ref, *refs):
+    for source, target in ((keys_ref, refs[-2]), (vals_ref, refs[-1])):
+        target[...] = source[...]
+
+
+def gather_columns(nx, nz, payload, ready):
     place = lambda x, z, c: ((x % nx) * nz + z % nz) * 2 + c
     every = [(x, z, c) for x in range(nx) for z in range(nz) for c in range(2)]
     route = lambda f: [(place(*d), place(*f(*d))) for d in every]
     across = route(lambda x, z, c: (x, z, 1 - c))
-    along_x = route(lambda x, z, c: (x + 1 - 2 * c, z, c))
-    along_z = route(lambda x, z, c: (x, z + 1 - 2 * c, c))
+    along = route(lambda x, z, c: (x, z + 1 - 2 * c, c))
     send = lambda a, r: lax.ppermute(a, "ctx", r)
-    lines = [[place(x, z, c) for z in range(nz)] for x in range(nx) for c in range(2)]
-
-    line = [vals] + [send(vals, route(lambda x, z, c, n=n: (x - n, z, c))) for n in range(1, nx)]
-    own = jnp.stack(line)
-    chip = jnp.stack([own, send(own, across)])
-    v_pieces = [chip]
-    own_k = lax.all_to_all(jnp.broadcast_to(keys[None], (nz,) + keys.shape), "ctx", 0, 0, axis_index_groups=lines)
-    moving = chip
-    for n in range(1, nz // 2):
-        moving = send(moving, along_z)
-        v_pieces += [moving, send(moving, across)]
-    last = send(moving[0], along_z)
-    v_pieces += [last, send(last, across)]
-
-    chip_k = jnp.stack([own_k, send(own_k, across)])
-    one = send(chip_k, along_x)
-    two = send(one[0], along_x)
-    k_pieces = [chip_k, one, send(one, across), two, send(two, across)]
-
-    def where(me):
-        return me // (2 * nz), (me // 2) % nz, me % 2
-
-    def entry(x, z, c, slot):
-        return (((x + nx) % nx * nz + (z + nz) % nz) * 2 + c) * CAP + slot
-
-    def k_origin(hops, mirrored, half):
-        def origin(me, i):
-            x, z, c = where(me)
-            side = (2 * c - 1) * hops
-            h = half if half is not None else i // (nz * CAP)
-            core = jnp.where(h == 0, c, 1 - c)
-            i = i % (nz * CAP)
-            if mirrored:
-                side, core = -side, 1 - core
-            return entry(x + side, i // CAP, core, i % CAP)
-
-        return origin
-
-    def v_origin(hops, mirrored, half):
-        def origin(me, i):
-            x, z, c = where(me)
-            side = (2 * c - 1) * hops
-            h = half if half is not None else i // (nx * CAP)
-            core = jnp.where(h == 0, c, 1 - c)
-            i = i % (nx * CAP)
-            if mirrored:
-                side, core = -side, 1 - core
-            return entry(x + i // CAP, z + side, core, i % CAP)
-
-        return origin
-
-    k_origins = [
-        k_origin(0, False, None),
-        k_origin(1, False, None),
-        k_origin(1, True, None),
-        k_origin(2, False, 0),
-        k_origin(2, True, 0),
-    ]
-    v_origins = [v_origin(0, False, None)]
-    for n in range(1, nz // 2):
-        v_origins += [v_origin(n, False, None), v_origin(n, True, None)]
-    v_origins += [v_origin(nz // 2, False, 0), v_origin(nz // 2, True, 0)]
-    flat = lambda pieces: [p.reshape(-1, BLOCK, HEAD) for p in pieces]
-    return flat(k_pieces), tuple(k_origins), flat(v_pieces), tuple(v_origins)
+
+    shape = jax.ShapeDtypeStruct
+    call = functools.partial(pl.pallas_call, compiler_params=PARAMS)
+    size = nx * CAP
+    line = [payload] + [send(payload, route(lambda x, z, c, n=n: (x - n, z, c))) for n in range(1, nx)]
+    own = call(
+        line_kernel,
+        out_shape=shape((2, size, BLOCK, HEAD), BF16),
+        in_specs=[VMEM()] * nx,
+        out_specs=VMEM(),
+        name="line",
+    )(*line)
+    moving = call(
+        chip_kernel,
+        out_shape=[shape((2 * size, BLOCK, HEAD), BF16)] * 2,
+        in_specs=[VMEM()] * 2,
+        out_specs=[VMEM()] * 2,
+        name="chip",
+    )(own, send(own, across))
+    pieces = [[m] for m in moving]
+    for n in range(1, nz // 2 + 1):
+        if n == nz // 2:
+            moving = call(
+                half_kernel,
+                grid=(1,),
+                out_shape=[shape((size, BLOCK, HEAD), BF16)] * 2,
+                in_specs=[pl.BlockSpec((size, BLOCK, HEAD), lambda i: (0, 0, 0))] * 2 + [ANY()] * len(ready),
+                out_specs=[VMEM()] * 2,
+                name="half",
+            )(*moving, *ready)
+        moving = [send(m, along) for m in moving]
+        for which in range(2):
+            pieces[which] += [moving[which], send(moving[which], across)]
+
+    return pieces
+
+
+def arrivals(nx, nz, me):
+    x, z, c = lax.div(me, 2 * nz), lax.rem(lax.div(me, 2), nz), lax.rem(me, 2)
+    lines = [lax.rem(x + n, nx) * nz for n in range(nx)]
+    entries = []
+
+    def piece(hops, mirrored, halves):
+        side = (2 * c - 1) * hops
+        at = lax.rem(z + nz + (-side if mirrored else side), nz)
+        for half in range(halves):
+            core = 1 - c if mirrored != (half == 1) else c
+            for n in range(nx):
+                entries.extend(((lines[n] + at) * 2 + core, slot) for slot in range(CAP))
+
+    piece(0, False, 2)
+    for n in range(1, nz // 2 + 1):
+        for mirrored in (False, True):
+            piece(n, mirrored, 2 if n < nz // 2 else 1)
+    return entries
+
+
+def cost(us):
+    return pl.CostEstimate(flops=0, bytes_accessed=int(us * 3.0e6), transcendentals=0)
 
 
 def per_device(queries, keys, values, column_block_table, slash_offsets, out_weight):
@@ -349,24 +369,24 @@
     shape = jax.ShapeDtypeStruct
     i32 = jnp.int32
 
-    send_keys, send_vals, ahead, back = pl.pallas_call(
+    payload, ahead, back = pl.pallas_call(
         functools.partial(pack_kernel, ctx_count),
-        out_shape=[shape((CAP, BLOCK, HEAD), BF16)] * 2 + [shape((2, STRETCH, HEAD), BF16)] * 2,
+        out_shape=[shape((2, CAP, BLOCK, HEAD), BF16)] + [shape((2, STRETCH, HEAD), BF16)] * 2,
         in_specs=[SMEM(), VMEM(), VMEM(), VMEM()],
-        out_specs=[VMEM()] * 4,
+        out_specs=[VMEM()] * 3,
         compiler_params=PARAMS,
         name="pack",
     )(me, column_block_table, k.reshape(4, BLOCK, HEAD), v.reshape(4, BLOCK, HEAD))
 
-    k_pieces, k_origins, v_pieces, v_origins = gather_columns((X_CHIPS, ctx_count // (2 * X_CHIPS)), send_keys, send_vals)
-
-    blk, inv, meta = pl.pallas_call(
-        functools.partial(plan_kernel, ctx_count),
-        out_shape=[shape((128,), i32), shape((256,), i32), shape((16,), i32)],
+    sides = (X_CHIPS, ctx_count // (2 * X_CHIPS))
+    blk, at, meta = pl.pallas_call(
+        functools.partial(plan_kernel, ctx_count, functools.partial(arrivals, *sides)),
+        out_shape=[shape((128,), i32), shape((CAP * ctx_count,), i32), shape((16,), i32)],
         in_specs=[SMEM(), SMEM()],
         out_specs=[SMEM()] * 3,
-        scratch_shapes=[pltpu.SMEM((ctx_count,), i32), pltpu.SMEM((4 * ctx_count,), i32)],
+        scratch_shapes=[pltpu.SMEM((ctx_count,), i32), pltpu.SMEM((4 * ctx_count,), i32), pltpu.SMEM((4 * ctx_count,), i32)],
         compiler_params=PARAMS,
+        cost_estimate=cost(8),
         name="plan",
     )(me, column_block_table)
 
@@ -387,43 +407,49 @@
         in_specs=[SMEM(), SMEM(), VMEM(), VMEM(), VMEM(), VMEM()],
         out_specs=[VMEM(), VMEM()],
         compiler_params=PARAMS,
+        cost_estimate=cost(3),
         name="band",
     )(meta, slash_offsets, q, k, before, after)
 
+    k_pieces, v_pieces = gather_columns(*sides, payload, [mask])
+
     columns, top = pl.pallas_call(
-        functools.partial(top_kernel, k_origins),
+        top_kernel,
         out_shape=[shape((LISTED, BLOCK, HEAD), BF16), shape((2, HEADS, STRETCH, BLOCK), F32)],
         in_specs=[SMEM(), SMEM(), SMEM(), VMEM(), VMEM()] + [ANY()] * len(k_pieces),
         out_specs=[VMEM(), VMEM()],
         scratch_shapes=[pltpu.SemaphoreType.DMA((LISTED // GROUP,))],
         compiler_params=PARAMS,
+        cost_estimate=cost(9),
         name="top",
-    )(meta, blk, inv, q, top, *k_pieces)
+    )(meta, blk, at, q, top, *k_pieces)
 
     mixed = column_vals = None
     for st in range(2):
-        arriving = st == 0
+        first = st == 0
+        extra = [*v_pieces, *slabs] if first else [column_vals]
         result = pl.pallas_call(
-            functools.partial(out_kernel, ctx_count, st, v_origins if arriving else ()),
+            functools.partial(out_kernel, ctx_count, st, len(v_pieces) if first else 0),
             grid=(1,),
-            out_shape=[shape((STRETCH, HEADS * HEAD), BF16)] + [shape((LISTED, BLOCK, HEAD), BF16)] * arriving,
+            out_shape=[shape((STRETCH, HEADS * HEAD), BF16)] + [shape((LISTED, BLOCK, HEAD), BF16)] * first,
             in_specs=[
                 SMEM(), SMEM(), SMEM(),
                 pl.BlockSpec((1, STRETCH, HEADS * HEAD), lambda i, st=st: (st, 0, 0)),
                 VMEM(),
                 pl.BlockSpec((1, HEADS, STRETCH, BLOCK), lambda i, st=st: (st, 0, 0, 0)),
                 VMEM(), VMEM(), VMEM(), VMEM(), VMEM(),
-            ] + ([ANY()] * len(v_pieces) if arriving else [VMEM()]),
-            out_specs=[VMEM()] * (1 + arriving),
+            ] + ([ANY()] * len(extra) if first else [VMEM()]),
+            out_specs=[VMEM()] * (1 + first),
             scratch_shapes=[
                 pltpu.VMEM((HEADS, STRETCH, BLOCK), F32),
                 pltpu.VMEM((HEADS, STRETCH, HEAD), F32),
-            ] + [pltpu.SemaphoreType.DMA((LISTED // GROUP,))] * arriving,
+            ] + [pltpu.SemaphoreType.DMA((LISTED // GROUP,))] * first,
             compiler_params=PARAMS,
+            cost_estimate=cost(8),
             name=f"attend{st}",
-        )(meta, blk, inv, q, columns, top, mask, k, v, before, after, *(v_pieces if arriving else [column_vals]))
+        )(meta, blk, at, q, columns, top, mask, k, v, before, after, *extra)
         head_out = result[0]
-        if arriving:
+        if first:
             column_vals = result[1]
         parts = [head_out] + [from_ahead(head_out, "tp", shift) for shift in range(1, tp)]
         tile = width // 4
@@ -437,6 +463,7 @@
             out_specs=pl.BlockSpec((1, STRETCH, tile), lambda i, st=st: (st, 0, i)),
             input_output_aliases={8: 0} if st else {},
             compiler_params=PARAMS,
+            cost_estimate=cost(3),
             name=f"mix{st}",
         )(*parts, *slabs, *([mixed] if st else []))
     return mixed[None]

time: 165 us -> 150 us (0.909)
  the two profiles are of different devices: /device:TPU:1 before, /device:TPU:96 now
where the time goes in v3:
time: 150 us; the launch traced here: 147 us
  Pallas kernels  54.4 us (36%)
  starting transfers between devices  44.8 us (30%)
  waiting for transfers between devices  37.2 us (25%)
  local copies, waits for them, and re-layouts  10.4 us (7%)
    ppermute x20, starting transfers between devices, gather_columns(): send = lambda a, r: lax.ppermute(a, 'ctx', r)  26.3 us
    pallas_call x2, Pallas kernels, per_device(): pl.pallas_call(functools.partial(out_kernel, ctx_count, st, len(v_pieces)...  26 us
    ppermute x20, waiting for transfers between devices, gather_columns(): send = lambda a, r: lax.ppermute(a, 'ctx', r)  21.6 us
    ppermute x9, starting transfers between devices, from_ahead(): return lax.ppermute(x, axis, [((i + shift) % n, i) for i in range(n)])  14.6 us
    pallas_call x1, Pallas kernels, per_device(): pl.pallas_call(top_kernel, out_shape=[shape((LISTED, BLOCK, HEAD), BF16),...  13.6 us
    ppermute x9, waiting for transfers between devices, from_ahead(): return lax.ppermute(x, axis, [((i + shift) % n, i) for i in range(n)])  7.29 us
    unnamed x44, local copies, waits for them, and re-layouts  6.4 us
    pallas_call x2, Pallas kernels, per_device(): pl.pallas_call(mix_kernel, grid=(width // tile,), out_shape=shape((2, STR...  6.19 us
  transfers between devices with their start and end apart: 31, of which 12 were waited for; matrix products, arithmetic and copies ran while one was open for 3% of the time, Pallas kernels for 27%

profile of v3, /device:TPU:96, one launch (start us, length us, event | category | flops | bytes accessed | tf_op | source)
XLA Modules:
  0.0 147.0 jit_solution(1622813169963359970)
XLA Ops:
  3.0 1.6 %collective-permute-start.4 = (bf16[2,2,128,128]{3,2,1,0:T(8,128)(2,1)S(1)}, bf16[2,2,128,128]{3,2,1,0:T(8,128)(2,1)S(1)}, u32[]{:S(2)}, u32[]{:S(2)}) collective-permute-start(bf16[2,2,128,128]{3,2,1,0:T(8,128)(2,1)S(1)} %get-tuple-element.27.refs_0_), channel_id=1, source_target_pairs={{0,64},{4,68},{8,72},{12,76},{16,80},{20,84},{24,88},{28,92},{32,9... | collective-permute-start | bytes 393224 | tf_op jit(solution)/shard_map/ppermute | solution.py:301
  4.6 2.7 %collective-permute-start.3 = (bf16[2,2,128,128]{3,2,1,0:T(8,128)(2,1)S(1)}, bf16[2,2,128,128]{3,2,1,0:T(8,128)(2,1)S(1)}, u32[]{:S(2)}, u32[]{:S(2)}) collective-permute-start(bf16[2,2,128,128]{3,2,1,0:T(8,128)(2,1)S(1)} %get-tuple-element.27.refs_0_), channel_id=1, source_target_pairs={{0,128},{4,132},{8,136},{12,140},{16,144},{20,148},{24,152},{28,15... | collective-permute-start | bytes 393224 | tf_op jit(solution)/shard_map/ppermute | solution.py:301
  7.3 1.4 collective-permute-start.2
  9.7 3.6 %collective-permute-done.3.refs_2_ = bf16[2,2,128,128]{3,2,1,0:T(8,128)(2,1)S(1)} collective-permute-done((bf16[2,2,128,128]{3,2,1,0:T(8,128)(2,1)S(1)}, bf16[2,2,128,128]{3,2,1,0:T(8,128)(2,1)S(1)}, u32[]{:S(2)}, u32[]{:S(2)}) %collective-permute-start.3) | collective-permute-done | bytes 131104 | tf_op jit(solution)/shard_map/ppermute | solution.py:301
  13.5 1.9 %collective-permute-done.5.other_ref = bf16[2,8,128,128]{3,2,1,0:T(8,128)(2,1)S(1)} collective-permute-done((bf16[2,8,128,128]{3,2,1,0:T(8,128)(2,1)S(1)}, bf16[2,8,128,128]{3,2,1,0:T(8,128)(2,1)S(1)}, u32[]{:S(2)}, u32[]{:S(2)}) %collective-permute-start.5) | collective-permute-done | bytes 524320 | tf_op jit(solution)/shard_map/ppermute | solution.py:301
  15.4 3.2 %collective-permute-start.6 = (bf16[16,128,128]{2,1,0:T(8,128)(2,1)S(1)}, bf16[16,128,128]{2,1,0:T(8,128)(2,1)S(1)}, u32[]{:S(2)}, u32[]{:S(2)}) collective-permute-start(bf16[16,128,128]{2,1,0:T(8,128)(2,1)S(1)} %get-tuple-element.28.refs_0_), channel_id=1, source_target_pairs={{0,8},{4,60},{8,16},{12,4},{16,24},{20,12},{24,32},{28,20},{32,40}... | collective-permute-start | bytes 1572872 | tf_op jit(solution)/shard_map/ppermute | solution.py:301
  19.7 5.7 %collective-permute-done.6.refs_1_ = bf16[16,128,128]{2,1,0:T(8,128)(2,1)S(1)} collective-permute-done((bf16[16,128,128]{2,1,0:T(8,128)(2,1)S(1)}, bf16[16,128,128]{2,1,0:T(8,128)(2,1)S(1)}, u32[]{:S(2)}, u32[]{:S(2)}) %collective-permute-start.6) | collective-permute-done | bytes 524320 | tf_op jit(solution)/shard_map/ppermute | solution.py:301
  25.3 3.7 %collective-permute-start.8 = (bf16[16,128,128]{2,1,0:T(8,128)(2,1)S(1)}, bf16[16,128,128]{2,1,0:T(8,128)(2,1)S(1)}, u32[]{:S(2)}, u32[]{:S(2)}) collective-permute-start(bf16[16,128,128]{2,1,0:T(8,128)(2,1)S(1)} %collective-permute-done.6.refs_1_), channel_id=1, source_target_pairs={{0,8},{4,60},{8,16},{12,4},{16,24},{20,12},{24,32},{28,20},{32,40}... | collective-permute-start | bytes 1572872 | tf_op jit(solution)/shard_map/ppermute | solution.py:301
  29.0 1.9 %collective-permute-done.12.refs_1_ = bf16[16,128,128]{2,1,0:T(8,128)(2,1)S(1)} collective-permute-done((bf16[16,128,128]{2,1,0:T(8,128)(2,1)S(1)}, bf16[16,128,128]{2,1,0:T(8,128)(2,1)S(1)}, u32[]{:S(2)}, u32[]{:S(2)}) %collective-permute-start.12) | collective-permute-done | bytes 524320 | tf_op jit(solution)/shard_map/ppermute | solution.py:301
  31.0 3.7 %collective-permute-start.13 = (bf16[16,128,128]{2,1,0:T(8,128)(2,1)S(1)}, bf16[16,128,128]{2,1,0:T(8,128)(2,1)S(1)}, u32[]{:S(2)}, u32[]{:S(2)}) collective-permute-start(bf16[16,128,128]{2,1,0:T(8,128)(2,1)S(1)} %collective-permute-done.12.refs_1_), channel_id=1, source_target_pairs={{0,8},{4,60},{8,16},{12,4},{16,24},{20,12},{24,32},{28,20},{32,40}... | collective-permute-start | bytes 1572872 | tf_op jit(solution)/shard_map/ppermute | solution.py:301
  34.7 4.0 %constant_dynamic-slice_fusion = (bf16[512,1024]{1,0:T(8,128)(2,1)S(1)}, bf16[512,1024]{1,0:T(8,128)(2,1)S(1)}, bf16[512,1024]{1,0:T(8,128)(2,1)}, bf16[512,1024]{1,0:T(8,128)(2,1)}) fusion(bf16[512,4096]{1,0:T(8,128)(2,1)} %param.11, s32[]{:T(128)S(6)} %select_n.15, s32[]{:T(128)S(6)} %select_n.13, s32[]{:T(128)S(6)} %select_n.12, s32[]{:T(128)S(6)} %select_n.14), kind=kLoop, calls=%fused_computation | loop fusion | bytes 8388624 | tf_op jit(solution)/shard_map/dynamic_slice | solution.py:401
  38.7 1.6 %collective-permute-start.24 = (bf16[512,1024]{1,0:T(8,128)(2,1)S(1)}, bf16[512,1024]{1,0:T(8,128)(2,1)S(1)}, u32[]{:S(2)}, u32[]{:S(2)}) collective-permute-start(bf16[512,1024]{1,0:T(8,128)(2,1)S(1)} %get-tuple-element.37), channel_id=1, source_target_pairs={{3,0},{0,1},{1,2},{2,3},{7,4},{4,5},{5,6},{6,7},{11,8},{8,9},{9,10... | collective-permute-start | bytes 3145736 | tf_op jit(solution)/shard_map/ppermute | solution.py:273
  40.2 1.7 %collective-permute-start.22 = (bf16[512,1024]{1,0:T(8,128)(2,1)S(1)}, bf16[512,1024]{1,0:T(8,128)(2,1)S(1)}, u32[]{:S(2)}, u32[]{:S(2)}) collective-permute-start(bf16[512,1024]{1,0:T(8,128)(2,1)S(1)} %get-tuple-element.38), channel_id=1, source_target_pairs={{1,0},{2,1},{3,2},{0,3},{5,4},{6,5},{7,6},{4,7},{9,8},{10,9},{11,1... | collective-permute-start | bytes 3145736 | tf_op jit(solution)/shard_map/ppermute | solution.py:273
  42.2 3.7 %collective-permute-start.14 = (bf16[16,128,128]{2,1,0:T(8,128)(2,1)S(1)}, bf16[16,128,128]{2,1,0:T(8,128)(2,1)S(1)}, u32[]{:S(2)}, u32[]{:S(2)}) collective-permute-start(bf16[16,128,128]{2,1,0:T(8,128)(2,1)S(1)} %collective-permute-done.13.refs_3_), channel_id=1, source_target_pairs={{0,8},{4,60},{8,16},{12,4},{16,24},{20,12},{24,32},{28,20},{32,40}... | collective-permute-start | bytes 1572872 | tf_op jit(solution)/shard_map/ppermute | solution.py:301
  45.9 1.9 %collective-permute-start = (bf16[2,256,128]{2,1,0:T(8,128)(2,1)S(1)}, bf16[2,256,128]{2,1,0:T(8,128)(2,1)S(1)}, u32[]{:S(2)}, u32[]{:S(2)}) collective-permute-start(bf16[2,256,128]{2,1,0:T(8,128)(2,1)S(1)} %get-tuple-element.24), channel_id=1, source_target_pairs={{0,4},{4,8},{8,12},{12,16},{16,20},{20,24},{24,28},{28,32},{32,36}... | collective-permute-start | bytes 393224 | tf_op jit(solution)/shard_map/ppermute | solution.py:394
  47.8 5.8 %collective-permute-done.ahead_ref = bf16[2,256,128]{2,1,0:T(8,128)(2,1)S(1)} collective-permute-done((bf16[2,256,128]{2,1,0:T(8,128)(2,1)S(1)}, bf16[2,256,128]{2,1,0:T(8,128)(2,1)S(1)}, u32[]{:S(2)}, u32[]{:S(2)}) %collective-permute-start) | collective-permute-done | bytes 131104 | tf_op jit(solution)/shard_map/ppermute | solution.py:394
  53.6 1.9 %collective-permute-start.1 = (bf16[2,256,128]{2,1,0:T(8,128)(2,1)S(1)}, bf16[2,256,128]{2,1,0:T(8,128)(2,1)S(1)}, u32[]{:S(2)}, u32[]{:S(2)}) collective-permute-start(bf16[2,256,128]{2,1,0:T(8,128)(2,1)S(1)} %get-tuple-element.25), channel_id=1, source_target_pairs={{4,0},{8,4},{12,8},{16,12},{20,16},{24,20},{28,24},{32,28},{36,32}... | collective-permute-start | bytes 393224 | tf_op jit(solution)/shard_map/ppermute | solution.py:395
  55.5 2.5 %collective-permute-done.1.back_ref = bf16[2,256,128]{2,1,0:T(8,128)(2,1)S(1)} collective-permute-done((bf16[2,256,128]{2,1,0:T(8,128)(2,1)S(1)}, bf16[2,256,128]{2,1,0:T(8,128)(2,1)S(1)}, u32[]{:S(2)}, u32[]{:S(2)}) %collective-permute-start.1) | collective-permute-done | bytes 131104 | tf_op jit(solution)/shard_map/ppermute | solution.py:395
  58.0 1.7 %collective-permute-start.7 = (bf16[16,128,128]{2,1,0:T(8,128)(2,1)S(1)}, bf16[16,128,128]{2,1,0:T(8,128)(2,1)S(1)}, u32[]{:S(2)}, u32[]{:S(2)}) collective-permute-start(bf16[16,128,128]{2,1,0:T(8,128)(2,1)S(1)} %collective-permute-done.6.refs_1_), channel_id=1, source_target_pairs={{0,4},{4,0},{8,12},{12,8},{16,20},{20,16},{24,28},{28,24},{32,36},... | collective-permute-start | bytes 1572872 | tf_op jit(solution)/shard_map/ppermute | solution.py:301
  59.8 6.0 %plan.1 = (s32[128]{0:T(128)S(1)}, s32[128]{0:T(128)S(1)}, s32[16]{0:T(128)S(1)}) custom-call(s32[1]{0:T(128)} %bitcast.me_ref, s32[1,64]{1,0:T(1,128)S(1)} %copy-done.21), custom_call_target="tpu_custom_call" | custom-call | bytes 24000000 | tf_op jit(solution)/shard_map/plan/pallas_call | solution.py:382
  65.8 1.9 %band.1 = (f32[4,256,512]{2,1,0:T(8,128)S(1)}, f32[2,4,256,128]{3,2,1,0:T(8,128)S(1)}) custom-call(s32[16]{0:T(128)S(1)} %get-tuple-element.21.meta_ref, s32[4,64]{1,0:T(4,128)S(1)} %copy-done.19, bf16[2,256,512]{2,1,0:T(8,128)(2,1)S(1)} %bitcast.7, bf16[2,256,128]{2,1,0:T(8,128)(2,1)S(1)} %bitcast.12, ...), custom_call_target="tpu_custom_call" | custom-call | bytes 9000000 | tf_op jit(solution)/shard_map/band/pallas_call | solution.py:404
  68.7 2.9 %collective-permute-start.23 = (bf16[512,1024]{1,0:T(8,128)(2,1)}, bf16[512,1024]{1,0:T(8,128)(2,1)S(1)}, u32[]{:S(2)}, u32[]{:S(2)}) collective-permute-start(bf16[512,1024]{1,0:T(8,128)(2,1)} %get-tuple-element.40), channel_id=1, source_target_pairs={{2,0},{3,1},{0,2},{1,3},{6,4},{7,5},{4,6},{5,7},{10,8},{11,9},{8,1... | collective-permute-start | bytes 3145736 | tf_op jit(solution)/shard_map/ppermute | solution.py:273
  72.9 5.2 %collective-permute-done.15.refs_7_ = bf16[8,128,128]{2,1,0:T(8,128)(2,1)S(1)} collective-permute-done((bf16[8,128,128]{2,1,0:T(8,128)(2,1)S(1)}, bf16[8,128,128]{2,1,0:T(8,128)(2,1)S(1)}, u32[]{:S(2)}, u32[]{:S(2)}) %collective-permute-start.15) | collective-permute-done | bytes 262176 | tf_op jit(solution)/shard_map/ppermute | solution.py:301
  79.0 1.9 %collective-permute-done.20.refs_7_ = bf16[8,128,128]{2,1,0:T(8,128)(2,1)S(1)} collective-permute-done((bf16[8,128,128]{2,1,0:T(8,128)(2,1)S(1)}, bf16[8,128,128]{2,1,0:T(8,128)(2,1)S(1)}, u32[]{:S(2)}, u32[]{:S(2)}) %collective-permute-start.20) | collective-permute-done | bytes 262176 | tf_op jit(solution)/shard_map/ppermute | solution.py:301
  82.3 13.6 %top.1 = (bf16[64,128,128]{2,1,0:T(8,128)(2,1)}, f32[2,4,256,128]{3,2,1,0:T(8,128)S(1)}) custom-call(s32[16]{0:T(128)S(1)} %get-tuple-element.21.meta_ref, s32[128]{0:T(128)S(1)} %get-tuple-element.22.blk_ref, s32[128]{0:T(128)S(1)} %get-tuple-element.23.at_ref, bf16[2,256,512]{2,1,0:T(8,128)(2,1)S(1)} %bitcast.8, f32[2,4,256,128]{3,2,1,0:T(8,128)} %copy-done.16, ...), custom_call_target="tpu_custom_call" | custom-call | bytes 27000000 | tf_op jit(solution)/shard_map/top/pallas_call | solution.py:416
  98.9 11.2 %attend0.1 = (bf16[256,512]{1,0:T(8,128)(2,1)S(1)}, bf16[64,128,128]{2,1,0:T(8,128)(2,1)}) custom-call(s32[16]{0:T(128)S(1)} %get-tuple-element.21.meta_ref, s32[128]{0:T(128)S(1)} %get-tuple-element.22.blk_ref, s32[128]{0:T(128)S(1)} %get-tuple-element.23.at_ref, bf16[2,256,512]{2,1,0:T(8,128)(2,1)S(1)} %bitcast.9, ...), custom_call_target="tpu_custom_call" | custom-call | bytes 24000000 | tf_op jit(solution)/shard_map/attend0/pallas_call | solution.py:431
  111.0 2.3 %collective-permute-start.29 = (bf16[256,512]{1,0:T(8,128)(2,1)S(1)}, bf16[256,512]{1,0:T(8,128)(2,1)S(1)}, u32[]{:S(2)}, u32[]{:S(2)}) collective-permute-start(bf16[256,512]{1,0:T(8,128)(2,1)S(1)} %get-tuple-element.36.a0), channel_id=1, source_target_pairs={{2,0},{3,1},{0,2},{1,3},{6,4},{7,5},{4,6},{5,7},{10,8},{11,9},{8,1... | collective-permute-start | bytes 786440 | tf_op jit(solution)/shard_map/ppermute | solution.py:273
  114.3 14.9 %attend1.1.a0 = bf16[256,512]{1,0:T(8,128)(2,1)S(1)} custom-call(s32[16]{0:T(128)S(1)} %get-tuple-element.21.meta_ref, s32[128]{0:T(128)S(1)} %get-tuple-element.22.blk_ref, s32[128]{0:T(128)S(1)} %get-tuple-element.23.at_ref, bf16[2,256,512]{2,1,0:T(8,128)(2,1)S(1)} %bitcast.10, bf16[64,128,128]{2,1,0:T(8,128)(2,1)S(1)} %copy-done.9, ...), custom_call_target="tpu_custom_call" | custom-call | bytes 24000000 | tf_op jit(solution)/shard_map/attend1/pallas_call | solution.py:431
  131.5 2.0 %collective-permute-start.25 = (bf16[256,512]{1,0:T(8,128)(2,1)S(1)}, bf16[256,512]{1,0:T(8,128)(2,1)S(1)}, u32[]{:S(2)}, u32[]{:S(2)}) collective-permute-start(bf16[256,512]{1,0:T(8,128)(2,1)S(1)} %attend1.1.a0), channel_id=1, source_target_pairs={{1,0},{2,1},{3,2},{0,3},{5,4},{6,5},{7,6},{4,7},{9,8},{10,9},{11,1... | collective-permute-start | bytes 786440 | tf_op jit(solution)/shard_map/ppermute | solution.py:273
  133.5 3.1 %mix0.1.refs_0_ = bf16[2,256,1024]{2,1,0:T(8,128)(2,1)} custom-call(bf16[256,512]{1,0:T(8,128)(2,1)S(1)} %get-tuple-element.36.a0, bf16[256,512]{1,0:T(8,128)(2,1)S(1)} %collective-permute-done.28.a1, bf16[256,512]{1,0:T(8,128)(2,1)S(1)} %collective-permute-done.29.a2, bf16[256,512]{1,0:T(8,128)(2,1)S(1)} %collective-permute-done.30.a3, ...), custom_call_target="tpu_custom_call" | custom-call | bytes 9000000 | tf_op jit(solution)/shard_map/mix0/pallas_call | solution.py:456
  136.7 6.7 %collective-permute-done.27.a3 = bf16[256,512]{1,0:T(8,128)(2,1)S(1)} collective-permute-done((bf16[256,512]{1,0:T(8,128)(2,1)S(1)}, bf16[256,512]{1,0:T(8,128)(2,1)S(1)}, u32[]{:S(2)}, u32[]{:S(2)}) %collective-permute-start.27) | collective-permute-done | bytes 262176 | tf_op jit(solution)/shard_map/ppermute | solution.py:273
  143.9 3.1 %mix1.1 = bf16[2,256,1024]{2,1,0:T(8,128)(2,1)} custom-call(bf16[256,512]{1,0:T(8,128)(2,1)S(1)} %attend1.1.a0, bf16[256,512]{1,0:T(8,128)(2,1)S(1)} %collective-permute-done.25.a1, bf16[256,512]{1,0:T(8,128)(2,1)S(1)} %collective-permute-done.26.a2, bf16[256,512]{1,0:T(8,128)(2,1)S(1)} %collective-permute-done.27.a3, ...), custom_call_target="tpu_custom_call", output_to_operand_aliasing={{}: (8, {})} | custom-call | bytes 9000000 | tf_op jit(solution)/shard_map/mix1/pallas_call | solution.py:456
  (86 shorter events, 17.8 us)
Async XLA Ops:
  3.0 6.7 %collective-permute-start.4 = (bf16[2,2,128,128]{3,2,1,0:T(8,128)(2,1)S(1)}, bf16[2,2,128,128]{3,2,1,0:T(8,128)(2,1)S(1)}, u32[]{:S(2)}, u32[]{:S(2)}) collective-permute-start(bf16[2,2,128,128]{3,2,1,0:T(8,128)(2,1)S(1)} %get-tuple-element.27.refs_0_), channel_id=1, source_target_pairs={{0,64},{4,68},{8,72},{12,76},{16,80},{20,84},{24,88},{28,92},{32,9... | collective-permute-start | bytes 393224 | tf_op jit(solution)/shard_map/ppermute | solution.py:301
  4.6 8.7 %collective-permute-start.3 = (bf16[2,2,128,128]{3,2,1,0:T(8,128)(2,1)S(1)}, bf16[2,2,128,128]{3,2,1,0:T(8,128)(2,1)S(1)}, u32[]{:S(2)}, u32[]{:S(2)}) collective-permute-start(bf16[2,2,128,128]{3,2,1,0:T(8,128)(2,1)S(1)} %get-tuple-element.27.refs_0_), channel_id=1, source_target_pairs={{0,128},{4,132},{8,136},{12,140},{16,144},{20,148},{24,152},{28,15... | collective-permute-start | bytes 393224 | tf_op jit(solution)/shard_map/ppermute | solution.py:301
  7.3 6.0 %collective-permute-start.2 = (bf16[2,2,128,128]{3,2,1,0:T(8,128)(2,1)S(1)}, bf16[2,2,128,128]{3,2,1,0:T(8,128)(2,1)S(1)}, u32[]{:S(2)}, u32[]{:S(2)}) collective-permute-start(bf16[2,2,128,128]{3,2,1,0:T(8,128)(2,1)S(1)} %get-tuple-element.27.refs_0_), channel_id=1, source_target_pairs={{0,192},{4,196},{8,200},{12,204},{16,208},{20,212},{24,216},{28,22... | collective-permute-start | bytes 393224 | tf_op jit(solution)/shard_map/ppermute | solution.py:301
  13.4 2.0 %collective-permute-start.5 = (bf16[2,8,128,128]{3,2,1,0:T(8,128)(2,1)S(1)}, bf16[2,8,128,128]{3,2,1,0:T(8,128)(2,1)S(1)}, u32[]{:S(2)}, u32[]{:S(2)}) collective-permute-start(bf16[2,8,128,128]{3,2,1,0:T(8,128)(2,1)S(1)} %line.1.own_ref), channel_id=1, source_target_pairs={{0,4},{4,0},{8,12},{12,8},{16,20},{20,16},{24,28},{28,24},{32,36},... | collective-permute-start | bytes 1572872 | tf_op jit(solution)/shard_map/ppermute | solution.py:301
  15.4 9.9 %collective-permute-start.6 = (bf16[16,128,128]{2,1,0:T(8,128)(2,1)S(1)}, bf16[16,128,128]{2,1,0:T(8,128)(2,1)S(1)}, u32[]{:S(2)}, u32[]{:S(2)}) collective-permute-start(bf16[16,128,128]{2,1,0:T(8,128)(2,1)S(1)} %get-tuple-element.28.refs_0_), channel_id=1, source_target_pairs={{0,8},{4,60},{8,16},{12,4},{16,24},{20,12},{24,32},{28,20},{32,40}... | collective-permute-start | bytes 1572872 | tf_op jit(solution)/shard_map/ppermute | solution.py:301
  18.6 12.3 %collective-permute-start.12 = (bf16[16,128,128]{2,1,0:T(8,128)(2,1)S(1)}, bf16[16,128,128]{2,1,0:T(8,128)(2,1)S(1)}, u32[]{:S(2)}, u32[]{:S(2)}) collective-permute-start(bf16[16,128,128]{2,1,0:T(8,128)(2,1)S(1)} %get-tuple-element.29.refs_0_), channel_id=1, source_target_pairs={{0,8},{4,60},{8,16},{12,4},{16,24},{20,12},{24,32},{28,20},{32,40}... | collective-permute-start | bytes 1572872 | tf_op jit(solution)/shard_map/ppermute | solution.py:301
  19.7 46.2 %copy-start.19 = (s32[4,64]{1,0:T(4,128)S(1)}, s32[4,64]{1,0:T(4,128)}, u32[]{:S(2)}) copy-start(s32[4,64]{1,0:T(4,128)} %slash_ref.1) | copy-start | bytes 3076
  25.3 16.6 %collective-permute-start.8 = (bf16[16,128,128]{2,1,0:T(8,128)(2,1)S(1)}, bf16[16,128,128]{2,1,0:T(8,128)(2,1)S(1)}, u32[]{:S(2)}, u32[]{:S(2)}) collective-permute-start(bf16[16,128,128]{2,1,0:T(8,128)(2,1)S(1)} %collective-permute-done.6.refs_1_), channel_id=1, source_target_pairs={{0,8},{4,60},{8,16},{12,4},{16,24},{20,12},{24,32},{28,20},{32,40}... | collective-permute-start | bytes 1572872 | tf_op jit(solution)/shard_map/ppermute | solution.py:301
  31.0 11.2 %collective-permute-start.13 = (bf16[16,128,128]{2,1,0:T(8,128)(2,1)S(1)}, bf16[16,128,128]{2,1,0:T(8,128)(2,1)S(1)}, u32[]{:S(2)}, u32[]{:S(2)}) collective-permute-start(bf16[16,128,128]{2,1,0:T(8,128)(2,1)S(1)} %collective-permute-done.12.refs_1_), channel_id=1, source_target_pairs={{0,8},{4,60},{8,16},{12,4},{16,24},{20,12},{24,32},{28,20},{32,40}... | collective-permute-start | bytes 1572872 | tf_op jit(solution)/shard_map/ppermute | solution.py:301
  38.7 33.0 %collective-permute-start.24 = (bf16[512,1024]{1,0:T(8,128)(2,1)S(1)}, bf16[512,1024]{1,0:T(8,128)(2,1)S(1)}, u32[]{:S(2)}, u32[]{:S(2)}) collective-permute-start(bf16[512,1024]{1,0:T(8,128)(2,1)S(1)} %get-tuple-element.37), channel_id=1, source_target_pairs={{3,0},{0,1},{1,2},{2,3},{7,4},{4,5},{5,6},{6,7},{11,8},{8,9},{9,10... | collective-permute-start | bytes 3145736 | tf_op jit(solution)/shard_map/ppermute | solution.py:273
  40.2 31.5 %collective-permute-start.22 = (bf16[512,1024]{1,0:T(8,128)(2,1)S(1)}, bf16[512,1024]{1,0:T(8,128)(2,1)S(1)}, u32[]{:S(2)}, u32[]{:S(2)}) collective-permute-start(bf16[512,1024]{1,0:T(8,128)(2,1)S(1)} %get-tuple-element.38), channel_id=1, source_target_pairs={{1,0},{2,1},{3,2},{0,3},{5,4},{6,5},{7,6},{4,7},{9,8},{10,9},{11,1... | collective-permute-start | bytes 3145736 | tf_op jit(solution)/shard_map/ppermute | solution.py:273
  41.9 26.8 %collective-permute-start.10 = (bf16[16,128,128]{2,1,0:T(8,128)(2,1)S(1)}, bf16[16,128,128]{2,1,0:T(8,128)(2,1)S(1)}, u32[]{:S(2)}, u32[]{:S(2)}) collective-permute-start(bf16[16,128,128]{2,1,0:T(8,128)(2,1)S(1)} %collective-permute-done.8.refs_3_), channel_id=1, source_target_pairs={{0,8},{4,60},{8,16},{12,4},{16,24},{20,12},{24,32},{28,20},{32,40}... | collective-permute-start | bytes 1572872 | tf_op jit(solution)/shard_map/ppermute | solution.py:301
  42.2 29.4 %collective-permute-start.14 = (bf16[16,128,128]{2,1,0:T(8,128)(2,1)S(1)}, bf16[16,128,128]{2,1,0:T(8,128)(2,1)S(1)}, u32[]{:S(2)}, u32[]{:S(2)}) collective-permute-start(bf16[16,128,128]{2,1,0:T(8,128)(2,1)S(1)} %collective-permute-done.13.refs_3_), channel_id=1, source_target_pairs={{0,8},{4,60},{8,16},{12,4},{16,24},{20,12},{24,32},{28,20},{32,40}... | collective-permute-start | bytes 1572872 | tf_op jit(solution)/shard_map/ppermute | solution.py:301
  45.9 7.7 %collective-permute-start = (bf16[2,256,128]{2,1,0:T(8,128)(2,1)S(1)}, bf16[2,256,128]{2,1,0:T(8,128)(2,1)S(1)}, u32[]{:S(2)}, u32[]{:S(2)}) collective-permute-start(bf16[2,256,128]{2,1,0:T(8,128)(2,1)S(1)} %get-tuple-element.24), channel_id=1, source_target_pairs={{0,4},{4,8},{8,12},{12,16},{16,20},{20,24},{24,28},{28,32},{32,36}... | collective-permute-start | bytes 393224 | tf_op jit(solution)/shard_map/ppermute | solution.py:394
  53.6 4.4 %collective-permute-start.1 = (bf16[2,256,128]{2,1,0:T(8,128)(2,1)S(1)}, bf16[2,256,128]{2,1,0:T(8,128)(2,1)S(1)}, u32[]{:S(2)}, u32[]{:S(2)}) collective-permute-start(bf16[2,256,128]{2,1,0:T(8,128)(2,1)S(1)} %get-tuple-element.25), channel_id=1, source_target_pairs={{4,0},{8,4},{12,8},{16,12},{20,16},{24,20},{28,24},{32,28},{36,32}... | collective-permute-start | bytes 393224 | tf_op jit(solution)/shard_map/ppermute | solution.py:395
  58.0 14.6 %collective-permute-start.7 = (bf16[16,128,128]{2,1,0:T(8,128)(2,1)S(1)}, bf16[16,128,128]{2,1,0:T(8,128)(2,1)S(1)}, u32[]{:S(2)}, u32[]{:S(2)}) collective-permute-start(bf16[16,128,128]{2,1,0:T(8,128)(2,1)S(1)} %collective-permute-done.6.refs_1_), channel_id=1, source_target_pairs={{0,4},{4,0},{8,12},{12,8},{16,20},{20,16},{24,28},{28,24},{32,36},... | collective-permute-start | bytes 1572872 | tf_op jit(solution)/shard_map/ppermute | solution.py:301
  68.7 28.2 %collective-permute-start.23 = (bf16[512,1024]{1,0:T(8,128)(2,1)}, bf16[512,1024]{1,0:T(8,128)(2,1)S(1)}, u32[]{:S(2)}, u32[]{:S(2)}) collective-permute-start(bf16[512,1024]{1,0:T(8,128)(2,1)} %get-tuple-element.40), channel_id=1, source_target_pairs={{2,0},{3,1},{0,2},{1,3},{6,4},{7,5},{4,6},{5,7},{10,8},{11,9},{8,1... | collective-permute-start | bytes 3145736 | tf_op jit(solution)/shard_map/ppermute | solution.py:273
  71.6 7.4 %collective-permute-start.9 = (bf16[16,128,128]{2,1,0:T(8,128)(2,1)S(1)}, bf16[16,128,128]{2,1,0:T(8,128)(2,1)S(1)}, u32[]{:S(2)}, u32[]{:S(2)}) collective-permute-start(bf16[16,128,128]{2,1,0:T(8,128)(2,1)S(1)} %collective-permute-done.8.refs_3_), channel_id=1, source_target_pairs={{0,4},{4,0},{8,12},{12,8},{16,20},{20,16},{24,28},{28,24},{32,36},... | collective-permute-start | bytes 1572872 | tf_op jit(solution)/shard_map/ppermute | solution.py:301
  71.7 6.4 %collective-permute-start.15 = (bf16[8,128,128]{2,1,0:T(8,128)(2,1)S(1)}, bf16[8,128,128]{2,1,0:T(8,128)(2,1)S(1)}, u32[]{:S(2)}, u32[]{:S(2)}) collective-permute-start(bf16[8,128,128]{2,1,0:T(8,128)(2,1)S(1)} %get-tuple-element.31), channel_id=1, source_target_pairs={{0,8},{4,60},{8,16},{12,4},{16,24},{20,12},{24,32},{28,20},{32,40}... | collective-permute-start | bytes 786440 | tf_op jit(solution)/shard_map/ppermute | solution.py:301
  71.8 9.1 %collective-permute-start.20 = (bf16[8,128,128]{2,1,0:T(8,128)(2,1)S(1)}, bf16[8,128,128]{2,1,0:T(8,128)(2,1)S(1)}, u32[]{:S(2)}, u32[]{:S(2)}) collective-permute-start(bf16[8,128,128]{2,1,0:T(8,128)(2,1)S(1)} %get-tuple-element.34), channel_id=1, source_target_pairs={{0,8},{4,60},{8,16},{12,4},{16,24},{20,12},{24,32},{28,20},{32,40}... | collective-permute-start | bytes 786440 | tf_op jit(solution)/shard_map/ppermute | solution.py:301
  72.7 9.1 %collective-permute-start.11 = (bf16[16,128,128]{2,1,0:T(8,128)(2,1)S(1)}, bf16[16,128,128]{2,1,0:T(8,128)(2,1)S(1)}, u32[]{:S(2)}, u32[]{:S(2)}) collective-permute-start(bf16[16,128,128]{2,1,0:T(8,128)(2,1)S(1)} %collective-permute-done.10.keys_ref.refs_5_), channel_id=1, source_target_pairs={{0,4},{4,0},{8,12},{12,8},{16,20},{20,16},{24,28},{28,24},{32,36},... | collective-permute-start | bytes 1572872 | tf_op jit(solution)/shard_map/ppermute | solution.py:301
  78.1 3.7 %collective-permute-start.16 = (bf16[8,128,128]{2,1,0:T(8,128)(2,1)S(1)}, bf16[8,128,128]{2,1,0:T(8,128)(2,1)S(1)}, u32[]{:S(2)}, u32[]{:S(2)}) collective-permute-start(bf16[8,128,128]{2,1,0:T(8,128)(2,1)S(1)} %collective-permute-done.15.refs_7_), channel_id=1, source_target_pairs={{0,4},{4,0},{8,12},{12,8},{16,20},{20,16},{24,28},{28,24},{32,36},... | collective-permute-start | bytes 786440 | tf_op jit(solution)/shard_map/ppermute | solution.py:301
  79.0 17.9 %collective-permute-start.17 = (bf16[16,128,128]{2,1,0:T(8,128)(2,1)S(1)}, bf16[16,128,128]{2,1,0:T(8,128)(2,1)S(1)}, u32[]{:S(2)}, u32[]{:S(2)}) collective-permute-start(bf16[16,128,128]{2,1,0:T(8,128)(2,1)S(1)} %collective-permute-done.12.refs_1_), channel_id=1, source_target_pairs={{0,4},{4,0},{8,12},{12,8},{16,20},{20,16},{24,28},{28,24},{32,36},... | collective-permute-start | bytes 1572872 | tf_op jit(solution)/shard_map/ppermute | solution.py:301
  80.9 16.0 %collective-permute-start.18 = (bf16[16,128,128]{2,1,0:T(8,128)(2,1)S(1)}, bf16[16,128,128]{2,1,0:T(8,128)(2,1)S(1)}, u32[]{:S(2)}, u32[]{:S(2)}) collective-permute-start(bf16[16,128,128]{2,1,0:T(8,128)(2,1)S(1)} %collective-permute-done.13.refs_3_), channel_id=1, source_target_pairs={{0,4},{4,0},{8,12},{12,8},{16,20},{20,16},{24,28},{28,24},{32,36},... | collective-permute-start | bytes 1572872 | tf_op jit(solution)/shard_map/ppermute | solution.py:301
  81.8 15.9 %collective-permute-start.19 = (bf16[16,128,128]{2,1,0:T(8,128)(2,1)S(1)}, bf16[16,128,128]{2,1,0:T(8,128)(2,1)S(1)}, u32[]{:S(2)}, u32[]{:S(2)}) collective-permute-start(bf16[16,128,128]{2,1,0:T(8,128)(2,1)S(1)} %collective-permute-done.14.vals_ref.refs_5_), channel_id=1, source_target_pairs={{0,4},{4,0},{8,12},{12,8},{16,20},{20,16},{24,28},{28,24},{32,36},... | collective-permute-start | bytes 1572872 | tf_op jit(solution)/shard_map/ppermute | solution.py:301
  81.8 15.1 %collective-permute-start.21 = (bf16[8,128,128]{2,1,0:T(8,128)(2,1)S(1)}, bf16[8,128,128]{2,1,0:T(8,128)(2,1)S(1)}, u32[]{:S(2)}, u32[]{:S(2)}) collective-permute-start(bf16[8,128,128]{2,1,0:T(8,128)(2,1)S(1)} %collective-permute-done.20.refs_7_), channel_id=1, source_target_pairs={{0,4},{4,0},{8,12},{12,8},{16,20},{20,16},{24,28},{28,24},{32,36},... | collective-permute-start | bytes 786440 | tf_op jit(solution)/shard_map/ppermute | solution.py:301
  110.1 21.4 %collective-permute-start.30 = (bf16[256,512]{1,0:T(8,128)(2,1)S(1)}, bf16[256,512]{1,0:T(8,128)(2,1)S(1)}, u32[]{:S(2)}, u32[]{:S(2)}) collective-permute-start(bf16[256,512]{1,0:T(8,128)(2,1)S(1)} %get-tuple-element.36.a0), channel_id=1, source_target_pairs={{3,0},{0,1},{1,2},{2,3},{7,4},{4,5},{5,6},{6,7},{11,8},{8,9},{9,10... | collective-permute-start | bytes 786440 | tf_op jit(solution)/shard_map/ppermute | solution.py:273
  111.0 22.5 %collective-permute-start.29 = (bf16[256,512]{1,0:T(8,128)(2,1)S(1)}, bf16[256,512]{1,0:T(8,128)(2,1)S(1)}, u32[]{:S(2)}, u32[]{:S(2)}) collective-permute-start(bf16[256,512]{1,0:T(8,128)(2,1)S(1)} %get-tuple-element.36.a0), channel_id=1, source_target_pairs={{2,0},{3,1},{0,2},{1,3},{6,4},{7,5},{4,6},{5,7},{10,8},{11,9},{8,1... | collective-permute-start | bytes 786440 | tf_op jit(solution)/shard_map/ppermute | solution.py:273
  113.3 20.3 %collective-permute-start.28 = (bf16[256,512]{1,0:T(8,128)(2,1)S(1)}, bf16[256,512]{1,0:T(8,128)(2,1)S(1)}, u32[]{:S(2)}, u32[]{:S(2)}) collective-permute-start(bf16[256,512]{1,0:T(8,128)(2,1)S(1)} %get-tuple-element.36.a0), channel_id=1, source_target_pairs={{1,0},{2,1},{3,2},{0,3},{5,4},{6,5},{7,6},{4,7},{9,8},{10,9},{11,1... | collective-permute-start | bytes 786440 | tf_op jit(solution)/shard_map/ppermute | solution.py:273
  129.2 14.1 %collective-permute-start.27 = (bf16[256,512]{1,0:T(8,128)(2,1)S(1)}, bf16[256,512]{1,0:T(8,128)(2,1)S(1)}, u32[]{:S(2)}, u32[]{:S(2)}) collective-permute-start(bf16[256,512]{1,0:T(8,128)(2,1)S(1)} %attend1.1.a0), channel_id=1, source_target_pairs={{3,0},{0,1},{1,2},{2,3},{7,4},{4,5},{5,6},{6,7},{11,8},{8,9},{9,10... | collective-permute-start | bytes 786440 | tf_op jit(solution)/shard_map/ppermute | solution.py:273
  130.3 13.1 %collective-permute-start.26 = (bf16[256,512]{1,0:T(8,128)(2,1)S(1)}, bf16[256,512]{1,0:T(8,128)(2,1)S(1)}, u32[]{:S(2)}, u32[]{:S(2)}) collective-permute-start(bf16[256,512]{1,0:T(8,128)(2,1)S(1)} %attend1.1.a0), channel_id=1, source_target_pairs={{2,0},{3,1},{0,2},{1,3},{6,4},{7,5},{4,6},{5,7},{10,8},{11,9},{8,1... | collective-permute-start | bytes 786440 | tf_op jit(solution)/shard_map/ppermute | solution.py:273
  131.5 12.4 %collective-permute-start.25 = (bf16[256,512]{1,0:T(8,128)(2,1)S(1)}, bf16[256,512]{1,0:T(8,128)(2,1)S(1)}, u32[]{:S(2)}, u32[]{:S(2)}) collective-permute-start(bf16[256,512]{1,0:T(8,128)(2,1)S(1)} %attend1.1.a0), channel_id=1, source_target_pairs={{1,0},{2,1},{3,2},{0,3},{5,4},{6,5},{7,6},{4,7},{9,8},{10,9},{11,1... | collective-permute-start | bytes 786440 | tf_op jit(solution)/shard_map/ppermute | solution.py:273
  (21 other events, 338.4 us)

commit v4 on v3

--- a/solution.py
+++ b/solution.py
@@ -15,6 +15,7 @@
 GROUP = 8
 SPAN = GROUP * BLOCK
 LISTED = 64
+ROOM = LISTED + 1
 UNROLL = 4
 X_CHIPS = 4
 HEADS = 4
@@ -36,10 +37,8 @@
 def pack_kernel(ctx_count, me_ref, table_ref, k_ref, v_ref, pay_ref, ahead_ref, back_ref):
     me = me_ref[0]
     table = table_ref[...]
-    stretch = table // 2
-    first = stretch < ctx_count
-    owner = jnp.where(first, stretch, 2 * ctx_count - 1 - stretch)
-    local = jnp.where(first, 0, 2) + table % 2
+    owner = owned(table, ctx_count)
+    local = jnp.where(table // 2 < ctx_count, 0, 2) + table % 2
     at = lax.broadcasted_iota(jnp.int32, table.shape, 1)
     mine = owner == me
     for slot in range(CAP):
@@ -54,60 +53,36 @@
             ref[1, part * BLOCK : (part + 1) * BLOCK] = v_ref[2 * half + part]
 
 
-def plan_kernel(ctx_count, arrivals, me_ref, table_ref, blk_ref, at_ref, meta_ref, count, place, inv_ref):
+def owned(table, ctx_count):
+    stretch = table // 2
+    return jnp.where(stretch < ctx_count, stretch, 2 * ctx_count - 1 - stretch)
+
+
+def plan_kernel(ctx_count, sides, me_ref, row_ref, col_ref, blk_ref, at_ref, meta_ref):
     me = me_ref[0]
-    stretches = 2 * ctx_count
-    near, far = me, stretches - 1 - me
-
-    def clear(i, _):
-        for n in range(4):
-            place[4 * i + n] = -1
-        for n in range(CAP):
-            inv_ref[CAP * i + n] = -1
-        count[i] = 0
-        return 0
-
-    lax.fori_loop(0, ctx_count, clear, 0)
-
-    def assign(j, _):
-        b = table_ref[0, j]
-        stretch = lax.div(b, 2)
-        owner = jnp.where(stretch < ctx_count, stretch, stretches - 1 - stretch)
-        rank = count[owner]
-        count[owner] = rank + 1
-        place[b] = owner * CAP + rank
-        return 0
-
-    lax.fori_loop(0, LISTED, assign, 0)
-
-    def order(b, carry):
-        at, full0, seen0, full1, seen1 = carry
-        e = place[b]
-        blk_ref[at] = b
-        inv_ref[jnp.where(e >= 0, e, CAP * ctx_count)] = at
-        hit = jnp.where(e >= 0, 1, 0)
-        one = lambda test: jnp.where(test, hit, 0)
-        return (
-            at + hit,
-            full0 + one(b < 2 * near),
-            seen0 + one(b <= 2 * near + 1),
-            full1 + one(b < 2 * far),
-            seen1 + one(b <= 2 * far + 1),
-        )
-
-    zero = jnp.int32(0)
-    _, full0, seen0, full1, seen1 = lax.fori_loop(0, 4 * ctx_count, order, (zero,) * 5)
-    for i, (owner, slot) in enumerate(arrivals(me)):
-        at_ref[i] = inv_ref[owner * CAP + slot]
-    for st, (s, full, seen) in enumerate(((near, full0, seen0), (far, full1, seen1))):
-        meta_ref[8 * st] = full
-        meta_ref[8 * st + 1] = seen
-        meta_ref[8 * st + 2] = s
-        meta_ref[8 * st + 3] = me
+    row, col = row_ref[...], col_ref[...]
+    square = (LISTED, LISTED)
+    iota = lax.broadcasted_iota
+    total = functools.partial(jnp.sum, keepdims=True)
+    pick = lambda test, value, axis: total(jnp.where(test, value, 0), axis=axis)
+    place = pick(row < col, jnp.int32(1), 1)
+    earlier = iota(jnp.int32, square, 1) < iota(jnp.int32, square, 0)
+    owner = owned(col, ctx_count)
+    rank = pick((owned(row, ctx_count) == owner) & earlier, jnp.int32(1), 1)
+    blk_ref[...] = pick(place == iota(jnp.int32, square, 1), col, 0)
+    entry = arrivals(*sides, me, iota(jnp.int32, (1, CAP * ctx_count), 1))
+    at_ref[...] = LISTED + pick(owner * CAP + rank == entry, place - LISTED, 0)
+    lane = iota(jnp.int32, (1, 16), 1)
+    meta = jnp.where(lane % 8 == 3, me, 0)
+    for st, s in enumerate((me, 2 * ctx_count - 1 - me)):
+        found = [jnp.sum(jnp.where(row < 2 * s, 1, 0)), jnp.sum(jnp.where(row <= 2 * s + 1, 1, 0)), s]
+        for n, value in enumerate(found):
+            meta = jnp.where(lane == 8 * st + n, value, meta)
         for n in range(4):
             b = 2 * (s - 1) + n
-            free = place[jnp.maximum(b, 0)] < 0
-            meta_ref[8 * st + 4 + n] = jnp.where((b >= 0) & free, 1, 0)
+            free = 1 - jnp.max(jnp.where(row == b, 1, 0))
+            meta = jnp.where(lane == 8 * st + 4 + n, jnp.where(b >= 0, free, 0), meta)
+    meta_ref[...] = meta
 
 
 def band_halves(own_ref, ahead_ref, back_ref, which, st, me, ctx_count):
@@ -128,7 +103,7 @@
         row = jnp.where(hit, 1.0, 0.0).astype(F32)[:1]
         spread = jnp.broadcast_to(row, (STRETCH, 2 * STRETCH))
         mask_ref[h] = pltpu.roll(spread, 0, 1, stride=1, stride_axis=0)
-    me = meta_ref[3]
+    me = meta_ref[0, 3]
     for st in range(2):
         before = band_halves(k_ref, ahead_ref, back_ref, 0, st, me, ctx_count)
         for h in range(HEADS):
@@ -137,51 +112,33 @@
             for n in range(4):
                 part = before if n < 2 else k_ref[st]
                 s = dot_t(q, part[(n % 2) * BLOCK : (n % 2 + 1) * BLOCK])
-                ok = (mask_ref[h, :, n * BLOCK : (n + 1) * BLOCK] > 0.5) & (meta_ref[8 * st + 4 + n] > 0)
+                ok = (mask_ref[h, :, n * BLOCK : (n + 1) * BLOCK] > 0.5) & (meta_ref[0, 8 * st + 4 + n] > 0)
                 top = jnp.maximum(top, jnp.where(ok, s, -jnp.inf))
             top_ref[st, h] = top
 
 
-def fetch(at_ref, pieces, target_ref, sems):
+def fetch(at_ref, pieces, target_ref):
     base = 0
     for ref in pieces:
-        def start(i, _, ref=ref, base=base):
+        def copy(i, _, ref=ref, base=base):
             for n in range(UNROLL):
-                at = at_ref[base + i * UNROLL + n]
-
-                @pl.when(at >= 0)
-                def _(n=n, at=at):
-                    pltpu.make_async_copy(
-                        ref.at[i * UNROLL + n], target_ref.at[at], sems.at[lax.div(at, GROUP)]
-                    ).start()
-
+                target_ref[at_ref[0, base + i * UNROLL + n]] = ref[i * UNROLL + n]
             return 0
 
-        lax.fori_loop(0, ref.shape[0] // UNROLL, start, 0)
+        lax.fori_loop(0, ref.shape[0] // UNROLL, copy, 0)
         base += ref.shape[0]
-
-
-def arrived(target_ref, sems, g):
-    part = target_ref.at[pl.ds(g * GROUP, GROUP)]
-    pltpu.make_async_copy(part, part, sems.at[g]).wait()
 
 
 def causal(blk_ref, s, g):
     lead = lax.broadcasted_iota(jnp.int32, (STRETCH, BLOCK), 1) - lax.broadcasted_iota(jnp.int32, (STRETCH, BLOCK), 0)
-    return [lead <= s * STRETCH - blk_ref[g * GROUP + n] * BLOCK for n in range(GROUP)]
+    return [lead <= s * STRETCH - blk_ref[0, g * GROUP + n] * BLOCK for n in range(GROUP)]
 
 
 def top_kernel(meta_ref, blk_ref, at_ref, q_ref, top_in_ref, *refs):
-    pieces, (keys_ref, top_ref, sems) = refs[:-3], refs[-3:]
-    fetch(at_ref, pieces, keys_ref, sems)
-
-    def ready(g, _):
-        arrived(keys_ref, sems, g)
-        return 0
-
-    lax.fori_loop(0, LISTED // GROUP, ready, 0)
+    pieces, (keys_ref, top_ref) = refs[:-2], refs[-2:]
+    fetch(at_ref, pieces, keys_ref)
     for st in range(2):
-        full, seen, s = meta_ref[8 * st], meta_ref[8 * st + 1], meta_ref[8 * st + 2]
+        full, seen, s = meta_ref[0, 8 * st], meta_ref[0, 8 * st + 1], meta_ref[0, 8 * st + 2]
         plain, groups = full // GROUP, (seen + GROUP - 1) // GROUP
         for h in range(HEADS):
             top_ref[st, h] = top_in_ref[st, h]
@@ -207,12 +164,12 @@
 
 
 def out_kernel(ctx_count, st, arriving, meta_ref, blk_ref, at_ref, q_ref, keys_ref, top_ref, mask_ref, k_ref, v_ref, ahead_ref, back_ref, *refs):
-    full, seen, s = meta_ref[8 * st], meta_ref[8 * st + 1], meta_ref[8 * st + 2]
-    me = meta_ref[8 * st + 3]
+    full, seen, s = meta_ref[0, 8 * st], meta_ref[0, 8 * st + 1], meta_ref[0, 8 * st + 2]
+    me = meta_ref[0, 8 * st + 3]
     plain, groups = full // GROUP, (seen + GROUP - 1) // GROUP
     if arriving:
-        pieces, (out_ref, vals, total, acc, sems) = refs[:arriving], refs[-5:]
-        fetch(at_ref, pieces, vals, sems)
+        pieces, (out_ref, vals, total, acc) = refs[:arriving], refs[-4:]
+        fetch(at_ref, pieces, vals)
     else:
         vals, out_ref, total, acc = refs
     k_before = band_halves(k_ref, ahead_ref, back_ref, 0, st, me, ctx_count)
@@ -224,7 +181,7 @@
         expos = []
         for n in range(4):
             part = scores[n // 2][:, (n % 2) * BLOCK : (n % 2 + 1) * BLOCK]
-            ok = (mask_ref[h, :, n * BLOCK : (n + 1) * BLOCK] > 0.5) & (meta_ref[8 * st + 4 + n] > 0)
+            ok = (mask_ref[h, :, n * BLOCK : (n + 1) * BLOCK] > 0.5) & (meta_ref[0, 8 * st + 4 + n] > 0)
             expos.append(jnp.where(ok, jnp.exp2((part - top_ref[0, h]) * EXP_SCALE), 0.0))
         total[h] = (expos[0] + expos[1]) + (expos[2] + expos[3])
         weights = [e.astype(BF16) for e in expos]
@@ -233,8 +190,6 @@
         ) + jnp.dot(jnp.concatenate(weights[2:], axis=1), v_ref[st], preferred_element_type=F32)
 
     def step(masked, g, _):
-        if arriving:
-            arrived(vals, sems, g)
         keys = keys_ref[pl.ds(g * GROUP, GROUP)].reshape(SPAN, HEAD)
         values = vals[pl.ds(g * GROUP, GROUP)].reshape(SPAN, HEAD)
         ok = causal(blk_ref, s, g) if masked else None
@@ -251,12 +206,6 @@
 
     lax.fori_loop(0, plain, functools.partial(step, False), 0)
     lax.fori_loop(plain, groups, functools.partial(step, True), 0)
-    if arriving:
-        def ready(g, _):
-            arrived(vals, sems, g)
-            return 0
-
-        lax.fori_loop(groups, LISTED // GROUP, ready, 0)
     for h in range(HEADS):
         row = jnp.sum(total[h], axis=1, keepdims=True)
         out_ref[:, h * HEAD : (h + 1) * HEAD] = (acc[h] / row).astype(BF16)
@@ -274,25 +223,19 @@
 
 
 def line_kernel(*refs):
-    pieces, out_ref = refs[:-1], refs[-1]
+    pieces, out_ref = refs[:X_CHIPS], refs[-1]
     for n, ref in enumerate(pieces):
         for which in range(2):
             out_ref[which, n * CAP : (n + 1) * CAP] = ref[which]
 
 
-def chip_kernel(own_ref, other_ref, keys_ref, vals_ref):
+def chip_kernel(which, own_ref, other_ref, *refs):
     count = own_ref.shape[1]
-    for which, ref in ((0, keys_ref), (1, vals_ref)):
-        ref[:count] = own_ref[which]
-        ref[count:] = other_ref[which]
-
-
-def half_kernel(keys_ref, vals_ref, *refs):
-    for source, target in ((keys_ref, refs[-2]), (vals_ref, refs[-1])):
-        target[...] = source[...]
-
-
-def gather_columns(nx, nz, payload, ready):
+    refs[-1][:count] = own_ref[which]
+    refs[-1][count:] = other_ref[which]
+
+
+def gather_columns(nx, nz, payload, first, later):
     place = lambda x, z, c: ((x % nx) * nz + z % nz) * 2 + c
     every = [(x, z, c) for x in range(nx) for z in range(nz) for c in range(2)]
     route = lambda f: [(place(*d), place(*f(*d))) for d in every]
@@ -307,53 +250,43 @@
     own = call(
         line_kernel,
         out_shape=shape((2, size, BLOCK, HEAD), BF16),
-        in_specs=[VMEM()] * nx,
+        in_specs=[VMEM()] * nx + [ANY()] * len(first),
         out_specs=VMEM(),
         name="line",
-    )(*line)
-    moving = call(
-        chip_kernel,
-        out_shape=[shape((2 * size, BLOCK, HEAD), BF16)] * 2,
-        in_specs=[VMEM()] * 2,
-        out_specs=[VMEM()] * 2,
-        name="chip",
-    )(own, send(own, across))
-    pieces = [[m] for m in moving]
-    for n in range(1, nz // 2 + 1):
-        if n == nz // 2:
-            moving = call(
-                half_kernel,
-                grid=(1,),
-                out_shape=[shape((size, BLOCK, HEAD), BF16)] * 2,
-                in_specs=[pl.BlockSpec((size, BLOCK, HEAD), lambda i: (0, 0, 0))] * 2 + [ANY()] * len(ready),
-                out_specs=[VMEM()] * 2,
-                name="half",
-            )(*moving, *ready)
-        moving = [send(m, along) for m in moving]
-        for which in range(2):
-            pieces[which] += [moving[which], send(moving[which], across)]
-
+    )(*line, *first)
+    other = send(own, across)
+    pieces = []
+    waited = []
+    for which in range(2):
+        moving = call(
+            functools.partial(chip_kernel, which),
+            out_shape=shape((2 * size, BLOCK, HEAD), BF16),
+            in_specs=[VMEM()] * 2 + [ANY()] * len(waited),
+            out_specs=VMEM(),
+            name=f"chip{which}",
+        )(own, other, *waited)
+        held = [moving]
+        for n in range(1, nz // 2 + 1):
+            moving = send(moving, along)
+            held += [moving] + ([send(moving, across)] if n < nz // 2 else [])
+            if n == 1:
+                waited = [moving, *later]
+        pieces.append(held)
     return pieces
 
 
-def arrivals(nx, nz, me):
+def arrivals(nx, nz, me, entry):
     x, z, c = lax.div(me, 2 * nz), lax.rem(lax.div(me, 2), nz), lax.rem(me, 2)
-    lines = [lax.rem(x + n, nx) * nz for n in range(nx)]
-    entries = []
-
-    def piece(hops, mirrored, halves):
-        side = (2 * c - 1) * hops
-        at = lax.rem(z + nz + (-side if mirrored else side), nz)
-        for half in range(halves):
-            core = 1 - c if mirrored != (half == 1) else c
-            for n in range(nx):
-                entries.extend(((lines[n] + at) * 2 + core, slot) for slot in range(CAP))
-
-    piece(0, False, 2)
-    for n in range(1, nz // 2 + 1):
-        for mirrored in (False, True):
-            piece(n, mirrored, 2 if n < nz // 2 else 1)
-    return entries
+    size = nx * CAP
+    at = entry % (2 * size)
+    piece = entry // (2 * size)
+    hops = jnp.where(piece == 0, 0, (piece + 1) // 2)
+    mirrored = jnp.where(piece == 0, 0, (piece + 1) % 2)
+    half = at // size
+    side = jnp.where(mirrored == 1, 1 - 2 * c, 2 * c - 1) * hops
+    core = jnp.where(mirrored == half, c, 1 - c)
+    line = at % size // CAP
+    return (((x + line) % nx * nz + (z + nz + side) % nz) * 2 + core) * CAP + at % CAP
 
 
 def cost(us):
@@ -380,15 +313,14 @@
 
     sides = (X_CHIPS, ctx_count // (2 * X_CHIPS))
     blk, at, meta = pl.pallas_call(
-        functools.partial(plan_kernel, ctx_count, functools.partial(arrivals, *sides)),
-        out_shape=[shape((128,), i32), shape((CAP * ctx_count,), i32), shape((16,), i32)],
-        in_specs=[SMEM(), SMEM()],
-        out_specs=[SMEM()] * 3,
-        scratch_shapes=[pltpu.SMEM((ctx_count,), i32), pltpu.SMEM((4 * ctx_count,), i32), pltpu.SMEM((4 * ctx_count,), i32)],
+        functools.partial(plan_kernel, ctx_count, sides),
+        out_shape=[shape((1, LISTED), i32), shape((1, CAP * ctx_count), i32), shape((1, 16), i32)],
+        in_specs=[SMEM(), VMEM(), VMEM()],
+        out_specs=[VMEM()] * 3,
         compiler_params=PARAMS,
-        cost_estimate=cost(8),
+        cost_estimate=cost(2),
         name="plan",
-    )(me, column_block_table)
+    )(me, column_block_table, column_block_table.reshape(LISTED, 1))
 
     steps = range(ctx_count - 1)
     before = lax.ppermute(ahead, "ctx", [(i, i + 1) for i in steps])
@@ -411,14 +343,13 @@
         name="band",
     )(meta, slash_offsets, q, k, before, after)
 
-    k_pieces, v_pieces = gather_columns(*sides, payload, [mask])
+    k_pieces, v_pieces = gather_columns(*sides, payload, [before, after], [mask])
 
     columns, top = pl.pallas_call(
         top_kernel,
-        out_shape=[shape((LISTED, BLOCK, HEAD), BF16), shape((2, HEADS, STRETCH, BLOCK), F32)],
-        in_specs=[SMEM(), SMEM(), SMEM(), VMEM(), VMEM()] + [ANY()] * len(k_pieces),
+        out_shape=[shape((ROOM, BLOCK, HEAD), BF16), shape((2, HEADS, STRETCH, BLOCK), F32)],
+        in_specs=[SMEM(), SMEM(), SMEM(), VMEM(), VMEM()] + [VMEM()] * len(k_pieces),
         out_specs=[VMEM(), VMEM()],
-        scratch_shapes=[pltpu.SemaphoreType.DMA((LISTED // GROUP,))],
         compiler_params=PARAMS,
         cost_estimate=cost(9),
         name="top",
@@ -431,19 +362,19 @@
         result = pl.pallas_call(
             functools.partial(out_kernel, ctx_count, st, len(v_pieces) if first else 0),
             grid=(1,),
-            out_shape=[shape((STRETCH, HEADS * HEAD), BF16)] + [shape((LISTED, BLOCK, HEAD), BF16)] * first,
+            out_shape=[shape((STRETCH, HEADS * HEAD), BF16)] + [shape((ROOM, BLOCK, HEAD), BF16)] * first,
             in_specs=[
                 SMEM(), SMEM(), SMEM(),
                 pl.BlockSpec((1, STRETCH, HEADS * HEAD), lambda i, st=st: (st, 0, 0)),
                 VMEM(),
                 pl.BlockSpec((1, HEADS, STRETCH, BLOCK), lambda i, st=st: (st, 0, 0, 0)),
                 VMEM(), VMEM(), VMEM(), VMEM(), VMEM(),
-            ] + ([ANY()] * len(extra) if first else [VMEM()]),
+            ] + ([VMEM()] * len(v_pieces) + [ANY()] * tp if first else [VMEM()]),
             out_specs=[VMEM()] * (1 + first),
             scratch_shapes=[
                 pltpu.VMEM((HEADS, STRETCH, BLOCK), F32),
                 pltpu.VMEM((HEADS, STRETCH, HEAD), F32),
-            ] + [pltpu.SemaphoreType.DMA((LISTED // GROUP,))] * first,
+            ],
             compiler_params=PARAMS,
             cost_estimate=cost(8),
             name=f"attend{st}",

time: 150 us -> 136 us (0.907); the launches traced: 147 us -> 135 us
  Pallas kernels: 54.4 us -> 42 us
  starting transfers between devices: 44.8 us -> 38.6 us
  waiting for transfers between devices: 37.2 us -> 40.4 us
  local copies, waits for them, and re-layouts: 10.4 us -> 13.2 us
    ppermute x20 -> x18, waiting for transfers between devices: 21.6 us -> 32.4 us  [gather_columns(): send = lambda a, r: lax.ppermute(a, 'ctx', r)]
    pallas_call x4, Pallas kernels: 19.7 us -> 11.3 us  [the longest x1 10.1 us: per_device(): pl.pallas_call(top_kernel, out_shape=[shape((ROOM, BLOCK, HEAD), BF16), s...]
    ppermute x20 -> x18, starting transfers between devices: 26.3 us -> 18.9 us  [gather_columns(): send = lambda a, r: lax.ppermute(a, 'ctx', r)]
    ppermute x1, waiting for transfers between devices: 5.83 us -> 0.01 us  [per_device(): before = lax.ppermute(ahead, 'ctx', [(i, i + 1) for i in steps])]
    pallas_call x2, Pallas kernels: 26 us -> 22.1 us  [per_device(): pl.pallas_call(functools.partial(out_kernel, ctx_count, st, len(v_pieces)...]
    ppermute x1, waiting for transfers between devices: 2.5 us -> 0.01 us  [per_device(): after = lax.ppermute(back, 'ctx', [(i + 1, i) for i in steps])]
    unnamed x44 -> x46, local copies, waits for them, and re-layouts: 6.4 us -> 8.25 us
    ppermute x1, starting transfers between devices: 1.91 us -> 3.64 us  [per_device(): after = lax.ppermute(back, 'ctx', [(i + 1, i) for i in steps])]
  transfers between devices with their start and end apart: 31 -> 29, of which waited for: 12 -> 12; matrix products, arithmetic and copies ran while one was open for 3% -> 4% of each run, Pallas kernels for 27% -> 22%
where the time goes in v4:
time: 136 us; the launch traced here: 135 us
  Pallas kernels  42 us (31%)
  waiting for transfers between devices  40.4 us (30%)
  starting transfers between devices  38.6 us (28%)
  local copies, waits for them, and re-layouts  13.2 us (10%)
    ppermute x18, waiting for transfers between devices, gather_columns(): send = lambda a, r: lax.ppermute(a, 'ctx', r)  32.4 us
    pallas_call x2, Pallas kernels, per_device(): pl.pallas_call(functools.partial(out_kernel, ctx_count, st, len(v_pieces)...  22.1 us
    ppermute x18, starting transfers between devices, gather_columns(): send = lambda a, r: lax.ppermute(a, 'ctx', r)  18.9 us
    ppermute x9, starting transfers between devices, from_ahead(): return lax.ppermute(x, axis, [((i + shift) % n, i) for i in range(n)])  14.2 us
    pallas_call x1, Pallas kernels, per_device(): pl.pallas_call(top_kernel, out_shape=[shape((ROOM, BLOCK, HEAD), BF16), s...  10.1 us
    unnamed x46, local copies, waits for them, and re-layouts  8.25 us
    ppermute x9, waiting for transfers between devices, from_ahead(): return lax.ppermute(x, axis, [((i + shift) % n, i) for i in range(n)])  8.01 us
    pallas_call x2, Pallas kernels, per_device(): pl.pallas_call(mix_kernel, grid=(width // tile,), out_shape=shape((2, STR...  6.19 us
  transfers between devices with their start and end apart: 29, of which 12 were waited for; matrix products, arithmetic and copies ran while one was open for 4% of the time, Pallas kernels for 22%

profile of v4, /device:TPU:96, one launch (start us, length us, event | category | flops | bytes accessed | tf_op | source)
XLA Modules:
  0.0 134.6 jit_solution(8405926170712561630)
XLA Ops:
  3.0 1.9 %collective-permute-start = (bf16[2,256,128]{2,1,0:T(8,128)(2,1)S(1)}, bf16[2,256,128]{2,1,0:T(8,128)(2,1)S(1)}, u32[]{:S(2)}, u32[]{:S(2)}) collective-permute-start(bf16[2,256,128]{2,1,0:T(8,128)(2,1)S(1)} %get-tuple-element.20), channel_id=1, source_target_pairs={{0,4},{4,8},{8,12},{12,16},{16,20},{20,24},{24,28},{28,32},{32,36}... | collective-permute-start | bytes 393224 | tf_op jit(solution)/shard_map/ppermute | solution.py:326
  4.9 3.6 %collective-permute-start.1 = (bf16[2,256,128]{2,1,0:T(8,128)(2,1)S(1)}, bf16[2,256,128]{2,1,0:T(8,128)(2,1)S(1)}, u32[]{:S(2)}, u32[]{:S(2)}) collective-permute-start(bf16[2,256,128]{2,1,0:T(8,128)(2,1)S(1)} %get-tuple-element.21), channel_id=1, source_target_pairs={{4,0},{8,4},{12,8},{16,12},{20,16},{24,20},{28,24},{32,28},{36,32}... | collective-permute-start | bytes 393224 | tf_op jit(solution)/shard_map/ppermute | solution.py:327
  8.6 1.6 %collective-permute-start.4 = (bf16[2,2,128,128]{3,2,1,0:T(8,128)(2,1)S(1)}, bf16[2,2,128,128]{3,2,1,0:T(8,128)(2,1)S(1)}, u32[]{:S(2)}, u32[]{:S(2)}) collective-permute-start(bf16[2,2,128,128]{3,2,1,0:T(8,128)(2,1)S(1)} %get-tuple-element.23.refs_0_), channel_id=1, source_target_pairs={{0,64},{4,68},{8,72},{12,76},{16,80},{20,84},{24,88},{28,92},{32,9... | collective-permute-start | bytes 393224 | tf_op jit(solution)/shard_map/ppermute | solution.py:244
  10.2 2.7 %collective-permute-start.3 = (bf16[2,2,128,128]{3,2,1,0:T(8,128)(2,1)S(1)}, bf16[2,2,128,128]{3,2,1,0:T(8,128)(2,1)S(1)}, u32[]{:S(2)}, u32[]{:S(2)}) collective-permute-start(bf16[2,2,128,128]{3,2,1,0:T(8,128)(2,1)S(1)} %get-tuple-element.23.refs_0_), channel_id=1, source_target_pairs={{0,128},{4,132},{8,136},{12,140},{16,144},{20,148},{24,152},{28,15... | collective-permute-start | bytes 393224 | tf_op jit(solution)/shard_map/ppermute | solution.py:244
  14.3 1.4 %collective-permute-done.4.refs_3_ = bf16[2,2,128,128]{3,2,1,0:T(8,128)(2,1)S(1)} collective-permute-done((bf16[2,2,128,128]{3,2,1,0:T(8,128)(2,1)S(1)}, bf16[2,2,128,128]{3,2,1,0:T(8,128)(2,1)S(1)}, u32[]{:S(2)}, u32[]{:S(2)}) %collective-permute-start.4) | collective-permute-done | bytes 131104 | tf_op jit(solution)/shard_map/ppermute | solution.py:244
  15.8 3.8 %collective-permute-done.3.refs_2_ = bf16[2,2,128,128]{3,2,1,0:T(8,128)(2,1)S(1)} collective-permute-done((bf16[2,2,128,128]{3,2,1,0:T(8,128)(2,1)S(1)}, bf16[2,2,128,128]{3,2,1,0:T(8,128)(2,1)S(1)}, u32[]{:S(2)}, u32[]{:S(2)}) %collective-permute-start.3) | collective-permute-done | bytes 131104 | tf_op jit(solution)/shard_map/ppermute | solution.py:244
  20.0 1.7 %collective-permute-done.5.other_ref = bf16[2,8,128,128]{3,2,1,0:T(8,128)(2,1)S(1)} collective-permute-done((bf16[2,8,128,128]{3,2,1,0:T(8,128)(2,1)S(1)}, bf16[2,8,128,128]{3,2,1,0:T(8,128)(2,1)S(1)}, u32[]{:S(2)}, u32[]{:S(2)}) %collective-permute-start.5) | collective-permute-done | bytes 524320 | tf_op jit(solution)/shard_map/ppermute | solution.py:244
  23.3 2.5 %collective-permute-start.6 = (bf16[16,128,128]{2,1,0:T(8,128)(2,1)}, bf16[16,128,128]{2,1,0:T(8,128)(2,1)}, u32[]{:S(2)}, u32[]{:S(2)}) collective-permute-start(bf16[16,128,128]{2,1,0:T(8,128)(2,1)} %chip0.1.refs_0_), channel_id=1, source_target_pairs={{0,8},{4,60},{8,16},{12,4},{16,24},{20,12},{24,32},{28,20},{32,40}... | collective-permute-start | bytes 1572872 | tf_op jit(solution)/shard_map/ppermute | solution.py:244
  25.9 4.3 %constant_dynamic-slice_fusion = (bf16[512,1024]{1,0:T(8,128)(2,1)}, bf16[512,1024]{1,0:T(8,128)(2,1)}, bf16[512,1024]{1,0:T(8,128)(2,1)}, bf16[512,1024]{1,0:T(8,128)(2,1)}) fusion(bf16[512,4096]{1,0:T(8,128)(2,1)} %param.11, s32[]{:T(128)S(6)} %select_n.15, s32[]{:T(128)S(6)} %select_n.13, s32[]{:T(128)S(6)} %select_n.12, s32[]{:T(128)S(6)} %select_n.14), kind=kLoop, calls=%fused_computation | loop fusion | bytes 8388624 | tf_op jit(solution)/shard_map/dynamic_slice | solution.py:333
  30.2 1.6 %collective-permute-start.22 = (bf16[512,1024]{1,0:T(8,128)(2,1)}, bf16[512,1024]{1,0:T(8,128)(2,1)S(1)}, u32[]{:S(2)}, u32[]{:S(2)}) collective-permute-start(bf16[512,1024]{1,0:T(8,128)(2,1)} %get-tuple-element.29), channel_id=1, source_target_pairs={{3,0},{0,1},{1,2},{2,3},{7,4},{4,5},{5,6},{6,7},{11,8},{8,9},{9,10... | collective-permute-start | bytes 3145736 | tf_op jit(solution)/shard_map/ppermute | solution.py:222
  31.8 1.7 %collective-permute-start.20 = (bf16[512,1024]{1,0:T(8,128)(2,1)}, bf16[512,1024]{1,0:T(8,128)(2,1)S(1)}, u32[]{:S(2)}, u32[]{:S(2)}) collective-permute-start(bf16[512,1024]{1,0:T(8,128)(2,1)} %get-tuple-element.30), channel_id=1, source_target_pairs={{1,0},{2,1},{3,2},{0,3},{5,4},{6,5},{7,6},{4,7},{9,8},{10,9},{11,1... | collective-permute-start | bytes 3145736 | tf_op jit(solution)/shard_map/ppermute | solution.py:222
  35.2 1.9 %band.1 = (f32[4,256,512]{2,1,0:T(8,128)S(1)}, f32[2,4,256,128]{3,2,1,0:T(8,128)S(1)}) custom-call(s32[1,16]{1,0:T(1,128)S(1)} %get-tuple-element.17.meta_ref, s32[4,64]{1,0:T(4,128)S(1)} %copy-done.22, bf16[2,256,512]{2,1,0:T(8,128)(2,1)S(1)} %bitcast.8, bf16[2,256,128]{2,1,0:T(8,128)(2,1)S(1)} %bitcast.13, ...), custom_call_target="tpu_custom_call" | custom-call | bytes 9000000 | tf_op jit(solution)/shard_map/band/pallas_call | solution.py:336
  40.7 6.7 %collective-permute-done.8.refs_3_ = bf16[16,128,128]{2,1,0:T(8,128)(2,1)S(1)} collective-permute-done((bf16[16,128,128]{2,1,0:T(8,128)(2,1)}, bf16[16,128,128]{2,1,0:T(8,128)(2,1)S(1)}, u32[]{:S(2)}, u32[]{:S(2)}) %collective-permute-start.8) | collective-permute-done | bytes 524320 | tf_op jit(solution)/shard_map/ppermute | solution.py:244
  47.5 1.7 %collective-permute-start.10 = (bf16[16,128,128]{2,1,0:T(8,128)(2,1)S(1)}, bf16[16,128,128]{2,1,0:T(8,128)(2,1)S(1)}, u32[]{:S(2)}, u32[]{:S(2)}) collective-permute-start(bf16[16,128,128]{2,1,0:T(8,128)(2,1)S(1)} %collective-permute-done.8.refs_3_), channel_id=1, source_target_pairs={{0,8},{4,60},{8,16},{12,4},{16,24},{20,12},{24,32},{28,20},{32,40}... | collective-permute-start | bytes 1572872 | tf_op jit(solution)/shard_map/ppermute | solution.py:244
  49.1 3.9 %collective-permute-done.13.refs_1_ = bf16[16,128,128]{2,1,0:T(8,128)(2,1)S(1)} collective-permute-done((bf16[16,128,128]{2,1,0:T(8,128)(2,1)S(1)}, bf16[16,128,128]{2,1,0:T(8,128)(2,1)S(1)}, u32[]{:S(2)}, u32[]{:S(2)}) %collective-permute-start.13) | collective-permute-done | bytes 524320 | tf_op jit(solution)/shard_map/ppermute | solution.py:244
  53.1 1.7 %collective-permute-start.15 = (bf16[16,128,128]{2,1,0:T(8,128)(2,1)S(1)}, bf16[16,128,128]{2,1,0:T(8,128)(2,1)S(1)}, u32[]{:S(2)}, u32[]{:S(2)}) collective-permute-start(bf16[16,128,128]{2,1,0:T(8,128)(2,1)S(1)} %collective-permute-done.13.refs_1_), channel_id=1, source_target_pairs={{0,8},{4,60},{8,16},{12,4},{16,24},{20,12},{24,32},{28,20},{32,40}... | collective-permute-start | bytes 1572872 | tf_op jit(solution)/shard_map/ppermute | solution.py:244
  54.8 2.1 %collective-permute-start.21 = (bf16[512,1024]{1,0:T(8,128)(2,1)}, bf16[512,1024]{1,0:T(8,128)(2,1)S(1)}, u32[]{:S(2)}, u32[]{:S(2)}) collective-permute-start(bf16[512,1024]{1,0:T(8,128)(2,1)} %get-tuple-element.32), channel_id=1, source_target_pairs={{2,0},{3,1},{0,2},{1,3},{6,4},{7,5},{4,6},{5,7},{10,8},{11,9},{8,1... | collective-permute-start | bytes 3145736 | tf_op jit(solution)/shard_map/ppermute | solution.py:222
  57.0 1.7 %collective-permute-done.10.refs_5_ = bf16[16,128,128]{2,1,0:T(8,128)(2,1)S(1)} collective-permute-done((bf16[16,128,128]{2,1,0:T(8,128)(2,1)S(1)}, bf16[16,128,128]{2,1,0:T(8,128)(2,1)S(1)}, u32[]{:S(2)}, u32[]{:S(2)}) %collective-permute-start.10) | collective-permute-done | bytes 524320 | tf_op jit(solution)/shard_map/ppermute | solution.py:244
  58.7 1.7 %collective-permute-start.12 = (bf16[16,128,128]{2,1,0:T(8,128)(2,1)S(1)}, bf16[16,128,128]{2,1,0:T(8,128)(2,1)S(1)}, u32[]{:S(2)}, u32[]{:S(2)}) collective-permute-start(bf16[16,128,128]{2,1,0:T(8,128)(2,1)S(1)} %collective-permute-done.10.refs_5_), channel_id=1, source_target_pairs={{0,8},{4,60},{8,16},{12,4},{16,24},{20,12},{24,32},{28,20},{32,40}... | collective-permute-start | bytes 1572872 | tf_op jit(solution)/shard_map/ppermute | solution.py:244
  60.4 3.9 %collective-permute-done.15.refs_3_ = bf16[16,128,128]{2,1,0:T(8,128)(2,1)S(1)} collective-permute-done((bf16[16,128,128]{2,1,0:T(8,128)(2,1)S(1)}, bf16[16,128,128]{2,1,0:T(8,128)(2,1)S(1)}, u32[]{:S(2)}, u32[]{:S(2)}) %collective-permute-start.15) | collective-permute-done | bytes 524320 | tf_op jit(solution)/shard_map/ppermute | solution.py:244
  64.3 1.7 %collective-permute-start.17 = (bf16[16,128,128]{2,1,0:T(8,128)(2,1)S(1)}, bf16[16,128,128]{2,1,0:T(8,128)(2,1)S(1)}, u32[]{:S(2)}, u32[]{:S(2)}) collective-permute-start(bf16[16,128,128]{2,1,0:T(8,128)(2,1)S(1)} %collective-permute-done.15.refs_3_), channel_id=1, source_target_pairs={{0,8},{4,60},{8,16},{12,4},{16,24},{20,12},{24,32},{28,20},{32,40}... | collective-permute-start | bytes 1572872 | tf_op jit(solution)/shard_map/ppermute | solution.py:244
  66.5 3.4 %collective-permute-done.12.refs_7_ = bf16[16,128,128]{2,1,0:T(8,128)(2,1)S(1)} collective-permute-done((bf16[16,128,128]{2,1,0:T(8,128)(2,1)S(1)}, bf16[16,128,128]{2,1,0:T(8,128)(2,1)S(1)}, u32[]{:S(2)}, u32[]{:S(2)}) %collective-permute-start.12) | collective-permute-done | bytes 524320 | tf_op jit(solution)/shard_map/ppermute | solution.py:244
  69.9 5.6 %collective-permute-done.17.refs_5_ = bf16[16,128,128]{2,1,0:T(8,128)(2,1)S(1)} collective-permute-done((bf16[16,128,128]{2,1,0:T(8,128)(2,1)S(1)}, bf16[16,128,128]{2,1,0:T(8,128)(2,1)S(1)}, u32[]{:S(2)}, u32[]{:S(2)}) %collective-permute-start.17) | collective-permute-done | bytes 524320 | tf_op jit(solution)/shard_map/ppermute | solution.py:244
  75.6 1.7 %collective-permute-start.19 = (bf16[16,128,128]{2,1,0:T(8,128)(2,1)S(1)}, bf16[16,128,128]{2,1,0:T(8,128)(2,1)S(1)}, u32[]{:S(2)}, u32[]{:S(2)}) collective-permute-start(bf16[16,128,128]{2,1,0:T(8,128)(2,1)S(1)} %collective-permute-done.17.refs_5_), channel_id=1, source_target_pairs={{0,8},{4,60},{8,16},{12,4},{16,24},{20,12},{24,32},{28,20},{32,40}... | collective-permute-start | bytes 1572872 | tf_op jit(solution)/shard_map/ppermute | solution.py:244
  77.2 10.1 %top.1 = (bf16[65,128,128]{2,1,0:T(8,128)(2,1)}, f32[2,4,256,128]{3,2,1,0:T(8,128)S(1)}) custom-call(s32[1,16]{1,0:T(1,128)S(1)} %get-tuple-element.17.meta_ref, s32[1,64]{1,0:T(1,128)S(1)} %get-tuple-element.18.blk_ref, s32[1,128]{1,0:T(1,128)S(1)} %get-tuple-element.19.at_ref, bf16[2,256,512]{2,1,0:T(8,128)(2,1)S(1)} %bitcast.9, ...), custom_call_target="tpu_custom_call" | custom-call | bytes 27000000 | tf_op jit(solution)/shard_map/top/pallas_call | solution.py:348
  89.3 7.3 %attend0.1 = (bf16[256,512]{1,0:T(8,128)(2,1)S(1)}, bf16[65,128,128]{2,1,0:T(8,128)(2,1)}) custom-call(s32[1,16]{1,0:T(1,128)S(1)} %get-tuple-element.17.meta_ref, s32[1,64]{1,0:T(1,128)S(1)} %get-tuple-element.18.blk_ref, s32[1,128]{1,0:T(1,128)S(1)} %get-tuple-element.19.at_ref, bf16[2,256,512]{2,1,0:T(8,128)(2,1)S(1)} %bitcast.10, ...), custom_call_target="tpu_custom_call" | custom-call | bytes 24000000 | tf_op jit(solution)/shard_map/attend0/pallas_call | solution.py:362
  97.0 2.9 %collective-permute-start.27 = (bf16[256,512]{1,0:T(8,128)(2,1)S(1)}, bf16[256,512]{1,0:T(8,128)(2,1)S(1)}, u32[]{:S(2)}, u32[]{:S(2)}) collective-permute-start(bf16[256,512]{1,0:T(8,128)(2,1)S(1)} %get-tuple-element.28.a0), channel_id=1, source_target_pairs={{2,0},{3,1},{0,2},{1,3},{6,4},{7,5},{4,6},{5,7},{10,8},{11,9},{8,1... | collective-permute-start | bytes 786440 | tf_op jit(solution)/shard_map/ppermute | solution.py:222
  101.3 14.8 %attend1.1.a0 = bf16[256,512]{1,0:T(8,128)(2,1)S(1)} custom-call(s32[1,16]{1,0:T(1,128)S(1)} %get-tuple-element.17.meta_ref, s32[1,64]{1,0:T(1,128)S(1)} %get-tuple-element.18.blk_ref, s32[1,128]{1,0:T(1,128)S(1)} %get-tuple-element.19.at_ref, bf16[2,256,512]{2,1,0:T(8,128)(2,1)S(1)} %bitcast.11, bf16[65,128,128]{2,1,0:T(8,128)(2,1)} %get-tuple-element.24.keys_ref, ...), custom_call_target="tpu_custom_call" | custom-call | bytes 24000000 | tf_op jit(solution)/shard_map/attend1/pallas_call | solution.py:362
  117.8 2.5 %collective-permute-start.23 = (bf16[256,512]{1,0:T(8,128)(2,1)S(1)}, bf16[256,512]{1,0:T(8,128)(2,1)S(1)}, u32[]{:S(2)}, u32[]{:S(2)}) collective-permute-start(bf16[256,512]{1,0:T(8,128)(2,1)S(1)} %attend1.1.a0), channel_id=1, source_target_pairs={{1,0},{2,1},{3,2},{0,3},{5,4},{6,5},{7,6},{4,7},{9,8},{10,9},{11,1... | collective-permute-start | bytes 786440 | tf_op jit(solution)/shard_map/ppermute | solution.py:222
  120.4 3.1 %mix0.1.refs_0_ = bf16[2,256,1024]{2,1,0:T(8,128)(2,1)} custom-call(bf16[256,512]{1,0:T(8,128)(2,1)S(1)} %get-tuple-element.28.a0, bf16[256,512]{1,0:T(8,128)(2,1)S(1)} %collective-permute-done.26.a1, bf16[256,512]{1,0:T(8,128)(2,1)S(1)} %collective-permute-done.27.a2, bf16[256,512]{1,0:T(8,128)(2,1)S(1)} %collective-permute-done.28.a3, ...), custom_call_target="tpu_custom_call" | custom-call | bytes 9000000 | tf_op jit(solution)/shard_map/mix0/pallas_call | solution.py:387
  123.5 7.4 %collective-permute-done.25.a3 = bf16[256,512]{1,0:T(8,128)(2,1)S(1)} collective-permute-done((bf16[256,512]{1,0:T(8,128)(2,1)S(1)}, bf16[256,512]{1,0:T(8,128)(2,1)S(1)}, u32[]{:S(2)}, u32[]{:S(2)}) %collective-permute-start.25) | collective-permute-done | bytes 262176 | tf_op jit(solution)/shard_map/ppermute | solution.py:222
  131.5 3.1 %mix1.1 = bf16[2,256,1024]{2,1,0:T(8,128)(2,1)} custom-call(bf16[256,512]{1,0:T(8,128)(2,1)S(1)} %attend1.1.a0, bf16[256,512]{1,0:T(8,128)(2,1)S(1)} %collective-permute-done.23.a1, bf16[256,512]{1,0:T(8,128)(2,1)S(1)} %collective-permute-done.24.a2, bf16[256,512]{1,0:T(8,128)(2,1)S(1)} %collective-permute-done.25.a3, ...), custom_call_target="tpu_custom_call", output_to_operand_aliasing={{}: (8, {})} | custom-call | bytes 9000000 | tf_op jit(solution)/shard_map/mix1/pallas_call | solution.py:387
  (85 shorter events, 18.6 us)
Async XLA Ops:
  3.0 11.3 %collective-permute-start = (bf16[2,256,128]{2,1,0:T(8,128)(2,1)S(1)}, bf16[2,256,128]{2,1,0:T(8,128)(2,1)S(1)}, u32[]{:S(2)}, u32[]{:S(2)}) collective-permute-start(bf16[2,256,128]{2,1,0:T(8,128)(2,1)S(1)} %get-tuple-element.20), channel_id=1, source_target_pairs={{0,4},{4,8},{8,12},{12,16},{16,20},{20,24},{24,28},{28,32},{32,36}... | collective-permute-start | bytes 393224 | tf_op jit(solution)/shard_map/ppermute | solution.py:326
  4.9 9.4 %collective-permute-start.1 = (bf16[2,256,128]{2,1,0:T(8,128)(2,1)S(1)}, bf16[2,256,128]{2,1,0:T(8,128)(2,1)S(1)}, u32[]{:S(2)}, u32[]{:S(2)}) collective-permute-start(bf16[2,256,128]{2,1,0:T(8,128)(2,1)S(1)} %get-tuple-element.21), channel_id=1, source_target_pairs={{4,0},{8,4},{12,8},{16,12},{20,16},{24,20},{28,24},{32,28},{36,32}... | collective-permute-start | bytes 393224 | tf_op jit(solution)/shard_map/ppermute | solution.py:327
  8.6 7.2 %collective-permute-start.4 = (bf16[2,2,128,128]{3,2,1,0:T(8,128)(2,1)S(1)}, bf16[2,2,128,128]{3,2,1,0:T(8,128)(2,1)S(1)}, u32[]{:S(2)}, u32[]{:S(2)}) collective-permute-start(bf16[2,2,128,128]{3,2,1,0:T(8,128)(2,1)S(1)} %get-tuple-element.23.refs_0_), channel_id=1, source_target_pairs={{0,64},{4,68},{8,72},{12,76},{16,80},{20,84},{24,88},{28,92},{32,9... | collective-permute-start | bytes 393224 | tf_op jit(solution)/shard_map/ppermute | solution.py:244
  10.2 9.4 %collective-permute-start.3 = (bf16[2,2,128,128]{3,2,1,0:T(8,128)(2,1)S(1)}, bf16[2,2,128,128]{3,2,1,0:T(8,128)(2,1)S(1)}, u32[]{:S(2)}, u32[]{:S(2)}) collective-permute-start(bf16[2,2,128,128]{3,2,1,0:T(8,128)(2,1)S(1)} %get-tuple-element.23.refs_0_), channel_id=1, source_target_pairs={{0,128},{4,132},{8,136},{12,140},{16,144},{20,148},{24,152},{28,15... | collective-permute-start | bytes 393224 | tf_op jit(solution)/shard_map/ppermute | solution.py:244
  12.9 6.8 %collective-permute-start.2 = (bf16[2,2,128,128]{3,2,1,0:T(8,128)(2,1)S(1)}, bf16[2,2,128,128]{3,2,1,0:T(8,128)(2,1)S(1)}, u32[]{:S(2)}, u32[]{:S(2)}) collective-permute-start(bf16[2,2,128,128]{3,2,1,0:T(8,128)(2,1)S(1)} %get-tuple-element.23.refs_0_), channel_id=1, source_target_pairs={{0,192},{4,196},{8,200},{12,204},{16,208},{20,212},{24,216},{28,22... | collective-permute-start | bytes 393224 | tf_op jit(solution)/shard_map/ppermute | solution.py:244
  19.7 2.0 %collective-permute-start.5 = (bf16[2,8,128,128]{3,2,1,0:T(8,128)(2,1)S(1)}, bf16[2,8,128,128]{3,2,1,0:T(8,128)(2,1)S(1)}, u32[]{:S(2)}, u32[]{:S(2)}) collective-permute-start(bf16[2,8,128,128]{3,2,1,0:T(8,128)(2,1)S(1)} %line.1.own_ref), channel_id=1, source_target_pairs={{0,4},{4,0},{8,12},{12,8},{16,20},{20,16},{24,28},{28,24},{32,36},... | collective-permute-start | bytes 1572872 | tf_op jit(solution)/shard_map/ppermute | solution.py:244
  23.3 14.7 %collective-permute-start.6 = (bf16[16,128,128]{2,1,0:T(8,128)(2,1)}, bf16[16,128,128]{2,1,0:T(8,128)(2,1)}, u32[]{:S(2)}, u32[]{:S(2)}) collective-permute-start(bf16[16,128,128]{2,1,0:T(8,128)(2,1)} %chip0.1.refs_0_), channel_id=1, source_target_pairs={{0,8},{4,60},{8,16},{12,4},{16,24},{20,12},{24,32},{28,20},{32,40}... | collective-permute-start | bytes 1572872 | tf_op jit(solution)/shard_map/ppermute | solution.py:244
  30.2 24.6 %collective-permute-start.22 = (bf16[512,1024]{1,0:T(8,128)(2,1)}, bf16[512,1024]{1,0:T(8,128)(2,1)S(1)}, u32[]{:S(2)}, u32[]{:S(2)}) collective-permute-start(bf16[512,1024]{1,0:T(8,128)(2,1)} %get-tuple-element.29), channel_id=1, source_target_pairs={{3,0},{0,1},{1,2},{2,3},{7,4},{4,5},{5,6},{6,7},{11,8},{8,9},{9,10... | collective-permute-start | bytes 3145736 | tf_op jit(solution)/shard_map/ppermute | solution.py:222
  31.8 25.1 %collective-permute-start.20 = (bf16[512,1024]{1,0:T(8,128)(2,1)}, bf16[512,1024]{1,0:T(8,128)(2,1)S(1)}, u32[]{:S(2)}, u32[]{:S(2)}) collective-permute-start(bf16[512,1024]{1,0:T(8,128)(2,1)} %get-tuple-element.30), channel_id=1, source_target_pairs={{1,0},{2,1},{3,2},{0,3},{5,4},{6,5},{7,6},{4,7},{9,8},{10,9},{11,1... | collective-permute-start | bytes 3145736 | tf_op jit(solution)/shard_map/ppermute | solution.py:222
  38.1 49.3 %copy-start = (f32[4,256,512]{2,1,0:T(8,128)}, f32[4,256,512]{2,1,0:T(8,128)S(1)}, u32[]{:S(2)}) copy-start(f32[4,256,512]{2,1,0:T(8,128)S(1)} %get-tuple-element.26.refs_1_.mask_ref) | copy-start | bytes 6291460
  38.1 9.4 %collective-permute-start.8 = (bf16[16,128,128]{2,1,0:T(8,128)(2,1)}, bf16[16,128,128]{2,1,0:T(8,128)(2,1)S(1)}, u32[]{:S(2)}, u32[]{:S(2)}) collective-permute-start(bf16[16,128,128]{2,1,0:T(8,128)(2,1)} %collective-permute-done.6.refs_1_.refs_0_), channel_id=1, source_target_pairs={{0,8},{4,60},{8,16},{12,4},{16,24},{20,12},{24,32},{28,20},{32,40}... | collective-permute-start | bytes 1572872 | tf_op jit(solution)/shard_map/ppermute | solution.py:244
  39.9 13.2 %collective-permute-start.13 = (bf16[16,128,128]{2,1,0:T(8,128)(2,1)S(1)}, bf16[16,128,128]{2,1,0:T(8,128)(2,1)S(1)}, u32[]{:S(2)}, u32[]{:S(2)}) collective-permute-start(bf16[16,128,128]{2,1,0:T(8,128)(2,1)S(1)} %chip1.1.refs_0_), channel_id=1, source_target_pairs={{0,8},{4,60},{8,16},{12,4},{16,24},{20,12},{24,32},{28,20},{32,40}... | collective-permute-start | bytes 1572872 | tf_op jit(solution)/shard_map/ppermute | solution.py:244
  47.5 11.2 %collective-permute-start.10 = (bf16[16,128,128]{2,1,0:T(8,128)(2,1)S(1)}, bf16[16,128,128]{2,1,0:T(8,128)(2,1)S(1)}, u32[]{:S(2)}, u32[]{:S(2)}) collective-permute-start(bf16[16,128,128]{2,1,0:T(8,128)(2,1)S(1)} %collective-permute-done.8.refs_3_), channel_id=1, source_target_pairs={{0,8},{4,60},{8,16},{12,4},{16,24},{20,12},{24,32},{28,20},{32,40}... | collective-permute-start | bytes 1572872 | tf_op jit(solution)/shard_map/ppermute | solution.py:244
  53.1 11.2 %collective-permute-start.15 = (bf16[16,128,128]{2,1,0:T(8,128)(2,1)S(1)}, bf16[16,128,128]{2,1,0:T(8,128)(2,1)S(1)}, u32[]{:S(2)}, u32[]{:S(2)}) collective-permute-start(bf16[16,128,128]{2,1,0:T(8,128)(2,1)S(1)} %collective-permute-done.13.refs_1_), channel_id=1, source_target_pairs={{0,8},{4,60},{8,16},{12,4},{16,24},{20,12},{24,32},{28,20},{32,40}... | collective-permute-start | bytes 1572872 | tf_op jit(solution)/shard_map/ppermute | solution.py:244
  54.8 11.2 %collective-permute-start.7 = (bf16[16,128,128]{2,1,0:T(8,128)(2,1)}, bf16[16,128,128]{2,1,0:T(8,128)(2,1)S(1)}, u32[]{:S(2)}, u32[]{:S(2)}) collective-permute-start(bf16[16,128,128]{2,1,0:T(8,128)(2,1)} %collective-permute-done.6.refs_1_.refs_0_), channel_id=1, source_target_pairs={{0,4},{4,0},{8,12},{12,8},{16,20},{20,16},{24,28},{28,24},{32,36},... | collective-permute-start | bytes 1572872 | tf_op jit(solution)/shard_map/ppermute | solution.py:244
  54.8 32.6 %copy-start.3 = (bf16[512,1024]{1,0:T(8,128)(2,1)}, bf16[512,1024]{1,0:T(8,128)(2,1)S(1)}, u32[]{:S(2)}) copy-start(bf16[512,1024]{1,0:T(8,128)(2,1)S(1)} %collective-permute-done.22.refs_11_.w3) | copy-start | bytes 3145732
  54.8 33.6 %collective-permute-start.21 = (bf16[512,1024]{1,0:T(8,128)(2,1)}, bf16[512,1024]{1,0:T(8,128)(2,1)S(1)}, u32[]{:S(2)}, u32[]{:S(2)}) collective-permute-start(bf16[512,1024]{1,0:T(8,128)(2,1)} %get-tuple-element.32), channel_id=1, source_target_pairs={{2,0},{3,1},{0,2},{1,3},{6,4},{7,5},{4,6},{5,7},{10,8},{11,9},{8,1... | collective-permute-start | bytes 3145736 | tf_op jit(solution)/shard_map/ppermute | solution.py:222
  56.8 30.5 %copy-start.5 = (bf16[512,1024]{1,0:T(8,128)(2,1)}, bf16[512,1024]{1,0:T(8,128)(2,1)S(1)}, u32[]{:S(2)}) copy-start(bf16[512,1024]{1,0:T(8,128)(2,1)S(1)} %collective-permute-done.20.refs_9_.w1) | copy-start | bytes 3145732
  56.8 9.2 %collective-permute-start.9 = (bf16[16,128,128]{2,1,0:T(8,128)(2,1)S(1)}, bf16[16,128,128]{2,1,0:T(8,128)(2,1)S(1)}, u32[]{:S(2)}, u32[]{:S(2)}) collective-permute-start(bf16[16,128,128]{2,1,0:T(8,128)(2,1)S(1)} %collective-permute-done.8.refs_3_), channel_id=1, source_target_pairs={{0,4},{4,0},{8,12},{12,8},{16,20},{20,16},{24,28},{28,24},{32,36},... | collective-permute-start | bytes 1572872 | tf_op jit(solution)/shard_map/ppermute | solution.py:244
  58.7 11.2 %collective-permute-start.12 = (bf16[16,128,128]{2,1,0:T(8,128)(2,1)S(1)}, bf16[16,128,128]{2,1,0:T(8,128)(2,1)S(1)}, u32[]{:S(2)}, u32[]{:S(2)}) collective-permute-start(bf16[16,128,128]{2,1,0:T(8,128)(2,1)S(1)} %collective-permute-done.10.refs_5_), channel_id=1, source_target_pairs={{0,8},{4,60},{8,16},{12,4},{16,24},{20,12},{24,32},{28,20},{32,40}... | collective-permute-start | bytes 1572872 | tf_op jit(solution)/shard_map/ppermute | solution.py:244
  64.3 11.2 %collective-permute-start.17 = (bf16[16,128,128]{2,1,0:T(8,128)(2,1)S(1)}, bf16[16,128,128]{2,1,0:T(8,128)(2,1)S(1)}, u32[]{:S(2)}, u32[]{:S(2)}) collective-permute-start(bf16[16,128,128]{2,1,0:T(8,128)(2,1)S(1)} %collective-permute-done.15.refs_3_), channel_id=1, source_target_pairs={{0,8},{4,60},{8,16},{12,4},{16,24},{20,12},{24,32},{28,20},{32,40}... | collective-permute-start | bytes 1572872 | tf_op jit(solution)/shard_map/ppermute | solution.py:244
  66.0 11.2 %collective-permute-start.11 = (bf16[16,128,128]{2,1,0:T(8,128)(2,1)S(1)}, bf16[16,128,128]{2,1,0:T(8,128)(2,1)S(1)}, u32[]{:S(2)}, u32[]{:S(2)}) collective-permute-start(bf16[16,128,128]{2,1,0:T(8,128)(2,1)S(1)} %collective-permute-done.10.refs_5_), channel_id=1, source_target_pairs={{0,4},{4,0},{8,12},{12,8},{16,20},{20,16},{24,28},{28,24},{32,36},... | collective-permute-start | bytes 1572872 | tf_op jit(solution)/shard_map/ppermute | solution.py:244
  66.0 22.3 %collective-permute-start.14 = (bf16[16,128,128]{2,1,0:T(8,128)(2,1)S(1)}, bf16[16,128,128]{2,1,0:T(8,128)(2,1)S(1)}, u32[]{:S(2)}, u32[]{:S(2)}) collective-permute-start(bf16[16,128,128]{2,1,0:T(8,128)(2,1)S(1)} %collective-permute-done.13.refs_1_), channel_id=1, source_target_pairs={{0,4},{4,0},{8,12},{12,8},{16,20},{20,16},{24,28},{28,24},{32,36},... | collective-permute-start | bytes 1572872 | tf_op jit(solution)/shard_map/ppermute | solution.py:244
  69.9 18.4 %collective-permute-start.16 = (bf16[16,128,128]{2,1,0:T(8,128)(2,1)S(1)}, bf16[16,128,128]{2,1,0:T(8,128)(2,1)S(1)}, u32[]{:S(2)}, u32[]{:S(2)}) collective-permute-start(bf16[16,128,128]{2,1,0:T(8,128)(2,1)S(1)} %collective-permute-done.15.refs_3_), channel_id=1, source_target_pairs={{0,4},{4,0},{8,12},{12,8},{16,20},{20,16},{24,28},{28,24},{32,36},... | collective-permute-start | bytes 1572872 | tf_op jit(solution)/shard_map/ppermute | solution.py:244
  75.6 12.8 %collective-permute-start.19 = (bf16[16,128,128]{2,1,0:T(8,128)(2,1)S(1)}, bf16[16,128,128]{2,1,0:T(8,128)(2,1)S(1)}, u32[]{:S(2)}, u32[]{:S(2)}) collective-permute-start(bf16[16,128,128]{2,1,0:T(8,128)(2,1)S(1)} %collective-permute-done.17.refs_5_), channel_id=1, source_target_pairs={{0,8},{4,60},{8,16},{12,4},{16,24},{20,12},{24,32},{28,20},{32,40}... | collective-permute-start | bytes 1572872 | tf_op jit(solution)/shard_map/ppermute | solution.py:244
  77.2 11.1 %collective-permute-start.18 = (bf16[16,128,128]{2,1,0:T(8,128)(2,1)S(1)}, bf16[16,128,128]{2,1,0:T(8,128)(2,1)S(1)}, u32[]{:S(2)}, u32[]{:S(2)}) collective-permute-start(bf16[16,128,128]{2,1,0:T(8,128)(2,1)S(1)} %collective-permute-done.17.refs_5_), channel_id=1, source_target_pairs={{0,4},{4,0},{8,12},{12,8},{16,20},{20,16},{24,28},{28,24},{32,36},... | collective-permute-start | bytes 1572872 | tf_op jit(solution)/shard_map/ppermute | solution.py:244
  96.6 21.2 %collective-permute-start.28 = (bf16[256,512]{1,0:T(8,128)(2,1)S(1)}, bf16[256,512]{1,0:T(8,128)(2,1)S(1)}, u32[]{:S(2)}, u32[]{:S(2)}) collective-permute-start(bf16[256,512]{1,0:T(8,128)(2,1)S(1)} %get-tuple-element.28.a0), channel_id=1, source_target_pairs={{3,0},{0,1},{1,2},{2,3},{7,4},{4,5},{5,6},{6,7},{11,8},{8,9},{9,10... | collective-permute-start | bytes 786440 | tf_op jit(solution)/shard_map/ppermute | solution.py:222
  97.0 23.4 %collective-permute-start.27 = (bf16[256,512]{1,0:T(8,128)(2,1)S(1)}, bf16[256,512]{1,0:T(8,128)(2,1)S(1)}, u32[]{:S(2)}, u32[]{:S(2)}) collective-permute-start(bf16[256,512]{1,0:T(8,128)(2,1)S(1)} %get-tuple-element.28.a0), channel_id=1, source_target_pairs={{2,0},{3,1},{0,2},{1,3},{6,4},{7,5},{4,6},{5,7},{10,8},{11,9},{8,1... | collective-permute-start | bytes 786440 | tf_op jit(solution)/shard_map/ppermute | solution.py:222
  99.9 20.5 %collective-permute-start.26 = (bf16[256,512]{1,0:T(8,128)(2,1)S(1)}, bf16[256,512]{1,0:T(8,128)(2,1)S(1)}, u32[]{:S(2)}, u32[]{:S(2)}) collective-permute-start(bf16[256,512]{1,0:T(8,128)(2,1)S(1)} %get-tuple-element.28.a0), channel_id=1, source_target_pairs={{1,0},{2,1},{3,2},{0,3},{5,4},{6,5},{7,6},{4,7},{9,8},{10,9},{11,1... | collective-permute-start | bytes 786440 | tf_op jit(solution)/shard_map/ppermute | solution.py:222
  116.1 14.8 %collective-permute-start.25 = (bf16[256,512]{1,0:T(8,128)(2,1)S(1)}, bf16[256,512]{1,0:T(8,128)(2,1)S(1)}, u32[]{:S(2)}, u32[]{:S(2)}) collective-permute-start(bf16[256,512]{1,0:T(8,128)(2,1)S(1)} %attend1.1.a0), channel_id=1, source_target_pairs={{3,0},{0,1},{1,2},{2,3},{7,4},{4,5},{5,6},{6,7},{11,8},{8,9},{9,10... | collective-permute-start | bytes 786440 | tf_op jit(solution)/shard_map/ppermute | solution.py:222
  116.8 14.0 %collective-permute-start.24 = (bf16[256,512]{1,0:T(8,128)(2,1)S(1)}, bf16[256,512]{1,0:T(8,128)(2,1)S(1)}, u32[]{:S(2)}, u32[]{:S(2)}) collective-permute-start(bf16[256,512]{1,0:T(8,128)(2,1)S(1)} %attend1.1.a0), channel_id=1, source_target_pairs={{2,0},{3,1},{0,2},{1,3},{6,4},{7,5},{4,6},{5,7},{10,8},{11,9},{8,1... | collective-permute-start | bytes 786440 | tf_op jit(solution)/shard_map/ppermute | solution.py:222
  117.8 13.7 %collective-permute-start.23 = (bf16[256,512]{1,0:T(8,128)(2,1)S(1)}, bf16[256,512]{1,0:T(8,128)(2,1)S(1)}, u32[]{:S(2)}, u32[]{:S(2)}) collective-permute-start(bf16[256,512]{1,0:T(8,128)(2,1)S(1)} %attend1.1.a0), channel_id=1, source_target_pairs={{1,0},{2,1},{3,2},{0,3},{5,4},{6,5},{7,6},{4,7},{9,8},{10,9},{11,1... | collective-permute-start | bytes 786440 | tf_op jit(solution)/shard_map/ppermute | solution.py:222
  (20 other events, 156.1 us)

commit v5 on v4

--- a/solution.py
+++ b/solution.py
@@ -34,7 +34,15 @@
     return lax.dot_general(a, b, (((1,), (1,)), ((), ())), preferred_element_type=F32)
 
 
-def pack_kernel(ctx_count, me_ref, table_ref, k_ref, v_ref, pay_ref, ahead_ref, back_ref):
+def pack_kernel(ctx_count, me_ref, table_hbm, k_hbm, v_hbm, pay_ref, ahead_ref, back_ref, table_ref, k_ref, v_ref, sems):
+    copies = [
+        pltpu.make_async_copy(source, target, sems.at[n])
+        for n, (source, target) in enumerate(((table_hbm, table_ref), (k_hbm, k_ref), (v_hbm, v_ref)))
+    ]
+    for copy in copies:
+        copy.start()
+    for copy in copies:
+        copy.wait()
     me = me_ref[0]
     table = table_ref[...]
     owner = owned(table, ctx_count)
@@ -58,7 +66,7 @@
     return jnp.where(stretch < ctx_count, stretch, 2 * ctx_count - 1 - stretch)
 
 
-def plan_kernel(ctx_count, sides, me_ref, row_ref, col_ref, blk_ref, at_ref, meta_ref):
+def plan_kernel(ctx_count, sides, me_ref, row_ref, col_ref, blk_ref, key_at_ref, val_at_ref, meta_ref):
     me = me_ref[0]
     row, col = row_ref[...], col_ref[...]
     square = (LISTED, LISTED)
@@ -70,8 +78,9 @@
     owner = owned(col, ctx_count)
     rank = pick((owned(row, ctx_count) == owner) & earlier, jnp.int32(1), 1)
     blk_ref[...] = pick(place == iota(jnp.int32, square, 1), col, 0)
-    entry = arrivals(*sides, me, iota(jnp.int32, (1, CAP * ctx_count), 1))
-    at_ref[...] = LISTED + pick(owner * CAP + rank == entry, place - LISTED, 0)
+    for halves, ref in ((True, key_at_ref), (False, val_at_ref)):
+        entry = arrivals(*sides, halves, me, iota(jnp.int32, (1, CAP * ctx_count), 1))
+        ref[...] = LISTED + pick(owner * CAP + rank == entry, place - LISTED, 0)
     lane = iota(jnp.int32, (1, 16), 1)
     meta = jnp.where(lane % 8 == 3, me, 0)
     for st, s in enumerate((me, 2 * ctx_count - 1 - me)):
@@ -235,7 +244,11 @@
     refs[-1][count:] = other_ref[which]
 
 
-def gather_columns(nx, nz, payload, first, later):
+def copy_kernel(source_ref, out_ref):
+    out_ref[...] = source_ref[...]
+
+
+def gather_columns(nx, nz, payload, later):
     place = lambda x, z, c: ((x % nx) * nz + z % nz) * 2 + c
     every = [(x, z, c) for x in range(nx) for z in range(nz) for c in range(2)]
     route = lambda f: [(place(*d), place(*f(*d))) for d in every]
@@ -250,10 +263,10 @@
     own = call(
         line_kernel,
         out_shape=shape((2, size, BLOCK, HEAD), BF16),
-        in_specs=[VMEM()] * nx + [ANY()] * len(first),
+        in_specs=[VMEM()] * nx,
         out_specs=VMEM(),
         name="line",
-    )(*line, *first)
+    )(*line)
     other = send(own, across)
     pieces = []
     waited = []
@@ -267,15 +280,25 @@
         )(own, other, *waited)
         held = [moving]
         for n in range(1, nz // 2 + 1):
+            last = n == nz // 2
+            if which == 0 and last:
+                moving = call(
+                    copy_kernel,
+                    grid=(1,),
+                    out_shape=shape((size, BLOCK, HEAD), BF16),
+                    in_specs=[pl.BlockSpec((size, BLOCK, HEAD), lambda i: (0, 0, 0))],
+                    out_specs=VMEM(),
+                    name="half",
+                )(moving)
             moving = send(moving, along)
-            held += [moving] + ([send(moving, across)] if n < nz // 2 else [])
+            held += [moving] + ([] if which == 1 and last else [send(moving, across)])
             if n == 1:
                 waited = [moving, *later]
         pieces.append(held)
     return pieces
 
 
-def arrivals(nx, nz, me, entry):
+def arrivals(nx, nz, halves, me, entry):
     x, z, c = lax.div(me, 2 * nz), lax.rem(lax.div(me, 2), nz), lax.rem(me, 2)
     size = nx * CAP
     at = entry % (2 * size)
@@ -283,6 +306,9 @@
     hops = jnp.where(piece == 0, 0, (piece + 1) // 2)
     mirrored = jnp.where(piece == 0, 0, (piece + 1) % 2)
     half = at // size
+    if halves:
+        last = piece == nz - 1
+        mirrored, half = jnp.where(last, half, mirrored), jnp.where(last, 0, half)
     side = jnp.where(mirrored == 1, 1 - 2 * c, 2 * c - 1) * hops
     core = jnp.where(mirrored == half, c, 1 - c)
     line = at % size // CAP
@@ -305,18 +331,24 @@
     payload, ahead, back = pl.pallas_call(
         functools.partial(pack_kernel, ctx_count),
         out_shape=[shape((2, CAP, BLOCK, HEAD), BF16)] + [shape((2, STRETCH, HEAD), BF16)] * 2,
-        in_specs=[SMEM(), VMEM(), VMEM(), VMEM()],
+        in_specs=[SMEM()] + [ANY()] * 3,
         out_specs=[VMEM()] * 3,
-        compiler_params=PARAMS,
+        scratch_shapes=[
+            pltpu.VMEM(column_block_table.shape, i32),
+            pltpu.VMEM((4, BLOCK, HEAD), BF16),
+            pltpu.VMEM((4, BLOCK, HEAD), BF16),
+            pltpu.SemaphoreType.DMA((3,)),
+        ],
+        compiler_params=pltpu.CompilerParams(vmem_limit_bytes=60 * 1024 * 1024),
         name="pack",
     )(me, column_block_table, k.reshape(4, BLOCK, HEAD), v.reshape(4, BLOCK, HEAD))
 
     sides = (X_CHIPS, ctx_count // (2 * X_CHIPS))
-    blk, at, meta = pl.pallas_call(
+    blk, key_at, val_at, meta = pl.pallas_call(
         functools.partial(plan_kernel, ctx_count, sides),
-        out_shape=[shape((1, LISTED), i32), shape((1, CAP * ctx_count), i32), shape((1, 16), i32)],
+        out_shape=[shape((1, LISTED), i32)] + [shape((1, CAP * ctx_count), i32)] * 2 + [shape((1, 16), i32)],
         in_specs=[SMEM(), VMEM(), VMEM()],
-        out_specs=[VMEM()] * 3,
+        out_specs=[VMEM()] * 4,
         compiler_params=PARAMS,
         cost_estimate=cost(2),
         name="plan",
@@ -343,7 +375,7 @@
         name="band",
     )(meta, slash_offsets, q, k, before, after)
 
-    k_pieces, v_pieces = gather_columns(*sides, payload, [before, after], [mask])
+    k_pieces, v_pieces = gather_columns(*sides, payload, [mask])
 
     columns, top = pl.pallas_call(
         top_kernel,
@@ -353,7 +385,7 @@
         compiler_params=PARAMS,
         cost_estimate=cost(9),
         name="top",
-    )(meta, blk, at, q, top, *k_pieces)
+    )(meta, blk, key_at, q, top, *k_pieces)
 
     mixed = column_vals = None
     for st in range(2):
@@ -378,7 +410,7 @@
             compiler_params=PARAMS,
             cost_estimate=cost(8),
             name=f"attend{st}",
-        )(meta, blk, at, q, columns, top, mask, k, v, before, after, *extra)
+        )(meta, blk, val_at, q, columns, top, mask, k, v, before, after, *extra)
         head_out = result[0]
         if first:
             column_vals = result[1]

time: 136 us -> 134 us (0.985)
  waiting for transfers between devices: 40.4 us -> 30.3 us
  starting transfers between devices: 38.6 us -> 46.8 us
  Pallas kernels: 42 us -> 43.7 us
    ppermute x18 -> x19, waiting for transfers between devices: 32.4 us -> 21.9 us  [gather_columns(): send = lambda a, r: lax.ppermute(a, 'ctx', r)]
    ppermute x18 -> x19, starting transfers between devices: 18.9 us -> 27.5 us  [gather_columns(): send = lambda a, r: lax.ppermute(a, 'ctx', r)]
    pallas_call x1, Pallas kernels: 0.53 us -> 2.19 us  [per_device(): pl.pallas_call(functools.partial(pack_kernel, ctx_count), out_shape=[shap...]
    unnamed x46 -> x44, local copies, waits for them, and re-layouts: 8.25 us -> 6.85 us
  transfers between devices with their start and end apart: 29 -> 30, of which waited for: 12 -> 12; matrix products, arithmetic and copies ran while one was open for 4% -> 4% of each run, Pallas kernels for 22% -> 23%
where the time goes in v5:
time: 134 us; the launch traced here: 133 us
  starting transfers between devices  46.8 us (35%)
  Pallas kernels  43.7 us (33%)
  waiting for transfers between devices  30.3 us (23%)
  local copies, waits for them, and re-layouts  11.9 us (9%)
    ppermute x19, starting transfers between devices, gather_columns(): send = lambda a, r: lax.ppermute(a, 'ctx', r)  27.5 us
    pallas_call x2, Pallas kernels, per_device(): pl.pallas_call(functools.partial(out_kernel, ctx_count, st, len(v_pieces)...  22.3 us
    ppermute x19, waiting for transfers between devices, gather_columns(): send = lambda a, r: lax.ppermute(a, 'ctx', r)  21.9 us
    ppermute x9, starting transfers between devices, from_ahead(): return lax.ppermute(x, axis, [((i + shift) % n, i) for i in range(n)])  13.8 us
    pallas_call x1, Pallas kernels, per_device(): pl.pallas_call(top_kernel, out_shape=[shape((ROOM, BLOCK, HEAD), BF16), s...  10.1 us
    ppermute x9, waiting for transfers between devices, from_ahead(): return lax.ppermute(x, axis, [((i + shift) % n, i) for i in range(n)])  8.41 us
    unnamed x44, local copies, waits for them, and re-layouts  6.85 us
    pallas_call x2, Pallas kernels, per_device(): pl.pallas_call(mix_kernel, grid=(width // tile,), out_shape=shape((2, STR...  6.19 us
  transfers between devices with their start and end apart: 30, of which 12 were waited for; matrix products, arithmetic and copies ran while one was open for 4% of the time, Pallas kernels for 23%

profile of v5, /device:TPU:96, one launch (start us, length us, event | category | flops | bytes accessed | tf_op | source)
XLA Modules:
  0.0 133.1 jit_solution(7115896191103991189)
XLA Ops:
  0.0 2.2 %pack.1 = (bf16[2,2,128,128]{3,2,1,0:T(8,128)(2,1)}, bf16[2,256,128]{2,1,0:T(8,128)(2,1)}, bf16[2,256,128]{2,1,0:T(8,128)(2,1)}) custom-call(s32[1]{0:T(128)} %bitcast.me_ref, s32[1,64]{1,0:T(1,128)} %table_hbm.1, bf16[4,128,128]{2,1,0:T(8,128)(2,1)} %bitcast.12, bf16[4,128,128]{2,1,0:T(8,128)(2,1)} %bitcast.16), custom_call_target="tpu_custom_call" | custom-call | tf_op jit(solution)/shard_map/pack/pallas_call | solution.py:331
  2.2 1.6 %collective-permute-start.4 = (bf16[2,2,128,128]{3,2,1,0:T(8,128)(2,1)}, bf16[2,2,128,128]{3,2,1,0:T(8,128)(2,1)S(1)}, u32[]{:S(2)}, u32[]{:S(2)}) collective-permute-start(bf16[2,2,128,128]{3,2,1,0:T(8,128)(2,1)} %get-tuple-element.25.refs_0_), channel_id=1, source_target_pairs={{0,64},{4,68},{8,72},{12,76},{16,80},{20,84},{24,88},{28,92},{32,9... | collective-permute-start | bytes 393224 | tf_op jit(solution)/shard_map/ppermute | solution.py:257
  3.8 2.7 %collective-permute-start.3 = (bf16[2,2,128,128]{3,2,1,0:T(8,128)(2,1)}, bf16[2,2,128,128]{3,2,1,0:T(8,128)(2,1)S(1)}, u32[]{:S(2)}, u32[]{:S(2)}) collective-permute-start(bf16[2,2,128,128]{3,2,1,0:T(8,128)(2,1)} %get-tuple-element.25.refs_0_), channel_id=1, source_target_pairs={{0,128},{4,132},{8,136},{12,140},{16,144},{20,148},{24,152},{28,15... | collective-permute-start | bytes 393224 | tf_op jit(solution)/shard_map/ppermute | solution.py:257
  9.1 3.6 %collective-permute-done.3.refs_2_ = bf16[2,2,128,128]{3,2,1,0:T(8,128)(2,1)S(1)} collective-permute-done((bf16[2,2,128,128]{3,2,1,0:T(8,128)(2,1)}, bf16[2,2,128,128]{3,2,1,0:T(8,128)(2,1)S(1)}, u32[]{:S(2)}, u32[]{:S(2)}) %collective-permute-start.3) | collective-permute-done | bytes 131104 | tf_op jit(solution)/shard_map/ppermute | solution.py:257
  13.8 1.9 %collective-permute-done.5.other_ref = bf16[2,8,128,128]{3,2,1,0:T(8,128)(2,1)S(1)} collective-permute-done((bf16[2,8,128,128]{3,2,1,0:T(8,128)(2,1)S(1)}, bf16[2,8,128,128]{3,2,1,0:T(8,128)(2,1)S(1)}, u32[]{:S(2)}, u32[]{:S(2)}) %collective-permute-start.5) | collective-permute-done | bytes 524320 | tf_op jit(solution)/shard_map/ppermute | solution.py:257
  17.3 3.1 %collective-permute-start.6 = (bf16[16,128,128]{2,1,0:T(8,128)(2,1)}, bf16[16,128,128]{2,1,0:T(8,128)(2,1)}, u32[]{:S(2)}, u32[]{:S(2)}) collective-permute-start(bf16[16,128,128]{2,1,0:T(8,128)(2,1)} %chip0.1.refs_0_), channel_id=1, source_target_pairs={{0,8},{4,60},{8,16},{12,4},{16,24},{20,12},{24,32},{28,20},{32,40}... | collective-permute-start | bytes 1572872 | tf_op jit(solution)/shard_map/ppermute | solution.py:257
  20.5 1.9 %collective-permute-start = (bf16[2,256,128]{2,1,0:T(8,128)(2,1)}, bf16[2,256,128]{2,1,0:T(8,128)(2,1)S(1)}, u32[]{:S(2)}, u32[]{:S(2)}) collective-permute-start(bf16[2,256,128]{2,1,0:T(8,128)(2,1)} %get-tuple-element.22), channel_id=1, source_target_pairs={{0,4},{4,8},{8,12},{12,16},{16,20},{20,24},{24,28},{28,32},{32,36}... | collective-permute-start | bytes 393224 | tf_op jit(solution)/shard_map/ppermute | solution.py:358
  22.4 3.6 %collective-permute-start.1 = (bf16[2,256,128]{2,1,0:T(8,128)(2,1)}, bf16[2,256,128]{2,1,0:T(8,128)(2,1)S(1)}, u32[]{:S(2)}, u32[]{:S(2)}) collective-permute-start(bf16[2,256,128]{2,1,0:T(8,128)(2,1)} %get-tuple-element.23), channel_id=1, source_target_pairs={{4,0},{8,4},{12,8},{16,12},{20,16},{24,20},{28,24},{32,28},{36,32}... | collective-permute-start | bytes 393224 | tf_op jit(solution)/shard_map/ppermute | solution.py:359
  26.1 4.3 %constant_dynamic-slice_fusion = (bf16[512,1024]{1,0:T(8,128)(2,1)}, bf16[512,1024]{1,0:T(8,128)(2,1)}, bf16[512,1024]{1,0:T(8,128)(2,1)}, bf16[512,1024]{1,0:T(8,128)(2,1)}) fusion(bf16[512,4096]{1,0:T(8,128)(2,1)} %param.11, s32[]{:T(128)S(6)} %select_n.15, s32[]{:T(128)S(6)} %select_n.13, s32[]{:T(128)S(6)} %select_n.12, s32[]{:T(128)S(6)} %select_n.14), kind=kLoop, calls=%fused_computation | loop fusion | bytes 8388624 | tf_op jit(solution)/shard_map/dynamic_slice | solution.py:365
  30.4 1.6 %collective-permute-start.23 = (bf16[512,1024]{1,0:T(8,128)(2,1)}, bf16[512,1024]{1,0:T(8,128)(2,1)S(1)}, u32[]{:S(2)}, u32[]{:S(2)}) collective-permute-start(bf16[512,1024]{1,0:T(8,128)(2,1)} %get-tuple-element.31), channel_id=1, source_target_pairs={{3,0},{0,1},{1,2},{2,3},{7,4},{4,5},{5,6},{6,7},{11,8},{8,9},{9,10... | collective-permute-start | bytes 3145736 | tf_op jit(solution)/shard_map/ppermute | solution.py:231
  32.0 1.7 %collective-permute-start.21 = (bf16[512,1024]{1,0:T(8,128)(2,1)}, bf16[512,1024]{1,0:T(8,128)(2,1)S(1)}, u32[]{:S(2)}, u32[]{:S(2)}) collective-permute-start(bf16[512,1024]{1,0:T(8,128)(2,1)} %get-tuple-element.32), channel_id=1, source_target_pairs={{1,0},{2,1},{3,2},{0,3},{5,4},{6,5},{7,6},{4,7},{9,8},{10,9},{11,1... | collective-permute-start | bytes 3145736 | tf_op jit(solution)/shard_map/ppermute | solution.py:231
  35.4 2.3 %collective-permute-start.8 = (bf16[16,128,128]{2,1,0:T(8,128)(2,1)}, bf16[16,128,128]{2,1,0:T(8,128)(2,1)S(1)}, u32[]{:S(2)}, u32[]{:S(2)}) collective-permute-start(bf16[16,128,128]{2,1,0:T(8,128)(2,1)} %collective-permute-done.6.refs_1_.refs_0_), channel_id=1, source_target_pairs={{0,8},{4,60},{8,16},{12,4},{16,24},{20,12},{24,32},{28,20},{32,40}... | collective-permute-start | bytes 1572872 | tf_op jit(solution)/shard_map/ppermute | solution.py:257
  37.8 1.8 %band.1 = (f32[4,256,512]{2,1,0:T(8,128)S(1)}, f32[2,4,256,128]{3,2,1,0:T(8,128)S(1)}) custom-call(s32[1,16]{1,0:T(1,128)S(1)} %get-tuple-element.18.meta_ref, s32[4,64]{1,0:T(4,128)S(1)} %copy-done.20, bf16[2,256,512]{2,1,0:T(8,128)(2,1)S(1)} %bitcast.8, bf16[2,256,128]{2,1,0:T(8,128)(2,1)S(1)} %bitcast.13, ...), custom_call_target="tpu_custom_call" | custom-call | bytes 9000000 | tf_op jit(solution)/shard_map/band/pallas_call | solution.py:368
  42.1 2.8 %collective-permute-done.8.refs_3_ = bf16[16,128,128]{2,1,0:T(8,128)(2,1)S(1)} collective-permute-done((bf16[16,128,128]{2,1,0:T(8,128)(2,1)}, bf16[16,128,128]{2,1,0:T(8,128)(2,1)S(1)}, u32[]{:S(2)}, u32[]{:S(2)}) %collective-permute-start.8) | collective-permute-done | bytes 524320 | tf_op jit(solution)/shard_map/ppermute | solution.py:257
  44.9 3.4 %collective-permute-start.10 = (bf16[16,128,128]{2,1,0:T(8,128)(2,1)S(1)}, bf16[16,128,128]{2,1,0:T(8,128)(2,1)S(1)}, u32[]{:S(2)}, u32[]{:S(2)}) collective-permute-start(bf16[16,128,128]{2,1,0:T(8,128)(2,1)S(1)} %collective-permute-done.8.refs_3_), channel_id=1, source_target_pairs={{0,8},{4,60},{8,16},{12,4},{16,24},{20,12},{24,32},{28,20},{32,40}... | collective-permute-start | bytes 1572872 | tf_op jit(solution)/shard_map/ppermute | solution.py:257
  48.4 2.9 %collective-permute-done.14.refs_1_ = bf16[16,128,128]{2,1,0:T(8,128)(2,1)S(1)} collective-permute-done((bf16[16,128,128]{2,1,0:T(8,128)(2,1)S(1)}, bf16[16,128,128]{2,1,0:T(8,128)(2,1)S(1)}, u32[]{:S(2)}, u32[]{:S(2)}) %collective-permute-start.14) | collective-permute-done | bytes 524320 | tf_op jit(solution)/shard_map/ppermute | solution.py:257
  51.3 2.7 %collective-permute-start.16 = (bf16[16,128,128]{2,1,0:T(8,128)(2,1)S(1)}, bf16[16,128,128]{2,1,0:T(8,128)(2,1)S(1)}, u32[]{:S(2)}, u32[]{:S(2)}) collective-permute-start(bf16[16,128,128]{2,1,0:T(8,128)(2,1)S(1)} %collective-permute-done.14.refs_1_), channel_id=1, source_target_pairs={{0,8},{4,60},{8,16},{12,4},{16,24},{20,12},{24,32},{28,20},{32,40}... | collective-permute-start | bytes 1572872 | tf_op jit(solution)/shard_map/ppermute | solution.py:257
  54.0 2.9 %collective-permute-done.10.source_ref.refs_5_ = bf16[16,128,128]{2,1,0:T(8,128)(2,1)S(1)} collective-permute-done((bf16[16,128,128]{2,1,0:T(8,128)(2,1)S(1)}, bf16[16,128,128]{2,1,0:T(8,128)(2,1)S(1)}, u32[]{:S(2)}, u32[]{:S(2)}) %collective-permute-start.10) | collective-permute-done | bytes 524320 | tf_op jit(solution)/shard_map/ppermute | solution.py:257
  57.0 2.9 %collective-permute-start.12 = (bf16[8,128,128]{2,1,0:T(8,128)(2,1)S(1)}, bf16[8,128,128]{2,1,0:T(8,128)(2,1)S(1)}, u32[]{:S(2)}, u32[]{:S(2)}) collective-permute-start(bf16[8,128,128]{2,1,0:T(8,128)(2,1)S(1)} %half.1), channel_id=1, source_target_pairs={{0,8},{4,60},{8,16},{12,4},{16,24},{20,12},{24,32},{28,20},{32,40}... | collective-permute-start | bytes 786440 | tf_op jit(solution)/shard_map/ppermute | solution.py:257
  59.9 2.1 %collective-permute-start.22 = (bf16[512,1024]{1,0:T(8,128)(2,1)S(1)}, bf16[512,1024]{1,0:T(8,128)(2,1)S(1)}, u32[]{:S(2)}, u32[]{:S(2)}) collective-permute-start(bf16[512,1024]{1,0:T(8,128)(2,1)S(1)} %copy-done.21), channel_id=1, source_target_pairs={{2,0},{3,1},{0,2},{1,3},{6,4},{7,5},{4,6},{5,7},{10,8},{11,9},{8,1... | collective-permute-start | bytes 3145736 | tf_op jit(solution)/shard_map/ppermute | solution.py:231
  62.5 2.7 %collective-permute-start.18 = (bf16[16,128,128]{2,1,0:T(8,128)(2,1)S(1)}, bf16[16,128,128]{2,1,0:T(8,128)(2,1)S(1)}, u32[]{:S(2)}, u32[]{:S(2)}) collective-permute-start(bf16[16,128,128]{2,1,0:T(8,128)(2,1)S(1)} %collective-permute-done.16.refs_3_), channel_id=1, source_target_pairs={{0,8},{4,60},{8,16},{12,4},{16,24},{20,12},{24,32},{28,20},{32,40}... | collective-permute-start | bytes 1572872 | tf_op jit(solution)/shard_map/ppermute | solution.py:257
  65.8 1.7 %collective-permute-done.13.refs_8_ = bf16[8,128,128]{2,1,0:T(8,128)(2,1)S(1)} collective-permute-done((bf16[8,128,128]{2,1,0:T(8,128)(2,1)S(1)}, bf16[8,128,128]{2,1,0:T(8,128)(2,1)S(1)}, u32[]{:S(2)}, u32[]{:S(2)}) %collective-permute-start.13) | collective-permute-done | bytes 262176 | tf_op jit(solution)/shard_map/ppermute | solution.py:257
  67.6 4.3 %collective-permute-done.18.refs_5_ = bf16[16,128,128]{2,1,0:T(8,128)(2,1)S(1)} collective-permute-done((bf16[16,128,128]{2,1,0:T(8,128)(2,1)S(1)}, bf16[16,128,128]{2,1,0:T(8,128)(2,1)S(1)}, u32[]{:S(2)}, u32[]{:S(2)}) %collective-permute-start.18) | collective-permute-done | bytes 524320 | tf_op jit(solution)/shard_map/ppermute | solution.py:257
  71.9 3.7 %collective-permute-start.20 = (bf16[16,128,128]{2,1,0:T(8,128)(2,1)S(1)}, bf16[16,128,128]{2,1,0:T(8,128)(2,1)S(1)}, u32[]{:S(2)}, u32[]{:S(2)}) collective-permute-start(bf16[16,128,128]{2,1,0:T(8,128)(2,1)S(1)} %collective-permute-done.18.refs_5_), channel_id=1, source_target_pairs={{0,8},{4,60},{8,16},{12,4},{16,24},{20,12},{24,32},{28,20},{32,40}... | collective-permute-start | bytes 1572872 | tf_op jit(solution)/shard_map/ppermute | solution.py:257
  75.6 10.1 %top.1 = (bf16[65,128,128]{2,1,0:T(8,128)(2,1)}, f32[2,4,256,128]{3,2,1,0:T(8,128)S(1)}) custom-call(s32[1,16]{1,0:T(1,128)S(1)} %get-tuple-element.18.meta_ref, s32[1,64]{1,0:T(1,128)S(1)} %get-tuple-element.19.blk_ref, s32[1,128]{1,0:T(1,128)S(1)} %get-tuple-element.21.at_ref, bf16[2,256,512]{2,1,0:T(8,128)(2,1)S(1)} %bitcast.9, ...), custom_call_target="tpu_custom_call" | custom-call | bytes 27000000 | tf_op jit(solution)/shard_map/top/pallas_call | solution.py:380
  87.6 7.5 %attend0.1 = (bf16[256,512]{1,0:T(8,128)(2,1)S(1)}, bf16[65,128,128]{2,1,0:T(8,128)(2,1)}) custom-call(s32[1,16]{1,0:T(1,128)S(1)} %get-tuple-element.18.meta_ref, s32[1,64]{1,0:T(1,128)S(1)} %get-tuple-element.19.blk_ref, s32[1,128]{1,0:T(1,128)S(1)} %get-tuple-element.20.at_ref, bf16[2,256,512]{2,1,0:T(8,128)(2,1)S(1)} %bitcast.10, ...), custom_call_target="tpu_custom_call" | custom-call | bytes 24000000 | tf_op jit(solution)/shard_map/attend0/pallas_call | solution.py:394
  95.5 2.9 %collective-permute-start.28 = (bf16[256,512]{1,0:T(8,128)(2,1)S(1)}, bf16[256,512]{1,0:T(8,128)(2,1)S(1)}, u32[]{:S(2)}, u32[]{:S(2)}) collective-permute-start(bf16[256,512]{1,0:T(8,128)(2,1)S(1)} %get-tuple-element.30.a0), channel_id=1, source_target_pairs={{2,0},{3,1},{0,2},{1,3},{6,4},{7,5},{4,6},{5,7},{10,8},{11,9},{8,1... | collective-permute-start | bytes 786440 | tf_op jit(solution)/shard_map/ppermute | solution.py:231
  99.8 14.8 %attend1.1.a0 = bf16[256,512]{1,0:T(8,128)(2,1)S(1)} custom-call(s32[1,16]{1,0:T(1,128)S(1)} %get-tuple-element.18.meta_ref, s32[1,64]{1,0:T(1,128)S(1)} %get-tuple-element.19.blk_ref, s32[1,128]{1,0:T(1,128)S(1)} %get-tuple-element.20.at_ref, bf16[2,256,512]{2,1,0:T(8,128)(2,1)S(1)} %bitcast.11, bf16[65,128,128]{2,1,0:T(8,128)(2,1)} %get-tuple-element.26.keys_ref, ...), custom_call_target="tpu_custom_call" | custom-call | bytes 24000000 | tf_op jit(solution)/shard_map/attend1/pallas_call | solution.py:394
  116.1 2.3 %collective-permute-start.24 = (bf16[256,512]{1,0:T(8,128)(2,1)S(1)}, bf16[256,512]{1,0:T(8,128)(2,1)S(1)}, u32[]{:S(2)}, u32[]{:S(2)}) collective-permute-start(bf16[256,512]{1,0:T(8,128)(2,1)S(1)} %attend1.1.a0), channel_id=1, source_target_pairs={{1,0},{2,1},{3,2},{0,3},{5,4},{6,5},{7,6},{4,7},{9,8},{10,9},{11,1... | collective-permute-start | bytes 786440 | tf_op jit(solution)/shard_map/ppermute | solution.py:231
  118.5 3.1 %mix0.1.refs_0_ = bf16[2,256,1024]{2,1,0:T(8,128)(2,1)} custom-call(bf16[256,512]{1,0:T(8,128)(2,1)S(1)} %get-tuple-element.30.a0, bf16[256,512]{1,0:T(8,128)(2,1)S(1)} %collective-permute-done.27.a1, bf16[256,512]{1,0:T(8,128)(2,1)S(1)} %collective-permute-done.28.a2, bf16[256,512]{1,0:T(8,128)(2,1)S(1)} %collective-permute-done.29.a3, ...), custom_call_target="tpu_custom_call" | custom-call | bytes 9000000 | tf_op jit(solution)/shard_map/mix0/pallas_call | solution.py:419
  121.6 7.8 %collective-permute-done.26.a3 = bf16[256,512]{1,0:T(8,128)(2,1)S(1)} collective-permute-done((bf16[256,512]{1,0:T(8,128)(2,1)S(1)}, bf16[256,512]{1,0:T(8,128)(2,1)S(1)}, u32[]{:S(2)}, u32[]{:S(2)}) %collective-permute-start.26) | collective-permute-done | bytes 262176 | tf_op jit(solution)/shard_map/ppermute | solution.py:231
  130.0 3.1 %mix1.1 = bf16[2,256,1024]{2,1,0:T(8,128)(2,1)} custom-call(bf16[256,512]{1,0:T(8,128)(2,1)S(1)} %attend1.1.a0, bf16[256,512]{1,0:T(8,128)(2,1)S(1)} %collective-permute-done.24.a1, bf16[256,512]{1,0:T(8,128)(2,1)S(1)} %collective-permute-done.25.a2, bf16[256,512]{1,0:T(8,128)(2,1)S(1)} %collective-permute-done.26.a3, ...), custom_call_target="tpu_custom_call", output_to_operand_aliasing={{}: (8, {})} | custom-call | bytes 9000000 | tf_op jit(solution)/shard_map/mix1/pallas_call | solution.py:419
  (86 shorter events, 16.8 us)
Async XLA Ops:
  2.2 6.9 %collective-permute-start.4 = (bf16[2,2,128,128]{3,2,1,0:T(8,128)(2,1)}, bf16[2,2,128,128]{3,2,1,0:T(8,128)(2,1)S(1)}, u32[]{:S(2)}, u32[]{:S(2)}) collective-permute-start(bf16[2,2,128,128]{3,2,1,0:T(8,128)(2,1)} %get-tuple-element.25.refs_0_), channel_id=1, source_target_pairs={{0,64},{4,68},{8,72},{12,76},{16,80},{20,84},{24,88},{28,92},{32,9... | collective-permute-start | bytes 393224 | tf_op jit(solution)/shard_map/ppermute | solution.py:257
  3.8 9.0 %collective-permute-start.3 = (bf16[2,2,128,128]{3,2,1,0:T(8,128)(2,1)}, bf16[2,2,128,128]{3,2,1,0:T(8,128)(2,1)S(1)}, u32[]{:S(2)}, u32[]{:S(2)}) collective-permute-start(bf16[2,2,128,128]{3,2,1,0:T(8,128)(2,1)} %get-tuple-element.25.refs_0_), channel_id=1, source_target_pairs={{0,128},{4,132},{8,136},{12,140},{16,144},{20,148},{24,152},{28,15... | collective-permute-start | bytes 393224 | tf_op jit(solution)/shard_map/ppermute | solution.py:257
  6.5 6.2 %collective-permute-start.2 = (bf16[2,2,128,128]{3,2,1,0:T(8,128)(2,1)}, bf16[2,2,128,128]{3,2,1,0:T(8,128)(2,1)S(1)}, u32[]{:S(2)}, u32[]{:S(2)}) collective-permute-start(bf16[2,2,128,128]{3,2,1,0:T(8,128)(2,1)} %get-tuple-element.25.refs_0_), channel_id=1, source_target_pairs={{0,192},{4,196},{8,200},{12,204},{16,208},{20,212},{24,216},{28,22... | collective-permute-start | bytes 393224 | tf_op jit(solution)/shard_map/ppermute | solution.py:257
  13.7 2.0 %collective-permute-start.5 = (bf16[2,8,128,128]{3,2,1,0:T(8,128)(2,1)S(1)}, bf16[2,8,128,128]{3,2,1,0:T(8,128)(2,1)S(1)}, u32[]{:S(2)}, u32[]{:S(2)}) collective-permute-start(bf16[2,8,128,128]{3,2,1,0:T(8,128)(2,1)S(1)} %line.1.own_ref), channel_id=1, source_target_pairs={{0,4},{4,0},{8,12},{12,8},{16,20},{20,16},{24,28},{28,24},{32,36},... | collective-permute-start | bytes 1572872 | tf_op jit(solution)/shard_map/ppermute | solution.py:257
  17.3 18.1 %collective-permute-start.6 = (bf16[16,128,128]{2,1,0:T(8,128)(2,1)}, bf16[16,128,128]{2,1,0:T(8,128)(2,1)}, u32[]{:S(2)}, u32[]{:S(2)}) collective-permute-start(bf16[16,128,128]{2,1,0:T(8,128)(2,1)} %chip0.1.refs_0_), channel_id=1, source_target_pairs={{0,8},{4,60},{8,16},{12,4},{16,24},{20,12},{24,32},{28,20},{32,40}... | collective-permute-start | bytes 1572872 | tf_op jit(solution)/shard_map/ppermute | solution.py:257
  20.5 17.3 %collective-permute-start = (bf16[2,256,128]{2,1,0:T(8,128)(2,1)}, bf16[2,256,128]{2,1,0:T(8,128)(2,1)S(1)}, u32[]{:S(2)}, u32[]{:S(2)}) collective-permute-start(bf16[2,256,128]{2,1,0:T(8,128)(2,1)} %get-tuple-element.22), channel_id=1, source_target_pairs={{0,4},{4,8},{8,12},{12,16},{16,20},{20,24},{24,28},{28,32},{32,36}... | collective-permute-start | bytes 393224 | tf_op jit(solution)/shard_map/ppermute | solution.py:358
  22.4 15.4 %collective-permute-start.1 = (bf16[2,256,128]{2,1,0:T(8,128)(2,1)}, bf16[2,256,128]{2,1,0:T(8,128)(2,1)S(1)}, u32[]{:S(2)}, u32[]{:S(2)}) collective-permute-start(bf16[2,256,128]{2,1,0:T(8,128)(2,1)} %get-tuple-element.23), channel_id=1, source_target_pairs={{4,0},{8,4},{12,8},{16,12},{20,16},{24,20},{28,24},{32,28},{36,32}... | collective-permute-start | bytes 393224 | tf_op jit(solution)/shard_map/ppermute | solution.py:359
  30.4 26.5 %collective-permute-start.23 = (bf16[512,1024]{1,0:T(8,128)(2,1)}, bf16[512,1024]{1,0:T(8,128)(2,1)S(1)}, u32[]{:S(2)}, u32[]{:S(2)}) collective-permute-start(bf16[512,1024]{1,0:T(8,128)(2,1)} %get-tuple-element.31), channel_id=1, source_target_pairs={{3,0},{0,1},{1,2},{2,3},{7,4},{4,5},{5,6},{6,7},{11,8},{8,9},{9,10... | collective-permute-start | bytes 3145736 | tf_op jit(solution)/shard_map/ppermute | solution.py:231
  32.0 27.9 %collective-permute-start.21 = (bf16[512,1024]{1,0:T(8,128)(2,1)}, bf16[512,1024]{1,0:T(8,128)(2,1)S(1)}, u32[]{:S(2)}, u32[]{:S(2)}) collective-permute-start(bf16[512,1024]{1,0:T(8,128)(2,1)} %get-tuple-element.32), channel_id=1, source_target_pairs={{1,0},{2,1},{3,2},{0,3},{5,4},{6,5},{7,6},{4,7},{9,8},{10,9},{11,1... | collective-permute-start | bytes 3145736 | tf_op jit(solution)/shard_map/ppermute | solution.py:231
  35.4 9.5 %collective-permute-start.8 = (bf16[16,128,128]{2,1,0:T(8,128)(2,1)}, bf16[16,128,128]{2,1,0:T(8,128)(2,1)S(1)}, u32[]{:S(2)}, u32[]{:S(2)}) collective-permute-start(bf16[16,128,128]{2,1,0:T(8,128)(2,1)} %collective-permute-done.6.refs_1_.refs_0_), channel_id=1, source_target_pairs={{0,8},{4,60},{8,16},{12,4},{16,24},{20,12},{24,32},{28,20},{32,40}... | collective-permute-start | bytes 1572872 | tf_op jit(solution)/shard_map/ppermute | solution.py:257
  42.0 9.3 %collective-permute-start.14 = (bf16[16,128,128]{2,1,0:T(8,128)(2,1)S(1)}, bf16[16,128,128]{2,1,0:T(8,128)(2,1)S(1)}, u32[]{:S(2)}, u32[]{:S(2)}) collective-permute-start(bf16[16,128,128]{2,1,0:T(8,128)(2,1)S(1)} %chip1.1.refs_0_), channel_id=1, source_target_pairs={{0,8},{4,60},{8,16},{12,4},{16,24},{20,12},{24,32},{28,20},{32,40}... | collective-permute-start | bytes 1572872 | tf_op jit(solution)/shard_map/ppermute | solution.py:257
  44.9 12.0 %collective-permute-start.10 = (bf16[16,128,128]{2,1,0:T(8,128)(2,1)S(1)}, bf16[16,128,128]{2,1,0:T(8,128)(2,1)S(1)}, u32[]{:S(2)}, u32[]{:S(2)}) collective-permute-start(bf16[16,128,128]{2,1,0:T(8,128)(2,1)S(1)} %collective-permute-done.8.refs_3_), channel_id=1, source_target_pairs={{0,8},{4,60},{8,16},{12,4},{16,24},{20,12},{24,32},{28,20},{32,40}... | collective-permute-start | bytes 1572872 | tf_op jit(solution)/shard_map/ppermute | solution.py:257
  51.3 11.2 %collective-permute-start.16 = (bf16[16,128,128]{2,1,0:T(8,128)(2,1)S(1)}, bf16[16,128,128]{2,1,0:T(8,128)(2,1)S(1)}, u32[]{:S(2)}, u32[]{:S(2)}) collective-permute-start(bf16[16,128,128]{2,1,0:T(8,128)(2,1)S(1)} %collective-permute-done.14.refs_1_), channel_id=1, source_target_pairs={{0,8},{4,60},{8,16},{12,4},{16,24},{20,12},{24,32},{28,20},{32,40}... | collective-permute-start | bytes 1572872 | tf_op jit(solution)/shard_map/ppermute | solution.py:257
  54.0 11.2 %collective-permute-start.7 = (bf16[16,128,128]{2,1,0:T(8,128)(2,1)}, bf16[16,128,128]{2,1,0:T(8,128)(2,1)S(1)}, u32[]{:S(2)}, u32[]{:S(2)}) collective-permute-start(bf16[16,128,128]{2,1,0:T(8,128)(2,1)} %collective-permute-done.6.refs_1_.refs_0_), channel_id=1, source_target_pairs={{0,4},{4,0},{8,12},{12,8},{16,20},{20,16},{24,28},{28,24},{32,36},... | collective-permute-start | bytes 1572872 | tf_op jit(solution)/shard_map/ppermute | solution.py:257
  56.9 8.8 %collective-permute-start.9 = (bf16[16,128,128]{2,1,0:T(8,128)(2,1)S(1)}, bf16[16,128,128]{2,1,0:T(8,128)(2,1)S(1)}, u32[]{:S(2)}, u32[]{:S(2)}) collective-permute-start(bf16[16,128,128]{2,1,0:T(8,128)(2,1)S(1)} %collective-permute-done.8.refs_3_), channel_id=1, source_target_pairs={{0,4},{4,0},{8,12},{12,8},{16,20},{20,16},{24,28},{28,24},{32,36},... | collective-permute-start | bytes 1572872 | tf_op jit(solution)/shard_map/ppermute | solution.py:257
  56.9 28.7 %copy-start.3 = (bf16[512,1024]{1,0:T(8,128)(2,1)}, bf16[512,1024]{1,0:T(8,128)(2,1)S(1)}, u32[]{:S(2)}) copy-start(bf16[512,1024]{1,0:T(8,128)(2,1)S(1)} %collective-permute-done.23.refs_11_.w3) | copy-start | bytes 3145732
  57.0 8.4 %collective-permute-start.12 = (bf16[8,128,128]{2,1,0:T(8,128)(2,1)S(1)}, bf16[8,128,128]{2,1,0:T(8,128)(2,1)S(1)}, u32[]{:S(2)}, u32[]{:S(2)}) collective-permute-start(bf16[8,128,128]{2,1,0:T(8,128)(2,1)S(1)} %half.1), channel_id=1, source_target_pairs={{0,8},{4,60},{8,16},{12,4},{16,24},{20,12},{24,32},{28,20},{32,40}... | collective-permute-start | bytes 786440 | tf_op jit(solution)/shard_map/ppermute | solution.py:257
  59.9 25.8 %copy-start.5 = (bf16[512,1024]{1,0:T(8,128)(2,1)}, bf16[512,1024]{1,0:T(8,128)(2,1)S(1)}, u32[]{:S(2)}) copy-start(bf16[512,1024]{1,0:T(8,128)(2,1)S(1)} %collective-permute-done.21.refs_9_.w1) | copy-start | bytes 3145732
  59.9 26.7 %collective-permute-start.22 = (bf16[512,1024]{1,0:T(8,128)(2,1)S(1)}, bf16[512,1024]{1,0:T(8,128)(2,1)S(1)}, u32[]{:S(2)}, u32[]{:S(2)}) collective-permute-start(bf16[512,1024]{1,0:T(8,128)(2,1)S(1)} %copy-done.21), channel_id=1, source_target_pairs={{2,0},{3,1},{0,2},{1,3},{6,4},{7,5},{4,6},{5,7},{10,8},{11,9},{8,1... | collective-permute-start | bytes 3145736 | tf_op jit(solution)/shard_map/ppermute | solution.py:231
  62.5 9.4 %collective-permute-start.18 = (bf16[16,128,128]{2,1,0:T(8,128)(2,1)S(1)}, bf16[16,128,128]{2,1,0:T(8,128)(2,1)S(1)}, u32[]{:S(2)}, u32[]{:S(2)}) collective-permute-start(bf16[16,128,128]{2,1,0:T(8,128)(2,1)S(1)} %collective-permute-done.16.refs_3_), channel_id=1, source_target_pairs={{0,8},{4,60},{8,16},{12,4},{16,24},{20,12},{24,32},{28,20},{32,40}... | collective-permute-start | bytes 1572872 | tf_op jit(solution)/shard_map/ppermute | solution.py:257
  65.2 10.4 %collective-permute-start.11 = (bf16[16,128,128]{2,1,0:T(8,128)(2,1)S(1)}, bf16[16,128,128]{2,1,0:T(8,128)(2,1)S(1)}, u32[]{:S(2)}, u32[]{:S(2)}) collective-permute-start(bf16[16,128,128]{2,1,0:T(8,128)(2,1)S(1)} %collective-permute-done.10.source_ref.refs_5_), channel_id=1, source_target_pairs={{0,4},{4,0},{8,12},{12,8},{16,20},{20,16},{24,28},{28,24},{32,36},... | collective-permute-start | bytes 1572872 | tf_op jit(solution)/shard_map/ppermute | solution.py:257
  65.3 2.2 %collective-permute-start.13 = (bf16[8,128,128]{2,1,0:T(8,128)(2,1)S(1)}, bf16[8,128,128]{2,1,0:T(8,128)(2,1)S(1)}, u32[]{:S(2)}, u32[]{:S(2)}) collective-permute-start(bf16[8,128,128]{2,1,0:T(8,128)(2,1)S(1)} %collective-permute-done.12.refs_7_), channel_id=1, source_target_pairs={{0,4},{4,0},{8,12},{12,8},{16,20},{20,16},{24,28},{28,24},{32,36},... | collective-permute-start | bytes 786440 | tf_op jit(solution)/shard_map/ppermute | solution.py:257
  65.7 20.9 %collective-permute-start.15 = (bf16[16,128,128]{2,1,0:T(8,128)(2,1)S(1)}, bf16[16,128,128]{2,1,0:T(8,128)(2,1)S(1)}, u32[]{:S(2)}, u32[]{:S(2)}) collective-permute-start(bf16[16,128,128]{2,1,0:T(8,128)(2,1)S(1)} %collective-permute-done.14.refs_1_), channel_id=1, source_target_pairs={{0,4},{4,0},{8,12},{12,8},{16,20},{20,16},{24,28},{28,24},{32,36},... | collective-permute-start | bytes 1572872 | tf_op jit(solution)/shard_map/ppermute | solution.py:257
  67.5 19.2 %collective-permute-start.17 = (bf16[16,128,128]{2,1,0:T(8,128)(2,1)S(1)}, bf16[16,128,128]{2,1,0:T(8,128)(2,1)S(1)}, u32[]{:S(2)}, u32[]{:S(2)}) collective-permute-start(bf16[16,128,128]{2,1,0:T(8,128)(2,1)S(1)} %collective-permute-done.16.refs_3_), channel_id=1, source_target_pairs={{0,4},{4,0},{8,12},{12,8},{16,20},{20,16},{24,28},{28,24},{32,36},... | collective-permute-start | bytes 1572872 | tf_op jit(solution)/shard_map/ppermute | solution.py:257
  71.9 14.8 %collective-permute-start.20 = (bf16[16,128,128]{2,1,0:T(8,128)(2,1)S(1)}, bf16[16,128,128]{2,1,0:T(8,128)(2,1)S(1)}, u32[]{:S(2)}, u32[]{:S(2)}) collective-permute-start(bf16[16,128,128]{2,1,0:T(8,128)(2,1)S(1)} %collective-permute-done.18.refs_5_), channel_id=1, source_target_pairs={{0,8},{4,60},{8,16},{12,4},{16,24},{20,12},{24,32},{28,20},{32,40}... | collective-permute-start | bytes 1572872 | tf_op jit(solution)/shard_map/ppermute | solution.py:257
  75.6 11.1 %collective-permute-start.19 = (bf16[16,128,128]{2,1,0:T(8,128)(2,1)S(1)}, bf16[16,128,128]{2,1,0:T(8,128)(2,1)S(1)}, u32[]{:S(2)}, u32[]{:S(2)}) collective-permute-start(bf16[16,128,128]{2,1,0:T(8,128)(2,1)S(1)} %collective-permute-done.18.refs_5_), channel_id=1, source_target_pairs={{0,4},{4,0},{8,12},{12,8},{16,20},{20,16},{24,28},{28,24},{32,36},... | collective-permute-start | bytes 1572872 | tf_op jit(solution)/shard_map/ppermute | solution.py:257
  95.1 21.0 %collective-permute-start.29 = (bf16[256,512]{1,0:T(8,128)(2,1)S(1)}, bf16[256,512]{1,0:T(8,128)(2,1)S(1)}, u32[]{:S(2)}, u32[]{:S(2)}) collective-permute-start(bf16[256,512]{1,0:T(8,128)(2,1)S(1)} %get-tuple-element.30.a0), channel_id=1, source_target_pairs={{3,0},{0,1},{1,2},{2,3},{7,4},{4,5},{5,6},{6,7},{11,8},{8,9},{9,10... | collective-permute-start | bytes 786440 | tf_op jit(solution)/shard_map/ppermute | solution.py:231
  95.5 22.9 %collective-permute-start.28 = (bf16[256,512]{1,0:T(8,128)(2,1)S(1)}, bf16[256,512]{1,0:T(8,128)(2,1)S(1)}, u32[]{:S(2)}, u32[]{:S(2)}) collective-permute-start(bf16[256,512]{1,0:T(8,128)(2,1)S(1)} %get-tuple-element.30.a0), channel_id=1, source_target_pairs={{2,0},{3,1},{0,2},{1,3},{6,4},{7,5},{4,6},{5,7},{10,8},{11,9},{8,1... | collective-permute-start | bytes 786440 | tf_op jit(solution)/shard_map/ppermute | solution.py:231
  98.4 20.1 %collective-permute-start.27 = (bf16[256,512]{1,0:T(8,128)(2,1)S(1)}, bf16[256,512]{1,0:T(8,128)(2,1)S(1)}, u32[]{:S(2)}, u32[]{:S(2)}) collective-permute-start(bf16[256,512]{1,0:T(8,128)(2,1)S(1)} %get-tuple-element.30.a0), channel_id=1, source_target_pairs={{1,0},{2,1},{3,2},{0,3},{5,4},{6,5},{7,6},{4,7},{9,8},{10,9},{11,1... | collective-permute-start | bytes 786440 | tf_op jit(solution)/shard_map/ppermute | solution.py:231
  114.6 14.8 %collective-permute-start.26 = (bf16[256,512]{1,0:T(8,128)(2,1)S(1)}, bf16[256,512]{1,0:T(8,128)(2,1)S(1)}, u32[]{:S(2)}, u32[]{:S(2)}) collective-permute-start(bf16[256,512]{1,0:T(8,128)(2,1)S(1)} %attend1.1.a0), channel_id=1, source_target_pairs={{3,0},{0,1},{1,2},{2,3},{7,4},{4,5},{5,6},{6,7},{11,8},{8,9},{9,10... | collective-permute-start | bytes 786440 | tf_op jit(solution)/shard_map/ppermute | solution.py:231
  115.3 14.0 %collective-permute-start.25 = (bf16[256,512]{1,0:T(8,128)(2,1)S(1)}, bf16[256,512]{1,0:T(8,128)(2,1)S(1)}, u32[]{:S(2)}, u32[]{:S(2)}) collective-permute-start(bf16[256,512]{1,0:T(8,128)(2,1)S(1)} %attend1.1.a0), channel_id=1, source_target_pairs={{2,0},{3,1},{0,2},{1,3},{6,4},{7,5},{4,6},{5,7},{10,8},{11,9},{8,1... | collective-permute-start | bytes 786440 | tf_op jit(solution)/shard_map/ppermute | solution.py:231
  116.1 13.8 %collective-permute-start.24 = (bf16[256,512]{1,0:T(8,128)(2,1)S(1)}, bf16[256,512]{1,0:T(8,128)(2,1)S(1)}, u32[]{:S(2)}, u32[]{:S(2)}) collective-permute-start(bf16[256,512]{1,0:T(8,128)(2,1)S(1)} %attend1.1.a0), channel_id=1, source_target_pairs={{1,0},{2,1},{3,2},{0,3},{5,4},{6,5},{7,6},{4,7},{9,8},{10,9},{11,1... | collective-permute-start | bytes 786440 | tf_op jit(solution)/shard_map/ppermute | solution.py:231
  (20 other events, 194.8 us)

commit v6 on v5

--- a/solution.py
+++ b/solution.py
@@ -34,15 +34,7 @@
     return lax.dot_general(a, b, (((1,), (1,)), ((), ())), preferred_element_type=F32)
 
 
-def pack_kernel(ctx_count, me_ref, table_hbm, k_hbm, v_hbm, pay_ref, ahead_ref, back_ref, table_ref, k_ref, v_ref, sems):
-    copies = [
-        pltpu.make_async_copy(source, target, sems.at[n])
-        for n, (source, target) in enumerate(((table_hbm, table_ref), (k_hbm, k_ref), (v_hbm, v_ref)))
-    ]
-    for copy in copies:
-        copy.start()
-    for copy in copies:
-        copy.wait()
+def pack_kernel(ctx_count, me_ref, table_ref, k_ref, v_ref, pay_ref, ahead_ref, back_ref):
     me = me_ref[0]
     table = table_ref[...]
     owner = owned(table, ctx_count)
@@ -315,6 +307,13 @@
     return (((x + line) % nx * nz + (z + nz + side) % nz) * 2 + core) * CAP + at % CAP
 
 
+def slab_kernel(tp, index_ref, weight_ref, *refs):
+    width = weight_ref.shape[1] // tp
+    for shift, ref in enumerate(refs[1:]):
+        target = lax.rem(index_ref[0] + tp - shift, tp)
+        ref[...] = weight_ref[:, pl.ds(pl.multiple_of(target * width, width), width)]
+
+
 def cost(us):
     return pl.CostEstimate(flops=0, bytes_accessed=int(us * 3.0e6), transcendentals=0)
 
@@ -331,15 +330,9 @@
     payload, ahead, back = pl.pallas_call(
         functools.partial(pack_kernel, ctx_count),
         out_shape=[shape((2, CAP, BLOCK, HEAD), BF16)] + [shape((2, STRETCH, HEAD), BF16)] * 2,
-        in_specs=[SMEM()] + [ANY()] * 3,
+        in_specs=[SMEM(), VMEM(), VMEM(), VMEM()],
         out_specs=[VMEM()] * 3,
-        scratch_shapes=[
-            pltpu.VMEM(column_block_table.shape, i32),
-            pltpu.VMEM((4, BLOCK, HEAD), BF16),
-            pltpu.VMEM((4, BLOCK, HEAD), BF16),
-            pltpu.SemaphoreType.DMA((3,)),
-        ],
-        compiler_params=pltpu.CompilerParams(vmem_limit_bytes=60 * 1024 * 1024),
+        compiler_params=PARAMS,
         name="pack",
     )(me, column_block_table, k.reshape(4, BLOCK, HEAD), v.reshape(4, BLOCK, HEAD))
 
@@ -358,13 +351,6 @@
     before = lax.ppermute(ahead, "ctx", [(i, i + 1) for i in steps])
     after = lax.ppermute(back, "ctx", [(i + 1, i) for i in steps])
 
-    width = out_weight.shape[1] // tp
-    slabs = []
-    for shift in range(tp):
-        target = lax.rem(tp_index + tp - shift, tp)
-        slab = lax.dynamic_slice(out_weight, (0, target * width), (out_weight.shape[0], width))
-        slabs.append(slab if shift == 0 else from_ahead(slab, "tp", shift))
-
     mask, top = pl.pallas_call(
         functools.partial(band_kernel, ctx_count),
         out_shape=[shape((HEADS, STRETCH, 2 * STRETCH), F32), shape((2, HEADS, STRETCH, BLOCK), F32)],
@@ -377,6 +363,20 @@
 
     k_pieces, v_pieces = gather_columns(*sides, payload, [mask])
 
+    width = out_weight.shape[1] // tp
+    depth = out_weight.shape[0]
+    slabs = pl.pallas_call(
+        functools.partial(slab_kernel, tp),
+        grid=(depth // 128,),
+        out_shape=[shape((depth, width), BF16)] * tp,
+        in_specs=[SMEM(), pl.BlockSpec((128, out_weight.shape[1]), lambda i: (i, 0)), ANY()],
+        out_specs=[pl.BlockSpec((128, width), lambda i: (i, 0))] * tp,
+        compiler_params=PARAMS,
+        cost_estimate=cost(3),
+        name="slabs",
+    )(tp_index.reshape(1).astype(i32), out_weight, v_pieces[0])
+    slabs = [slabs[0]] + [from_ahead(slabs[shift], "tp", shift) for shift in range(1, tp)]
+
     columns, top = pl.pallas_call(
         top_kernel,
         out_shape=[shape((ROOM, BLOCK, HEAD), BF16), shape((2, HEADS, STRETCH, BLOCK), F32)],
@@ -390,7 +390,7 @@
     mixed = column_vals = None
     for st in range(2):
         first = st == 0
-        extra = [*v_pieces, *slabs] if first else [column_vals]
+        extra = [*v_pieces, slabs[1], slabs[3]] if first else [column_vals]
         result = pl.pallas_call(
             functools.partial(out_kernel, ctx_count, st, len(v_pieces) if first else 0),
             grid=(1,),
@@ -401,7 +401,7 @@
                 VMEM(),
                 pl.BlockSpec((1, HEADS, STRETCH, BLOCK), lambda i, st=st: (st, 0, 0, 0)),
                 VMEM(), VMEM(), VMEM(), VMEM(), VMEM(),
-            ] + ([VMEM()] * len(v_pieces) + [ANY()] * tp if first else [VMEM()]),
+            ] + ([VMEM()] * len(v_pieces) + [ANY()] * 2 if first else [VMEM()]),
             out_specs=[VMEM()] * (1 + first),
             scratch_shapes=[
                 pltpu.VMEM((HEADS, STRETCH, BLOCK), F32),

time: 134 us -> 130 us (0.970)
  local copies, waits for them, and re-layouts: 11.9 us -> 5.47 us
  starting transfers between devices: 46.8 us -> 43.1 us
  waiting for transfers between devices: 30.3 us -> 33.2 us
  Pallas kernels: 43.7 us -> 45.9 us
    ppermute x9, waiting for transfers between devices: 8.41 us -> 16.4 us  [from_ahead(): return lax.ppermute(x, axis, [((i + shift) % n, i) for i in range(n)])]
    ppermute x19, waiting for transfers between devices: 21.9 us -> 16.8 us  [gather_columns(): send = lambda a, r: lax.ppermute(a, 'ctx', r)]
    pallas_call x0 -> x1, Pallas kernels: none -> 4.88 us  [per_device(): pl.pallas_call(functools.partial(slab_kernel, tp), grid=(depth // 128,),...]
    dynamic_slice x1 -> x0, local copies, waits for them, and re-layouts: 4.32 us -> none  [per_device(): lax.dynamic_slice(out_weight, (0, target * width), (out_weight.shape[0],...]
    ppermute x19, starting transfers between devices: 27.5 us -> 25 us  [gather_columns(): send = lambda a, r: lax.ppermute(a, 'ctx', r)]
    pallas_call x1, Pallas kernels: 2.19 us -> 0.53 us  [per_device(): pl.pallas_call(functools.partial(pack_kernel, ctx_count), out_shape=[shap...]
    unnamed x44 -> x38, local copies, waits for them, and re-layouts: 6.85 us -> 5.37 us
  transfers between devices with their start and end apart: 30 -> 30, of which waited for: 12 -> 11; matrix products, arithmetic and copies ran while one was open for 4% -> 0% of each run, Pallas kernels for 23% -> 33%
where the time goes in v6:
time: 130 us; the launch traced here: 128 us
  Pallas kernels  45.9 us (35%)
  starting transfers between devices  43.1 us (33%)
  waiting for transfers between devices  33.2 us (26%)
  local copies, waits for them, and re-layouts  5.47 us (4%)
    ppermute x19, starting transfers between devices, gather_columns(): send = lambda a, r: lax.ppermute(a, 'ctx', r)  25 us
    pallas_call x2, Pallas kernels, per_device(): pl.pallas_call(functools.partial(out_kernel, ctx_count, st, len(v_pieces)...  22.2 us
    ppermute x19, waiting for transfers between devices, gather_columns(): send = lambda a, r: lax.ppermute(a, 'ctx', r)  16.8 us
    ppermute x9, waiting for transfers between devices, from_ahead(): return lax.ppermute(x, axis, [((i + shift) % n, i) for i in range(n)])  16.4 us
    ppermute x9, starting transfers between devices, from_ahead(): return lax.ppermute(x, axis, [((i + shift) % n, i) for i in range(n)])  12.5 us
    pallas_call x1, Pallas kernels, per_device(): pl.pallas_call(top_kernel, out_shape=[shape((ROOM, BLOCK, HEAD), BF16), s...  9.82 us
    pallas_call x2, Pallas kernels, per_device(): pl.pallas_call(mix_kernel, grid=(width // tile,), out_shape=shape((2, STR...  6.19 us
    unnamed x38, local copies, waits for them, and re-layouts  5.37 us
  transfers between devices with their start and end apart: 30, of which 11 were waited for; matrix products, arithmetic and copies ran while one was open for 0% of the time, Pallas kernels for 33%

profile of v6, /device:TPU:96, one launch (start us, length us, event | category | flops | bytes accessed | tf_op | source)
XLA Modules:
  0.0 127.8 jit_solution(9754359146366473401)
XLA Ops:
  3.1 1.6 %collective-permute-start.4 = (bf16[2,2,128,128]{3,2,1,0:T(8,128)(2,1)S(1)}, bf16[2,2,128,128]{3,2,1,0:T(8,128)(2,1)S(1)}, u32[]{:S(2)}, u32[]{:S(2)}) collective-permute-start(bf16[2,2,128,128]{3,2,1,0:T(8,128)(2,1)S(1)} %get-tuple-element.29.refs_0_), channel_id=1, source_target_pairs={{0,64},{4,68},{8,72},{12,76},{16,80},{20,84},{24,88},{28,92},{32,9... | collective-permute-start | bytes 393224 | tf_op jit(solution)/shard_map/ppermute | solution.py:249
  4.6 2.7 %collective-permute-start.3 = (bf16[2,2,128,128]{3,2,1,0:T(8,128)(2,1)S(1)}, bf16[2,2,128,128]{3,2,1,0:T(8,128)(2,1)S(1)}, u32[]{:S(2)}, u32[]{:S(2)}) collective-permute-start(bf16[2,2,128,128]{3,2,1,0:T(8,128)(2,1)S(1)} %get-tuple-element.29.refs_0_), channel_id=1, source_target_pairs={{0,128},{4,132},{8,136},{12,140},{16,144},{20,148},{24,152},{28,15... | collective-permute-start | bytes 393224 | tf_op jit(solution)/shard_map/ppermute | solution.py:249
  7.4 1.4 %collective-permute-start.2 = (bf16[2,2,128,128]{3,2,1,0:T(8,128)(2,1)S(1)}, bf16[2,2,128,128]{3,2,1,0:T(8,128)(2,1)S(1)}, u32[]{:S(2)}, u32[]{:S(2)}) collective-permute-start(bf16[2,2,128,128]{3,2,1,0:T(8,128)(2,1)S(1)} %get-tuple-element.29.refs_0_), channel_id=1, source_target_pairs={{0,192},{4,196},{8,200},{12,204},{16,208},{20,212},{24,216},{28,22... | collective-permute-start | bytes 393224 | tf_op jit(solution)/shard_map/ppermute | solution.py:249
  9.8 3.6 %collective-permute-done.3.refs_2_ = bf16[2,2,128,128]{3,2,1,0:T(8,128)(2,1)S(1)} collective-permute-done((bf16[2,2,128,128]{3,2,1,0:T(8,128)(2,1)S(1)}, bf16[2,2,128,128]{3,2,1,0:T(8,128)(2,1)S(1)}, u32[]{:S(2)}, u32[]{:S(2)}) %collective-permute-start.3) | collective-permute-done | bytes 131104 | tf_op jit(solution)/shard_map/ppermute | solution.py:249
  13.5 1.9 %collective-permute-done.5.other_ref = bf16[2,8,128,128]{3,2,1,0:T(8,128)(2,1)S(1)} collective-permute-done((bf16[2,8,128,128]{3,2,1,0:T(8,128)(2,1)S(1)}, bf16[2,8,128,128]{3,2,1,0:T(8,128)(2,1)S(1)}, u32[]{:S(2)}, u32[]{:S(2)}) %collective-permute-start.5) | collective-permute-done | bytes 524320 | tf_op jit(solution)/shard_map/ppermute | solution.py:249
  15.5 3.2 %collective-permute-start.6 = (bf16[16,128,128]{2,1,0:T(8,128)(2,1)S(1)}, bf16[16,128,128]{2,1,0:T(8,128)(2,1)S(1)}, u32[]{:S(2)}, u32[]{:S(2)}) collective-permute-start(bf16[16,128,128]{2,1,0:T(8,128)(2,1)S(1)} %chip0.1.refs_0_), channel_id=1, source_target_pairs={{0,8},{4,60},{8,16},{12,4},{16,24},{20,12},{24,32},{28,20},{32,40}... | collective-permute-start | bytes 1572872 | tf_op jit(solution)/shard_map/ppermute | solution.py:249
  18.7 1.9 %collective-permute-start = (bf16[2,256,128]{2,1,0:T(8,128)(2,1)S(1)}, bf16[2,256,128]{2,1,0:T(8,128)(2,1)S(1)}, u32[]{:S(2)}, u32[]{:S(2)}) collective-permute-start(bf16[2,256,128]{2,1,0:T(8,128)(2,1)S(1)} %get-tuple-element.26), channel_id=1, source_target_pairs={{0,4},{4,8},{8,12},{12,16},{16,20},{20,24},{24,28},{28,32},{32,36}... | collective-permute-start | bytes 393224 | tf_op jit(solution)/shard_map/ppermute | solution.py:351
  20.6 3.6 %collective-permute-start.1 = (bf16[2,256,128]{2,1,0:T(8,128)(2,1)S(1)}, bf16[2,256,128]{2,1,0:T(8,128)(2,1)S(1)}, u32[]{:S(2)}, u32[]{:S(2)}) collective-permute-start(bf16[2,256,128]{2,1,0:T(8,128)(2,1)S(1)} %get-tuple-element.27), channel_id=1, source_target_pairs={{4,0},{8,4},{12,8},{16,12},{20,16},{24,20},{28,24},{32,28},{36,32}... | collective-permute-start | bytes 393224 | tf_op jit(solution)/shard_map/ppermute | solution.py:352
  24.6 2.1 %collective-permute-done.6.refs_1_.refs_0_ = bf16[16,128,128]{2,1,0:T(8,128)(2,1)S(1)} collective-permute-done((bf16[16,128,128]{2,1,0:T(8,128)(2,1)S(1)}, bf16[16,128,128]{2,1,0:T(8,128)(2,1)S(1)}, u32[]{:S(2)}, u32[]{:S(2)}) %collective-permute-start.6) | collective-permute-done | bytes 524320 | tf_op jit(solution)/shard_map/ppermute | solution.py:249
  26.8 3.7 %collective-permute-start.8 = (bf16[16,128,128]{2,1,0:T(8,128)(2,1)S(1)}, bf16[16,128,128]{2,1,0:T(8,128)(2,1)S(1)}, u32[]{:S(2)}, u32[]{:S(2)}) collective-permute-start(bf16[16,128,128]{2,1,0:T(8,128)(2,1)S(1)} %collective-permute-done.6.refs_1_.refs_0_), channel_id=1, source_target_pairs={{0,8},{4,60},{8,16},{12,4},{16,24},{20,12},{24,32},{28,20},{32,40}... | collective-permute-start | bytes 1572872 | tf_op jit(solution)/shard_map/ppermute | solution.py:249
  30.5 1.9 %band.1 = (f32[4,256,512]{2,1,0:T(8,128)S(1)}, f32[2,4,256,128]{3,2,1,0:T(8,128)S(1)}) custom-call(s32[1,16]{1,0:T(1,128)S(1)} %get-tuple-element.22.meta_ref, s32[4,64]{1,0:T(4,128)S(1)} %copy-done.18, bf16[2,256,512]{2,1,0:T(8,128)(2,1)S(1)} %bitcast.9, bf16[2,256,128]{2,1,0:T(8,128)(2,1)S(1)} %bitcast.14, ...), custom_call_target="tpu_custom_call" | custom-call | bytes 9000000 | tf_op jit(solution)/shard_map/band/pallas_call | solution.py:354
  32.6 4.9 %slabs.1 = (bf16[512,1024]{1,0:T(8,128)(2,1)S(1)}, bf16[512,1024]{1,0:T(8,128)(2,1)S(1)}, bf16[512,1024]{1,0:T(8,128)(2,1)}, bf16[512,1024]{1,0:T(8,128)(2,1)S(1)}) custom-call(s32[1]{0:T(128)} %bitcast.7.index_ref, bf16[512,4096]{1,0:T(8,128)(2,1)} %weight_ref.1, bf16[16,128,128]{2,1,0:T(8,128)(2,1)S(1)} %chip1.1.refs_0_), custom_call_target="tpu_custom_call" | custom-call | bytes 9000000 | tf_op jit(solution)/shard_map/slabs/pallas_call | solution.py:368
  37.4 3.0 %collective-permute-start.21 = (bf16[512,1024]{1,0:T(8,128)(2,1)S(1)}, bf16[512,1024]{1,0:T(8,128)(2,1)S(1)}, u32[]{:S(2)}, u32[]{:S(2)}) collective-permute-start(bf16[512,1024]{1,0:T(8,128)(2,1)S(1)} %get-tuple-element.33), channel_id=1, source_target_pairs={{1,0},{2,1},{3,2},{0,3},{5,4},{6,5},{7,6},{4,7},{9,8},{10,9},{11,1... | collective-permute-start | bytes 3145736 | tf_op jit(solution)/shard_map/ppermute | solution.py:223
  40.9 1.9 %collective-permute-done.14.refs_1_ = bf16[16,128,128]{2,1,0:T(8,128)(2,1)S(1)} collective-permute-done((bf16[16,128,128]{2,1,0:T(8,128)(2,1)S(1)}, bf16[16,128,128]{2,1,0:T(8,128)(2,1)S(1)}, u32[]{:S(2)}, u32[]{:S(2)}) %collective-permute-start.14) | collective-permute-done | bytes 524320 | tf_op jit(solution)/shard_map/ppermute | solution.py:249
  42.8 3.7 %collective-permute-start.16 = (bf16[16,128,128]{2,1,0:T(8,128)(2,1)S(1)}, bf16[16,128,128]{2,1,0:T(8,128)(2,1)S(1)}, u32[]{:S(2)}, u32[]{:S(2)}) collective-permute-start(bf16[16,128,128]{2,1,0:T(8,128)(2,1)S(1)} %collective-permute-done.14.refs_1_), channel_id=1, source_target_pairs={{0,8},{4,60},{8,16},{12,4},{16,24},{20,12},{24,32},{28,20},{32,40}... | collective-permute-start | bytes 1572872 | tf_op jit(solution)/shard_map/ppermute | solution.py:249
  46.5 3.1 %collective-permute-done.10.source_ref.refs_5_ = bf16[16,128,128]{2,1,0:T(8,128)(2,1)S(1)} collective-permute-done((bf16[16,128,128]{2,1,0:T(8,128)(2,1)S(1)}, bf16[16,128,128]{2,1,0:T(8,128)(2,1)S(1)}, u32[]{:S(2)}, u32[]{:S(2)}) %collective-permute-start.10) | collective-permute-done | bytes 524320 | tf_op jit(solution)/shard_map/ppermute | solution.py:249
  49.7 2.5 %collective-permute-start.12 = (bf16[8,128,128]{2,1,0:T(8,128)(2,1)S(1)}, bf16[8,128,128]{2,1,0:T(8,128)(2,1)S(1)}, u32[]{:S(2)}, u32[]{:S(2)}) collective-permute-start(bf16[8,128,128]{2,1,0:T(8,128)(2,1)S(1)} %half.1), channel_id=1, source_target_pairs={{0,8},{4,60},{8,16},{12,4},{16,24},{20,12},{24,32},{28,20},{32,40}... | collective-permute-start | bytes 786440 | tf_op jit(solution)/shard_map/ppermute | solution.py:249
  52.2 3.0 %collective-permute-done.16.refs_3_ = bf16[16,128,128]{2,1,0:T(8,128)(2,1)S(1)} collective-permute-done((bf16[16,128,128]{2,1,0:T(8,128)(2,1)S(1)}, bf16[16,128,128]{2,1,0:T(8,128)(2,1)S(1)}, u32[]{:S(2)}, u32[]{:S(2)}) %collective-permute-start.16) | collective-permute-done | bytes 524320 | tf_op jit(solution)/shard_map/ppermute | solution.py:249
  55.2 2.5 %collective-permute-start.18 = (bf16[16,128,128]{2,1,0:T(8,128)(2,1)S(1)}, bf16[16,128,128]{2,1,0:T(8,128)(2,1)S(1)}, u32[]{:S(2)}, u32[]{:S(2)}) collective-permute-start(bf16[16,128,128]{2,1,0:T(8,128)(2,1)S(1)} %collective-permute-done.16.refs_3_), channel_id=1, source_target_pairs={{0,8},{4,60},{8,16},{12,4},{16,24},{20,12},{24,32},{28,20},{32,40}... | collective-permute-start | bytes 1572872 | tf_op jit(solution)/shard_map/ppermute | solution.py:249
  57.7 4.6 %collective-permute-done.21.refs_8_.w1 = bf16[512,1024]{1,0:T(8,128)(2,1)S(1)} collective-permute-done((bf16[512,1024]{1,0:T(8,128)(2,1)S(1)}, bf16[512,1024]{1,0:T(8,128)(2,1)S(1)}, u32[]{:S(2)}, u32[]{:S(2)}) %collective-permute-start.21) | collective-permute-done | bytes 1048608 | tf_op jit(solution)/shard_map/ppermute | solution.py:223
  62.9 2.9 %collective-permute-done.22.refs_9_.w3 = bf16[512,1024]{1,0:T(8,128)(2,1)S(1)} collective-permute-done((bf16[512,1024]{1,0:T(8,128)(2,1)S(1)}, bf16[512,1024]{1,0:T(8,128)(2,1)S(1)}, u32[]{:S(2)}, u32[]{:S(2)}) %collective-permute-start.22) | collective-permute-done | bytes 1048608 | tf_op jit(solution)/shard_map/ppermute | solution.py:223
  66.4 2.0 %collective-permute-start.20 = (bf16[16,128,128]{2,1,0:T(8,128)(2,1)S(1)}, bf16[16,128,128]{2,1,0:T(8,128)(2,1)S(1)}, u32[]{:S(2)}, u32[]{:S(2)}) collective-permute-start(bf16[16,128,128]{2,1,0:T(8,128)(2,1)S(1)} %collective-permute-done.18.refs_5_), channel_id=1, source_target_pairs={{0,8},{4,60},{8,16},{12,4},{16,24},{20,12},{24,32},{28,20},{32,40}... | collective-permute-start | bytes 1572872 | tf_op jit(solution)/shard_map/ppermute | solution.py:249
  68.4 9.8 %top.1 = (bf16[65,128,128]{2,1,0:T(8,128)(2,1)}, f32[2,4,256,128]{3,2,1,0:T(8,128)S(1)}) custom-call(s32[1,16]{1,0:T(1,128)S(1)} %get-tuple-element.22.meta_ref, s32[1,64]{1,0:T(1,128)S(1)} %get-tuple-element.23.blk_ref, s32[1,128]{1,0:T(1,128)S(1)} %get-tuple-element.25.at_ref, bf16[2,256,512]{2,1,0:T(8,128)(2,1)S(1)} %bitcast.10, ...), custom_call_target="tpu_custom_call" | custom-call | bytes 27000000 | tf_op jit(solution)/shard_map/top/pallas_call | solution.py:380
  81.1 7.3 %attend0.1 = (bf16[256,512]{1,0:T(8,128)(2,1)S(1)}, bf16[65,128,128]{2,1,0:T(8,128)(2,1)}) custom-call(s32[1,16]{1,0:T(1,128)S(1)} %get-tuple-element.22.meta_ref, s32[1,64]{1,0:T(1,128)S(1)} %get-tuple-element.23.blk_ref, s32[1,128]{1,0:T(1,128)S(1)} %get-tuple-element.24.at_ref, bf16[2,256,512]{2,1,0:T(8,128)(2,1)S(1)} %bitcast.11, ...), custom_call_target="tpu_custom_call" | custom-call | bytes 24000000 | tf_op jit(solution)/shard_map/attend0/pallas_call | solution.py:394
  89.6 2.9 %collective-permute-start.28 = (bf16[256,512]{1,0:T(8,128)(2,1)S(1)}, bf16[256,512]{1,0:T(8,128)(2,1)S(1)}, u32[]{:S(2)}, u32[]{:S(2)}) collective-permute-start(bf16[256,512]{1,0:T(8,128)(2,1)S(1)} %get-tuple-element.38.a0), channel_id=1, source_target_pairs={{2,0},{3,1},{0,2},{1,3},{6,4},{7,5},{4,6},{5,7},{10,8},{11,9},{8,1... | collective-permute-start | bytes 786440 | tf_op jit(solution)/shard_map/ppermute | solution.py:223
  92.5 1.9 %collective-permute-start.27 = (bf16[256,512]{1,0:T(8,128)(2,1)S(1)}, bf16[256,512]{1,0:T(8,128)(2,1)S(1)}, u32[]{:S(2)}, u32[]{:S(2)}) collective-permute-start(bf16[256,512]{1,0:T(8,128)(2,1)S(1)} %get-tuple-element.38.a0), channel_id=1, source_target_pairs={{1,0},{2,1},{3,2},{0,3},{5,4},{6,5},{7,6},{4,7},{9,8},{10,9},{11,1... | collective-permute-start | bytes 786440 | tf_op jit(solution)/shard_map/ppermute | solution.py:223
  94.4 14.9 %attend1.1.a0 = bf16[256,512]{1,0:T(8,128)(2,1)S(1)} custom-call(s32[1,16]{1,0:T(1,128)S(1)} %get-tuple-element.22.meta_ref, s32[1,64]{1,0:T(1,128)S(1)} %get-tuple-element.23.blk_ref, s32[1,128]{1,0:T(1,128)S(1)} %get-tuple-element.24.at_ref, bf16[2,256,512]{2,1,0:T(8,128)(2,1)S(1)} %bitcast.12, bf16[65,128,128]{2,1,0:T(8,128)(2,1)} %get-tuple-element.30.keys_ref, ...), custom_call_target="tpu_custom_call" | custom-call | bytes 24000000 | tf_op jit(solution)/shard_map/attend1/pallas_call | solution.py:394
  109.5 1.3 %collective-permute-start.24 = (bf16[256,512]{1,0:T(8,128)(2,1)S(1)}, bf16[256,512]{1,0:T(8,128)(2,1)S(1)}, u32[]{:S(2)}, u32[]{:S(2)}) collective-permute-start(bf16[256,512]{1,0:T(8,128)(2,1)S(1)} %attend1.1.a0), channel_id=1, source_target_pairs={{2,0},{3,1},{0,2},{1,3},{6,4},{7,5},{4,6},{5,7},{10,8},{11,9},{8,1... | collective-permute-start | bytes 786440 | tf_op jit(solution)/shard_map/ppermute | solution.py:223
  110.9 1.8 %collective-permute-start.23 = (bf16[256,512]{1,0:T(8,128)(2,1)S(1)}, bf16[256,512]{1,0:T(8,128)(2,1)S(1)}, u32[]{:S(2)}, u32[]{:S(2)}) collective-permute-start(bf16[256,512]{1,0:T(8,128)(2,1)S(1)} %attend1.1.a0), channel_id=1, source_target_pairs={{1,0},{2,1},{3,2},{0,3},{5,4},{6,5},{7,6},{4,7},{9,8},{10,9},{11,1... | collective-permute-start | bytes 786440 | tf_op jit(solution)/shard_map/ppermute | solution.py:223
  112.8 3.1 %mix0.1.refs_0_ = bf16[2,256,1024]{2,1,0:T(8,128)(2,1)} custom-call(bf16[256,512]{1,0:T(8,128)(2,1)S(1)} %get-tuple-element.38.a0, bf16[256,512]{1,0:T(8,128)(2,1)S(1)} %collective-permute-done.27.a1, bf16[256,512]{1,0:T(8,128)(2,1)S(1)} %collective-permute-done.28.a2, bf16[256,512]{1,0:T(8,128)(2,1)S(1)} %collective-permute-done.29.a3, ...), custom_call_target="tpu_custom_call" | custom-call | bytes 9000000 | tf_op jit(solution)/shard_map/mix0/pallas_call | solution.py:419
  115.9 8.3 %collective-permute-done.25.a3 = bf16[256,512]{1,0:T(8,128)(2,1)S(1)} collective-permute-done((bf16[256,512]{1,0:T(8,128)(2,1)S(1)}, bf16[256,512]{1,0:T(8,128)(2,1)S(1)}, u32[]{:S(2)}, u32[]{:S(2)}) %collective-permute-start.25) | collective-permute-done | bytes 262176 | tf_op jit(solution)/shard_map/ppermute | solution.py:223
  124.7 3.1 %mix1.1 = bf16[2,256,1024]{2,1,0:T(8,128)(2,1)} custom-call(bf16[256,512]{1,0:T(8,128)(2,1)S(1)} %attend1.1.a0, bf16[256,512]{1,0:T(8,128)(2,1)S(1)} %collective-permute-done.23.a1, bf16[256,512]{1,0:T(8,128)(2,1)S(1)} %collective-permute-done.24.a2, bf16[256,512]{1,0:T(8,128)(2,1)S(1)} %collective-permute-done.25.a3, ...), custom_call_target="tpu_custom_call", output_to_operand_aliasing={{}: (8, {})} | custom-call | bytes 9000000 | tf_op jit(solution)/shard_map/mix1/pallas_call | solution.py:419
  (80 shorter events, 11.2 us)
Async XLA Ops:
  0.0 30.5 %copy-start.6 = (bf16[1,2,256,512]{3,2,1,0:T(8,128)(2,1)S(1)}, bf16[1,2,256,512]{3,2,1,0:T(8,128)(2,1)}, u32[]{:S(2)}) copy-start(bf16[1,2,256,512]{3,2,1,0:T(8,128)(2,1)} %param.6) | copy-start | bytes 1572868
  2.5 28.0 %copy-start.18 = (s32[4,64]{1,0:T(4,128)S(1)}, s32[4,64]{1,0:T(4,128)}, u32[]{:S(2)}) copy-start(s32[4,64]{1,0:T(4,128)} %slash_ref.1) | copy-start | bytes 3076
  3.1 6.7 %collective-permute-start.4 = (bf16[2,2,128,128]{3,2,1,0:T(8,128)(2,1)S(1)}, bf16[2,2,128,128]{3,2,1,0:T(8,128)(2,1)S(1)}, u32[]{:S(2)}, u32[]{:S(2)}) collective-permute-start(bf16[2,2,128,128]{3,2,1,0:T(8,128)(2,1)S(1)} %get-tuple-element.29.refs_0_), channel_id=1, source_target_pairs={{0,64},{4,68},{8,72},{12,76},{16,80},{20,84},{24,88},{28,92},{32,9... | collective-permute-start | bytes 393224 | tf_op jit(solution)/shard_map/ppermute | solution.py:249
  4.6 8.7 %collective-permute-start.3 = (bf16[2,2,128,128]{3,2,1,0:T(8,128)(2,1)S(1)}, bf16[2,2,128,128]{3,2,1,0:T(8,128)(2,1)S(1)}, u32[]{:S(2)}, u32[]{:S(2)}) collective-permute-start(bf16[2,2,128,128]{3,2,1,0:T(8,128)(2,1)S(1)} %get-tuple-element.29.refs_0_), channel_id=1, source_target_pairs={{0,128},{4,132},{8,136},{12,140},{16,144},{20,148},{24,152},{28,15... | collective-permute-start | bytes 393224 | tf_op jit(solution)/shard_map/ppermute | solution.py:249
  7.4 6.0 %collective-permute-start.2 = (bf16[2,2,128,128]{3,2,1,0:T(8,128)(2,1)S(1)}, bf16[2,2,128,128]{3,2,1,0:T(8,128)(2,1)S(1)}, u32[]{:S(2)}, u32[]{:S(2)}) collective-permute-start(bf16[2,2,128,128]{3,2,1,0:T(8,128)(2,1)S(1)} %get-tuple-element.29.refs_0_), channel_id=1, source_target_pairs={{0,192},{4,196},{8,200},{12,204},{16,208},{20,212},{24,216},{28,22... | collective-permute-start | bytes 393224 | tf_op jit(solution)/shard_map/ppermute | solution.py:249
  13.4 2.0 %collective-permute-start.5 = (bf16[2,8,128,128]{3,2,1,0:T(8,128)(2,1)S(1)}, bf16[2,8,128,128]{3,2,1,0:T(8,128)(2,1)S(1)}, u32[]{:S(2)}, u32[]{:S(2)}) collective-permute-start(bf16[2,8,128,128]{3,2,1,0:T(8,128)(2,1)S(1)} %line.1.own_ref), channel_id=1, source_target_pairs={{0,4},{4,0},{8,12},{12,8},{16,20},{20,16},{24,28},{28,24},{32,36},... | collective-permute-start | bytes 1572872 | tf_op jit(solution)/shard_map/ppermute | solution.py:249
  15.5 11.3 %collective-permute-start.6 = (bf16[16,128,128]{2,1,0:T(8,128)(2,1)S(1)}, bf16[16,128,128]{2,1,0:T(8,128)(2,1)S(1)}, u32[]{:S(2)}, u32[]{:S(2)}) collective-permute-start(bf16[16,128,128]{2,1,0:T(8,128)(2,1)S(1)} %chip0.1.refs_0_), channel_id=1, source_target_pairs={{0,8},{4,60},{8,16},{12,4},{16,24},{20,12},{24,32},{28,20},{32,40}... | collective-permute-start | bytes 1572872 | tf_op jit(solution)/shard_map/ppermute | solution.py:249
  18.7 11.8 %collective-permute-start = (bf16[2,256,128]{2,1,0:T(8,128)(2,1)S(1)}, bf16[2,256,128]{2,1,0:T(8,128)(2,1)S(1)}, u32[]{:S(2)}, u32[]{:S(2)}) collective-permute-start(bf16[2,256,128]{2,1,0:T(8,128)(2,1)S(1)} %get-tuple-element.26), channel_id=1, source_target_pairs={{0,4},{4,8},{8,12},{12,16},{16,20},{20,24},{24,28},{28,32},{32,36}... | collective-permute-start | bytes 393224 | tf_op jit(solution)/shard_map/ppermute | solution.py:351
  20.6 9.9 %collective-permute-start.1 = (bf16[2,256,128]{2,1,0:T(8,128)(2,1)S(1)}, bf16[2,256,128]{2,1,0:T(8,128)(2,1)S(1)}, u32[]{:S(2)}, u32[]{:S(2)}) collective-permute-start(bf16[2,256,128]{2,1,0:T(8,128)(2,1)S(1)} %get-tuple-element.27), channel_id=1, source_target_pairs={{4,0},{8,4},{12,8},{16,12},{20,16},{24,20},{28,24},{32,28},{36,32}... | collective-permute-start | bytes 393224 | tf_op jit(solution)/shard_map/ppermute | solution.py:352
  26.8 13.7 %collective-permute-start.8 = (bf16[16,128,128]{2,1,0:T(8,128)(2,1)S(1)}, bf16[16,128,128]{2,1,0:T(8,128)(2,1)S(1)}, u32[]{:S(2)}, u32[]{:S(2)}) collective-permute-start(bf16[16,128,128]{2,1,0:T(8,128)(2,1)S(1)} %collective-permute-done.6.refs_1_.refs_0_), channel_id=1, source_target_pairs={{0,8},{4,60},{8,16},{12,4},{16,24},{20,12},{24,32},{28,20},{32,40}... | collective-permute-start | bytes 1572872 | tf_op jit(solution)/shard_map/ppermute | solution.py:249
  32.5 10.3 %collective-permute-start.14 = (bf16[16,128,128]{2,1,0:T(8,128)(2,1)S(1)}, bf16[16,128,128]{2,1,0:T(8,128)(2,1)S(1)}, u32[]{:S(2)}, u32[]{:S(2)}) collective-permute-start(bf16[16,128,128]{2,1,0:T(8,128)(2,1)S(1)} %chip1.1.refs_0_), channel_id=1, source_target_pairs={{0,8},{4,60},{8,16},{12,4},{16,24},{20,12},{24,32},{28,20},{32,40}... | collective-permute-start | bytes 1572872 | tf_op jit(solution)/shard_map/ppermute | solution.py:249
  37.4 24.9 %collective-permute-start.21 = (bf16[512,1024]{1,0:T(8,128)(2,1)S(1)}, bf16[512,1024]{1,0:T(8,128)(2,1)S(1)}, u32[]{:S(2)}, u32[]{:S(2)}) collective-permute-start(bf16[512,1024]{1,0:T(8,128)(2,1)S(1)} %get-tuple-element.33), channel_id=1, source_target_pairs={{1,0},{2,1},{3,2},{0,3},{5,4},{6,5},{7,6},{4,7},{9,8},{10,9},{11,1... | collective-permute-start | bytes 3145736 | tf_op jit(solution)/shard_map/ppermute | solution.py:223
  40.4 25.3 %collective-permute-start.22 = (bf16[512,1024]{1,0:T(8,128)(2,1)S(1)}, bf16[512,1024]{1,0:T(8,128)(2,1)S(1)}, u32[]{:S(2)}, u32[]{:S(2)}) collective-permute-start(bf16[512,1024]{1,0:T(8,128)(2,1)S(1)} %get-tuple-element.34), channel_id=1, source_target_pairs={{3,0},{0,1},{1,2},{2,3},{7,4},{4,5},{5,6},{6,7},{11,8},{8,9},{9,10... | collective-permute-start | bytes 3145736 | tf_op jit(solution)/shard_map/ppermute | solution.py:223
  40.4 9.2 %collective-permute-start.10 = (bf16[16,128,128]{2,1,0:T(8,128)(2,1)S(1)}, bf16[16,128,128]{2,1,0:T(8,128)(2,1)S(1)}, u32[]{:S(2)}, u32[]{:S(2)}) collective-permute-start(bf16[16,128,128]{2,1,0:T(8,128)(2,1)S(1)} %collective-permute-done.8.refs_3_), channel_id=1, source_target_pairs={{0,8},{4,60},{8,16},{12,4},{16,24},{20,12},{24,32},{28,20},{32,40}... | collective-permute-start | bytes 1572872 | tf_op jit(solution)/shard_map/ppermute | solution.py:249
  40.9 8.8 %collective-permute-start.7 = (bf16[16,128,128]{2,1,0:T(8,128)(2,1)S(1)}, bf16[16,128,128]{2,1,0:T(8,128)(2,1)S(1)}, u32[]{:S(2)}, u32[]{:S(2)}) collective-permute-start(bf16[16,128,128]{2,1,0:T(8,128)(2,1)S(1)} %collective-permute-done.6.refs_1_.refs_0_), channel_id=1, source_target_pairs={{0,4},{4,0},{8,12},{12,8},{16,20},{20,16},{24,28},{28,24},{32,36},... | collective-permute-start | bytes 1572872 | tf_op jit(solution)/shard_map/ppermute | solution.py:249
  42.8 12.5 %collective-permute-start.16 = (bf16[16,128,128]{2,1,0:T(8,128)(2,1)S(1)}, bf16[16,128,128]{2,1,0:T(8,128)(2,1)S(1)}, u32[]{:S(2)}, u32[]{:S(2)}) collective-permute-start(bf16[16,128,128]{2,1,0:T(8,128)(2,1)S(1)} %collective-permute-done.14.refs_1_), channel_id=1, source_target_pairs={{0,8},{4,60},{8,16},{12,4},{16,24},{20,12},{24,32},{28,20},{32,40}... | collective-permute-start | bytes 1572872 | tf_op jit(solution)/shard_map/ppermute | solution.py:249
  49.6 16.2 %collective-permute-start.9 = (bf16[16,128,128]{2,1,0:T(8,128)(2,1)S(1)}, bf16[16,128,128]{2,1,0:T(8,128)(2,1)S(1)}, u32[]{:S(2)}, u32[]{:S(2)}) collective-permute-start(bf16[16,128,128]{2,1,0:T(8,128)(2,1)S(1)} %collective-permute-done.8.refs_3_), channel_id=1, source_target_pairs={{0,4},{4,0},{8,12},{12,8},{16,20},{20,16},{24,28},{28,24},{32,36},... | collective-permute-start | bytes 1572872 | tf_op jit(solution)/shard_map/ppermute | solution.py:249
  49.7 12.7 %collective-permute-start.12 = (bf16[8,128,128]{2,1,0:T(8,128)(2,1)S(1)}, bf16[8,128,128]{2,1,0:T(8,128)(2,1)S(1)}, u32[]{:S(2)}, u32[]{:S(2)}) collective-permute-start(bf16[8,128,128]{2,1,0:T(8,128)(2,1)S(1)} %half.1), channel_id=1, source_target_pairs={{0,8},{4,60},{8,16},{12,4},{16,24},{20,12},{24,32},{28,20},{32,40}... | collective-permute-start | bytes 786440 | tf_op jit(solution)/shard_map/ppermute | solution.py:249
  55.2 11.1 %collective-permute-start.18 = (bf16[16,128,128]{2,1,0:T(8,128)(2,1)S(1)}, bf16[16,128,128]{2,1,0:T(8,128)(2,1)S(1)}, u32[]{:S(2)}, u32[]{:S(2)}) collective-permute-start(bf16[16,128,128]{2,1,0:T(8,128)(2,1)S(1)} %collective-permute-done.16.refs_3_), channel_id=1, source_target_pairs={{0,8},{4,60},{8,16},{12,4},{16,24},{20,12},{24,32},{28,20},{32,40}... | collective-permute-start | bytes 1572872 | tf_op jit(solution)/shard_map/ppermute | solution.py:249
  62.4 6.0 %collective-permute-start.11 = (bf16[16,128,128]{2,1,0:T(8,128)(2,1)S(1)}, bf16[16,128,128]{2,1,0:T(8,128)(2,1)S(1)}, u32[]{:S(2)}, u32[]{:S(2)}) collective-permute-start(bf16[16,128,128]{2,1,0:T(8,128)(2,1)S(1)} %collective-permute-done.10.source_ref.refs_5_), channel_id=1, source_target_pairs={{0,4},{4,0},{8,12},{12,8},{16,20},{20,16},{24,28},{28,24},{32,36},... | collective-permute-start | bytes 1572872 | tf_op jit(solution)/shard_map/ppermute | solution.py:249
  62.4 3.5 %collective-permute-start.13 = (bf16[8,128,128]{2,1,0:T(8,128)(2,1)S(1)}, bf16[8,128,128]{2,1,0:T(8,128)(2,1)S(1)}, u32[]{:S(2)}, u32[]{:S(2)}) collective-permute-start(bf16[8,128,128]{2,1,0:T(8,128)(2,1)S(1)} %collective-permute-done.12.refs_7_), channel_id=1, source_target_pairs={{0,4},{4,0},{8,12},{12,8},{16,20},{20,16},{24,28},{28,24},{32,36},... | collective-permute-start | bytes 786440 | tf_op jit(solution)/shard_map/ppermute | solution.py:249
  65.8 43.8 %collective-permute-start.26 = (bf16[512,1024]{1,0:T(8,128)(2,1)}, bf16[512,1024]{1,0:T(8,128)(2,1)S(1)}, u32[]{:S(2)}, u32[]{:S(2)}) collective-permute-start(bf16[512,1024]{1,0:T(8,128)(2,1)} %get-tuple-element.37), channel_id=1, source_target_pairs={{2,0},{3,1},{0,2},{1,3},{6,4},{7,5},{4,6},{5,7},{10,8},{11,9},{8,1... | collective-permute-start | bytes 3145736 | tf_op jit(solution)/shard_map/ppermute | solution.py:223
  65.8 13.4 %collective-permute-start.15 = (bf16[16,128,128]{2,1,0:T(8,128)(2,1)S(1)}, bf16[16,128,128]{2,1,0:T(8,128)(2,1)S(1)}, u32[]{:S(2)}, u32[]{:S(2)}) collective-permute-start(bf16[16,128,128]{2,1,0:T(8,128)(2,1)S(1)} %collective-permute-done.14.refs_1_), channel_id=1, source_target_pairs={{0,4},{4,0},{8,12},{12,8},{16,20},{20,16},{24,28},{28,24},{32,36},... | collective-permute-start | bytes 1572872 | tf_op jit(solution)/shard_map/ppermute | solution.py:249
  65.9 13.3 %collective-permute-start.17 = (bf16[16,128,128]{2,1,0:T(8,128)(2,1)S(1)}, bf16[16,128,128]{2,1,0:T(8,128)(2,1)S(1)}, u32[]{:S(2)}, u32[]{:S(2)}) collective-permute-start(bf16[16,128,128]{2,1,0:T(8,128)(2,1)S(1)} %collective-permute-done.16.refs_3_), channel_id=1, source_target_pairs={{0,4},{4,0},{8,12},{12,8},{16,20},{20,16},{24,28},{28,24},{32,36},... | collective-permute-start | bytes 1572872 | tf_op jit(solution)/shard_map/ppermute | solution.py:249
  66.4 12.8 %collective-permute-start.20 = (bf16[16,128,128]{2,1,0:T(8,128)(2,1)S(1)}, bf16[16,128,128]{2,1,0:T(8,128)(2,1)S(1)}, u32[]{:S(2)}, u32[]{:S(2)}) collective-permute-start(bf16[16,128,128]{2,1,0:T(8,128)(2,1)S(1)} %collective-permute-done.18.refs_5_), channel_id=1, source_target_pairs={{0,8},{4,60},{8,16},{12,4},{16,24},{20,12},{24,32},{28,20},{32,40}... | collective-permute-start | bytes 1572872 | tf_op jit(solution)/shard_map/ppermute | solution.py:249
  68.4 10.8 %collective-permute-start.19 = (bf16[16,128,128]{2,1,0:T(8,128)(2,1)S(1)}, bf16[16,128,128]{2,1,0:T(8,128)(2,1)S(1)}, u32[]{:S(2)}, u32[]{:S(2)}) collective-permute-start(bf16[16,128,128]{2,1,0:T(8,128)(2,1)S(1)} %collective-permute-done.18.refs_5_), channel_id=1, source_target_pairs={{0,4},{4,0},{8,12},{12,8},{16,20},{20,16},{24,28},{28,24},{32,36},... | collective-permute-start | bytes 1572872 | tf_op jit(solution)/shard_map/ppermute | solution.py:249
  88.3 22.5 %collective-permute-start.29 = (bf16[256,512]{1,0:T(8,128)(2,1)S(1)}, bf16[256,512]{1,0:T(8,128)(2,1)S(1)}, u32[]{:S(2)}, u32[]{:S(2)}) collective-permute-start(bf16[256,512]{1,0:T(8,128)(2,1)S(1)} %get-tuple-element.38.a0), channel_id=1, source_target_pairs={{3,0},{0,1},{1,2},{2,3},{7,4},{4,5},{5,6},{6,7},{11,8},{8,9},{9,10... | collective-permute-start | bytes 786440 | tf_op jit(solution)/shard_map/ppermute | solution.py:223
  89.6 23.1 %collective-permute-start.28 = (bf16[256,512]{1,0:T(8,128)(2,1)S(1)}, bf16[256,512]{1,0:T(8,128)(2,1)S(1)}, u32[]{:S(2)}, u32[]{:S(2)}) collective-permute-start(bf16[256,512]{1,0:T(8,128)(2,1)S(1)} %get-tuple-element.38.a0), channel_id=1, source_target_pairs={{2,0},{3,1},{0,2},{1,3},{6,4},{7,5},{4,6},{5,7},{10,8},{11,9},{8,1... | collective-permute-start | bytes 786440 | tf_op jit(solution)/shard_map/ppermute | solution.py:223
  92.5 20.2 %collective-permute-start.27 = (bf16[256,512]{1,0:T(8,128)(2,1)S(1)}, bf16[256,512]{1,0:T(8,128)(2,1)S(1)}, u32[]{:S(2)}, u32[]{:S(2)}) collective-permute-start(bf16[256,512]{1,0:T(8,128)(2,1)S(1)} %get-tuple-element.38.a0), channel_id=1, source_target_pairs={{1,0},{2,1},{3,2},{0,3},{5,4},{6,5},{7,6},{4,7},{9,8},{10,9},{11,1... | collective-permute-start | bytes 786440 | tf_op jit(solution)/shard_map/ppermute | solution.py:223
  109.3 14.8 %collective-permute-start.25 = (bf16[256,512]{1,0:T(8,128)(2,1)S(1)}, bf16[256,512]{1,0:T(8,128)(2,1)S(1)}, u32[]{:S(2)}, u32[]{:S(2)}) collective-permute-start(bf16[256,512]{1,0:T(8,128)(2,1)S(1)} %attend1.1.a0), channel_id=1, source_target_pairs={{3,0},{0,1},{1,2},{2,3},{7,4},{4,5},{5,6},{6,7},{11,8},{8,9},{9,10... | collective-permute-start | bytes 786440 | tf_op jit(solution)/shard_map/ppermute | solution.py:223
  109.5 14.6 %collective-permute-start.24 = (bf16[256,512]{1,0:T(8,128)(2,1)S(1)}, bf16[256,512]{1,0:T(8,128)(2,1)S(1)}, u32[]{:S(2)}, u32[]{:S(2)}) collective-permute-start(bf16[256,512]{1,0:T(8,128)(2,1)S(1)} %attend1.1.a0), channel_id=1, source_target_pairs={{2,0},{3,1},{0,2},{1,3},{6,4},{7,5},{4,6},{5,7},{10,8},{11,9},{8,1... | collective-permute-start | bytes 786440 | tf_op jit(solution)/shard_map/ppermute | solution.py:223
  110.9 13.8 %collective-permute-start.23 = (bf16[256,512]{1,0:T(8,128)(2,1)S(1)}, bf16[256,512]{1,0:T(8,128)(2,1)S(1)}, u32[]{:S(2)}, u32[]{:S(2)}) collective-permute-start(bf16[256,512]{1,0:T(8,128)(2,1)S(1)} %attend1.1.a0), channel_id=1, source_target_pairs={{1,0},{2,1},{3,2},{0,3},{5,4},{6,5},{7,6},{4,7},{9,8},{10,9},{11,1... | collective-permute-start | bytes 786440 | tf_op jit(solution)/shard_map/ppermute | solution.py:223
  (17 other events, 168.4 us)

commit v7 on v6

--- a/solution.py
+++ b/solution.py
@@ -240,7 +240,7 @@
     out_ref[...] = source_ref[...]
 
 
-def gather_columns(nx, nz, payload, later):
+def gather_columns(nx, nz, payload):
     place = lambda x, z, c: ((x % nx) * nz + z % nz) * 2 + c
     every = [(x, z, c) for x in range(nx) for z in range(nz) for c in range(2)]
     route = lambda f: [(place(*d), place(*f(*d))) for d in every]
@@ -285,7 +285,7 @@
             moving = send(moving, along)
             held += [moving] + ([] if which == 1 and last else [send(moving, across)])
             if n == 1:
-                waited = [moving, *later]
+                waited = [moving]
         pieces.append(held)
     return pieces
 
@@ -307,9 +307,9 @@
     return (((x + line) % nx * nz + (z + nz + side) % nz) * 2 + core) * CAP + at % CAP
 
 
-def slab_kernel(tp, index_ref, weight_ref, *refs):
+def slab_kernel(tp, shifts, index_ref, weight_ref, *refs):
     width = weight_ref.shape[1] // tp
-    for shift, ref in enumerate(refs[1:]):
+    for shift, ref in zip(shifts, refs[-len(shifts):]):
         target = lax.rem(index_ref[0] + tp - shift, tp)
         ref[...] = weight_ref[:, pl.ds(pl.multiple_of(target * width, width), width)]
 
@@ -361,20 +361,23 @@
         name="band",
     )(meta, slash_offsets, q, k, before, after)
 
-    k_pieces, v_pieces = gather_columns(*sides, payload, [mask])
+    k_pieces, v_pieces = gather_columns(*sides, payload)
 
     width = out_weight.shape[1] // tp
     depth = out_weight.shape[0]
-    slabs = pl.pallas_call(
-        functools.partial(slab_kernel, tp),
-        grid=(depth // 128,),
-        out_shape=[shape((depth, width), BF16)] * tp,
-        in_specs=[SMEM(), pl.BlockSpec((128, out_weight.shape[1]), lambda i: (i, 0)), ANY()],
-        out_specs=[pl.BlockSpec((128, width), lambda i: (i, 0))] * tp,
-        compiler_params=PARAMS,
-        cost_estimate=cost(3),
-        name="slabs",
-    )(tp_index.reshape(1).astype(i32), out_weight, v_pieces[0])
+    slabs = {}
+    for shifts, earlier in (((0, 1, 3), v_pieces[0]), ((2,), mask)):
+        cut = pl.pallas_call(
+            functools.partial(slab_kernel, tp, shifts),
+            grid=(depth // 128,),
+            out_shape=[shape((depth, width), BF16)] * len(shifts),
+            in_specs=[SMEM(), pl.BlockSpec((128, out_weight.shape[1]), lambda i: (i, 0)), ANY()],
+            out_specs=[pl.BlockSpec((128, width), lambda i: (i, 0))] * len(shifts),
+            compiler_params=PARAMS,
+            cost_estimate=cost(len(shifts)),
+            name=f"slabs{shifts[0]}",
+        )(tp_index.reshape(1).astype(i32), out_weight, earlier)
+        slabs.update(zip(shifts, cut))
     slabs = [slabs[0]] + [from_ahead(slabs[shift], "tp", shift) for shift in range(1, tp)]
 
     columns, top = pl.pallas_call(

time: 130 us -> 138 us (1.062)
  Pallas kernels: 45.9 us -> 52 us
  starting transfers between devices: 43.1 us -> 39.6 us
  local copies, waits for them, and re-layouts: 5.47 us -> 8.48 us
  waiting for transfers between devices: 33.2 us -> 36 us
    ppermute x9, waiting for transfers between devices: 16.4 us -> 8.25 us  [from_ahead(): return lax.ppermute(x, axis, [((i + shift) % n, i) for i in range(n)])]
    ppermute x1, waiting for transfers between devices: 0.01 us -> 5.83 us  [per_device(): before = lax.ppermute(ahead, 'ctx', [(i, i + 1) for i in steps])]
    pallas_call x1 -> x2, Pallas kernels: 4.88 us -> 8.22 us  [per_device(): pl.pallas_call(functools.partial(slab_kernel, tp, shifts), grid=(depth //...]
    ppermute x19, waiting for transfers between devices: 16.8 us -> 19.7 us  [gather_columns(): send = lambda a, r: lax.ppermute(a, 'ctx', r)]
    ppermute x19, starting transfers between devices: 25 us -> 22.2 us  [gather_columns(): send = lambda a, r: lax.ppermute(a, 'ctx', r)]
    ppermute x1, waiting for transfers between devices: 0.01 us -> 2.26 us  [per_device(): after = lax.ppermute(back, 'ctx', [(i + 1, i) for i in steps])]
    unnamed x38 -> x56, local copies, waits for them, and re-layouts: 5.37 us -> 7.52 us
    ppermute x1, starting transfers between devices: 3.64 us -> 1.91 us  [per_device(): after = lax.ppermute(back, 'ctx', [(i + 1, i) for i in steps])]
  transfers between devices with their start and end apart: 30 -> 30, of which waited for: 11 -> 11; matrix products, arithmetic and copies ran while one was open for 0% -> 1% of each run, Pallas kernels for 33% -> 35%
where the time goes in v7:
time: 138 us; the launch traced here: 136 us
  Pallas kernels  52 us (38%)
  starting transfers between devices  39.6 us (29%)
  waiting for transfers between devices  36 us (26%)
  local copies, waits for them, and re-layouts  8.48 us (6%)
    pallas_call x2, Pallas kernels, per_device(): pl.pallas_call(functools.partial(out_kernel, ctx_count, st, len(v_pieces)...  22.5 us
    ppermute x19, starting transfers between devices, gather_columns(): send = lambda a, r: lax.ppermute(a, 'ctx', r)  22.2 us
    ppermute x19, waiting for transfers between devices, gather_columns(): send = lambda a, r: lax.ppermute(a, 'ctx', r)  19.7 us
    ppermute x9, starting transfers between devices, from_ahead(): return lax.ppermute(x, axis, [((i + shift) % n, i) for i in range(n)])  13.6 us
    pallas_call x1, Pallas kernels, per_device(): pl.pallas_call(top_kernel, out_shape=[shape((ROOM, BLOCK, HEAD), BF16), s...  10.7 us
    ppermute x9, waiting for transfers between devices, from_ahead(): return lax.ppermute(x, axis, [((i + shift) % n, i) for i in range(n)])  8.25 us
    pallas_call x2, Pallas kernels, per_device(): pl.pallas_call(functools.partial(slab_kernel, tp, shifts), grid=(depth //...  8.22 us
    unnamed x56, local copies, waits for them, and re-layouts  7.52 us
  transfers between devices with their start and end apart: 30, of which 11 were waited for; matrix products, arithmetic and copies ran while one was open for 1% of the time, Pallas kernels for 35%

profile of v7, /device:TPU:96, one launch (start us, length us, event | category | flops | bytes accessed | tf_op | source)
XLA Modules:
  0.0 136.5 jit_solution(8799102722452558783)
XLA Ops:
  3.7 2.8 %collective-permute-start.2 = (bf16[2,2,128,128]{3,2,1,0:T(8,128)(2,1)S(1)}, bf16[2,2,128,128]{3,2,1,0:T(8,128)(2,1)S(1)}, u32[]{:S(2)}, u32[]{:S(2)}) collective-permute-start(bf16[2,2,128,128]{3,2,1,0:T(8,128)(2,1)S(1)} %get-tuple-element.28.refs_0_), channel_id=1, source_target_pairs={{0,192},{4,196},{8,200},{12,204},{16,208},{20,212},{24,216},{28,22... | collective-permute-start | bytes 393224 | tf_op jit(solution)/shard_map/ppermute | solution.py:249
  8.1 3.9 %collective-permute-done.2.refs_1_ = bf16[2,2,128,128]{3,2,1,0:T(8,128)(2,1)S(1)} collective-permute-done((bf16[2,2,128,128]{3,2,1,0:T(8,128)(2,1)S(1)}, bf16[2,2,128,128]{3,2,1,0:T(8,128)(2,1)S(1)}, u32[]{:S(2)}, u32[]{:S(2)}) %collective-permute-start.2) | collective-permute-done | bytes 131104 | tf_op jit(solution)/shard_map/ppermute | solution.py:249
  12.0 2.3 %collective-permute-done.3.refs_2_ = bf16[2,2,128,128]{3,2,1,0:T(8,128)(2,1)S(1)} collective-permute-done((bf16[2,2,128,128]{3,2,1,0:T(8,128)(2,1)S(1)}, bf16[2,2,128,128]{3,2,1,0:T(8,128)(2,1)S(1)}, u32[]{:S(2)}, u32[]{:S(2)}) %collective-permute-start.3) | collective-permute-done | bytes 131104 | tf_op jit(solution)/shard_map/ppermute | solution.py:249
  14.3 1.4 %collective-permute-done.4.refs_3_ = bf16[2,2,128,128]{3,2,1,0:T(8,128)(2,1)S(1)} collective-permute-done((bf16[2,2,128,128]{3,2,1,0:T(8,128)(2,1)S(1)}, bf16[2,2,128,128]{3,2,1,0:T(8,128)(2,1)S(1)}, u32[]{:S(2)}, u32[]{:S(2)}) %collective-permute-start.4) | collective-permute-done | bytes 131104 | tf_op jit(solution)/shard_map/ppermute | solution.py:249
  15.8 1.9 %collective-permute-done.5.other_ref = bf16[2,8,128,128]{3,2,1,0:T(8,128)(2,1)S(1)} collective-permute-done((bf16[2,8,128,128]{3,2,1,0:T(8,128)(2,1)S(1)}, bf16[2,8,128,128]{3,2,1,0:T(8,128)(2,1)S(1)}, u32[]{:S(2)}, u32[]{:S(2)}) %collective-permute-start.5) | collective-permute-done | bytes 524320 | tf_op jit(solution)/shard_map/ppermute | solution.py:249
  17.8 3.2 %collective-permute-start.6 = (bf16[16,128,128]{2,1,0:T(8,128)(2,1)S(1)}, bf16[16,128,128]{2,1,0:T(8,128)(2,1)}, u32[]{:S(2)}, u32[]{:S(2)}) collective-permute-start(bf16[16,128,128]{2,1,0:T(8,128)(2,1)S(1)} %chip0.1.refs_0_), channel_id=1, source_target_pairs={{0,8},{4,60},{8,16},{12,4},{16,24},{20,12},{24,32},{28,20},{32,40}... | collective-permute-start | bytes 1572872 | tf_op jit(solution)/shard_map/ppermute | solution.py:249
  21.8 5.9 %collective-permute-done.6.refs_1_.refs_0_ = bf16[16,128,128]{2,1,0:T(8,128)(2,1)} collective-permute-done((bf16[16,128,128]{2,1,0:T(8,128)(2,1)S(1)}, bf16[16,128,128]{2,1,0:T(8,128)(2,1)}, u32[]{:S(2)}, u32[]{:S(2)}) %collective-permute-start.6) | collective-permute-done | bytes 524320 | tf_op jit(solution)/shard_map/ppermute | solution.py:249
  27.7 3.8 %collective-permute-start.8 = (bf16[16,128,128]{2,1,0:T(8,128)(2,1)}, bf16[16,128,128]{2,1,0:T(8,128)(2,1)}, u32[]{:S(2)}, u32[]{:S(2)}) collective-permute-start(bf16[16,128,128]{2,1,0:T(8,128)(2,1)} %collective-permute-done.6.refs_1_.refs_0_), channel_id=1, source_target_pairs={{0,8},{4,60},{8,16},{12,4},{16,24},{20,12},{24,32},{28,20},{32,40}... | collective-permute-start | bytes 1572872 | tf_op jit(solution)/shard_map/ppermute | solution.py:249
  31.7 4.1 %slabs0.1 = (bf16[512,1024]{1,0:T(8,128)(2,1)S(1)}, bf16[512,1024]{1,0:T(8,128)(2,1)S(1)}, bf16[512,1024]{1,0:T(8,128)(2,1)}) custom-call(s32[1]{0:T(128)} %bitcast.7.index_ref, bf16[512,4096]{1,0:T(8,128)(2,1)} %weight_ref.3, bf16[16,128,128]{2,1,0:T(8,128)(2,1)S(1)} %chip1.1.refs_0_), custom_call_target="tpu_custom_call" | custom-call | bytes 9000000 | tf_op jit(solution)/shard_map/slabs0/pallas_call | solution.py:370
  36.8 3.0 %collective-permute-start.21 = (bf16[512,1024]{1,0:T(8,128)(2,1)S(1)}, bf16[512,1024]{1,0:T(8,128)(2,1)S(1)}, u32[]{:S(2)}, u32[]{:S(2)}) collective-permute-start(bf16[512,1024]{1,0:T(8,128)(2,1)S(1)} %get-tuple-element.32), channel_id=1, source_target_pairs={{1,0},{2,1},{3,2},{0,3},{5,4},{6,5},{7,6},{4,7},{9,8},{10,9},{11,1... | collective-permute-start | bytes 3145736 | tf_op jit(solution)/shard_map/ppermute | solution.py:223
  39.8 2.4 %collective-permute-start.10 = (bf16[16,128,128]{2,1,0:T(8,128)(2,1)}, bf16[16,128,128]{2,1,0:T(8,128)(2,1)}, u32[]{:S(2)}, u32[]{:S(2)}) collective-permute-start(bf16[16,128,128]{2,1,0:T(8,128)(2,1)} %collective-permute-done.8.refs_3_), channel_id=1, source_target_pairs={{0,8},{4,60},{8,16},{12,4},{16,24},{20,12},{24,32},{28,20},{32,40}... | collective-permute-start | bytes 1572872 | tf_op jit(solution)/shard_map/ppermute | solution.py:249
  42.2 1.9 %collective-permute-start = (bf16[2,256,128]{2,1,0:T(8,128)(2,1)S(1)}, bf16[2,256,128]{2,1,0:T(8,128)(2,1)S(1)}, u32[]{:S(2)}, u32[]{:S(2)}) collective-permute-start(bf16[2,256,128]{2,1,0:T(8,128)(2,1)S(1)} %get-tuple-element.25), channel_id=1, source_target_pairs={{0,4},{4,8},{8,12},{12,16},{16,20},{20,24},{24,28},{28,32},{32,36}... | collective-permute-start | bytes 393224 | tf_op jit(solution)/shard_map/ppermute | solution.py:351
  44.1 5.8 %collective-permute-done.ahead_ref = bf16[2,256,128]{2,1,0:T(8,128)(2,1)S(1)} collective-permute-done((bf16[2,256,128]{2,1,0:T(8,128)(2,1)S(1)}, bf16[2,256,128]{2,1,0:T(8,128)(2,1)S(1)}, u32[]{:S(2)}, u32[]{:S(2)}) %collective-permute-start) | collective-permute-done | bytes 131104 | tf_op jit(solution)/shard_map/ppermute | solution.py:351
  49.9 1.3 collective-permute-start.16
  51.2 1.9 %collective-permute-start.1 = (bf16[2,256,128]{2,1,0:T(8,128)(2,1)S(1)}, bf16[2,256,128]{2,1,0:T(8,128)(2,1)S(1)}, u32[]{:S(2)}, u32[]{:S(2)}) collective-permute-start(bf16[2,256,128]{2,1,0:T(8,128)(2,1)S(1)} %copy-done.27), channel_id=1, source_target_pairs={{4,0},{8,4},{12,8},{16,12},{20,16},{24,20},{28,24},{32,28},{36,32}... | collective-permute-start | bytes 393224 | tf_op jit(solution)/shard_map/ppermute | solution.py:352
  53.1 1.7 %half.1 = bf16[8,128,128]{2,1,0:T(8,128)(2,1)} custom-call(bf16[16,128,128]{2,1,0:T(8,128)(2,1)} %collective-permute-done.10.source_ref.refs_5_), custom_call_target="tpu_custom_call" | custom-call | tf_op jit(solution)/shard_map/half/pallas_call | solution.py:277
  54.8 2.3 %collective-permute-done.1.back_ref = bf16[2,256,128]{2,1,0:T(8,128)(2,1)S(1)} collective-permute-done((bf16[2,256,128]{2,1,0:T(8,128)(2,1)S(1)}, bf16[2,256,128]{2,1,0:T(8,128)(2,1)S(1)}, u32[]{:S(2)}, u32[]{:S(2)}) %collective-permute-start.1) | collective-permute-done | bytes 131104 | tf_op jit(solution)/shard_map/ppermute | solution.py:352
  57.1 4.2 %collective-permute-start.9 = (bf16[16,128,128]{2,1,0:T(8,128)(2,1)}, bf16[16,128,128]{2,1,0:T(8,128)(2,1)}, u32[]{:S(2)}, u32[]{:S(2)}) collective-permute-start(bf16[16,128,128]{2,1,0:T(8,128)(2,1)} %collective-permute-done.8.refs_3_), channel_id=1, source_target_pairs={{0,4},{4,0},{8,12},{12,8},{16,20},{20,16},{24,28},{28,24},{32,36},... | collective-permute-start | bytes 1572872 | tf_op jit(solution)/shard_map/ppermute | solution.py:249
  64.4 4.3 %collective-permute-done.12.refs_7_ = bf16[8,128,128]{2,1,0:T(8,128)(2,1)} collective-permute-done((bf16[8,128,128]{2,1,0:T(8,128)(2,1)}, bf16[8,128,128]{2,1,0:T(8,128)(2,1)}, u32[]{:S(2)}, u32[]{:S(2)}) %collective-permute-start.12) | collective-permute-done | bytes 262176 | tf_op jit(solution)/shard_map/ppermute | solution.py:249
  68.8 1.9 %band.1 = (f32[4,256,512]{2,1,0:T(8,128)S(1)}, f32[2,4,256,128]{3,2,1,0:T(8,128)S(1)}) custom-call(s32[1,16]{1,0:T(1,128)S(1)} %get-tuple-element.21.meta_ref, s32[4,64]{1,0:T(4,128)S(1)} %copy-done.25, bf16[2,256,512]{2,1,0:T(8,128)(2,1)S(1)} %bitcast.9, bf16[2,256,128]{2,1,0:T(8,128)(2,1)S(1)} %bitcast.14, ...), custom_call_target="tpu_custom_call" | custom-call | bytes 9000000 | tf_op jit(solution)/shard_map/band/pallas_call | solution.py:354
  70.7 4.1 %slabs2.1 = bf16[512,1024]{1,0:T(8,128)(2,1)S(1)} custom-call(s32[1]{0:T(128)} %bitcast.7.index_ref, bf16[512,4096]{1,0:T(8,128)(2,1)} %weight_ref.3, f32[4,256,512]{2,1,0:T(8,128)S(1)} %get-tuple-element.31.mask_ref.refs_0_), custom_call_target="tpu_custom_call" | custom-call | bytes 3000000 | tf_op jit(solution)/shard_map/slabs2/pallas_call | solution.py:370
  74.9 2.9 %collective-permute-start.26 = (bf16[512,1024]{1,0:T(8,128)(2,1)S(1)}, bf16[512,1024]{1,0:T(8,128)(2,1)S(1)}, u32[]{:S(2)}, u32[]{:S(2)}) collective-permute-start(bf16[512,1024]{1,0:T(8,128)(2,1)S(1)} %slabs2.1), channel_id=1, source_target_pairs={{2,0},{3,1},{0,2},{1,3},{6,4},{7,5},{4,6},{5,7},{10,8},{11,9},{8,1... | collective-permute-start | bytes 3145736 | tf_op jit(solution)/shard_map/ppermute | solution.py:223
  78.5 1.7 %collective-permute-start.20 = (bf16[16,128,128]{2,1,0:T(8,128)(2,1)}, bf16[16,128,128]{2,1,0:T(8,128)(2,1)S(1)}, u32[]{:S(2)}, u32[]{:S(2)}) collective-permute-start(bf16[16,128,128]{2,1,0:T(8,128)(2,1)} %collective-permute-done.18.refs_5_), channel_id=1, source_target_pairs={{0,8},{4,60},{8,16},{12,4},{16,24},{20,12},{24,32},{28,20},{32,40}... | collective-permute-start | bytes 1572872 | tf_op jit(solution)/shard_map/ppermute | solution.py:249
  80.2 10.7 %top.1 = (bf16[65,128,128]{2,1,0:T(8,128)(2,1)}, f32[2,4,256,128]{3,2,1,0:T(8,128)S(1)}) custom-call(s32[1,16]{1,0:T(1,128)S(1)} %get-tuple-element.21.meta_ref, s32[1,64]{1,0:T(1,128)S(1)} %get-tuple-element.22.blk_ref, s32[1,128]{1,0:T(1,128)S(1)} %get-tuple-element.24.at_ref, bf16[2,256,512]{2,1,0:T(8,128)(2,1)S(1)} %bitcast.10, ...), custom_call_target="tpu_custom_call" | custom-call | bytes 27000000 | tf_op jit(solution)/shard_map/top/pallas_call | solution.py:383
  91.8 7.6 %attend0.1 = (bf16[256,512]{1,0:T(8,128)(2,1)S(1)}, bf16[65,128,128]{2,1,0:T(8,128)(2,1)}) custom-call(s32[1,16]{1,0:T(1,128)S(1)} %get-tuple-element.21.meta_ref, s32[1,64]{1,0:T(1,128)S(1)} %get-tuple-element.22.blk_ref, s32[1,128]{1,0:T(1,128)S(1)} %get-tuple-element.23.at_ref, bf16[2,256,512]{2,1,0:T(8,128)(2,1)S(1)} %bitcast.11, ...), custom_call_target="tpu_custom_call" | custom-call | bytes 24000000 | tf_op jit(solution)/shard_map/attend0/pallas_call | solution.py:397
  100.5 1.8 %collective-permute-start.28 = (bf16[256,512]{1,0:T(8,128)(2,1)S(1)}, bf16[256,512]{1,0:T(8,128)(2,1)S(1)}, u32[]{:S(2)}, u32[]{:S(2)}) collective-permute-start(bf16[256,512]{1,0:T(8,128)(2,1)S(1)} %get-tuple-element.36.a0), channel_id=1, source_target_pairs={{2,0},{3,1},{0,2},{1,3},{6,4},{7,5},{4,6},{5,7},{10,8},{11,9},{8,1... | collective-permute-start | bytes 786440 | tf_op jit(solution)/shard_map/ppermute | solution.py:223
  102.4 14.9 %attend1.1.a0 = bf16[256,512]{1,0:T(8,128)(2,1)S(1)} custom-call(s32[1,16]{1,0:T(1,128)S(1)} %get-tuple-element.21.meta_ref, s32[1,64]{1,0:T(1,128)S(1)} %get-tuple-element.22.blk_ref, s32[1,128]{1,0:T(1,128)S(1)} %get-tuple-element.23.at_ref, bf16[2,256,512]{2,1,0:T(8,128)(2,1)S(1)} %bitcast.12, bf16[65,128,128]{2,1,0:T(8,128)(2,1)} %get-tuple-element.29.keys_ref, ...), custom_call_target="tpu_custom_call" | custom-call | bytes 24000000 | tf_op jit(solution)/shard_map/attend1/pallas_call | solution.py:397
  117.3 3.3 %collective-permute-start.23 = (bf16[256,512]{1,0:T(8,128)(2,1)S(1)}, bf16[256,512]{1,0:T(8,128)(2,1)S(1)}, u32[]{:S(2)}, u32[]{:S(2)}) collective-permute-start(bf16[256,512]{1,0:T(8,128)(2,1)S(1)} %attend1.1.a0), channel_id=1, source_target_pairs={{1,0},{2,1},{3,2},{0,3},{5,4},{6,5},{7,6},{4,7},{9,8},{10,9},{11,1... | collective-permute-start | bytes 786440 | tf_op jit(solution)/shard_map/ppermute | solution.py:223
  122.1 3.1 %mix0.1.refs_0_ = bf16[2,256,1024]{2,1,0:T(8,128)(2,1)} custom-call(bf16[256,512]{1,0:T(8,128)(2,1)S(1)} %get-tuple-element.36.a0, bf16[256,512]{1,0:T(8,128)(2,1)S(1)} %collective-permute-done.27.a1, bf16[256,512]{1,0:T(8,128)(2,1)S(1)} %collective-permute-done.28.a2, bf16[256,512]{1,0:T(8,128)(2,1)S(1)} %collective-permute-done.29.a3, ...), custom_call_target="tpu_custom_call" | custom-call | bytes 9000000 | tf_op jit(solution)/shard_map/mix0/pallas_call | solution.py:422
  125.2 4.5 %collective-permute-done.23.a1 = bf16[256,512]{1,0:T(8,128)(2,1)S(1)} collective-permute-done((bf16[256,512]{1,0:T(8,128)(2,1)S(1)}, bf16[256,512]{1,0:T(8,128)(2,1)S(1)}, u32[]{:S(2)}, u32[]{:S(2)}) %collective-permute-start.23) | collective-permute-done | bytes 262176 | tf_op jit(solution)/shard_map/ppermute | solution.py:223
  130.7 2.7 %collective-permute-done.25.a3 = bf16[256,512]{1,0:T(8,128)(2,1)S(1)} collective-permute-done((bf16[256,512]{1,0:T(8,128)(2,1)S(1)}, bf16[256,512]{1,0:T(8,128)(2,1)S(1)}, u32[]{:S(2)}, u32[]{:S(2)}) %collective-permute-start.25) | collective-permute-done | bytes 262176 | tf_op jit(solution)/shard_map/ppermute | solution.py:223
  133.4 3.1 %mix1.1 = bf16[2,256,1024]{2,1,0:T(8,128)(2,1)} custom-call(bf16[256,512]{1,0:T(8,128)(2,1)S(1)} %attend1.1.a0, bf16[256,512]{1,0:T(8,128)(2,1)S(1)} %collective-permute-done.23.a1, bf16[256,512]{1,0:T(8,128)(2,1)S(1)} %collective-permute-done.24.a2, bf16[256,512]{1,0:T(8,128)(2,1)S(1)} %collective-permute-done.25.a3, ...), custom_call_target="tpu_custom_call", output_to_operand_aliasing={{}: (8, {})} | custom-call | bytes 9000000 | tf_op jit(solution)/shard_map/mix1/pallas_call | solution.py:422
  (99 shorter events, 15.9 us)
Async XLA Ops:
  3.7 8.4 %collective-permute-start.2 = (bf16[2,2,128,128]{3,2,1,0:T(8,128)(2,1)S(1)}, bf16[2,2,128,128]{3,2,1,0:T(8,128)(2,1)S(1)}, u32[]{:S(2)}, u32[]{:S(2)}) collective-permute-start(bf16[2,2,128,128]{3,2,1,0:T(8,128)(2,1)S(1)} %get-tuple-element.28.refs_0_), channel_id=1, source_target_pairs={{0,192},{4,196},{8,200},{12,204},{16,208},{20,212},{24,216},{28,22... | collective-permute-start | bytes 393224 | tf_op jit(solution)/shard_map/ppermute | solution.py:249
  6.4 7.9 %collective-permute-start.3 = (bf16[2,2,128,128]{3,2,1,0:T(8,128)(2,1)S(1)}, bf16[2,2,128,128]{3,2,1,0:T(8,128)(2,1)S(1)}, u32[]{:S(2)}, u32[]{:S(2)}) collective-permute-start(bf16[2,2,128,128]{3,2,1,0:T(8,128)(2,1)S(1)} %get-tuple-element.28.refs_0_), channel_id=1, source_target_pairs={{0,128},{4,132},{8,136},{12,140},{16,144},{20,148},{24,152},{28,15... | collective-permute-start | bytes 393224 | tf_op jit(solution)/shard_map/ppermute | solution.py:249
  7.2 8.5 %collective-permute-start.4 = (bf16[2,2,128,128]{3,2,1,0:T(8,128)(2,1)S(1)}, bf16[2,2,128,128]{3,2,1,0:T(8,128)(2,1)S(1)}, u32[]{:S(2)}, u32[]{:S(2)}) collective-permute-start(bf16[2,2,128,128]{3,2,1,0:T(8,128)(2,1)S(1)} %get-tuple-element.28.refs_0_), channel_id=1, source_target_pairs={{0,64},{4,68},{8,72},{12,76},{16,80},{20,84},{24,88},{28,92},{32,9... | collective-permute-start | bytes 393224 | tf_op jit(solution)/shard_map/ppermute | solution.py:249
  15.7 2.0 %collective-permute-start.5 = (bf16[2,8,128,128]{3,2,1,0:T(8,128)(2,1)S(1)}, bf16[2,8,128,128]{3,2,1,0:T(8,128)(2,1)S(1)}, u32[]{:S(2)}, u32[]{:S(2)}) collective-permute-start(bf16[2,8,128,128]{3,2,1,0:T(8,128)(2,1)S(1)} %line.1.own_ref), channel_id=1, source_target_pairs={{0,4},{4,0},{8,12},{12,8},{16,20},{20,16},{24,28},{28,24},{32,36},... | collective-permute-start | bytes 1572872 | tf_op jit(solution)/shard_map/ppermute | solution.py:249
  17.8 9.9 %collective-permute-start.6 = (bf16[16,128,128]{2,1,0:T(8,128)(2,1)S(1)}, bf16[16,128,128]{2,1,0:T(8,128)(2,1)}, u32[]{:S(2)}, u32[]{:S(2)}) collective-permute-start(bf16[16,128,128]{2,1,0:T(8,128)(2,1)S(1)} %chip0.1.refs_0_), channel_id=1, source_target_pairs={{0,8},{4,60},{8,16},{12,4},{16,24},{20,12},{24,32},{28,20},{32,40}... | collective-permute-start | bytes 1572872 | tf_op jit(solution)/shard_map/ppermute | solution.py:249
  27.7 12.2 %collective-permute-start.8 = (bf16[16,128,128]{2,1,0:T(8,128)(2,1)}, bf16[16,128,128]{2,1,0:T(8,128)(2,1)}, u32[]{:S(2)}, u32[]{:S(2)}) collective-permute-start(bf16[16,128,128]{2,1,0:T(8,128)(2,1)} %collective-permute-done.6.refs_1_.refs_0_), channel_id=1, source_target_pairs={{0,8},{4,60},{8,16},{12,4},{16,24},{20,12},{24,32},{28,20},{32,40}... | collective-permute-start | bytes 1572872 | tf_op jit(solution)/shard_map/ppermute | solution.py:249
  31.5 18.4 %collective-permute-start.14 = (bf16[16,128,128]{2,1,0:T(8,128)(2,1)S(1)}, bf16[16,128,128]{2,1,0:T(8,128)(2,1)S(1)}, u32[]{:S(2)}, u32[]{:S(2)}) collective-permute-start(bf16[16,128,128]{2,1,0:T(8,128)(2,1)S(1)} %chip1.1.refs_0_), channel_id=1, source_target_pairs={{0,8},{4,60},{8,16},{12,4},{16,24},{20,12},{24,32},{28,20},{32,40}... | collective-permute-start | bytes 1572872 | tf_op jit(solution)/shard_map/ppermute | solution.py:249
  31.6 37.2 %copy-start.6 = (bf16[1,2,256,512]{3,2,1,0:T(8,128)(2,1)S(1)}, bf16[1,2,256,512]{3,2,1,0:T(8,128)(2,1)}, u32[]{:S(2)}) copy-start(bf16[1,2,256,512]{3,2,1,0:T(8,128)(2,1)} %param.6) | copy-start | bytes 1572868
  31.6 37.2 %copy-start.12 = (bf16[1,2,256,128]{3,2,1,0:T(8,128)(2,1)S(1)}, bf16[1,2,256,128]{3,2,1,0:T(8,128)(2,1)}, u32[]{:S(2)}) copy-start(bf16[1,2,256,128]{3,2,1,0:T(8,128)(2,1)} %param.7) | copy-start | bytes 393220
  36.8 25.5 %collective-permute-start.21 = (bf16[512,1024]{1,0:T(8,128)(2,1)S(1)}, bf16[512,1024]{1,0:T(8,128)(2,1)S(1)}, u32[]{:S(2)}, u32[]{:S(2)}) collective-permute-start(bf16[512,1024]{1,0:T(8,128)(2,1)S(1)} %get-tuple-element.32), channel_id=1, source_target_pairs={{1,0},{2,1},{3,2},{0,3},{5,4},{6,5},{7,6},{4,7},{9,8},{10,9},{11,1... | collective-permute-start | bytes 3145736 | tf_op jit(solution)/shard_map/ppermute | solution.py:223
  39.8 35.0 %collective-permute-start.22 = (bf16[512,1024]{1,0:T(8,128)(2,1)}, bf16[512,1024]{1,0:T(8,128)(2,1)S(1)}, u32[]{:S(2)}, u32[]{:S(2)}) collective-permute-start(bf16[512,1024]{1,0:T(8,128)(2,1)} %get-tuple-element.33), channel_id=1, source_target_pairs={{3,0},{0,1},{1,2},{2,3},{7,4},{4,5},{5,6},{6,7},{11,8},{8,9},{9,10... | collective-permute-start | bytes 3145736 | tf_op jit(solution)/shard_map/ppermute | solution.py:223
  39.8 11.4 %collective-permute-start.10 = (bf16[16,128,128]{2,1,0:T(8,128)(2,1)}, bf16[16,128,128]{2,1,0:T(8,128)(2,1)}, u32[]{:S(2)}, u32[]{:S(2)}) collective-permute-start(bf16[16,128,128]{2,1,0:T(8,128)(2,1)} %collective-permute-done.8.refs_3_), channel_id=1, source_target_pairs={{0,8},{4,60},{8,16},{12,4},{16,24},{20,12},{24,32},{28,20},{32,40}... | collective-permute-start | bytes 1572872 | tf_op jit(solution)/shard_map/ppermute | solution.py:249
  42.2 7.7 %collective-permute-start = (bf16[2,256,128]{2,1,0:T(8,128)(2,1)S(1)}, bf16[2,256,128]{2,1,0:T(8,128)(2,1)S(1)}, u32[]{:S(2)}, u32[]{:S(2)}) collective-permute-start(bf16[2,256,128]{2,1,0:T(8,128)(2,1)S(1)} %get-tuple-element.25), channel_id=1, source_target_pairs={{0,4},{4,8},{8,12},{12,16},{16,20},{20,24},{24,28},{28,32},{32,36}... | collective-permute-start | bytes 393224 | tf_op jit(solution)/shard_map/ppermute | solution.py:351
  49.9 11.3 %collective-permute-start.7 = (bf16[16,128,128]{2,1,0:T(8,128)(2,1)}, bf16[16,128,128]{2,1,0:T(8,128)(2,1)S(1)}, u32[]{:S(2)}, u32[]{:S(2)}) collective-permute-start(bf16[16,128,128]{2,1,0:T(8,128)(2,1)} %collective-permute-done.6.refs_1_.refs_0_), channel_id=1, source_target_pairs={{0,4},{4,0},{8,12},{12,8},{16,20},{20,16},{24,28},{28,24},{32,36},... | collective-permute-start | bytes 1572872 | tf_op jit(solution)/shard_map/ppermute | solution.py:249
  49.9 12.4 %collective-permute-start.16 = (bf16[16,128,128]{2,1,0:T(8,128)(2,1)S(1)}, bf16[16,128,128]{2,1,0:T(8,128)(2,1)}, u32[]{:S(2)}, u32[]{:S(2)}) collective-permute-start(bf16[16,128,128]{2,1,0:T(8,128)(2,1)S(1)} %collective-permute-done.14.refs_1_), channel_id=1, source_target_pairs={{0,8},{4,60},{8,16},{12,4},{16,24},{20,12},{24,32},{28,20},{32,40}... | collective-permute-start | bytes 1572872 | tf_op jit(solution)/shard_map/ppermute | solution.py:249
  51.2 5.8 %collective-permute-start.1 = (bf16[2,256,128]{2,1,0:T(8,128)(2,1)S(1)}, bf16[2,256,128]{2,1,0:T(8,128)(2,1)S(1)}, u32[]{:S(2)}, u32[]{:S(2)}) collective-permute-start(bf16[2,256,128]{2,1,0:T(8,128)(2,1)S(1)} %copy-done.27), channel_id=1, source_target_pairs={{4,0},{8,4},{12,8},{16,12},{20,16},{24,20},{28,24},{32,28},{36,32}... | collective-permute-start | bytes 393224 | tf_op jit(solution)/shard_map/ppermute | solution.py:352
  57.1 20.7 %collective-permute-start.9 = (bf16[16,128,128]{2,1,0:T(8,128)(2,1)}, bf16[16,128,128]{2,1,0:T(8,128)(2,1)}, u32[]{:S(2)}, u32[]{:S(2)}) collective-permute-start(bf16[16,128,128]{2,1,0:T(8,128)(2,1)} %collective-permute-done.8.refs_3_), channel_id=1, source_target_pairs={{0,4},{4,0},{8,12},{12,8},{16,20},{20,16},{24,28},{28,24},{32,36},... | collective-permute-start | bytes 1572872 | tf_op jit(solution)/shard_map/ppermute | solution.py:249
  62.0 6.7 %collective-permute-start.12 = (bf16[8,128,128]{2,1,0:T(8,128)(2,1)}, bf16[8,128,128]{2,1,0:T(8,128)(2,1)}, u32[]{:S(2)}, u32[]{:S(2)}) collective-permute-start(bf16[8,128,128]{2,1,0:T(8,128)(2,1)} %half.1), channel_id=1, source_target_pairs={{0,8},{4,60},{8,16},{12,4},{16,24},{20,12},{24,32},{28,20},{32,40}... | collective-permute-start | bytes 786440 | tf_op jit(solution)/shard_map/ppermute | solution.py:249
  62.3 16.0 %collective-permute-start.18 = (bf16[16,128,128]{2,1,0:T(8,128)(2,1)}, bf16[16,128,128]{2,1,0:T(8,128)(2,1)}, u32[]{:S(2)}, u32[]{:S(2)}) collective-permute-start(bf16[16,128,128]{2,1,0:T(8,128)(2,1)} %collective-permute-done.16.refs_3_), channel_id=1, source_target_pairs={{0,8},{4,60},{8,16},{12,4},{16,24},{20,12},{24,32},{28,20},{32,40}... | collective-permute-start | bytes 1572872 | tf_op jit(solution)/shard_map/ppermute | solution.py:249
  62.3 16.1 %collective-permute-start.11 = (bf16[16,128,128]{2,1,0:T(8,128)(2,1)}, bf16[16,128,128]{2,1,0:T(8,128)(2,1)}, u32[]{:S(2)}, u32[]{:S(2)}) collective-permute-start(bf16[16,128,128]{2,1,0:T(8,128)(2,1)} %collective-permute-done.10.source_ref.refs_5_), channel_id=1, source_target_pairs={{0,4},{4,0},{8,12},{12,8},{16,20},{20,16},{24,28},{28,24},{32,36},... | collective-permute-start | bytes 1572872 | tf_op jit(solution)/shard_map/ppermute | solution.py:249
  68.7 9.2 %collective-permute-start.13 = (bf16[8,128,128]{2,1,0:T(8,128)(2,1)}, bf16[8,128,128]{2,1,0:T(8,128)(2,1)S(1)}, u32[]{:S(2)}, u32[]{:S(2)}) collective-permute-start(bf16[8,128,128]{2,1,0:T(8,128)(2,1)} %collective-permute-done.12.refs_7_), channel_id=1, source_target_pairs={{0,4},{4,0},{8,12},{12,8},{16,20},{20,16},{24,28},{28,24},{32,36},... | collective-permute-start | bytes 786440 | tf_op jit(solution)/shard_map/ppermute | solution.py:249
  74.9 45.7 %collective-permute-start.26 = (bf16[512,1024]{1,0:T(8,128)(2,1)S(1)}, bf16[512,1024]{1,0:T(8,128)(2,1)S(1)}, u32[]{:S(2)}, u32[]{:S(2)}) collective-permute-start(bf16[512,1024]{1,0:T(8,128)(2,1)S(1)} %slabs2.1), channel_id=1, source_target_pairs={{2,0},{3,1},{0,2},{1,3},{6,4},{7,5},{4,6},{5,7},{10,8},{11,9},{8,1... | collective-permute-start | bytes 3145736 | tf_op jit(solution)/shard_map/ppermute | solution.py:223
  77.8 14.0 %collective-permute-start.15 = (bf16[16,128,128]{2,1,0:T(8,128)(2,1)S(1)}, bf16[16,128,128]{2,1,0:T(8,128)(2,1)S(1)}, u32[]{:S(2)}, u32[]{:S(2)}) collective-permute-start(bf16[16,128,128]{2,1,0:T(8,128)(2,1)S(1)} %copy-done.19), channel_id=1, source_target_pairs={{0,4},{4,0},{8,12},{12,8},{16,20},{20,16},{24,28},{28,24},{32,36},... | collective-permute-start | bytes 1572872 | tf_op jit(solution)/shard_map/ppermute | solution.py:249
  78.0 13.8 %collective-permute-start.17 = (bf16[16,128,128]{2,1,0:T(8,128)(2,1)}, bf16[16,128,128]{2,1,0:T(8,128)(2,1)S(1)}, u32[]{:S(2)}, u32[]{:S(2)}) collective-permute-start(bf16[16,128,128]{2,1,0:T(8,128)(2,1)} %collective-permute-done.16.refs_3_), channel_id=1, source_target_pairs={{0,4},{4,0},{8,12},{12,8},{16,20},{20,16},{24,28},{28,24},{32,36},... | collective-permute-start | bytes 1572872 | tf_op jit(solution)/shard_map/ppermute | solution.py:249
  78.3 13.5 %collective-permute-start.19 = (bf16[16,128,128]{2,1,0:T(8,128)(2,1)}, bf16[16,128,128]{2,1,0:T(8,128)(2,1)S(1)}, u32[]{:S(2)}, u32[]{:S(2)}) collective-permute-start(bf16[16,128,128]{2,1,0:T(8,128)(2,1)} %collective-permute-done.18.refs_5_), channel_id=1, source_target_pairs={{0,4},{4,0},{8,12},{12,8},{16,20},{20,16},{24,28},{28,24},{32,36},... | collective-permute-start | bytes 1572872 | tf_op jit(solution)/shard_map/ppermute | solution.py:249
  78.5 13.3 %collective-permute-start.20 = (bf16[16,128,128]{2,1,0:T(8,128)(2,1)}, bf16[16,128,128]{2,1,0:T(8,128)(2,1)S(1)}, u32[]{:S(2)}, u32[]{:S(2)}) collective-permute-start(bf16[16,128,128]{2,1,0:T(8,128)(2,1)} %collective-permute-done.18.refs_5_), channel_id=1, source_target_pairs={{0,8},{4,60},{8,16},{12,4},{16,24},{20,12},{24,32},{28,20},{32,40}... | collective-permute-start | bytes 1572872 | tf_op jit(solution)/shard_map/ppermute | solution.py:249
  99.4 21.6 %collective-permute-start.27 = (bf16[256,512]{1,0:T(8,128)(2,1)S(1)}, bf16[256,512]{1,0:T(8,128)(2,1)S(1)}, u32[]{:S(2)}, u32[]{:S(2)}) collective-permute-start(bf16[256,512]{1,0:T(8,128)(2,1)S(1)} %get-tuple-element.36.a0), channel_id=1, source_target_pairs={{1,0},{2,1},{3,2},{0,3},{5,4},{6,5},{7,6},{4,7},{9,8},{10,9},{11,1... | collective-permute-start | bytes 786440 | tf_op jit(solution)/shard_map/ppermute | solution.py:223
  100.5 21.5 %collective-permute-start.28 = (bf16[256,512]{1,0:T(8,128)(2,1)S(1)}, bf16[256,512]{1,0:T(8,128)(2,1)S(1)}, u32[]{:S(2)}, u32[]{:S(2)}) collective-permute-start(bf16[256,512]{1,0:T(8,128)(2,1)S(1)} %get-tuple-element.36.a0), channel_id=1, source_target_pairs={{2,0},{3,1},{0,2},{1,3},{6,4},{7,5},{4,6},{5,7},{10,8},{11,9},{8,1... | collective-permute-start | bytes 786440 | tf_op jit(solution)/shard_map/ppermute | solution.py:223
  102.3 19.7 %collective-permute-start.29 = (bf16[256,512]{1,0:T(8,128)(2,1)S(1)}, bf16[256,512]{1,0:T(8,128)(2,1)S(1)}, u32[]{:S(2)}, u32[]{:S(2)}) collective-permute-start(bf16[256,512]{1,0:T(8,128)(2,1)S(1)} %get-tuple-element.36.a0), channel_id=1, source_target_pairs={{3,0},{0,1},{1,2},{2,3},{7,4},{4,5},{5,6},{6,7},{11,8},{8,9},{9,10... | collective-permute-start | bytes 786440 | tf_op jit(solution)/shard_map/ppermute | solution.py:223
  117.3 12.4 %collective-permute-start.23 = (bf16[256,512]{1,0:T(8,128)(2,1)S(1)}, bf16[256,512]{1,0:T(8,128)(2,1)S(1)}, u32[]{:S(2)}, u32[]{:S(2)}) collective-permute-start(bf16[256,512]{1,0:T(8,128)(2,1)S(1)} %attend1.1.a0), channel_id=1, source_target_pairs={{1,0},{2,1},{3,2},{0,3},{5,4},{6,5},{7,6},{4,7},{9,8},{10,9},{11,1... | collective-permute-start | bytes 786440 | tf_op jit(solution)/shard_map/ppermute | solution.py:223
  120.6 10.1 %collective-permute-start.24 = (bf16[256,512]{1,0:T(8,128)(2,1)S(1)}, bf16[256,512]{1,0:T(8,128)(2,1)S(1)}, u32[]{:S(2)}, u32[]{:S(2)}) collective-permute-start(bf16[256,512]{1,0:T(8,128)(2,1)S(1)} %attend1.1.a0), channel_id=1, source_target_pairs={{2,0},{3,1},{0,2},{1,3},{6,4},{7,5},{4,6},{5,7},{10,8},{11,9},{8,1... | collective-permute-start | bytes 786440 | tf_op jit(solution)/shard_map/ppermute | solution.py:223
  121.1 12.3 %collective-permute-start.25 = (bf16[256,512]{1,0:T(8,128)(2,1)S(1)}, bf16[256,512]{1,0:T(8,128)(2,1)S(1)}, u32[]{:S(2)}, u32[]{:S(2)}) collective-permute-start(bf16[256,512]{1,0:T(8,128)(2,1)S(1)} %attend1.1.a0), channel_id=1, source_target_pairs={{3,0},{0,1},{1,2},{2,3},{7,4},{4,5},{5,6},{6,7},{11,8},{8,9},{9,10... | collective-permute-start | bytes 786440 | tf_op jit(solution)/shard_map/ppermute | solution.py:223
  (26 other events, 261.8 us)

commit v8 on v6

--- a/solution.py
+++ b/solution.py
@@ -236,8 +236,8 @@
     refs[-1][count:] = other_ref[which]
 
 
-def copy_kernel(source_ref, out_ref):
-    out_ref[...] = source_ref[...]
+def copy_kernel(source_ref, *refs):
+    refs[-1][...] = source_ref[...]
 
 
 def gather_columns(nx, nz, payload, later):
@@ -278,14 +278,14 @@
                     copy_kernel,
                     grid=(1,),
                     out_shape=shape((size, BLOCK, HEAD), BF16),
-                    in_specs=[pl.BlockSpec((size, BLOCK, HEAD), lambda i: (0, 0, 0))],
+                    in_specs=[pl.BlockSpec((size, BLOCK, HEAD), lambda i: (0, 0, 0))] + [ANY()] * len(later),
                     out_specs=VMEM(),
                     name="half",
-                )(moving)
+                )(moving, *later)
             moving = send(moving, along)
             held += [moving] + ([] if which == 1 and last else [send(moving, across)])
             if n == 1:
-                waited = [moving, *later]
+                waited = [moving]
         pieces.append(held)
     return pieces
 
@@ -309,7 +309,7 @@
 
 def slab_kernel(tp, index_ref, weight_ref, *refs):
     width = weight_ref.shape[1] // tp
-    for shift, ref in enumerate(refs[1:]):
+    for shift, ref in enumerate(refs[-tp:]):
         target = lax.rem(index_ref[0] + tp - shift, tp)
         ref[...] = weight_ref[:, pl.ds(pl.multiple_of(target * width, width), width)]
 
@@ -369,12 +369,12 @@
         functools.partial(slab_kernel, tp),
         grid=(depth // 128,),
         out_shape=[shape((depth, width), BF16)] * tp,
-        in_specs=[SMEM(), pl.BlockSpec((128, out_weight.shape[1]), lambda i: (i, 0)), ANY()],
+        in_specs=[SMEM(), pl.BlockSpec((128, out_weight.shape[1]), lambda i: (i, 0))] + [ANY()] * 3,
         out_specs=[pl.BlockSpec((128, width), lambda i: (i, 0))] * tp,
         compiler_params=PARAMS,
         cost_estimate=cost(3),
         name="slabs",
-    )(tp_index.reshape(1).astype(i32), out_weight, v_pieces[0])
+    )(tp_index.reshape(1).astype(i32), out_weight, v_pieces[0], before, after)
     slabs = [slabs[0]] + [from_ahead(slabs[shift], "tp", shift) for shift in range(1, tp)]
 
     columns, top = pl.pallas_call(

time: 130 us -> 128 us (0.985)
  waiting for transfers between devices: 33.2 us -> 26.5 us
  starting transfers between devices: 43.1 us -> 45.7 us
  Pallas kernels: 45.9 us -> 47.6 us
  local copies, waits for them, and re-layouts: 5.47 us -> 6.9 us
    ppermute x19, waiting for transfers between devices: 16.8 us -> 12.2 us  [gather_columns(): send = lambda a, r: lax.ppermute(a, 'ctx', r)]
    ppermute x19, starting transfers between devices: 25 us -> 28 us  [gather_columns(): send = lambda a, r: lax.ppermute(a, 'ctx', r)]
    ppermute x9, waiting for transfers between devices: 16.4 us -> 14.2 us  [from_ahead(): return lax.ppermute(x, axis, [((i + shift) % n, i) for i in range(n)])]
    unnamed x38 -> x44, local copies, waits for them, and re-layouts: 5.37 us -> 6.19 us
  transfers between devices with their start and end apart: 30 -> 30, of which waited for: 11 -> 11; matrix products, arithmetic and copies ran while one was open for 0% -> 1% of each run, Pallas kernels for 33% -> 35%
where the time goes in v8:
time: 128 us; the launch traced here: 127 us
  Pallas kernels  47.6 us (37%)
  starting transfers between devices  45.7 us (36%)
  waiting for transfers between devices  26.5 us (21%)
  local copies, waits for them, and re-layouts  6.9 us (5%)
    ppermute x19, starting transfers between devices, gather_columns(): send = lambda a, r: lax.ppermute(a, 'ctx', r)  28 us
    pallas_call x2, Pallas kernels, per_device(): pl.pallas_call(functools.partial(out_kernel, ctx_count, st, len(v_pieces)...  22.5 us
    ppermute x9, waiting for transfers between devices, from_ahead(): return lax.ppermute(x, axis, [((i + shift) % n, i) for i in range(n)])  14.2 us
    ppermute x19, waiting for transfers between devices, gather_columns(): send = lambda a, r: lax.ppermute(a, 'ctx', r)  12.2 us
    ppermute x9, starting transfers between devices, from_ahead(): return lax.ppermute(x, axis, [((i + shift) % n, i) for i in range(n)])  12.2 us
    pallas_call x1, Pallas kernels, per_device(): pl.pallas_call(top_kernel, out_shape=[shape((ROOM, BLOCK, HEAD), BF16), s...  10.4 us
    unnamed x44, local copies, waits for them, and re-layouts  6.19 us
    pallas_call x2, Pallas kernels, per_device(): pl.pallas_call(mix_kernel, grid=(width // tile,), out_shape=shape((2, STR...  6.19 us
  transfers between devices with their start and end apart: 30, of which 11 were waited for; matrix products, arithmetic and copies ran while one was open for 1% of the time, Pallas kernels for 35%

profile of v8, /device:TPU:96, one launch (start us, length us, event | category | flops | bytes accessed | tf_op | source)
XLA Modules:
  0.0 127.0 jit_solution(17709532525621757009)
XLA Ops:
  3.0 1.6 %collective-permute-start.4 = (bf16[2,2,128,128]{3,2,1,0:T(8,128)(2,1)S(1)}, bf16[2,2,128,128]{3,2,1,0:T(8,128)(2,1)S(1)}, u32[]{:S(2)}, u32[]{:S(2)}) collective-permute-start(bf16[2,2,128,128]{3,2,1,0:T(8,128)(2,1)S(1)} %get-tuple-element.29.refs_0_), channel_id=1, source_target_pairs={{0,64},{4,68},{8,72},{12,76},{16,80},{20,84},{24,88},{28,92},{32,9... | collective-permute-start | bytes 393224 | tf_op jit(solution)/shard_map/ppermute | solution.py:249
  4.6 2.7 %collective-permute-start.3 = (bf16[2,2,128,128]{3,2,1,0:T(8,128)(2,1)S(1)}, bf16[2,2,128,128]{3,2,1,0:T(8,128)(2,1)S(1)}, u32[]{:S(2)}, u32[]{:S(2)}) collective-permute-start(bf16[2,2,128,128]{3,2,1,0:T(8,128)(2,1)S(1)} %get-tuple-element.29.refs_0_), channel_id=1, source_target_pairs={{0,128},{4,132},{8,136},{12,140},{16,144},{20,148},{24,152},{28,15... | collective-permute-start | bytes 393224 | tf_op jit(solution)/shard_map/ppermute | solution.py:249
  7.3 1.4 %collective-permute-start.2 = (bf16[2,2,128,128]{3,2,1,0:T(8,128)(2,1)S(1)}, bf16[2,2,128,128]{3,2,1,0:T(8,128)(2,1)S(1)}, u32[]{:S(2)}, u32[]{:S(2)}) collective-permute-start(bf16[2,2,128,128]{3,2,1,0:T(8,128)(2,1)S(1)} %get-tuple-element.29.refs_0_), channel_id=1, source_target_pairs={{0,192},{4,196},{8,200},{12,204},{16,208},{20,212},{24,216},{28,22... | collective-permute-start | bytes 393224 | tf_op jit(solution)/shard_map/ppermute | solution.py:249
  9.7 3.6 %collective-permute-done.3.refs_2_ = bf16[2,2,128,128]{3,2,1,0:T(8,128)(2,1)S(1)} collective-permute-done((bf16[2,2,128,128]{3,2,1,0:T(8,128)(2,1)S(1)}, bf16[2,2,128,128]{3,2,1,0:T(8,128)(2,1)S(1)}, u32[]{:S(2)}, u32[]{:S(2)}) %collective-permute-start.3) | collective-permute-done | bytes 131104 | tf_op jit(solution)/shard_map/ppermute | solution.py:249
  13.5 1.9 %collective-permute-done.5.other_ref = bf16[2,8,128,128]{3,2,1,0:T(8,128)(2,1)S(1)} collective-permute-done((bf16[2,8,128,128]{3,2,1,0:T(8,128)(2,1)S(1)}, bf16[2,8,128,128]{3,2,1,0:T(8,128)(2,1)S(1)}, u32[]{:S(2)}, u32[]{:S(2)}) %collective-permute-start.5) | collective-permute-done | bytes 524320 | tf_op jit(solution)/shard_map/ppermute | solution.py:249
  15.4 3.2 %collective-permute-start.6 = (bf16[16,128,128]{2,1,0:T(8,128)(2,1)S(1)}, bf16[16,128,128]{2,1,0:T(8,128)(2,1)}, u32[]{:S(2)}, u32[]{:S(2)}) collective-permute-start(bf16[16,128,128]{2,1,0:T(8,128)(2,1)S(1)} %chip0.1.refs_0_), channel_id=1, source_target_pairs={{0,8},{4,60},{8,16},{12,4},{16,24},{20,12},{24,32},{28,20},{32,40}... | collective-permute-start | bytes 1572872 | tf_op jit(solution)/shard_map/ppermute | solution.py:249
  18.6 1.9 %collective-permute-start = (bf16[2,256,128]{2,1,0:T(8,128)(2,1)S(1)}, bf16[2,256,128]{2,1,0:T(8,128)(2,1)S(1)}, u32[]{:S(2)}, u32[]{:S(2)}) collective-permute-start(bf16[2,256,128]{2,1,0:T(8,128)(2,1)S(1)} %get-tuple-element.26), channel_id=1, source_target_pairs={{0,4},{4,8},{8,12},{12,16},{16,20},{20,24},{24,28},{28,32},{32,36}... | collective-permute-start | bytes 393224 | tf_op jit(solution)/shard_map/ppermute | solution.py:351
  20.5 3.6 %collective-permute-start.1 = (bf16[2,256,128]{2,1,0:T(8,128)(2,1)S(1)}, bf16[2,256,128]{2,1,0:T(8,128)(2,1)S(1)}, u32[]{:S(2)}, u32[]{:S(2)}) collective-permute-start(bf16[2,256,128]{2,1,0:T(8,128)(2,1)S(1)} %get-tuple-element.27), channel_id=1, source_target_pairs={{4,0},{8,4},{12,8},{16,12},{20,16},{24,20},{28,24},{32,28},{36,32}... | collective-permute-start | bytes 393224 | tf_op jit(solution)/shard_map/ppermute | solution.py:352
  24.2 2.5 %collective-permute-done.6.refs_1_.refs_0_ = bf16[16,128,128]{2,1,0:T(8,128)(2,1)} collective-permute-done((bf16[16,128,128]{2,1,0:T(8,128)(2,1)S(1)}, bf16[16,128,128]{2,1,0:T(8,128)(2,1)}, u32[]{:S(2)}, u32[]{:S(2)}) %collective-permute-start.6) | collective-permute-done | bytes 524320 | tf_op jit(solution)/shard_map/ppermute | solution.py:249
  26.7 3.8 %collective-permute-start.8 = (bf16[16,128,128]{2,1,0:T(8,128)(2,1)}, bf16[16,128,128]{2,1,0:T(8,128)(2,1)}, u32[]{:S(2)}, u32[]{:S(2)}) collective-permute-start(bf16[16,128,128]{2,1,0:T(8,128)(2,1)} %collective-permute-done.6.refs_1_.refs_0_), channel_id=1, source_target_pairs={{0,8},{4,60},{8,16},{12,4},{16,24},{20,12},{24,32},{28,20},{32,40}... | collective-permute-start | bytes 1572872 | tf_op jit(solution)/shard_map/ppermute | solution.py:249
  30.7 4.5 %slabs.1 = (bf16[512,1024]{1,0:T(8,128)(2,1)S(1)}, bf16[512,1024]{1,0:T(8,128)(2,1)}, bf16[512,1024]{1,0:T(8,128)(2,1)}, bf16[512,1024]{1,0:T(8,128)(2,1)}) custom-call(s32[1]{0:T(128)} %bitcast.7.index_ref, bf16[512,4096]{1,0:T(8,128)(2,1)} %weight_ref.1, bf16[16,128,128]{2,1,0:T(8,128)(2,1)S(1)} %chip1.1.refs_0_, ...), custom_call_target="tpu_custom_call" | custom-call | bytes 9000000 | tf_op jit(solution)/shard_map/slabs/pallas_call | solution.py:368
  36.2 3.0 %collective-permute-start.21 = (bf16[512,1024]{1,0:T(8,128)(2,1)}, bf16[512,1024]{1,0:T(8,128)(2,1)S(1)}, u32[]{:S(2)}, u32[]{:S(2)}) collective-permute-start(bf16[512,1024]{1,0:T(8,128)(2,1)} %get-tuple-element.33), channel_id=1, source_target_pairs={{1,0},{2,1},{3,2},{0,3},{5,4},{6,5},{7,6},{4,7},{9,8},{10,9},{11,1... | collective-permute-start | bytes 3145736 | tf_op jit(solution)/shard_map/ppermute | solution.py:223
  39.2 2.0 %collective-permute-start.10 = (bf16[16,128,128]{2,1,0:T(8,128)(2,1)}, bf16[16,128,128]{2,1,0:T(8,128)(2,1)}, u32[]{:S(2)}, u32[]{:S(2)}) collective-permute-start(bf16[16,128,128]{2,1,0:T(8,128)(2,1)} %collective-permute-done.8.refs_3_), channel_id=1, source_target_pairs={{0,8},{4,60},{8,16},{12,4},{16,24},{20,12},{24,32},{28,20},{32,40}... | collective-permute-start | bytes 1572872 | tf_op jit(solution)/shard_map/ppermute | solution.py:249
  41.2 1.8 %collective-permute-done.14.refs_1_ = bf16[16,128,128]{2,1,0:T(8,128)(2,1)} collective-permute-done((bf16[16,128,128]{2,1,0:T(8,128)(2,1)S(1)}, bf16[16,128,128]{2,1,0:T(8,128)(2,1)}, u32[]{:S(2)}, u32[]{:S(2)}) %collective-permute-start.14) | collective-permute-done | bytes 524320 | tf_op jit(solution)/shard_map/ppermute | solution.py:249
  43.0 3.8 %collective-permute-start.16 = (bf16[16,128,128]{2,1,0:T(8,128)(2,1)}, bf16[16,128,128]{2,1,0:T(8,128)(2,1)}, u32[]{:S(2)}, u32[]{:S(2)}) collective-permute-start(bf16[16,128,128]{2,1,0:T(8,128)(2,1)} %collective-permute-done.14.refs_1_), channel_id=1, source_target_pairs={{0,8},{4,60},{8,16},{12,4},{16,24},{20,12},{24,32},{28,20},{32,40}... | collective-permute-start | bytes 1572872 | tf_op jit(solution)/shard_map/ppermute | solution.py:249
  48.6 1.9 %band.1 = (f32[4,256,512]{2,1,0:T(8,128)S(1)}, f32[2,4,256,128]{3,2,1,0:T(8,128)S(1)}) custom-call(s32[1,16]{1,0:T(1,128)S(1)} %get-tuple-element.22.meta_ref, s32[4,64]{1,0:T(4,128)S(1)} %copy-done.21, bf16[2,256,512]{2,1,0:T(8,128)(2,1)S(1)} %bitcast.9, bf16[2,256,128]{2,1,0:T(8,128)(2,1)S(1)} %bitcast.14, ...), custom_call_target="tpu_custom_call" | custom-call | bytes 9000000 | tf_op jit(solution)/shard_map/band/pallas_call | solution.py:354
  51.5 1.2 half.1
  54.4 3.7 %collective-permute-start.18 = (bf16[16,128,128]{2,1,0:T(8,128)(2,1)}, bf16[16,128,128]{2,1,0:T(8,128)(2,1)S(1)}, u32[]{:S(2)}, u32[]{:S(2)}) collective-permute-start(bf16[16,128,128]{2,1,0:T(8,128)(2,1)} %collective-permute-done.16.refs_3_), channel_id=1, source_target_pairs={{0,8},{4,60},{8,16},{12,4},{16,24},{20,12},{24,32},{28,20},{32,40}... | collective-permute-start | bytes 1572872 | tf_op jit(solution)/shard_map/ppermute | solution.py:249
  58.1 2.6 %collective-permute-done.21.refs_8_.w1 = bf16[512,1024]{1,0:T(8,128)(2,1)S(1)} collective-permute-done((bf16[512,1024]{1,0:T(8,128)(2,1)}, bf16[512,1024]{1,0:T(8,128)(2,1)S(1)}, u32[]{:S(2)}, u32[]{:S(2)}) %collective-permute-start.21) | collective-permute-done | bytes 1048608 | tf_op jit(solution)/shard_map/ppermute | solution.py:223
  61.2 2.8 %collective-permute-done.22.refs_9_.w3 = bf16[512,1024]{1,0:T(8,128)(2,1)S(1)} collective-permute-done((bf16[512,1024]{1,0:T(8,128)(2,1)}, bf16[512,1024]{1,0:T(8,128)(2,1)S(1)}, u32[]{:S(2)}, u32[]{:S(2)}) %collective-permute-start.22) | collective-permute-done | bytes 1048608 | tf_op jit(solution)/shard_map/ppermute | solution.py:223
  65.1 3.6 %collective-permute-start.20 = (bf16[16,128,128]{2,1,0:T(8,128)(2,1)S(1)}, bf16[16,128,128]{2,1,0:T(8,128)(2,1)S(1)}, u32[]{:S(2)}, u32[]{:S(2)}) collective-permute-start(bf16[16,128,128]{2,1,0:T(8,128)(2,1)S(1)} %collective-permute-done.18.refs_5_), channel_id=1, source_target_pairs={{0,8},{4,60},{8,16},{12,4},{16,24},{20,12},{24,32},{28,20},{32,40}... | collective-permute-start | bytes 1572872 | tf_op jit(solution)/shard_map/ppermute | solution.py:249
  68.7 10.4 %top.1 = (bf16[65,128,128]{2,1,0:T(8,128)(2,1)}, f32[2,4,256,128]{3,2,1,0:T(8,128)S(1)}) custom-call(s32[1,16]{1,0:T(1,128)S(1)} %get-tuple-element.22.meta_ref, s32[1,64]{1,0:T(1,128)S(1)} %get-tuple-element.23.blk_ref, s32[1,128]{1,0:T(1,128)S(1)} %get-tuple-element.25.at_ref, bf16[2,256,512]{2,1,0:T(8,128)(2,1)S(1)} %bitcast.10, ...), custom_call_target="tpu_custom_call" | custom-call | bytes 27000000 | tf_op jit(solution)/shard_map/top/pallas_call | solution.py:380
  80.2 7.6 %attend0.1 = (bf16[256,512]{1,0:T(8,128)(2,1)S(1)}, bf16[65,128,128]{2,1,0:T(8,128)(2,1)}) custom-call(s32[1,16]{1,0:T(1,128)S(1)} %get-tuple-element.22.meta_ref, s32[1,64]{1,0:T(1,128)S(1)} %get-tuple-element.23.blk_ref, s32[1,128]{1,0:T(1,128)S(1)} %get-tuple-element.24.at_ref, bf16[2,256,512]{2,1,0:T(8,128)(2,1)S(1)} %bitcast.11, ...), custom_call_target="tpu_custom_call" | custom-call | bytes 24000000 | tf_op jit(solution)/shard_map/attend0/pallas_call | solution.py:394
  87.8 1.6 %collective-permute-start.29 = (bf16[256,512]{1,0:T(8,128)(2,1)S(1)}, bf16[256,512]{1,0:T(8,128)(2,1)S(1)}, u32[]{:S(2)}, u32[]{:S(2)}) collective-permute-start(bf16[256,512]{1,0:T(8,128)(2,1)S(1)} %get-tuple-element.38.a0), channel_id=1, source_target_pairs={{3,0},{0,1},{1,2},{2,3},{7,4},{4,5},{5,6},{6,7},{11,8},{8,9},{9,10... | collective-permute-start | bytes 786440 | tf_op jit(solution)/shard_map/ppermute | solution.py:223
  89.4 1.6 %collective-permute-start.28 = (bf16[256,512]{1,0:T(8,128)(2,1)S(1)}, bf16[256,512]{1,0:T(8,128)(2,1)S(1)}, u32[]{:S(2)}, u32[]{:S(2)}) collective-permute-start(bf16[256,512]{1,0:T(8,128)(2,1)S(1)} %get-tuple-element.38.a0), channel_id=1, source_target_pairs={{2,0},{3,1},{0,2},{1,3},{6,4},{7,5},{4,6},{5,7},{10,8},{11,9},{8,1... | collective-permute-start | bytes 786440 | tf_op jit(solution)/shard_map/ppermute | solution.py:223
  91.0 2.6 %collective-permute-start.27 = (bf16[256,512]{1,0:T(8,128)(2,1)S(1)}, bf16[256,512]{1,0:T(8,128)(2,1)S(1)}, u32[]{:S(2)}, u32[]{:S(2)}) collective-permute-start(bf16[256,512]{1,0:T(8,128)(2,1)S(1)} %get-tuple-element.38.a0), channel_id=1, source_target_pairs={{1,0},{2,1},{3,2},{0,3},{5,4},{6,5},{7,6},{4,7},{9,8},{10,9},{11,1... | collective-permute-start | bytes 786440 | tf_op jit(solution)/shard_map/ppermute | solution.py:223
  93.6 14.9 %attend1.1.a0 = bf16[256,512]{1,0:T(8,128)(2,1)S(1)} custom-call(s32[1,16]{1,0:T(1,128)S(1)} %get-tuple-element.22.meta_ref, s32[1,64]{1,0:T(1,128)S(1)} %get-tuple-element.23.blk_ref, s32[1,128]{1,0:T(1,128)S(1)} %get-tuple-element.24.at_ref, bf16[2,256,512]{2,1,0:T(8,128)(2,1)S(1)} %bitcast.12, bf16[65,128,128]{2,1,0:T(8,128)(2,1)} %get-tuple-element.31.keys_ref, ...), custom_call_target="tpu_custom_call" | custom-call | bytes 24000000 | tf_op jit(solution)/shard_map/attend1/pallas_call | solution.py:394
  108.6 1.5 %collective-permute-start.24 = (bf16[256,512]{1,0:T(8,128)(2,1)S(1)}, bf16[256,512]{1,0:T(8,128)(2,1)S(1)}, u32[]{:S(2)}, u32[]{:S(2)}) collective-permute-start(bf16[256,512]{1,0:T(8,128)(2,1)S(1)} %attend1.1.a0), channel_id=1, source_target_pairs={{2,0},{3,1},{0,2},{1,3},{6,4},{7,5},{4,6},{5,7},{10,8},{11,9},{8,1... | collective-permute-start | bytes 786440 | tf_op jit(solution)/shard_map/ppermute | solution.py:223
  110.1 1.8 %collective-permute-start.23 = (bf16[256,512]{1,0:T(8,128)(2,1)S(1)}, bf16[256,512]{1,0:T(8,128)(2,1)S(1)}, u32[]{:S(2)}, u32[]{:S(2)}) collective-permute-start(bf16[256,512]{1,0:T(8,128)(2,1)S(1)} %attend1.1.a0), channel_id=1, source_target_pairs={{1,0},{2,1},{3,2},{0,3},{5,4},{6,5},{7,6},{4,7},{9,8},{10,9},{11,1... | collective-permute-start | bytes 786440 | tf_op jit(solution)/shard_map/ppermute | solution.py:223
  112.0 3.1 %mix0.1.refs_0_ = bf16[2,256,1024]{2,1,0:T(8,128)(2,1)} custom-call(bf16[256,512]{1,0:T(8,128)(2,1)S(1)} %get-tuple-element.38.a0, bf16[256,512]{1,0:T(8,128)(2,1)S(1)} %collective-permute-done.27.a1, bf16[256,512]{1,0:T(8,128)(2,1)S(1)} %collective-permute-done.28.a2, bf16[256,512]{1,0:T(8,128)(2,1)S(1)} %collective-permute-done.29.a3, ...), custom_call_target="tpu_custom_call" | custom-call | bytes 9000000 | tf_op jit(solution)/shard_map/mix0/pallas_call | solution.py:419
  115.1 8.2 %collective-permute-done.25.a3 = bf16[256,512]{1,0:T(8,128)(2,1)S(1)} collective-permute-done((bf16[256,512]{1,0:T(8,128)(2,1)S(1)}, bf16[256,512]{1,0:T(8,128)(2,1)S(1)}, u32[]{:S(2)}, u32[]{:S(2)}) %collective-permute-start.25) | collective-permute-done | bytes 262176 | tf_op jit(solution)/shard_map/ppermute | solution.py:223
  123.9 3.1 %mix1.1 = bf16[2,256,1024]{2,1,0:T(8,128)(2,1)} custom-call(bf16[256,512]{1,0:T(8,128)(2,1)S(1)} %attend1.1.a0, bf16[256,512]{1,0:T(8,128)(2,1)S(1)} %collective-permute-done.23.a1, bf16[256,512]{1,0:T(8,128)(2,1)S(1)} %collective-permute-done.24.a2, bf16[256,512]{1,0:T(8,128)(2,1)S(1)} %collective-permute-done.25.a3, ...), custom_call_target="tpu_custom_call", output_to_operand_aliasing={{}: (8, {})} | custom-call | bytes 9000000 | tf_op jit(solution)/shard_map/mix1/pallas_call | solution.py:419
  (86 shorter events, 13.0 us)
Async XLA Ops:
  3.0 6.7 %collective-permute-start.4 = (bf16[2,2,128,128]{3,2,1,0:T(8,128)(2,1)S(1)}, bf16[2,2,128,128]{3,2,1,0:T(8,128)(2,1)S(1)}, u32[]{:S(2)}, u32[]{:S(2)}) collective-permute-start(bf16[2,2,128,128]{3,2,1,0:T(8,128)(2,1)S(1)} %get-tuple-element.29.refs_0_), channel_id=1, source_target_pairs={{0,64},{4,68},{8,72},{12,76},{16,80},{20,84},{24,88},{28,92},{32,9... | collective-permute-start | bytes 393224 | tf_op jit(solution)/shard_map/ppermute | solution.py:249
  4.6 8.7 %collective-permute-start.3 = (bf16[2,2,128,128]{3,2,1,0:T(8,128)(2,1)S(1)}, bf16[2,2,128,128]{3,2,1,0:T(8,128)(2,1)S(1)}, u32[]{:S(2)}, u32[]{:S(2)}) collective-permute-start(bf16[2,2,128,128]{3,2,1,0:T(8,128)(2,1)S(1)} %get-tuple-element.29.refs_0_), channel_id=1, source_target_pairs={{0,128},{4,132},{8,136},{12,140},{16,144},{20,148},{24,152},{28,15... | collective-permute-start | bytes 393224 | tf_op jit(solution)/shard_map/ppermute | solution.py:249
  7.3 6.0 %collective-permute-start.2 = (bf16[2,2,128,128]{3,2,1,0:T(8,128)(2,1)S(1)}, bf16[2,2,128,128]{3,2,1,0:T(8,128)(2,1)S(1)}, u32[]{:S(2)}, u32[]{:S(2)}) collective-permute-start(bf16[2,2,128,128]{3,2,1,0:T(8,128)(2,1)S(1)} %get-tuple-element.29.refs_0_), channel_id=1, source_target_pairs={{0,192},{4,196},{8,200},{12,204},{16,208},{20,212},{24,216},{28,22... | collective-permute-start | bytes 393224 | tf_op jit(solution)/shard_map/ppermute | solution.py:249
  13.4 2.0 %collective-permute-start.5 = (bf16[2,8,128,128]{3,2,1,0:T(8,128)(2,1)S(1)}, bf16[2,8,128,128]{3,2,1,0:T(8,128)(2,1)S(1)}, u32[]{:S(2)}, u32[]{:S(2)}) collective-permute-start(bf16[2,8,128,128]{3,2,1,0:T(8,128)(2,1)S(1)} %line.1.own_ref), channel_id=1, source_target_pairs={{0,4},{4,0},{8,12},{12,8},{16,20},{20,16},{24,28},{28,24},{32,36},... | collective-permute-start | bytes 1572872 | tf_op jit(solution)/shard_map/ppermute | solution.py:249
  15.4 11.3 %collective-permute-start.6 = (bf16[16,128,128]{2,1,0:T(8,128)(2,1)S(1)}, bf16[16,128,128]{2,1,0:T(8,128)(2,1)}, u32[]{:S(2)}, u32[]{:S(2)}) collective-permute-start(bf16[16,128,128]{2,1,0:T(8,128)(2,1)S(1)} %chip0.1.refs_0_), channel_id=1, source_target_pairs={{0,8},{4,60},{8,16},{12,4},{16,24},{20,12},{24,32},{28,20},{32,40}... | collective-permute-start | bytes 1572872 | tf_op jit(solution)/shard_map/ppermute | solution.py:249
  18.6 12.0 %collective-permute-start = (bf16[2,256,128]{2,1,0:T(8,128)(2,1)S(1)}, bf16[2,256,128]{2,1,0:T(8,128)(2,1)S(1)}, u32[]{:S(2)}, u32[]{:S(2)}) collective-permute-start(bf16[2,256,128]{2,1,0:T(8,128)(2,1)S(1)} %get-tuple-element.26), channel_id=1, source_target_pairs={{0,4},{4,8},{8,12},{12,16},{16,20},{20,24},{24,28},{28,32},{32,36}... | collective-permute-start | bytes 393224 | tf_op jit(solution)/shard_map/ppermute | solution.py:351
  20.5 10.1 %collective-permute-start.1 = (bf16[2,256,128]{2,1,0:T(8,128)(2,1)S(1)}, bf16[2,256,128]{2,1,0:T(8,128)(2,1)S(1)}, u32[]{:S(2)}, u32[]{:S(2)}) collective-permute-start(bf16[2,256,128]{2,1,0:T(8,128)(2,1)S(1)} %get-tuple-element.27), channel_id=1, source_target_pairs={{4,0},{8,4},{12,8},{16,12},{20,16},{24,20},{28,24},{32,28},{36,32}... | collective-permute-start | bytes 393224 | tf_op jit(solution)/shard_map/ppermute | solution.py:352
  26.7 12.5 %collective-permute-start.8 = (bf16[16,128,128]{2,1,0:T(8,128)(2,1)}, bf16[16,128,128]{2,1,0:T(8,128)(2,1)}, u32[]{:S(2)}, u32[]{:S(2)}) collective-permute-start(bf16[16,128,128]{2,1,0:T(8,128)(2,1)} %collective-permute-done.6.refs_1_.refs_0_), channel_id=1, source_target_pairs={{0,8},{4,60},{8,16},{12,4},{16,24},{20,12},{24,32},{28,20},{32,40}... | collective-permute-start | bytes 1572872 | tf_op jit(solution)/shard_map/ppermute | solution.py:249
  30.6 12.5 %collective-permute-start.14 = (bf16[16,128,128]{2,1,0:T(8,128)(2,1)S(1)}, bf16[16,128,128]{2,1,0:T(8,128)(2,1)}, u32[]{:S(2)}, u32[]{:S(2)}) collective-permute-start(bf16[16,128,128]{2,1,0:T(8,128)(2,1)S(1)} %chip1.1.refs_0_), channel_id=1, source_target_pairs={{0,8},{4,60},{8,16},{12,4},{16,24},{20,12},{24,32},{28,20},{32,40}... | collective-permute-start | bytes 1572872 | tf_op jit(solution)/shard_map/ppermute | solution.py:249
  36.2 24.5 %collective-permute-start.21 = (bf16[512,1024]{1,0:T(8,128)(2,1)}, bf16[512,1024]{1,0:T(8,128)(2,1)S(1)}, u32[]{:S(2)}, u32[]{:S(2)}) collective-permute-start(bf16[512,1024]{1,0:T(8,128)(2,1)} %get-tuple-element.33), channel_id=1, source_target_pairs={{1,0},{2,1},{3,2},{0,3},{5,4},{6,5},{7,6},{4,7},{9,8},{10,9},{11,1... | collective-permute-start | bytes 3145736 | tf_op jit(solution)/shard_map/ppermute | solution.py:223
  39.2 24.8 %collective-permute-start.22 = (bf16[512,1024]{1,0:T(8,128)(2,1)}, bf16[512,1024]{1,0:T(8,128)(2,1)S(1)}, u32[]{:S(2)}, u32[]{:S(2)}) collective-permute-start(bf16[512,1024]{1,0:T(8,128)(2,1)} %get-tuple-element.34), channel_id=1, source_target_pairs={{3,0},{0,1},{1,2},{2,3},{7,4},{4,5},{5,6},{6,7},{11,8},{8,9},{9,10... | collective-permute-start | bytes 3145736 | tf_op jit(solution)/shard_map/ppermute | solution.py:223
  39.2 12.3 %collective-permute-start.10 = (bf16[16,128,128]{2,1,0:T(8,128)(2,1)}, bf16[16,128,128]{2,1,0:T(8,128)(2,1)}, u32[]{:S(2)}, u32[]{:S(2)}) collective-permute-start(bf16[16,128,128]{2,1,0:T(8,128)(2,1)} %collective-permute-done.8.refs_3_), channel_id=1, source_target_pairs={{0,8},{4,60},{8,16},{12,4},{16,24},{20,12},{24,32},{28,20},{32,40}... | collective-permute-start | bytes 1572872 | tf_op jit(solution)/shard_map/ppermute | solution.py:249
  41.2 11.5 %collective-permute-start.7 = (bf16[16,128,128]{2,1,0:T(8,128)(2,1)}, bf16[16,128,128]{2,1,0:T(8,128)(2,1)}, u32[]{:S(2)}, u32[]{:S(2)}) collective-permute-start(bf16[16,128,128]{2,1,0:T(8,128)(2,1)} %collective-permute-done.6.refs_1_.refs_0_), channel_id=1, source_target_pairs={{0,4},{4,0},{8,12},{12,8},{16,20},{20,16},{24,28},{28,24},{32,36},... | collective-permute-start | bytes 1572872 | tf_op jit(solution)/shard_map/ppermute | solution.py:249
  43.0 11.3 %collective-permute-start.16 = (bf16[16,128,128]{2,1,0:T(8,128)(2,1)}, bf16[16,128,128]{2,1,0:T(8,128)(2,1)}, u32[]{:S(2)}, u32[]{:S(2)}) collective-permute-start(bf16[16,128,128]{2,1,0:T(8,128)(2,1)} %collective-permute-done.14.refs_1_), channel_id=1, source_target_pairs={{0,8},{4,60},{8,16},{12,4},{16,24},{20,12},{24,32},{28,20},{32,40}... | collective-permute-start | bytes 1572872 | tf_op jit(solution)/shard_map/ppermute | solution.py:249
  48.3 20.4 %copy-start.14 = (bf16[16,128,128]{2,1,0:T(8,128)(2,1)S(1)}, bf16[16,128,128]{2,1,0:T(8,128)(2,1)}, u32[]{:S(2)}) copy-start(bf16[16,128,128]{2,1,0:T(8,128)(2,1)} %copy-done.13) | copy-start | bytes 1572868
  51.5 27.6 %copy-start = (f32[4,256,512]{2,1,0:T(8,128)}, f32[4,256,512]{2,1,0:T(8,128)S(1)}, u32[]{:S(2)}) copy-start(f32[4,256,512]{2,1,0:T(8,128)S(1)} %get-tuple-element.30.refs_0_.mask_ref) | copy-start | bytes 6291460
  51.5 12.5 %collective-permute-start.9 = (bf16[16,128,128]{2,1,0:T(8,128)(2,1)}, bf16[16,128,128]{2,1,0:T(8,128)(2,1)S(1)}, u32[]{:S(2)}, u32[]{:S(2)}) collective-permute-start(bf16[16,128,128]{2,1,0:T(8,128)(2,1)} %collective-permute-done.8.refs_3_), channel_id=1, source_target_pairs={{0,4},{4,0},{8,12},{12,8},{16,20},{20,16},{24,28},{28,24},{32,36},... | collective-permute-start | bytes 1572872 | tf_op jit(solution)/shard_map/ppermute | solution.py:249
  52.7 8.0 %collective-permute-start.12 = (bf16[8,128,128]{2,1,0:T(8,128)(2,1)S(1)}, bf16[8,128,128]{2,1,0:T(8,128)(2,1)S(1)}, u32[]{:S(2)}, u32[]{:S(2)}) collective-permute-start(bf16[8,128,128]{2,1,0:T(8,128)(2,1)S(1)} %half.1), channel_id=1, source_target_pairs={{0,8},{4,60},{8,16},{12,4},{16,24},{20,12},{24,32},{28,20},{32,40}... | collective-permute-start | bytes 786440 | tf_op jit(solution)/shard_map/ppermute | solution.py:249
  54.4 10.7 %collective-permute-start.18 = (bf16[16,128,128]{2,1,0:T(8,128)(2,1)}, bf16[16,128,128]{2,1,0:T(8,128)(2,1)S(1)}, u32[]{:S(2)}, u32[]{:S(2)}) collective-permute-start(bf16[16,128,128]{2,1,0:T(8,128)(2,1)} %collective-permute-done.16.refs_3_), channel_id=1, source_target_pairs={{0,8},{4,60},{8,16},{12,4},{16,24},{20,12},{24,32},{28,20},{32,40}... | collective-permute-start | bytes 1572872 | tf_op jit(solution)/shard_map/ppermute | solution.py:249
  60.7 8.0 %collective-permute-start.11 = (bf16[16,128,128]{2,1,0:T(8,128)(2,1)}, bf16[16,128,128]{2,1,0:T(8,128)(2,1)S(1)}, u32[]{:S(2)}, u32[]{:S(2)}) collective-permute-start(bf16[16,128,128]{2,1,0:T(8,128)(2,1)} %collective-permute-done.10.source_ref.refs_5_), channel_id=1, source_target_pairs={{0,4},{4,0},{8,12},{12,8},{16,20},{20,16},{24,28},{28,24},{32,36},... | collective-permute-start | bytes 1572872 | tf_op jit(solution)/shard_map/ppermute | solution.py:249
  60.7 3.4 %collective-permute-start.13 = (bf16[8,128,128]{2,1,0:T(8,128)(2,1)S(1)}, bf16[8,128,128]{2,1,0:T(8,128)(2,1)S(1)}, u32[]{:S(2)}, u32[]{:S(2)}) collective-permute-start(bf16[8,128,128]{2,1,0:T(8,128)(2,1)S(1)} %collective-permute-done.12.refs_7_), channel_id=1, source_target_pairs={{0,4},{4,0},{8,12},{12,8},{16,20},{20,16},{24,28},{28,24},{32,36},... | collective-permute-start | bytes 786440 | tf_op jit(solution)/shard_map/ppermute | solution.py:249
  64.0 44.7 %collective-permute-start.26 = (bf16[512,1024]{1,0:T(8,128)(2,1)}, bf16[512,1024]{1,0:T(8,128)(2,1)S(1)}, u32[]{:S(2)}, u32[]{:S(2)}) collective-permute-start(bf16[512,1024]{1,0:T(8,128)(2,1)} %get-tuple-element.37), channel_id=1, source_target_pairs={{2,0},{3,1},{0,2},{1,3},{6,4},{7,5},{4,6},{5,7},{10,8},{11,9},{8,1... | collective-permute-start | bytes 3145736 | tf_op jit(solution)/shard_map/ppermute | solution.py:223
  64.0 16.2 %collective-permute-start.15 = (bf16[16,128,128]{2,1,0:T(8,128)(2,1)}, bf16[16,128,128]{2,1,0:T(8,128)(2,1)S(1)}, u32[]{:S(2)}, u32[]{:S(2)}) collective-permute-start(bf16[16,128,128]{2,1,0:T(8,128)(2,1)} %collective-permute-done.14.refs_1_), channel_id=1, source_target_pairs={{0,4},{4,0},{8,12},{12,8},{16,20},{20,16},{24,28},{28,24},{32,36},... | collective-permute-start | bytes 1572872 | tf_op jit(solution)/shard_map/ppermute | solution.py:249
  64.1 16.0 %collective-permute-start.17 = (bf16[16,128,128]{2,1,0:T(8,128)(2,1)}, bf16[16,128,128]{2,1,0:T(8,128)(2,1)S(1)}, u32[]{:S(2)}, u32[]{:S(2)}) collective-permute-start(bf16[16,128,128]{2,1,0:T(8,128)(2,1)} %collective-permute-done.16.refs_3_), channel_id=1, source_target_pairs={{0,4},{4,0},{8,12},{12,8},{16,20},{20,16},{24,28},{28,24},{32,36},... | collective-permute-start | bytes 1572872 | tf_op jit(solution)/shard_map/ppermute | solution.py:249
  65.1 15.0 %collective-permute-start.20 = (bf16[16,128,128]{2,1,0:T(8,128)(2,1)S(1)}, bf16[16,128,128]{2,1,0:T(8,128)(2,1)S(1)}, u32[]{:S(2)}, u32[]{:S(2)}) collective-permute-start(bf16[16,128,128]{2,1,0:T(8,128)(2,1)S(1)} %collective-permute-done.18.refs_5_), channel_id=1, source_target_pairs={{0,8},{4,60},{8,16},{12,4},{16,24},{20,12},{24,32},{28,20},{32,40}... | collective-permute-start | bytes 1572872 | tf_op jit(solution)/shard_map/ppermute | solution.py:249
  68.7 11.5 %collective-permute-start.19 = (bf16[16,128,128]{2,1,0:T(8,128)(2,1)S(1)}, bf16[16,128,128]{2,1,0:T(8,128)(2,1)S(1)}, u32[]{:S(2)}, u32[]{:S(2)}) collective-permute-start(bf16[16,128,128]{2,1,0:T(8,128)(2,1)S(1)} %collective-permute-done.18.refs_5_), channel_id=1, source_target_pairs={{0,4},{4,0},{8,12},{12,8},{16,20},{20,16},{24,28},{28,24},{32,36},... | collective-permute-start | bytes 1572872 | tf_op jit(solution)/shard_map/ppermute | solution.py:249
  87.8 22.3 %collective-permute-start.29 = (bf16[256,512]{1,0:T(8,128)(2,1)S(1)}, bf16[256,512]{1,0:T(8,128)(2,1)S(1)}, u32[]{:S(2)}, u32[]{:S(2)}) collective-permute-start(bf16[256,512]{1,0:T(8,128)(2,1)S(1)} %get-tuple-element.38.a0), channel_id=1, source_target_pairs={{3,0},{0,1},{1,2},{2,3},{7,4},{4,5},{5,6},{6,7},{11,8},{8,9},{9,10... | collective-permute-start | bytes 786440 | tf_op jit(solution)/shard_map/ppermute | solution.py:223
  89.4 22.6 %collective-permute-start.28 = (bf16[256,512]{1,0:T(8,128)(2,1)S(1)}, bf16[256,512]{1,0:T(8,128)(2,1)S(1)}, u32[]{:S(2)}, u32[]{:S(2)}) collective-permute-start(bf16[256,512]{1,0:T(8,128)(2,1)S(1)} %get-tuple-element.38.a0), channel_id=1, source_target_pairs={{2,0},{3,1},{0,2},{1,3},{6,4},{7,5},{4,6},{5,7},{10,8},{11,9},{8,1... | collective-permute-start | bytes 786440 | tf_op jit(solution)/shard_map/ppermute | solution.py:223
  91.0 21.0 %collective-permute-start.27 = (bf16[256,512]{1,0:T(8,128)(2,1)S(1)}, bf16[256,512]{1,0:T(8,128)(2,1)S(1)}, u32[]{:S(2)}, u32[]{:S(2)}) collective-permute-start(bf16[256,512]{1,0:T(8,128)(2,1)S(1)} %get-tuple-element.38.a0), channel_id=1, source_target_pairs={{1,0},{2,1},{3,2},{0,3},{5,4},{6,5},{7,6},{4,7},{9,8},{10,9},{11,1... | collective-permute-start | bytes 786440 | tf_op jit(solution)/shard_map/ppermute | solution.py:223
  108.5 14.8 %collective-permute-start.25 = (bf16[256,512]{1,0:T(8,128)(2,1)S(1)}, bf16[256,512]{1,0:T(8,128)(2,1)S(1)}, u32[]{:S(2)}, u32[]{:S(2)}) collective-permute-start(bf16[256,512]{1,0:T(8,128)(2,1)S(1)} %attend1.1.a0), channel_id=1, source_target_pairs={{3,0},{0,1},{1,2},{2,3},{7,4},{4,5},{5,6},{6,7},{11,8},{8,9},{9,10... | collective-permute-start | bytes 786440 | tf_op jit(solution)/shard_map/ppermute | solution.py:223
  108.6 14.7 %collective-permute-start.24 = (bf16[256,512]{1,0:T(8,128)(2,1)S(1)}, bf16[256,512]{1,0:T(8,128)(2,1)S(1)}, u32[]{:S(2)}, u32[]{:S(2)}) collective-permute-start(bf16[256,512]{1,0:T(8,128)(2,1)S(1)} %attend1.1.a0), channel_id=1, source_target_pairs={{2,0},{3,1},{0,2},{1,3},{6,4},{7,5},{4,6},{5,7},{10,8},{11,9},{8,1... | collective-permute-start | bytes 786440 | tf_op jit(solution)/shard_map/ppermute | solution.py:223
  110.1 13.8 %collective-permute-start.23 = (bf16[256,512]{1,0:T(8,128)(2,1)S(1)}, bf16[256,512]{1,0:T(8,128)(2,1)S(1)}, u32[]{:S(2)}, u32[]{:S(2)}) collective-permute-start(bf16[256,512]{1,0:T(8,128)(2,1)S(1)} %attend1.1.a0), channel_id=1, source_target_pairs={{1,0},{2,1},{3,2},{0,3},{5,4},{6,5},{7,6},{4,7},{9,8},{10,9},{11,1... | collective-permute-start | bytes 786440 | tf_op jit(solution)/shard_map/ppermute | solution.py:223
  (20 other events, 222.9 us)

commit v9 on v6

--- a/solution.py
+++ b/solution.py
@@ -20,7 +20,7 @@
 X_CHIPS = 4
 HEADS = 4
 EXP_SCALE = math.log2(math.e) * HEAD ** (-0.5)
-VMEM_LIMIT = 48 * 1024 * 1024
+VMEM_LIMIT = 24 * 1024 * 1024
 
 SMEM = functools.partial(pl.BlockSpec, memory_space=pltpu.SMEM)
 VMEM = functools.partial(pl.BlockSpec, memory_space=pltpu.VMEM)

time: 130 us -> 119 us (0.915)
  Pallas kernels: 45.9 us -> 34.5 us
  starting transfers between devices: 43.1 us -> 49.8 us
  waiting for transfers between devices: 33.2 us -> 28.7 us
    ppermute x19, starting transfers between devices: 25 us -> 31.5 us  [gather_columns(): send = lambda a, r: lax.ppermute(a, 'ctx', r)]
    pallas_call x2, Pallas kernels: 22.2 us -> 17.3 us  [per_device(): pl.pallas_call(functools.partial(out_kernel, ctx_count, st, len(v_pieces)...]
    pallas_call x1, Pallas kernels: 4.88 us -> 0.33 us  [per_device(): pl.pallas_call(functools.partial(slab_kernel, tp), grid=(depth // 128,),...]
    ppermute x9, waiting for transfers between devices: 16.4 us -> 13.8 us  [from_ahead(): return lax.ppermute(x, axis, [((i + shift) % n, i) for i in range(n)])]
    pallas_call x1, Pallas kernels: 9.82 us -> 7.93 us  [per_device(): pl.pallas_call(top_kernel, out_shape=[shape((ROOM, BLOCK, HEAD), BF16), s...]
    ppermute x19, waiting for transfers between devices: 16.8 us -> 15 us  [gather_columns(): send = lambda a, r: lax.ppermute(a, 'ctx', r)]
    unnamed x38 -> x18, local copies, waits for them, and re-layouts: 5.37 us -> 4.58 us
  transfers between devices with their start and end apart: 30 -> 30, of which waited for: 11 -> 12; matrix products, arithmetic and copies ran while one was open for 0% -> 0% of each run, Pallas kernels for 33% -> 26%
where the time goes in v9:
time: 119 us; the launch traced here: 118 us
  starting transfers between devices  49.8 us (42%)
  Pallas kernels  34.5 us (29%)
  waiting for transfers between devices  28.7 us (24%)
  local copies, waits for them, and re-layouts  4.68 us (4%)
    ppermute x19, starting transfers between devices, gather_columns(): send = lambda a, r: lax.ppermute(a, 'ctx', r)  31.5 us
    pallas_call x2, Pallas kernels, per_device(): pl.pallas_call(functools.partial(out_kernel, ctx_count, st, len(v_pieces)...  17.3 us
    ppermute x19, waiting for transfers between devices, gather_columns(): send = lambda a, r: lax.ppermute(a, 'ctx', r)  15 us
    ppermute x9, waiting for transfers between devices, from_ahead(): return lax.ppermute(x, axis, [((i + shift) % n, i) for i in range(n)])  13.8 us
    ppermute x9, starting transfers between devices, from_ahead(): return lax.ppermute(x, axis, [((i + shift) % n, i) for i in range(n)])  12.8 us
    pallas_call x1, Pallas kernels, per_device(): pl.pallas_call(top_kernel, out_shape=[shape((ROOM, BLOCK, HEAD), BF16), s...  7.93 us
    pallas_call x2, Pallas kernels, per_device(): pl.pallas_call(mix_kernel, grid=(width // tile,), out_shape=shape((2, STR...  6.18 us
    unnamed x18, local copies, waits for them, and re-layouts  4.58 us
  transfers between devices with their start and end apart: 30, of which 12 were waited for; matrix products, arithmetic and copies ran while one was open for 0% of the time, Pallas kernels for 26%

profile of v9, /device:TPU:96, one launch (start us, length us, event | category | flops | bytes accessed | tf_op | source)
XLA Modules:
  0.0 118.0 jit_solution(3507985899737993300)
XLA Ops:
  3.1 1.6 %collective-permute-start.4 = (bf16[2,2,128,128]{3,2,1,0:T(8,128)(2,1)S(1)}, bf16[2,2,128,128]{3,2,1,0:T(8,128)(2,1)S(1)}, u32[]{:S(2)}, u32[]{:S(2)}) collective-permute-start(bf16[2,2,128,128]{3,2,1,0:T(8,128)(2,1)S(1)} %get-tuple-element.29.refs_0_), channel_id=1, source_target_pairs={{0,64},{4,68},{8,72},{12,76},{16,80},{20,84},{24,88},{28,92},{32,9... | collective-permute-start | bytes 393224 | tf_op jit(solution)/shard_map/ppermute | solution.py:249
  4.6 2.7 %collective-permute-start.3 = (bf16[2,2,128,128]{3,2,1,0:T(8,128)(2,1)S(1)}, bf16[2,2,128,128]{3,2,1,0:T(8,128)(2,1)S(1)}, u32[]{:S(2)}, u32[]{:S(2)}) collective-permute-start(bf16[2,2,128,128]{3,2,1,0:T(8,128)(2,1)S(1)} %get-tuple-element.29.refs_0_), channel_id=1, source_target_pairs={{0,128},{4,132},{8,136},{12,140},{16,144},{20,148},{24,152},{28,15... | collective-permute-start | bytes 393224 | tf_op jit(solution)/shard_map/ppermute | solution.py:249
  7.4 1.4 %collective-permute-start.2 = (bf16[2,2,128,128]{3,2,1,0:T(8,128)(2,1)S(1)}, bf16[2,2,128,128]{3,2,1,0:T(8,128)(2,1)S(1)}, u32[]{:S(2)}, u32[]{:S(2)}) collective-permute-start(bf16[2,2,128,128]{3,2,1,0:T(8,128)(2,1)S(1)} %get-tuple-element.29.refs_0_), channel_id=1, source_target_pairs={{0,192},{4,196},{8,200},{12,204},{16,208},{20,212},{24,216},{28,22... | collective-permute-start | bytes 393224 | tf_op jit(solution)/shard_map/ppermute | solution.py:249
  9.8 3.6 %collective-permute-done.3.refs_2_ = bf16[2,2,128,128]{3,2,1,0:T(8,128)(2,1)S(1)} collective-permute-done((bf16[2,2,128,128]{3,2,1,0:T(8,128)(2,1)S(1)}, bf16[2,2,128,128]{3,2,1,0:T(8,128)(2,1)S(1)}, u32[]{:S(2)}, u32[]{:S(2)}) %collective-permute-start.3) | collective-permute-done | bytes 131104 | tf_op jit(solution)/shard_map/ppermute | solution.py:249
  13.5 1.9 %collective-permute-done.5.other_ref = bf16[2,8,128,128]{3,2,1,0:T(8,128)(2,1)S(1)} collective-permute-done((bf16[2,8,128,128]{3,2,1,0:T(8,128)(2,1)S(1)}, bf16[2,8,128,128]{3,2,1,0:T(8,128)(2,1)S(1)}, u32[]{:S(2)}, u32[]{:S(2)}) %collective-permute-start.5) | collective-permute-done | bytes 524320 | tf_op jit(solution)/shard_map/ppermute | solution.py:249
  15.5 3.2 %collective-permute-start.6 = (bf16[16,128,128]{2,1,0:T(8,128)(2,1)S(1)}, bf16[16,128,128]{2,1,0:T(8,128)(2,1)S(1)}, u32[]{:S(2)}, u32[]{:S(2)}) collective-permute-start(bf16[16,128,128]{2,1,0:T(8,128)(2,1)S(1)} %chip0.1.refs_0_), channel_id=1, source_target_pairs={{0,8},{4,60},{8,16},{12,4},{16,24},{20,12},{24,32},{28,20},{32,40}... | collective-permute-start | bytes 1572872 | tf_op jit(solution)/shard_map/ppermute | solution.py:249
  18.7 1.9 %collective-permute-start = (bf16[2,256,128]{2,1,0:T(8,128)(2,1)S(1)}, bf16[2,256,128]{2,1,0:T(8,128)(2,1)S(1)}, u32[]{:S(2)}, u32[]{:S(2)}) collective-permute-start(bf16[2,256,128]{2,1,0:T(8,128)(2,1)S(1)} %get-tuple-element.26), channel_id=1, source_target_pairs={{0,4},{4,8},{8,12},{12,16},{16,20},{20,24},{24,28},{28,32},{32,36}... | collective-permute-start | bytes 393224 | tf_op jit(solution)/shard_map/ppermute | solution.py:351
  20.6 3.6 %collective-permute-start.1 = (bf16[2,256,128]{2,1,0:T(8,128)(2,1)S(1)}, bf16[2,256,128]{2,1,0:T(8,128)(2,1)S(1)}, u32[]{:S(2)}, u32[]{:S(2)}) collective-permute-start(bf16[2,256,128]{2,1,0:T(8,128)(2,1)S(1)} %get-tuple-element.27), channel_id=1, source_target_pairs={{4,0},{8,4},{12,8},{16,12},{20,16},{24,20},{28,24},{32,28},{36,32}... | collective-permute-start | bytes 393224 | tf_op jit(solution)/shard_map/ppermute | solution.py:352
  24.6 2.1 %collective-permute-done.6.refs_1_.refs_0_ = bf16[16,128,128]{2,1,0:T(8,128)(2,1)S(1)} collective-permute-done((bf16[16,128,128]{2,1,0:T(8,128)(2,1)S(1)}, bf16[16,128,128]{2,1,0:T(8,128)(2,1)S(1)}, u32[]{:S(2)}, u32[]{:S(2)}) %collective-permute-start.6) | collective-permute-done | bytes 524320 | tf_op jit(solution)/shard_map/ppermute | solution.py:249
  26.8 3.7 %collective-permute-start.8 = (bf16[16,128,128]{2,1,0:T(8,128)(2,1)S(1)}, bf16[16,128,128]{2,1,0:T(8,128)(2,1)S(1)}, u32[]{:S(2)}, u32[]{:S(2)}) collective-permute-start(bf16[16,128,128]{2,1,0:T(8,128)(2,1)S(1)} %collective-permute-done.6.refs_1_.refs_0_), channel_id=1, source_target_pairs={{0,8},{4,60},{8,16},{12,4},{16,24},{20,12},{24,32},{28,20},{32,40}... | collective-permute-start | bytes 1572872 | tf_op jit(solution)/shard_map/ppermute | solution.py:249
  30.5 1.9 %band.1 = (f32[4,256,512]{2,1,0:T(8,128)S(1)}, f32[2,4,256,128]{3,2,1,0:T(8,128)S(1)}) custom-call(s32[1,16]{1,0:T(1,128)S(1)} %get-tuple-element.22.meta_ref, s32[4,64]{1,0:T(4,128)S(1)} %copy-done.8, bf16[2,256,512]{2,1,0:T(8,128)(2,1)S(1)} %bitcast.9, bf16[2,256,128]{2,1,0:T(8,128)(2,1)S(1)} %bitcast.14, ...), custom_call_target="tpu_custom_call" | custom-call | bytes 9000000 | tf_op jit(solution)/shard_map/band/pallas_call | solution.py:354
  32.5 2.0 %copy-done.1 = bf16[512,4096]{1,0:T(8,128)(2,1)S(1)} copy-done((bf16[512,4096]{1,0:T(8,128)(2,1)S(1)}, bf16[512,4096]{1,0:T(8,128)(2,1)}, u32[]{:S(2)}) %copy-start.1) | copy-done | bytes 4194328
  34.9 3.1 %collective-permute-start.21 = (bf16[512,1024]{1,0:T(8,128)(2,1)S(1)}, bf16[512,1024]{1,0:T(8,128)(2,1)S(1)}, u32[]{:S(2)}, u32[]{:S(2)}) collective-permute-start(bf16[512,1024]{1,0:T(8,128)(2,1)S(1)} %get-tuple-element.33), channel_id=1, source_target_pairs={{1,0},{2,1},{3,2},{0,3},{5,4},{6,5},{7,6},{4,7},{9,8},{10,9},{11,1... | collective-permute-start | bytes 3145736 | tf_op jit(solution)/shard_map/ppermute | solution.py:223
  38.0 2.8 %collective-permute-start.10 = (bf16[16,128,128]{2,1,0:T(8,128)(2,1)S(1)}, bf16[16,128,128]{2,1,0:T(8,128)(2,1)S(1)}, u32[]{:S(2)}, u32[]{:S(2)}) collective-permute-start(bf16[16,128,128]{2,1,0:T(8,128)(2,1)S(1)} %collective-permute-done.8.refs_3_), channel_id=1, source_target_pairs={{0,8},{4,60},{8,16},{12,4},{16,24},{20,12},{24,32},{28,20},{32,40}... | collective-permute-start | bytes 1572872 | tf_op jit(solution)/shard_map/ppermute | solution.py:249
  40.9 1.9 %collective-permute-done.14.refs_1_ = bf16[16,128,128]{2,1,0:T(8,128)(2,1)S(1)} collective-permute-done((bf16[16,128,128]{2,1,0:T(8,128)(2,1)S(1)}, bf16[16,128,128]{2,1,0:T(8,128)(2,1)S(1)}, u32[]{:S(2)}, u32[]{:S(2)}) %collective-permute-start.14) | collective-permute-done | bytes 524320 | tf_op jit(solution)/shard_map/ppermute | solution.py:249
  42.8 3.7 %collective-permute-start.16 = (bf16[16,128,128]{2,1,0:T(8,128)(2,1)S(1)}, bf16[16,128,128]{2,1,0:T(8,128)(2,1)S(1)}, u32[]{:S(2)}, u32[]{:S(2)}) collective-permute-start(bf16[16,128,128]{2,1,0:T(8,128)(2,1)S(1)} %collective-permute-done.14.refs_1_), channel_id=1, source_target_pairs={{0,8},{4,60},{8,16},{12,4},{16,24},{20,12},{24,32},{28,20},{32,40}... | collective-permute-start | bytes 1572872 | tf_op jit(solution)/shard_map/ppermute | solution.py:249
  46.5 1.9 %collective-permute-done.10.source_ref.refs_5_ = bf16[16,128,128]{2,1,0:T(8,128)(2,1)S(1)} collective-permute-done((bf16[16,128,128]{2,1,0:T(8,128)(2,1)S(1)}, bf16[16,128,128]{2,1,0:T(8,128)(2,1)S(1)}, u32[]{:S(2)}, u32[]{:S(2)}) %collective-permute-start.10) | collective-permute-done | bytes 524320 | tf_op jit(solution)/shard_map/ppermute | solution.py:249
  48.4 3.8 %collective-permute-start.12 = (bf16[8,128,128]{2,1,0:T(8,128)(2,1)S(1)}, bf16[8,128,128]{2,1,0:T(8,128)(2,1)S(1)}, u32[]{:S(2)}, u32[]{:S(2)}) collective-permute-start(bf16[8,128,128]{2,1,0:T(8,128)(2,1)S(1)} %half.1), channel_id=1, source_target_pairs={{0,8},{4,60},{8,16},{12,4},{16,24},{20,12},{24,32},{28,20},{32,40}... | collective-permute-start | bytes 786440 | tf_op jit(solution)/shard_map/ppermute | solution.py:249
  52.2 1.8 %collective-permute-done.16.refs_3_ = bf16[16,128,128]{2,1,0:T(8,128)(2,1)S(1)} collective-permute-done((bf16[16,128,128]{2,1,0:T(8,128)(2,1)S(1)}, bf16[16,128,128]{2,1,0:T(8,128)(2,1)S(1)}, u32[]{:S(2)}, u32[]{:S(2)}) %collective-permute-start.16) | collective-permute-done | bytes 524320 | tf_op jit(solution)/shard_map/ppermute | solution.py:249
  54.0 3.7 %collective-permute-start.18 = (bf16[16,128,128]{2,1,0:T(8,128)(2,1)S(1)}, bf16[16,128,128]{2,1,0:T(8,128)(2,1)S(1)}, u32[]{:S(2)}, u32[]{:S(2)}) collective-permute-start(bf16[16,128,128]{2,1,0:T(8,128)(2,1)S(1)} %collective-permute-done.16.refs_3_), channel_id=1, source_target_pairs={{0,8},{4,60},{8,16},{12,4},{16,24},{20,12},{24,32},{28,20},{32,40}... | collective-permute-start | bytes 1572872 | tf_op jit(solution)/shard_map/ppermute | solution.py:249
  57.7 2.1 %collective-permute-done.21.refs_8_.w1 = bf16[512,1024]{1,0:T(8,128)(2,1)S(1)} collective-permute-done((bf16[512,1024]{1,0:T(8,128)(2,1)S(1)}, bf16[512,1024]{1,0:T(8,128)(2,1)S(1)}, u32[]{:S(2)}, u32[]{:S(2)}) %collective-permute-start.21) | collective-permute-done | bytes 1048608 | tf_op jit(solution)/shard_map/ppermute | solution.py:223
  60.3 2.9 %collective-permute-done.22.refs_9_.w3 = bf16[512,1024]{1,0:T(8,128)(2,1)S(1)} collective-permute-done((bf16[512,1024]{1,0:T(8,128)(2,1)S(1)}, bf16[512,1024]{1,0:T(8,128)(2,1)S(1)}, u32[]{:S(2)}, u32[]{:S(2)}) %collective-permute-start.22) | collective-permute-done | bytes 1048608 | tf_op jit(solution)/shard_map/ppermute | solution.py:223
  64.4 3.7 %collective-permute-start.20 = (bf16[16,128,128]{2,1,0:T(8,128)(2,1)S(1)}, bf16[16,128,128]{2,1,0:T(8,128)(2,1)S(1)}, u32[]{:S(2)}, u32[]{:S(2)}) collective-permute-start(bf16[16,128,128]{2,1,0:T(8,128)(2,1)S(1)} %collective-permute-done.18.refs_5_), channel_id=1, source_target_pairs={{0,8},{4,60},{8,16},{12,4},{16,24},{20,12},{24,32},{28,20},{32,40}... | collective-permute-start | bytes 1572872 | tf_op jit(solution)/shard_map/ppermute | solution.py:249
  68.1 7.9 %top.1 = (bf16[65,128,128]{2,1,0:T(8,128)(2,1)S(1)}, f32[2,4,256,128]{3,2,1,0:T(8,128)S(1)}) custom-call(s32[1,16]{1,0:T(1,128)S(1)} %get-tuple-element.22.meta_ref, s32[1,64]{1,0:T(1,128)S(1)} %get-tuple-element.23.blk_ref, s32[1,128]{1,0:T(1,128)S(1)} %get-tuple-element.25.at_ref, bf16[2,256,512]{2,1,0:T(8,128)(2,1)S(1)} %bitcast.10, ...), custom_call_target="tpu_custom_call" | custom-call | bytes 27000000 | tf_op jit(solution)/shard_map/top/pallas_call | solution.py:380
  76.1 4.2 %attend0.1 = (bf16[256,512]{1,0:T(8,128)(2,1)S(1)}, bf16[65,128,128]{2,1,0:T(8,128)(2,1)S(1)}) custom-call(s32[1,16]{1,0:T(1,128)S(1)} %get-tuple-element.22.meta_ref, s32[1,64]{1,0:T(1,128)S(1)} %get-tuple-element.23.blk_ref, s32[1,128]{1,0:T(1,128)S(1)} %get-tuple-element.24.at_ref, bf16[2,256,512]{2,1,0:T(8,128)(2,1)S(1)} %bitcast.11, ...), custom_call_target="tpu_custom_call" | custom-call | bytes 24000000 | tf_op jit(solution)/shard_map/attend0/pallas_call | solution.py:394
  80.3 1.9 %collective-permute-start.29 = (bf16[256,512]{1,0:T(8,128)(2,1)S(1)}, bf16[256,512]{1,0:T(8,128)(2,1)S(1)}, u32[]{:S(2)}, u32[]{:S(2)}) collective-permute-start(bf16[256,512]{1,0:T(8,128)(2,1)S(1)} %get-tuple-element.38.a0), channel_id=1, source_target_pairs={{3,0},{0,1},{1,2},{2,3},{7,4},{4,5},{5,6},{6,7},{11,8},{8,9},{9,10... | collective-permute-start | bytes 786440 | tf_op jit(solution)/shard_map/ppermute | solution.py:223
  82.2 2.9 %collective-permute-start.28 = (bf16[256,512]{1,0:T(8,128)(2,1)S(1)}, bf16[256,512]{1,0:T(8,128)(2,1)S(1)}, u32[]{:S(2)}, u32[]{:S(2)}) collective-permute-start(bf16[256,512]{1,0:T(8,128)(2,1)S(1)} %get-tuple-element.38.a0), channel_id=1, source_target_pairs={{2,0},{3,1},{0,2},{1,3},{6,4},{7,5},{4,6},{5,7},{10,8},{11,9},{8,1... | collective-permute-start | bytes 786440 | tf_op jit(solution)/shard_map/ppermute | solution.py:223
  86.4 13.1 %attend1.1.a0 = bf16[256,512]{1,0:T(8,128)(2,1)S(1)} custom-call(s32[1,16]{1,0:T(1,128)S(1)} %get-tuple-element.22.meta_ref, s32[1,64]{1,0:T(1,128)S(1)} %get-tuple-element.23.blk_ref, s32[1,128]{1,0:T(1,128)S(1)} %get-tuple-element.24.at_ref, bf16[2,256,512]{2,1,0:T(8,128)(2,1)S(1)} %bitcast.12, bf16[65,128,128]{2,1,0:T(8,128)(2,1)S(1)} %get-tuple-element.30.keys_ref, ...), custom_call_target="tpu_custom_call" | custom-call | bytes 24000000 | tf_op jit(solution)/shard_map/attend1/pallas_call | solution.py:394
  101.1 2.0 %collective-permute-start.23 = (bf16[256,512]{1,0:T(8,128)(2,1)S(1)}, bf16[256,512]{1,0:T(8,128)(2,1)S(1)}, u32[]{:S(2)}, u32[]{:S(2)}) collective-permute-start(bf16[256,512]{1,0:T(8,128)(2,1)S(1)} %attend1.1.a0), channel_id=1, source_target_pairs={{1,0},{2,1},{3,2},{0,3},{5,4},{6,5},{7,6},{4,7},{9,8},{10,9},{11,1... | collective-permute-start | bytes 786440 | tf_op jit(solution)/shard_map/ppermute | solution.py:223
  103.1 3.1 %mix0.1.refs_0_ = bf16[2,256,1024]{2,1,0:T(8,128)(2,1)} custom-call(bf16[256,512]{1,0:T(8,128)(2,1)S(1)} %get-tuple-element.38.a0, bf16[256,512]{1,0:T(8,128)(2,1)S(1)} %collective-permute-done.27.a1, bf16[256,512]{1,0:T(8,128)(2,1)S(1)} %collective-permute-done.28.a2, bf16[256,512]{1,0:T(8,128)(2,1)S(1)} %collective-permute-done.29.a3, ...), custom_call_target="tpu_custom_call" | custom-call | bytes 9000000 | tf_op jit(solution)/shard_map/mix0/pallas_call | solution.py:419
  106.2 8.1 %collective-permute-done.25.a3 = bf16[256,512]{1,0:T(8,128)(2,1)S(1)} collective-permute-done((bf16[256,512]{1,0:T(8,128)(2,1)S(1)}, bf16[256,512]{1,0:T(8,128)(2,1)S(1)}, u32[]{:S(2)}, u32[]{:S(2)}) %collective-permute-start.25) | collective-permute-done | bytes 262176 | tf_op jit(solution)/shard_map/ppermute | solution.py:223
  114.9 3.1 %mix1.1 = bf16[2,256,1024]{2,1,0:T(8,128)(2,1)} custom-call(bf16[256,512]{1,0:T(8,128)(2,1)S(1)} %attend1.1.a0, bf16[256,512]{1,0:T(8,128)(2,1)S(1)} %collective-permute-done.23.a1, bf16[256,512]{1,0:T(8,128)(2,1)S(1)} %collective-permute-done.24.a2, bf16[256,512]{1,0:T(8,128)(2,1)S(1)} %collective-permute-done.25.a3, ...), custom_call_target="tpu_custom_call", output_to_operand_aliasing={{}: (8, {})} | custom-call | bytes 9000000 | tf_op jit(solution)/shard_map/mix1/pallas_call | solution.py:419
  (60 shorter events, 10.3 us)
Async XLA Ops:
  0.0 30.5 %copy-start = (bf16[1,2,256,512]{3,2,1,0:T(8,128)(2,1)S(1)}, bf16[1,2,256,512]{3,2,1,0:T(8,128)(2,1)}, u32[]{:S(2)}) copy-start(bf16[1,2,256,512]{3,2,1,0:T(8,128)(2,1)} %param.6) | copy-start | bytes 1572868
  2.5 28.0 %copy-start.8 = (s32[4,64]{1,0:T(4,128)S(1)}, s32[4,64]{1,0:T(4,128)}, u32[]{:S(2)}) copy-start(s32[4,64]{1,0:T(4,128)} %slash_ref.1) | copy-start | bytes 3076
  3.1 6.7 %collective-permute-start.4 = (bf16[2,2,128,128]{3,2,1,0:T(8,128)(2,1)S(1)}, bf16[2,2,128,128]{3,2,1,0:T(8,128)(2,1)S(1)}, u32[]{:S(2)}, u32[]{:S(2)}) collective-permute-start(bf16[2,2,128,128]{3,2,1,0:T(8,128)(2,1)S(1)} %get-tuple-element.29.refs_0_), channel_id=1, source_target_pairs={{0,64},{4,68},{8,72},{12,76},{16,80},{20,84},{24,88},{28,92},{32,9... | collective-permute-start | bytes 393224 | tf_op jit(solution)/shard_map/ppermute | solution.py:249
  4.6 8.7 %collective-permute-start.3 = (bf16[2,2,128,128]{3,2,1,0:T(8,128)(2,1)S(1)}, bf16[2,2,128,128]{3,2,1,0:T(8,128)(2,1)S(1)}, u32[]{:S(2)}, u32[]{:S(2)}) collective-permute-start(bf16[2,2,128,128]{3,2,1,0:T(8,128)(2,1)S(1)} %get-tuple-element.29.refs_0_), channel_id=1, source_target_pairs={{0,128},{4,132},{8,136},{12,140},{16,144},{20,148},{24,152},{28,15... | collective-permute-start | bytes 393224 | tf_op jit(solution)/shard_map/ppermute | solution.py:249
  7.4 6.0 %collective-permute-start.2 = (bf16[2,2,128,128]{3,2,1,0:T(8,128)(2,1)S(1)}, bf16[2,2,128,128]{3,2,1,0:T(8,128)(2,1)S(1)}, u32[]{:S(2)}, u32[]{:S(2)}) collective-permute-start(bf16[2,2,128,128]{3,2,1,0:T(8,128)(2,1)S(1)} %get-tuple-element.29.refs_0_), channel_id=1, source_target_pairs={{0,192},{4,196},{8,200},{12,204},{16,208},{20,212},{24,216},{28,22... | collective-permute-start | bytes 393224 | tf_op jit(solution)/shard_map/ppermute | solution.py:249
  13.4 2.0 %collective-permute-start.5 = (bf16[2,8,128,128]{3,2,1,0:T(8,128)(2,1)S(1)}, bf16[2,8,128,128]{3,2,1,0:T(8,128)(2,1)S(1)}, u32[]{:S(2)}, u32[]{:S(2)}) collective-permute-start(bf16[2,8,128,128]{3,2,1,0:T(8,128)(2,1)S(1)} %line.1.own_ref), channel_id=1, source_target_pairs={{0,4},{4,0},{8,12},{12,8},{16,20},{20,16},{24,28},{28,24},{32,36},... | collective-permute-start | bytes 1572872 | tf_op jit(solution)/shard_map/ppermute | solution.py:249
  15.5 11.3 %collective-permute-start.6 = (bf16[16,128,128]{2,1,0:T(8,128)(2,1)S(1)}, bf16[16,128,128]{2,1,0:T(8,128)(2,1)S(1)}, u32[]{:S(2)}, u32[]{:S(2)}) collective-permute-start(bf16[16,128,128]{2,1,0:T(8,128)(2,1)S(1)} %chip0.1.refs_0_), channel_id=1, source_target_pairs={{0,8},{4,60},{8,16},{12,4},{16,24},{20,12},{24,32},{28,20},{32,40}... | collective-permute-start | bytes 1572872 | tf_op jit(solution)/shard_map/ppermute | solution.py:249
  18.7 11.8 %collective-permute-start = (bf16[2,256,128]{2,1,0:T(8,128)(2,1)S(1)}, bf16[2,256,128]{2,1,0:T(8,128)(2,1)S(1)}, u32[]{:S(2)}, u32[]{:S(2)}) collective-permute-start(bf16[2,256,128]{2,1,0:T(8,128)(2,1)S(1)} %get-tuple-element.26), channel_id=1, source_target_pairs={{0,4},{4,8},{8,12},{12,16},{16,20},{20,24},{24,28},{28,32},{32,36}... | collective-permute-start | bytes 393224 | tf_op jit(solution)/shard_map/ppermute | solution.py:351
  20.6 9.9 %collective-permute-start.1 = (bf16[2,256,128]{2,1,0:T(8,128)(2,1)S(1)}, bf16[2,256,128]{2,1,0:T(8,128)(2,1)S(1)}, u32[]{:S(2)}, u32[]{:S(2)}) collective-permute-start(bf16[2,256,128]{2,1,0:T(8,128)(2,1)S(1)} %get-tuple-element.27), channel_id=1, source_target_pairs={{4,0},{8,4},{12,8},{16,12},{20,16},{24,20},{28,24},{32,28},{36,32}... | collective-permute-start | bytes 393224 | tf_op jit(solution)/shard_map/ppermute | solution.py:352
  26.8 11.2 %collective-permute-start.8 = (bf16[16,128,128]{2,1,0:T(8,128)(2,1)S(1)}, bf16[16,128,128]{2,1,0:T(8,128)(2,1)S(1)}, u32[]{:S(2)}, u32[]{:S(2)}) collective-permute-start(bf16[16,128,128]{2,1,0:T(8,128)(2,1)S(1)} %collective-permute-done.6.refs_1_.refs_0_), channel_id=1, source_target_pairs={{0,8},{4,60},{8,16},{12,4},{16,24},{20,12},{24,32},{28,20},{32,40}... | collective-permute-start | bytes 1572872 | tf_op jit(solution)/shard_map/ppermute | solution.py:249
  32.5 10.3 %collective-permute-start.14 = (bf16[16,128,128]{2,1,0:T(8,128)(2,1)S(1)}, bf16[16,128,128]{2,1,0:T(8,128)(2,1)S(1)}, u32[]{:S(2)}, u32[]{:S(2)}) collective-permute-start(bf16[16,128,128]{2,1,0:T(8,128)(2,1)S(1)} %chip1.1.refs_0_), channel_id=1, source_target_pairs={{0,8},{4,60},{8,16},{12,4},{16,24},{20,12},{24,32},{28,20},{32,40}... | collective-permute-start | bytes 1572872 | tf_op jit(solution)/shard_map/ppermute | solution.py:249
  34.9 24.9 %collective-permute-start.21 = (bf16[512,1024]{1,0:T(8,128)(2,1)S(1)}, bf16[512,1024]{1,0:T(8,128)(2,1)S(1)}, u32[]{:S(2)}, u32[]{:S(2)}) collective-permute-start(bf16[512,1024]{1,0:T(8,128)(2,1)S(1)} %get-tuple-element.33), channel_id=1, source_target_pairs={{1,0},{2,1},{3,2},{0,3},{5,4},{6,5},{7,6},{4,7},{9,8},{10,9},{11,1... | collective-permute-start | bytes 3145736 | tf_op jit(solution)/shard_map/ppermute | solution.py:223
  38.0 25.2 %collective-permute-start.22 = (bf16[512,1024]{1,0:T(8,128)(2,1)S(1)}, bf16[512,1024]{1,0:T(8,128)(2,1)S(1)}, u32[]{:S(2)}, u32[]{:S(2)}) collective-permute-start(bf16[512,1024]{1,0:T(8,128)(2,1)S(1)} %get-tuple-element.34), channel_id=1, source_target_pairs={{3,0},{0,1},{1,2},{2,3},{7,4},{4,5},{5,6},{6,7},{11,8},{8,9},{9,10... | collective-permute-start | bytes 3145736 | tf_op jit(solution)/shard_map/ppermute | solution.py:223
  38.0 10.4 %collective-permute-start.10 = (bf16[16,128,128]{2,1,0:T(8,128)(2,1)S(1)}, bf16[16,128,128]{2,1,0:T(8,128)(2,1)S(1)}, u32[]{:S(2)}, u32[]{:S(2)}) collective-permute-start(bf16[16,128,128]{2,1,0:T(8,128)(2,1)S(1)} %collective-permute-done.8.refs_3_), channel_id=1, source_target_pairs={{0,8},{4,60},{8,16},{12,4},{16,24},{20,12},{24,32},{28,20},{32,40}... | collective-permute-start | bytes 1572872 | tf_op jit(solution)/shard_map/ppermute | solution.py:249
  40.9 7.6 %collective-permute-start.7 = (bf16[16,128,128]{2,1,0:T(8,128)(2,1)S(1)}, bf16[16,128,128]{2,1,0:T(8,128)(2,1)S(1)}, u32[]{:S(2)}, u32[]{:S(2)}) collective-permute-start(bf16[16,128,128]{2,1,0:T(8,128)(2,1)S(1)} %collective-permute-done.6.refs_1_.refs_0_), channel_id=1, source_target_pairs={{0,4},{4,0},{8,12},{12,8},{16,20},{20,16},{24,28},{28,24},{32,36},... | collective-permute-start | bytes 1572872 | tf_op jit(solution)/shard_map/ppermute | solution.py:249
  42.8 11.2 %collective-permute-start.16 = (bf16[16,128,128]{2,1,0:T(8,128)(2,1)S(1)}, bf16[16,128,128]{2,1,0:T(8,128)(2,1)S(1)}, u32[]{:S(2)}, u32[]{:S(2)}) collective-permute-start(bf16[16,128,128]{2,1,0:T(8,128)(2,1)S(1)} %collective-permute-done.14.refs_1_), channel_id=1, source_target_pairs={{0,8},{4,60},{8,16},{12,4},{16,24},{20,12},{24,32},{28,20},{32,40}... | collective-permute-start | bytes 1572872 | tf_op jit(solution)/shard_map/ppermute | solution.py:249
  48.4 14.8 %collective-permute-start.9 = (bf16[16,128,128]{2,1,0:T(8,128)(2,1)S(1)}, bf16[16,128,128]{2,1,0:T(8,128)(2,1)S(1)}, u32[]{:S(2)}, u32[]{:S(2)}) collective-permute-start(bf16[16,128,128]{2,1,0:T(8,128)(2,1)S(1)} %collective-permute-done.8.refs_3_), channel_id=1, source_target_pairs={{0,4},{4,0},{8,12},{12,8},{16,20},{20,16},{24,28},{28,24},{32,36},... | collective-permute-start | bytes 1572872 | tf_op jit(solution)/shard_map/ppermute | solution.py:249
  48.4 11.4 %collective-permute-start.12 = (bf16[8,128,128]{2,1,0:T(8,128)(2,1)S(1)}, bf16[8,128,128]{2,1,0:T(8,128)(2,1)S(1)}, u32[]{:S(2)}, u32[]{:S(2)}) collective-permute-start(bf16[8,128,128]{2,1,0:T(8,128)(2,1)S(1)} %half.1), channel_id=1, source_target_pairs={{0,8},{4,60},{8,16},{12,4},{16,24},{20,12},{24,32},{28,20},{32,40}... | collective-permute-start | bytes 786440 | tf_op jit(solution)/shard_map/ppermute | solution.py:249
  54.0 10.4 %collective-permute-start.18 = (bf16[16,128,128]{2,1,0:T(8,128)(2,1)S(1)}, bf16[16,128,128]{2,1,0:T(8,128)(2,1)S(1)}, u32[]{:S(2)}, u32[]{:S(2)}) collective-permute-start(bf16[16,128,128]{2,1,0:T(8,128)(2,1)S(1)} %collective-permute-done.16.refs_3_), channel_id=1, source_target_pairs={{0,8},{4,60},{8,16},{12,4},{16,24},{20,12},{24,32},{28,20},{32,40}... | collective-permute-start | bytes 1572872 | tf_op jit(solution)/shard_map/ppermute | solution.py:249
  59.8 8.3 %collective-permute-start.11 = (bf16[16,128,128]{2,1,0:T(8,128)(2,1)S(1)}, bf16[16,128,128]{2,1,0:T(8,128)(2,1)S(1)}, u32[]{:S(2)}, u32[]{:S(2)}) collective-permute-start(bf16[16,128,128]{2,1,0:T(8,128)(2,1)S(1)} %collective-permute-done.10.source_ref.refs_5_), channel_id=1, source_target_pairs={{0,4},{4,0},{8,12},{12,8},{16,20},{20,16},{24,28},{28,24},{32,36},... | collective-permute-start | bytes 1572872 | tf_op jit(solution)/shard_map/ppermute | solution.py:249
  59.8 3.4 %collective-permute-start.13 = (bf16[8,128,128]{2,1,0:T(8,128)(2,1)S(1)}, bf16[8,128,128]{2,1,0:T(8,128)(2,1)S(1)}, u32[]{:S(2)}, u32[]{:S(2)}) collective-permute-start(bf16[8,128,128]{2,1,0:T(8,128)(2,1)S(1)} %collective-permute-done.12.refs_7_), channel_id=1, source_target_pairs={{0,4},{4,0},{8,12},{12,8},{16,20},{20,16},{24,28},{28,24},{32,36},... | collective-permute-start | bytes 786440 | tf_op jit(solution)/shard_map/ppermute | solution.py:249
  63.2 37.0 %collective-permute-start.26 = (bf16[512,1024]{1,0:T(8,128)(2,1)S(1)}, bf16[512,1024]{1,0:T(8,128)(2,1)S(1)}, u32[]{:S(2)}, u32[]{:S(2)}) collective-permute-start(bf16[512,1024]{1,0:T(8,128)(2,1)S(1)} %get-tuple-element.37), channel_id=1, source_target_pairs={{2,0},{3,1},{0,2},{1,3},{6,4},{7,5},{4,6},{5,7},{10,8},{11,9},{8,1... | collective-permute-start | bytes 3145736 | tf_op jit(solution)/shard_map/ppermute | solution.py:223
  63.2 12.8 %collective-permute-start.15 = (bf16[16,128,128]{2,1,0:T(8,128)(2,1)S(1)}, bf16[16,128,128]{2,1,0:T(8,128)(2,1)S(1)}, u32[]{:S(2)}, u32[]{:S(2)}) collective-permute-start(bf16[16,128,128]{2,1,0:T(8,128)(2,1)S(1)} %collective-permute-done.14.refs_1_), channel_id=1, source_target_pairs={{0,4},{4,0},{8,12},{12,8},{16,20},{20,16},{24,28},{28,24},{32,36},... | collective-permute-start | bytes 1572872 | tf_op jit(solution)/shard_map/ppermute | solution.py:249
  63.3 12.8 %collective-permute-start.17 = (bf16[16,128,128]{2,1,0:T(8,128)(2,1)S(1)}, bf16[16,128,128]{2,1,0:T(8,128)(2,1)S(1)}, u32[]{:S(2)}, u32[]{:S(2)}) collective-permute-start(bf16[16,128,128]{2,1,0:T(8,128)(2,1)S(1)} %collective-permute-done.16.refs_3_), channel_id=1, source_target_pairs={{0,4},{4,0},{8,12},{12,8},{16,20},{20,16},{24,28},{28,24},{32,36},... | collective-permute-start | bytes 1572872 | tf_op jit(solution)/shard_map/ppermute | solution.py:249
  64.4 11.7 %collective-permute-start.20 = (bf16[16,128,128]{2,1,0:T(8,128)(2,1)S(1)}, bf16[16,128,128]{2,1,0:T(8,128)(2,1)S(1)}, u32[]{:S(2)}, u32[]{:S(2)}) collective-permute-start(bf16[16,128,128]{2,1,0:T(8,128)(2,1)S(1)} %collective-permute-done.18.refs_5_), channel_id=1, source_target_pairs={{0,8},{4,60},{8,16},{12,4},{16,24},{20,12},{24,32},{28,20},{32,40}... | collective-permute-start | bytes 1572872 | tf_op jit(solution)/shard_map/ppermute | solution.py:249
  68.1 8.0 %collective-permute-start.19 = (bf16[16,128,128]{2,1,0:T(8,128)(2,1)S(1)}, bf16[16,128,128]{2,1,0:T(8,128)(2,1)S(1)}, u32[]{:S(2)}, u32[]{:S(2)}) collective-permute-start(bf16[16,128,128]{2,1,0:T(8,128)(2,1)S(1)} %collective-permute-done.18.refs_5_), channel_id=1, source_target_pairs={{0,4},{4,0},{8,12},{12,8},{16,20},{20,16},{24,28},{28,24},{32,36},... | collective-permute-start | bytes 1572872 | tf_op jit(solution)/shard_map/ppermute | solution.py:249
  80.3 20.8 %collective-permute-start.29 = (bf16[256,512]{1,0:T(8,128)(2,1)S(1)}, bf16[256,512]{1,0:T(8,128)(2,1)S(1)}, u32[]{:S(2)}, u32[]{:S(2)}) collective-permute-start(bf16[256,512]{1,0:T(8,128)(2,1)S(1)} %get-tuple-element.38.a0), channel_id=1, source_target_pairs={{3,0},{0,1},{1,2},{2,3},{7,4},{4,5},{5,6},{6,7},{11,8},{8,9},{9,10... | collective-permute-start | bytes 786440 | tf_op jit(solution)/shard_map/ppermute | solution.py:223
  82.2 20.9 %collective-permute-start.28 = (bf16[256,512]{1,0:T(8,128)(2,1)S(1)}, bf16[256,512]{1,0:T(8,128)(2,1)S(1)}, u32[]{:S(2)}, u32[]{:S(2)}) collective-permute-start(bf16[256,512]{1,0:T(8,128)(2,1)S(1)} %get-tuple-element.38.a0), channel_id=1, source_target_pairs={{2,0},{3,1},{0,2},{1,3},{6,4},{7,5},{4,6},{5,7},{10,8},{11,9},{8,1... | collective-permute-start | bytes 786440 | tf_op jit(solution)/shard_map/ppermute | solution.py:223
  85.1 18.0 %collective-permute-start.27 = (bf16[256,512]{1,0:T(8,128)(2,1)S(1)}, bf16[256,512]{1,0:T(8,128)(2,1)S(1)}, u32[]{:S(2)}, u32[]{:S(2)}) collective-permute-start(bf16[256,512]{1,0:T(8,128)(2,1)S(1)} %get-tuple-element.38.a0), channel_id=1, source_target_pairs={{1,0},{2,1},{3,2},{0,3},{5,4},{6,5},{7,6},{4,7},{9,8},{10,9},{11,1... | collective-permute-start | bytes 786440 | tf_op jit(solution)/shard_map/ppermute | solution.py:223
  99.5 14.8 %collective-permute-start.25 = (bf16[256,512]{1,0:T(8,128)(2,1)S(1)}, bf16[256,512]{1,0:T(8,128)(2,1)S(1)}, u32[]{:S(2)}, u32[]{:S(2)}) collective-permute-start(bf16[256,512]{1,0:T(8,128)(2,1)S(1)} %attend1.1.a0), channel_id=1, source_target_pairs={{3,0},{0,1},{1,2},{2,3},{7,4},{4,5},{5,6},{6,7},{11,8},{8,9},{9,10... | collective-permute-start | bytes 786440 | tf_op jit(solution)/shard_map/ppermute | solution.py:223
  100.3 14.0 %collective-permute-start.24 = (bf16[256,512]{1,0:T(8,128)(2,1)S(1)}, bf16[256,512]{1,0:T(8,128)(2,1)S(1)}, u32[]{:S(2)}, u32[]{:S(2)}) collective-permute-start(bf16[256,512]{1,0:T(8,128)(2,1)S(1)} %attend1.1.a0), channel_id=1, source_target_pairs={{2,0},{3,1},{0,2},{1,3},{6,4},{7,5},{4,6},{5,7},{10,8},{11,9},{8,1... | collective-permute-start | bytes 786440 | tf_op jit(solution)/shard_map/ppermute | solution.py:223
  101.1 13.8 %collective-permute-start.23 = (bf16[256,512]{1,0:T(8,128)(2,1)S(1)}, bf16[256,512]{1,0:T(8,128)(2,1)S(1)}, u32[]{:S(2)}, u32[]{:S(2)}) collective-permute-start(bf16[256,512]{1,0:T(8,128)(2,1)S(1)} %attend1.1.a0), channel_id=1, source_target_pairs={{1,0},{2,1},{3,2},{0,3},{5,4},{6,5},{7,6},{4,7},{9,8},{10,9},{11,1... | collective-permute-start | bytes 786440 | tf_op jit(solution)/shard_map/ppermute | solution.py:223
  (7 other events, 62.4 us)

commit v10 on v8

--- a/solution.py
+++ b/solution.py
@@ -20,7 +20,7 @@
 X_CHIPS = 4
 HEADS = 4
 EXP_SCALE = math.log2(math.e) * HEAD ** (-0.5)
-VMEM_LIMIT = 48 * 1024 * 1024
+VMEM_LIMIT = 24 * 1024 * 1024
 
 SMEM = functools.partial(pl.BlockSpec, memory_space=pltpu.SMEM)
 VMEM = functools.partial(pl.BlockSpec, memory_space=pltpu.VMEM)

time: 128 us -> 121 us (0.945)
  Pallas kernels: 47.6 us -> 38.8 us
    pallas_call x2, Pallas kernels: 22.5 us -> 17.9 us  [per_device(): pl.pallas_call(functools.partial(out_kernel, ctx_count, st, len(v_pieces)...]
    pallas_call x1, Pallas kernels: 4.48 us -> 1.94 us  [per_device(): pl.pallas_call(functools.partial(slab_kernel, tp), grid=(depth // 128,),...]
    pallas_call x1, Pallas kernels: 10.4 us -> 8.96 us  [per_device(): pl.pallas_call(top_kernel, out_shape=[shape((ROOM, BLOCK, HEAD), BF16), s...]
    unnamed x44 -> x32, local copies, waits for them, and re-layouts: 6.19 us -> 7.38 us
  transfers between devices with their start and end apart: 30 -> 30, of which waited for: 11 -> 10; matrix products, arithmetic and copies ran while one was open for 1% -> 1% of each run, Pallas kernels for 35% -> 29%
where the time goes in v10:
time: 121 us; the launch traced here: 120 us
  starting transfers between devices  46.2 us (38%)
  Pallas kernels  38.8 us (32%)
  waiting for transfers between devices  27 us (22%)
  local copies, waits for them, and re-layouts  8.08 us (7%)
    ppermute x19, starting transfers between devices, gather_columns(): send = lambda a, r: lax.ppermute(a, 'ctx', r)  27.9 us
    pallas_call x2, Pallas kernels, per_device(): pl.pallas_call(functools.partial(out_kernel, ctx_count, st, len(v_pieces)...  17.9 us
    ppermute x9, waiting for transfers between devices, from_ahead(): return lax.ppermute(x, axis, [((i + shift) % n, i) for i in range(n)])  14.7 us
    ppermute x9, starting transfers between devices, from_ahead(): return lax.ppermute(x, axis, [((i + shift) % n, i) for i in range(n)])  12.7 us
    ppermute x19, waiting for transfers between devices, gather_columns(): send = lambda a, r: lax.ppermute(a, 'ctx', r)  12.2 us
    pallas_call x1, Pallas kernels, per_device(): pl.pallas_call(top_kernel, out_shape=[shape((ROOM, BLOCK, HEAD), BF16), s...  8.96 us
    unnamed x32, local copies, waits for them, and re-layouts  7.38 us
    pallas_call x2, Pallas kernels, per_device(): pl.pallas_call(mix_kernel, grid=(width // tile,), out_shape=shape((2, STR...  6.19 us
  transfers between devices with their start and end apart: 30, of which 10 were waited for; matrix products, arithmetic and copies ran while one was open for 1% of the time, Pallas kernels for 29%

profile of v10, /device:TPU:96, one launch (start us, length us, event | category | flops | bytes accessed | tf_op | source)
XLA Modules:
  0.0 120.3 jit_solution(1237967096916228557)
XLA Ops:
  3.0 1.6 %collective-permute-start.4 = (bf16[2,2,128,128]{3,2,1,0:T(8,128)(2,1)S(1)}, bf16[2,2,128,128]{3,2,1,0:T(8,128)(2,1)S(1)}, u32[]{:S(2)}, u32[]{:S(2)}) collective-permute-start(bf16[2,2,128,128]{3,2,1,0:T(8,128)(2,1)S(1)} %get-tuple-element.29.refs_0_), channel_id=1, source_target_pairs={{0,64},{4,68},{8,72},{12,76},{16,80},{20,84},{24,88},{28,92},{32,9... | collective-permute-start | bytes 393224 | tf_op jit(solution)/shard_map/ppermute | solution.py:249
  4.6 2.7 %collective-permute-start.3 = (bf16[2,2,128,128]{3,2,1,0:T(8,128)(2,1)S(1)}, bf16[2,2,128,128]{3,2,1,0:T(8,128)(2,1)S(1)}, u32[]{:S(2)}, u32[]{:S(2)}) collective-permute-start(bf16[2,2,128,128]{3,2,1,0:T(8,128)(2,1)S(1)} %get-tuple-element.29.refs_0_), channel_id=1, source_target_pairs={{0,128},{4,132},{8,136},{12,140},{16,144},{20,148},{24,152},{28,15... | collective-permute-start | bytes 393224 | tf_op jit(solution)/shard_map/ppermute | solution.py:249
  7.3 1.4 %collective-permute-start.2 = (bf16[2,2,128,128]{3,2,1,0:T(8,128)(2,1)S(1)}, bf16[2,2,128,128]{3,2,1,0:T(8,128)(2,1)S(1)}, u32[]{:S(2)}, u32[]{:S(2)}) collective-permute-start(bf16[2,2,128,128]{3,2,1,0:T(8,128)(2,1)S(1)} %get-tuple-element.29.refs_0_), channel_id=1, source_target_pairs={{0,192},{4,196},{8,200},{12,204},{16,208},{20,212},{24,216},{28,22... | collective-permute-start | bytes 393224 | tf_op jit(solution)/shard_map/ppermute | solution.py:249
  9.7 3.6 %collective-permute-done.3.refs_2_ = bf16[2,2,128,128]{3,2,1,0:T(8,128)(2,1)S(1)} collective-permute-done((bf16[2,2,128,128]{3,2,1,0:T(8,128)(2,1)S(1)}, bf16[2,2,128,128]{3,2,1,0:T(8,128)(2,1)S(1)}, u32[]{:S(2)}, u32[]{:S(2)}) %collective-permute-start.3) | collective-permute-done | bytes 131104 | tf_op jit(solution)/shard_map/ppermute | solution.py:249
  13.5 1.9 %collective-permute-done.5.other_ref = bf16[2,8,128,128]{3,2,1,0:T(8,128)(2,1)S(1)} collective-permute-done((bf16[2,8,128,128]{3,2,1,0:T(8,128)(2,1)S(1)}, bf16[2,8,128,128]{3,2,1,0:T(8,128)(2,1)S(1)}, u32[]{:S(2)}, u32[]{:S(2)}) %collective-permute-start.5) | collective-permute-done | bytes 524320 | tf_op jit(solution)/shard_map/ppermute | solution.py:249
  15.4 3.2 %collective-permute-start.6 = (bf16[16,128,128]{2,1,0:T(8,128)(2,1)S(1)}, bf16[16,128,128]{2,1,0:T(8,128)(2,1)}, u32[]{:S(2)}, u32[]{:S(2)}) collective-permute-start(bf16[16,128,128]{2,1,0:T(8,128)(2,1)S(1)} %chip0.1.refs_0_), channel_id=1, source_target_pairs={{0,8},{4,60},{8,16},{12,4},{16,24},{20,12},{24,32},{28,20},{32,40}... | collective-permute-start | bytes 1572872 | tf_op jit(solution)/shard_map/ppermute | solution.py:249
  18.6 1.9 %collective-permute-start = (bf16[2,256,128]{2,1,0:T(8,128)(2,1)S(1)}, bf16[2,256,128]{2,1,0:T(8,128)(2,1)S(1)}, u32[]{:S(2)}, u32[]{:S(2)}) collective-permute-start(bf16[2,256,128]{2,1,0:T(8,128)(2,1)S(1)} %get-tuple-element.26), channel_id=1, source_target_pairs={{0,4},{4,8},{8,12},{12,16},{16,20},{20,24},{24,28},{28,32},{32,36}... | collective-permute-start | bytes 393224 | tf_op jit(solution)/shard_map/ppermute | solution.py:351
  20.5 3.6 %collective-permute-start.1 = (bf16[2,256,128]{2,1,0:T(8,128)(2,1)S(1)}, bf16[2,256,128]{2,1,0:T(8,128)(2,1)S(1)}, u32[]{:S(2)}, u32[]{:S(2)}) collective-permute-start(bf16[2,256,128]{2,1,0:T(8,128)(2,1)S(1)} %get-tuple-element.27), channel_id=1, source_target_pairs={{4,0},{8,4},{12,8},{16,12},{20,16},{24,20},{28,24},{32,28},{36,32}... | collective-permute-start | bytes 393224 | tf_op jit(solution)/shard_map/ppermute | solution.py:352
  24.2 2.5 %collective-permute-done.6.refs_1_.refs_0_ = bf16[16,128,128]{2,1,0:T(8,128)(2,1)} collective-permute-done((bf16[16,128,128]{2,1,0:T(8,128)(2,1)S(1)}, bf16[16,128,128]{2,1,0:T(8,128)(2,1)}, u32[]{:S(2)}, u32[]{:S(2)}) %collective-permute-start.6) | collective-permute-done | bytes 524320 | tf_op jit(solution)/shard_map/ppermute | solution.py:249
  26.7 3.8 %collective-permute-start.8 = (bf16[16,128,128]{2,1,0:T(8,128)(2,1)}, bf16[16,128,128]{2,1,0:T(8,128)(2,1)}, u32[]{:S(2)}, u32[]{:S(2)}) collective-permute-start(bf16[16,128,128]{2,1,0:T(8,128)(2,1)} %collective-permute-done.6.refs_1_.refs_0_), channel_id=1, source_target_pairs={{0,8},{4,60},{8,16},{12,4},{16,24},{20,12},{24,32},{28,20},{32,40}... | collective-permute-start | bytes 1572872 | tf_op jit(solution)/shard_map/ppermute | solution.py:249
  30.7 2.2 %copy-done.1 = bf16[512,4096]{1,0:T(8,128)(2,1)S(1)} copy-done((bf16[512,4096]{1,0:T(8,128)(2,1)S(1)}, bf16[512,4096]{1,0:T(8,128)(2,1)}, u32[]{:S(2)}) %copy-start.1) | copy-done | bytes 4194328
  32.9 1.9 %slabs.1 = (bf16[512,1024]{1,0:T(8,128)(2,1)S(1)}, bf16[512,1024]{1,0:T(8,128)(2,1)}, bf16[512,1024]{1,0:T(8,128)(2,1)S(1)}, bf16[512,1024]{1,0:T(8,128)(2,1)}) custom-call(s32[1]{0:T(128)} %bitcast.7.index_ref, bf16[512,4096]{1,0:T(8,128)(2,1)S(1)} %copy-done.1, bf16[16,128,128]{2,1,0:T(8,128)(2,1)S(1)} %chip1.1.refs_0_, ...), custom_call_target="tpu_custom_call" | custom-call | bytes 9000000 | tf_op jit(solution)/shard_map/slabs/pallas_call | solution.py:368
  36.8 3.0 %collective-permute-start.21 = (bf16[512,1024]{1,0:T(8,128)(2,1)}, bf16[512,1024]{1,0:T(8,128)(2,1)S(1)}, u32[]{:S(2)}, u32[]{:S(2)}) collective-permute-start(bf16[512,1024]{1,0:T(8,128)(2,1)} %get-tuple-element.33), channel_id=1, source_target_pairs={{1,0},{2,1},{3,2},{0,3},{5,4},{6,5},{7,6},{4,7},{9,8},{10,9},{11,1... | collective-permute-start | bytes 3145736 | tf_op jit(solution)/shard_map/ppermute | solution.py:223
  39.8 1.4 %collective-permute-start.10 = (bf16[16,128,128]{2,1,0:T(8,128)(2,1)}, bf16[16,128,128]{2,1,0:T(8,128)(2,1)}, u32[]{:S(2)}, u32[]{:S(2)}) collective-permute-start(bf16[16,128,128]{2,1,0:T(8,128)(2,1)} %collective-permute-done.8.refs_3_), channel_id=1, source_target_pairs={{0,8},{4,60},{8,16},{12,4},{16,24},{20,12},{24,32},{28,20},{32,40}... | collective-permute-start | bytes 1572872 | tf_op jit(solution)/shard_map/ppermute | solution.py:249
  41.2 1.8 %collective-permute-done.14.refs_1_ = bf16[16,128,128]{2,1,0:T(8,128)(2,1)} collective-permute-done((bf16[16,128,128]{2,1,0:T(8,128)(2,1)S(1)}, bf16[16,128,128]{2,1,0:T(8,128)(2,1)}, u32[]{:S(2)}, u32[]{:S(2)}) %collective-permute-start.14) | collective-permute-done | bytes 524320 | tf_op jit(solution)/shard_map/ppermute | solution.py:249
  43.0 3.8 %collective-permute-start.16 = (bf16[16,128,128]{2,1,0:T(8,128)(2,1)}, bf16[16,128,128]{2,1,0:T(8,128)(2,1)}, u32[]{:S(2)}, u32[]{:S(2)}) collective-permute-start(bf16[16,128,128]{2,1,0:T(8,128)(2,1)} %collective-permute-done.14.refs_1_), channel_id=1, source_target_pairs={{0,8},{4,60},{8,16},{12,4},{16,24},{20,12},{24,32},{28,20},{32,40}... | collective-permute-start | bytes 1572872 | tf_op jit(solution)/shard_map/ppermute | solution.py:249
  48.6 1.9 %band.1 = (f32[4,256,512]{2,1,0:T(8,128)S(1)}, f32[2,4,256,128]{3,2,1,0:T(8,128)S(1)}) custom-call(s32[1,16]{1,0:T(1,128)S(1)} %get-tuple-element.22.meta_ref, s32[4,64]{1,0:T(4,128)S(1)} %copy-done.13, bf16[2,256,512]{2,1,0:T(8,128)(2,1)S(1)} %bitcast.9, bf16[2,256,128]{2,1,0:T(8,128)(2,1)S(1)} %bitcast.14, ...), custom_call_target="tpu_custom_call" | custom-call | bytes 9000000 | tf_op jit(solution)/shard_map/band/pallas_call | solution.py:354
  51.6 1.9 %collective-permute-start.12 = (bf16[8,128,128]{2,1,0:T(8,128)(2,1)S(1)}, bf16[8,128,128]{2,1,0:T(8,128)(2,1)S(1)}, u32[]{:S(2)}, u32[]{:S(2)}) collective-permute-start(bf16[8,128,128]{2,1,0:T(8,128)(2,1)S(1)} %half.1), channel_id=1, source_target_pairs={{0,8},{4,60},{8,16},{12,4},{16,24},{20,12},{24,32},{28,20},{32,40}... | collective-permute-start | bytes 786440 | tf_op jit(solution)/shard_map/ppermute | solution.py:249
  53.5 1.4 %collective-permute-done.16.refs_3_ = bf16[16,128,128]{2,1,0:T(8,128)(2,1)} collective-permute-done((bf16[16,128,128]{2,1,0:T(8,128)(2,1)}, bf16[16,128,128]{2,1,0:T(8,128)(2,1)}, u32[]{:S(2)}, u32[]{:S(2)}) %collective-permute-start.16) | collective-permute-done | bytes 524320 | tf_op jit(solution)/shard_map/ppermute | solution.py:249
  54.9 3.2 %collective-permute-start.18 = (bf16[16,128,128]{2,1,0:T(8,128)(2,1)}, bf16[16,128,128]{2,1,0:T(8,128)(2,1)S(1)}, u32[]{:S(2)}, u32[]{:S(2)}) collective-permute-start(bf16[16,128,128]{2,1,0:T(8,128)(2,1)} %collective-permute-done.16.refs_3_), channel_id=1, source_target_pairs={{0,8},{4,60},{8,16},{12,4},{16,24},{20,12},{24,32},{28,20},{32,40}... | collective-permute-start | bytes 1572872 | tf_op jit(solution)/shard_map/ppermute | solution.py:249
  58.1 3.2 %collective-permute-done.21.refs_8_.w1 = bf16[512,1024]{1,0:T(8,128)(2,1)S(1)} collective-permute-done((bf16[512,1024]{1,0:T(8,128)(2,1)}, bf16[512,1024]{1,0:T(8,128)(2,1)S(1)}, u32[]{:S(2)}, u32[]{:S(2)}) %collective-permute-start.21) | collective-permute-done | bytes 1048608 | tf_op jit(solution)/shard_map/ppermute | solution.py:223
  61.8 2.8 %collective-permute-done.22.refs_9_.w3 = bf16[512,1024]{1,0:T(8,128)(2,1)S(1)} collective-permute-done((bf16[512,1024]{1,0:T(8,128)(2,1)}, bf16[512,1024]{1,0:T(8,128)(2,1)S(1)}, u32[]{:S(2)}, u32[]{:S(2)}) %collective-permute-start.22) | collective-permute-done | bytes 1048608 | tf_op jit(solution)/shard_map/ppermute | solution.py:223
  65.2 3.5 %collective-permute-start.20 = (bf16[16,128,128]{2,1,0:T(8,128)(2,1)S(1)}, bf16[16,128,128]{2,1,0:T(8,128)(2,1)S(1)}, u32[]{:S(2)}, u32[]{:S(2)}) collective-permute-start(bf16[16,128,128]{2,1,0:T(8,128)(2,1)S(1)} %collective-permute-done.18.refs_5_), channel_id=1, source_target_pairs={{0,8},{4,60},{8,16},{12,4},{16,24},{20,12},{24,32},{28,20},{32,40}... | collective-permute-start | bytes 1572872 | tf_op jit(solution)/shard_map/ppermute | solution.py:249
  68.7 9.0 %top.1 = (bf16[65,128,128]{2,1,0:T(8,128)(2,1)S(1)}, f32[2,4,256,128]{3,2,1,0:T(8,128)S(1)}) custom-call(s32[1,16]{1,0:T(1,128)S(1)} %get-tuple-element.22.meta_ref, s32[1,64]{1,0:T(1,128)S(1)} %get-tuple-element.23.blk_ref, s32[1,128]{1,0:T(1,128)S(1)} %get-tuple-element.25.at_ref, bf16[2,256,512]{2,1,0:T(8,128)(2,1)S(1)} %bitcast.10, ...), custom_call_target="tpu_custom_call" | custom-call | bytes 27000000 | tf_op jit(solution)/shard_map/top/pallas_call | solution.py:380
  77.7 4.9 %attend0.1 = (bf16[256,512]{1,0:T(8,128)(2,1)S(1)}, bf16[65,128,128]{2,1,0:T(8,128)(2,1)S(1)}) custom-call(s32[1,16]{1,0:T(1,128)S(1)} %get-tuple-element.22.meta_ref, s32[1,64]{1,0:T(1,128)S(1)} %get-tuple-element.23.blk_ref, s32[1,128]{1,0:T(1,128)S(1)} %get-tuple-element.24.at_ref, bf16[2,256,512]{2,1,0:T(8,128)(2,1)S(1)} %bitcast.11, ...), custom_call_target="tpu_custom_call" | custom-call | bytes 24000000 | tf_op jit(solution)/shard_map/attend0/pallas_call | solution.py:394
  82.6 1.9 %collective-permute-start.29 = (bf16[256,512]{1,0:T(8,128)(2,1)S(1)}, bf16[256,512]{1,0:T(8,128)(2,1)S(1)}, u32[]{:S(2)}, u32[]{:S(2)}) collective-permute-start(bf16[256,512]{1,0:T(8,128)(2,1)S(1)} %get-tuple-element.38.a0), channel_id=1, source_target_pairs={{3,0},{0,1},{1,2},{2,3},{7,4},{4,5},{5,6},{6,7},{11,8},{8,9},{9,10... | collective-permute-start | bytes 786440 | tf_op jit(solution)/shard_map/ppermute | solution.py:223
  84.5 2.9 %collective-permute-start.28 = (bf16[256,512]{1,0:T(8,128)(2,1)S(1)}, bf16[256,512]{1,0:T(8,128)(2,1)S(1)}, u32[]{:S(2)}, u32[]{:S(2)}) collective-permute-start(bf16[256,512]{1,0:T(8,128)(2,1)S(1)} %get-tuple-element.38.a0), channel_id=1, source_target_pairs={{2,0},{3,1},{0,2},{1,3},{6,4},{7,5},{4,6},{5,7},{10,8},{11,9},{8,1... | collective-permute-start | bytes 786440 | tf_op jit(solution)/shard_map/ppermute | solution.py:223
  88.7 13.1 %attend1.1.a0 = bf16[256,512]{1,0:T(8,128)(2,1)S(1)} custom-call(s32[1,16]{1,0:T(1,128)S(1)} %get-tuple-element.22.meta_ref, s32[1,64]{1,0:T(1,128)S(1)} %get-tuple-element.23.blk_ref, s32[1,128]{1,0:T(1,128)S(1)} %get-tuple-element.24.at_ref, bf16[2,256,512]{2,1,0:T(8,128)(2,1)S(1)} %bitcast.12, bf16[65,128,128]{2,1,0:T(8,128)(2,1)S(1)} %get-tuple-element.31.keys_ref, ...), custom_call_target="tpu_custom_call" | custom-call | bytes 24000000 | tf_op jit(solution)/shard_map/attend1/pallas_call | solution.py:394
  103.4 2.0 %collective-permute-start.23 = (bf16[256,512]{1,0:T(8,128)(2,1)S(1)}, bf16[256,512]{1,0:T(8,128)(2,1)S(1)}, u32[]{:S(2)}, u32[]{:S(2)}) collective-permute-start(bf16[256,512]{1,0:T(8,128)(2,1)S(1)} %attend1.1.a0), channel_id=1, source_target_pairs={{1,0},{2,1},{3,2},{0,3},{5,4},{6,5},{7,6},{4,7},{9,8},{10,9},{11,1... | collective-permute-start | bytes 786440 | tf_op jit(solution)/shard_map/ppermute | solution.py:223
  105.4 3.1 %mix0.1.refs_0_ = bf16[2,256,1024]{2,1,0:T(8,128)(2,1)} custom-call(bf16[256,512]{1,0:T(8,128)(2,1)S(1)} %get-tuple-element.38.a0, bf16[256,512]{1,0:T(8,128)(2,1)S(1)} %collective-permute-done.27.a1, bf16[256,512]{1,0:T(8,128)(2,1)S(1)} %collective-permute-done.28.a2, bf16[256,512]{1,0:T(8,128)(2,1)S(1)} %collective-permute-done.29.a3, ...), custom_call_target="tpu_custom_call" | custom-call | bytes 9000000 | tf_op jit(solution)/shard_map/mix0/pallas_call | solution.py:419
  108.5 8.1 %collective-permute-done.25.a3 = bf16[256,512]{1,0:T(8,128)(2,1)S(1)} collective-permute-done((bf16[256,512]{1,0:T(8,128)(2,1)S(1)}, bf16[256,512]{1,0:T(8,128)(2,1)S(1)}, u32[]{:S(2)}, u32[]{:S(2)}) %collective-permute-start.25) | collective-permute-done | bytes 262176 | tf_op jit(solution)/shard_map/ppermute | solution.py:223
  117.2 3.1 %mix1.1 = bf16[2,256,1024]{2,1,0:T(8,128)(2,1)} custom-call(bf16[256,512]{1,0:T(8,128)(2,1)S(1)} %attend1.1.a0, bf16[256,512]{1,0:T(8,128)(2,1)S(1)} %collective-permute-done.23.a1, bf16[256,512]{1,0:T(8,128)(2,1)S(1)} %collective-permute-done.24.a2, bf16[256,512]{1,0:T(8,128)(2,1)S(1)} %collective-permute-done.25.a3, ...), custom_call_target="tpu_custom_call", output_to_operand_aliasing={{}: (8, {})} | custom-call | bytes 9000000 | tf_op jit(solution)/shard_map/mix1/pallas_call | solution.py:419
  (74 shorter events, 13.7 us)
Async XLA Ops:
  3.0 6.7 %collective-permute-start.4 = (bf16[2,2,128,128]{3,2,1,0:T(8,128)(2,1)S(1)}, bf16[2,2,128,128]{3,2,1,0:T(8,128)(2,1)S(1)}, u32[]{:S(2)}, u32[]{:S(2)}) collective-permute-start(bf16[2,2,128,128]{3,2,1,0:T(8,128)(2,1)S(1)} %get-tuple-element.29.refs_0_), channel_id=1, source_target_pairs={{0,64},{4,68},{8,72},{12,76},{16,80},{20,84},{24,88},{28,92},{32,9... | collective-permute-start | bytes 393224 | tf_op jit(solution)/shard_map/ppermute | solution.py:249
  4.6 8.7 %collective-permute-start.3 = (bf16[2,2,128,128]{3,2,1,0:T(8,128)(2,1)S(1)}, bf16[2,2,128,128]{3,2,1,0:T(8,128)(2,1)S(1)}, u32[]{:S(2)}, u32[]{:S(2)}) collective-permute-start(bf16[2,2,128,128]{3,2,1,0:T(8,128)(2,1)S(1)} %get-tuple-element.29.refs_0_), channel_id=1, source_target_pairs={{0,128},{4,132},{8,136},{12,140},{16,144},{20,148},{24,152},{28,15... | collective-permute-start | bytes 393224 | tf_op jit(solution)/shard_map/ppermute | solution.py:249
  7.3 6.0 %collective-permute-start.2 = (bf16[2,2,128,128]{3,2,1,0:T(8,128)(2,1)S(1)}, bf16[2,2,128,128]{3,2,1,0:T(8,128)(2,1)S(1)}, u32[]{:S(2)}, u32[]{:S(2)}) collective-permute-start(bf16[2,2,128,128]{3,2,1,0:T(8,128)(2,1)S(1)} %get-tuple-element.29.refs_0_), channel_id=1, source_target_pairs={{0,192},{4,196},{8,200},{12,204},{16,208},{20,212},{24,216},{28,22... | collective-permute-start | bytes 393224 | tf_op jit(solution)/shard_map/ppermute | solution.py:249
  13.4 2.0 %collective-permute-start.5 = (bf16[2,8,128,128]{3,2,1,0:T(8,128)(2,1)S(1)}, bf16[2,8,128,128]{3,2,1,0:T(8,128)(2,1)S(1)}, u32[]{:S(2)}, u32[]{:S(2)}) collective-permute-start(bf16[2,8,128,128]{3,2,1,0:T(8,128)(2,1)S(1)} %line.1.own_ref), channel_id=1, source_target_pairs={{0,4},{4,0},{8,12},{12,8},{16,20},{20,16},{24,28},{28,24},{32,36},... | collective-permute-start | bytes 1572872 | tf_op jit(solution)/shard_map/ppermute | solution.py:249
  15.4 19.4 %copy-start.6 = (bf16[16,128,128]{2,1,0:T(8,128)(2,1)}, bf16[16,128,128]{2,1,0:T(8,128)(2,1)S(1)}, u32[]{:S(2)}) copy-start(bf16[16,128,128]{2,1,0:T(8,128)(2,1)S(1)} %chip0.1.refs_0_) | copy-start | bytes 1572868
  15.4 11.3 %collective-permute-start.6 = (bf16[16,128,128]{2,1,0:T(8,128)(2,1)S(1)}, bf16[16,128,128]{2,1,0:T(8,128)(2,1)}, u32[]{:S(2)}, u32[]{:S(2)}) collective-permute-start(bf16[16,128,128]{2,1,0:T(8,128)(2,1)S(1)} %chip0.1.refs_0_), channel_id=1, source_target_pairs={{0,8},{4,60},{8,16},{12,4},{16,24},{20,12},{24,32},{28,20},{32,40}... | collective-permute-start | bytes 1572872 | tf_op jit(solution)/shard_map/ppermute | solution.py:249
  18.6 12.0 %collective-permute-start = (bf16[2,256,128]{2,1,0:T(8,128)(2,1)S(1)}, bf16[2,256,128]{2,1,0:T(8,128)(2,1)S(1)}, u32[]{:S(2)}, u32[]{:S(2)}) collective-permute-start(bf16[2,256,128]{2,1,0:T(8,128)(2,1)S(1)} %get-tuple-element.26), channel_id=1, source_target_pairs={{0,4},{4,8},{8,12},{12,16},{16,20},{20,24},{24,28},{28,32},{32,36}... | collective-permute-start | bytes 393224 | tf_op jit(solution)/shard_map/ppermute | solution.py:351
  20.5 10.1 %collective-permute-start.1 = (bf16[2,256,128]{2,1,0:T(8,128)(2,1)S(1)}, bf16[2,256,128]{2,1,0:T(8,128)(2,1)S(1)}, u32[]{:S(2)}, u32[]{:S(2)}) collective-permute-start(bf16[2,256,128]{2,1,0:T(8,128)(2,1)S(1)} %get-tuple-element.27), channel_id=1, source_target_pairs={{4,0},{8,4},{12,8},{16,12},{20,16},{24,20},{28,24},{32,28},{36,32}... | collective-permute-start | bytes 393224 | tf_op jit(solution)/shard_map/ppermute | solution.py:352
  26.7 13.1 %collective-permute-start.8 = (bf16[16,128,128]{2,1,0:T(8,128)(2,1)}, bf16[16,128,128]{2,1,0:T(8,128)(2,1)}, u32[]{:S(2)}, u32[]{:S(2)}) collective-permute-start(bf16[16,128,128]{2,1,0:T(8,128)(2,1)} %collective-permute-done.6.refs_1_.refs_0_), channel_id=1, source_target_pairs={{0,8},{4,60},{8,16},{12,4},{16,24},{20,12},{24,32},{28,20},{32,40}... | collective-permute-start | bytes 1572872 | tf_op jit(solution)/shard_map/ppermute | solution.py:249
  30.6 12.5 %collective-permute-start.14 = (bf16[16,128,128]{2,1,0:T(8,128)(2,1)S(1)}, bf16[16,128,128]{2,1,0:T(8,128)(2,1)}, u32[]{:S(2)}, u32[]{:S(2)}) collective-permute-start(bf16[16,128,128]{2,1,0:T(8,128)(2,1)S(1)} %chip1.1.refs_0_), channel_id=1, source_target_pairs={{0,8},{4,60},{8,16},{12,4},{16,24},{20,12},{24,32},{28,20},{32,40}... | collective-permute-start | bytes 1572872 | tf_op jit(solution)/shard_map/ppermute | solution.py:249
  36.8 24.5 %collective-permute-start.21 = (bf16[512,1024]{1,0:T(8,128)(2,1)}, bf16[512,1024]{1,0:T(8,128)(2,1)S(1)}, u32[]{:S(2)}, u32[]{:S(2)}) collective-permute-start(bf16[512,1024]{1,0:T(8,128)(2,1)} %get-tuple-element.33), channel_id=1, source_target_pairs={{1,0},{2,1},{3,2},{0,3},{5,4},{6,5},{7,6},{4,7},{9,8},{10,9},{11,1... | collective-permute-start | bytes 3145736 | tf_op jit(solution)/shard_map/ppermute | solution.py:223
  39.8 24.8 %collective-permute-start.22 = (bf16[512,1024]{1,0:T(8,128)(2,1)}, bf16[512,1024]{1,0:T(8,128)(2,1)S(1)}, u32[]{:S(2)}, u32[]{:S(2)}) collective-permute-start(bf16[512,1024]{1,0:T(8,128)(2,1)} %get-tuple-element.34), channel_id=1, source_target_pairs={{3,0},{0,1},{1,2},{2,3},{7,4},{4,5},{5,6},{6,7},{11,8},{8,9},{9,10... | collective-permute-start | bytes 3145736 | tf_op jit(solution)/shard_map/ppermute | solution.py:223
  39.8 10.7 %collective-permute-start.10 = (bf16[16,128,128]{2,1,0:T(8,128)(2,1)}, bf16[16,128,128]{2,1,0:T(8,128)(2,1)}, u32[]{:S(2)}, u32[]{:S(2)}) collective-permute-start(bf16[16,128,128]{2,1,0:T(8,128)(2,1)} %collective-permute-done.8.refs_3_), channel_id=1, source_target_pairs={{0,8},{4,60},{8,16},{12,4},{16,24},{20,12},{24,32},{28,20},{32,40}... | collective-permute-start | bytes 1572872 | tf_op jit(solution)/shard_map/ppermute | solution.py:249
  41.2 10.4 %collective-permute-start.7 = (bf16[16,128,128]{2,1,0:T(8,128)(2,1)}, bf16[16,128,128]{2,1,0:T(8,128)(2,1)}, u32[]{:S(2)}, u32[]{:S(2)}) collective-permute-start(bf16[16,128,128]{2,1,0:T(8,128)(2,1)} %collective-permute-done.6.refs_1_.refs_0_), channel_id=1, source_target_pairs={{0,4},{4,0},{8,12},{12,8},{16,20},{20,16},{24,28},{28,24},{32,36},... | collective-permute-start | bytes 1572872 | tf_op jit(solution)/shard_map/ppermute | solution.py:249
  43.0 11.8 %collective-permute-start.16 = (bf16[16,128,128]{2,1,0:T(8,128)(2,1)}, bf16[16,128,128]{2,1,0:T(8,128)(2,1)}, u32[]{:S(2)}, u32[]{:S(2)}) collective-permute-start(bf16[16,128,128]{2,1,0:T(8,128)(2,1)} %collective-permute-done.14.refs_1_), channel_id=1, source_target_pairs={{0,8},{4,60},{8,16},{12,4},{16,24},{20,12},{24,32},{28,20},{32,40}... | collective-permute-start | bytes 1572872 | tf_op jit(solution)/shard_map/ppermute | solution.py:249
  48.3 20.4 %copy-start.7 = (bf16[16,128,128]{2,1,0:T(8,128)(2,1)S(1)}, bf16[16,128,128]{2,1,0:T(8,128)(2,1)}, u32[]{:S(2)}) copy-start(bf16[16,128,128]{2,1,0:T(8,128)(2,1)} %copy-done.6) | copy-start | bytes 1572868
  50.5 14.1 %collective-permute-start.9 = (bf16[16,128,128]{2,1,0:T(8,128)(2,1)}, bf16[16,128,128]{2,1,0:T(8,128)(2,1)S(1)}, u32[]{:S(2)}, u32[]{:S(2)}) collective-permute-start(bf16[16,128,128]{2,1,0:T(8,128)(2,1)} %collective-permute-done.8.refs_3_), channel_id=1, source_target_pairs={{0,4},{4,0},{8,12},{12,8},{16,20},{20,16},{24,28},{28,24},{32,36},... | collective-permute-start | bytes 1572872 | tf_op jit(solution)/shard_map/ppermute | solution.py:249
  51.6 9.7 %collective-permute-start.12 = (bf16[8,128,128]{2,1,0:T(8,128)(2,1)S(1)}, bf16[8,128,128]{2,1,0:T(8,128)(2,1)S(1)}, u32[]{:S(2)}, u32[]{:S(2)}) collective-permute-start(bf16[8,128,128]{2,1,0:T(8,128)(2,1)S(1)} %half.1), channel_id=1, source_target_pairs={{0,8},{4,60},{8,16},{12,4},{16,24},{20,12},{24,32},{28,20},{32,40}... | collective-permute-start | bytes 786440 | tf_op jit(solution)/shard_map/ppermute | solution.py:249
  54.9 10.3 %collective-permute-start.18 = (bf16[16,128,128]{2,1,0:T(8,128)(2,1)}, bf16[16,128,128]{2,1,0:T(8,128)(2,1)S(1)}, u32[]{:S(2)}, u32[]{:S(2)}) collective-permute-start(bf16[16,128,128]{2,1,0:T(8,128)(2,1)} %collective-permute-done.16.refs_3_), channel_id=1, source_target_pairs={{0,8},{4,60},{8,16},{12,4},{16,24},{20,12},{24,32},{28,20},{32,40}... | collective-permute-start | bytes 1572872 | tf_op jit(solution)/shard_map/ppermute | solution.py:249
  61.3 7.4 %collective-permute-start.11 = (bf16[16,128,128]{2,1,0:T(8,128)(2,1)}, bf16[16,128,128]{2,1,0:T(8,128)(2,1)S(1)}, u32[]{:S(2)}, u32[]{:S(2)}) collective-permute-start(bf16[16,128,128]{2,1,0:T(8,128)(2,1)} %collective-permute-done.10.source_ref.refs_5_), channel_id=1, source_target_pairs={{0,4},{4,0},{8,12},{12,8},{16,20},{20,16},{24,28},{28,24},{32,36},... | collective-permute-start | bytes 1572872 | tf_op jit(solution)/shard_map/ppermute | solution.py:249
  61.3 3.4 %collective-permute-start.13 = (bf16[8,128,128]{2,1,0:T(8,128)(2,1)S(1)}, bf16[8,128,128]{2,1,0:T(8,128)(2,1)S(1)}, u32[]{:S(2)}, u32[]{:S(2)}) collective-permute-start(bf16[8,128,128]{2,1,0:T(8,128)(2,1)S(1)} %collective-permute-done.12.refs_7_), channel_id=1, source_target_pairs={{0,4},{4,0},{8,12},{12,8},{16,20},{20,16},{24,28},{28,24},{32,36},... | collective-permute-start | bytes 786440 | tf_op jit(solution)/shard_map/ppermute | solution.py:249
  64.6 38.0 %collective-permute-start.26 = (bf16[512,1024]{1,0:T(8,128)(2,1)S(1)}, bf16[512,1024]{1,0:T(8,128)(2,1)S(1)}, u32[]{:S(2)}, u32[]{:S(2)}) collective-permute-start(bf16[512,1024]{1,0:T(8,128)(2,1)S(1)} %copy-done.15), channel_id=1, source_target_pairs={{2,0},{3,1},{0,2},{1,3},{6,4},{7,5},{4,6},{5,7},{10,8},{11,9},{8,1... | collective-permute-start | bytes 3145736 | tf_op jit(solution)/shard_map/ppermute | solution.py:223
  64.6 13.1 %collective-permute-start.15 = (bf16[16,128,128]{2,1,0:T(8,128)(2,1)}, bf16[16,128,128]{2,1,0:T(8,128)(2,1)S(1)}, u32[]{:S(2)}, u32[]{:S(2)}) collective-permute-start(bf16[16,128,128]{2,1,0:T(8,128)(2,1)} %collective-permute-done.14.refs_1_), channel_id=1, source_target_pairs={{0,4},{4,0},{8,12},{12,8},{16,20},{20,16},{24,28},{28,24},{32,36},... | collective-permute-start | bytes 1572872 | tf_op jit(solution)/shard_map/ppermute | solution.py:249
  64.7 13.0 %collective-permute-start.17 = (bf16[16,128,128]{2,1,0:T(8,128)(2,1)}, bf16[16,128,128]{2,1,0:T(8,128)(2,1)S(1)}, u32[]{:S(2)}, u32[]{:S(2)}) collective-permute-start(bf16[16,128,128]{2,1,0:T(8,128)(2,1)} %collective-permute-done.16.refs_3_), channel_id=1, source_target_pairs={{0,4},{4,0},{8,12},{12,8},{16,20},{20,16},{24,28},{28,24},{32,36},... | collective-permute-start | bytes 1572872 | tf_op jit(solution)/shard_map/ppermute | solution.py:249
  65.2 12.5 %collective-permute-start.20 = (bf16[16,128,128]{2,1,0:T(8,128)(2,1)S(1)}, bf16[16,128,128]{2,1,0:T(8,128)(2,1)S(1)}, u32[]{:S(2)}, u32[]{:S(2)}) collective-permute-start(bf16[16,128,128]{2,1,0:T(8,128)(2,1)S(1)} %collective-permute-done.18.refs_5_), channel_id=1, source_target_pairs={{0,8},{4,60},{8,16},{12,4},{16,24},{20,12},{24,32},{28,20},{32,40}... | collective-permute-start | bytes 1572872 | tf_op jit(solution)/shard_map/ppermute | solution.py:249
  68.7 9.0 %collective-permute-start.19 = (bf16[16,128,128]{2,1,0:T(8,128)(2,1)S(1)}, bf16[16,128,128]{2,1,0:T(8,128)(2,1)S(1)}, u32[]{:S(2)}, u32[]{:S(2)}) collective-permute-start(bf16[16,128,128]{2,1,0:T(8,128)(2,1)S(1)} %collective-permute-done.18.refs_5_), channel_id=1, source_target_pairs={{0,4},{4,0},{8,12},{12,8},{16,20},{20,16},{24,28},{28,24},{32,36},... | collective-permute-start | bytes 1572872 | tf_op jit(solution)/shard_map/ppermute | solution.py:249
  82.6 20.8 %collective-permute-start.29 = (bf16[256,512]{1,0:T(8,128)(2,1)S(1)}, bf16[256,512]{1,0:T(8,128)(2,1)S(1)}, u32[]{:S(2)}, u32[]{:S(2)}) collective-permute-start(bf16[256,512]{1,0:T(8,128)(2,1)S(1)} %get-tuple-element.38.a0), channel_id=1, source_target_pairs={{3,0},{0,1},{1,2},{2,3},{7,4},{4,5},{5,6},{6,7},{11,8},{8,9},{9,10... | collective-permute-start | bytes 786440 | tf_op jit(solution)/shard_map/ppermute | solution.py:223
  84.5 20.9 %collective-permute-start.28 = (bf16[256,512]{1,0:T(8,128)(2,1)S(1)}, bf16[256,512]{1,0:T(8,128)(2,1)S(1)}, u32[]{:S(2)}, u32[]{:S(2)}) collective-permute-start(bf16[256,512]{1,0:T(8,128)(2,1)S(1)} %get-tuple-element.38.a0), channel_id=1, source_target_pairs={{2,0},{3,1},{0,2},{1,3},{6,4},{7,5},{4,6},{5,7},{10,8},{11,9},{8,1... | collective-permute-start | bytes 786440 | tf_op jit(solution)/shard_map/ppermute | solution.py:223
  87.4 18.0 %collective-permute-start.27 = (bf16[256,512]{1,0:T(8,128)(2,1)S(1)}, bf16[256,512]{1,0:T(8,128)(2,1)S(1)}, u32[]{:S(2)}, u32[]{:S(2)}) collective-permute-start(bf16[256,512]{1,0:T(8,128)(2,1)S(1)} %get-tuple-element.38.a0), channel_id=1, source_target_pairs={{1,0},{2,1},{3,2},{0,3},{5,4},{6,5},{7,6},{4,7},{9,8},{10,9},{11,1... | collective-permute-start | bytes 786440 | tf_op jit(solution)/shard_map/ppermute | solution.py:223
  101.8 14.8 %collective-permute-start.25 = (bf16[256,512]{1,0:T(8,128)(2,1)S(1)}, bf16[256,512]{1,0:T(8,128)(2,1)S(1)}, u32[]{:S(2)}, u32[]{:S(2)}) collective-permute-start(bf16[256,512]{1,0:T(8,128)(2,1)S(1)} %attend1.1.a0), channel_id=1, source_target_pairs={{3,0},{0,1},{1,2},{2,3},{7,4},{4,5},{5,6},{6,7},{11,8},{8,9},{9,10... | collective-permute-start | bytes 786440 | tf_op jit(solution)/shard_map/ppermute | solution.py:223
  102.6 14.0 %collective-permute-start.24 = (bf16[256,512]{1,0:T(8,128)(2,1)S(1)}, bf16[256,512]{1,0:T(8,128)(2,1)S(1)}, u32[]{:S(2)}, u32[]{:S(2)}) collective-permute-start(bf16[256,512]{1,0:T(8,128)(2,1)S(1)} %attend1.1.a0), channel_id=1, source_target_pairs={{2,0},{3,1},{0,2},{1,3},{6,4},{7,5},{4,6},{5,7},{10,8},{11,9},{8,1... | collective-permute-start | bytes 786440 | tf_op jit(solution)/shard_map/ppermute | solution.py:223
  103.4 13.8 %collective-permute-start.23 = (bf16[256,512]{1,0:T(8,128)(2,1)S(1)}, bf16[256,512]{1,0:T(8,128)(2,1)S(1)}, u32[]{:S(2)}, u32[]{:S(2)}) collective-permute-start(bf16[256,512]{1,0:T(8,128)(2,1)S(1)} %attend1.1.a0), channel_id=1, source_target_pairs={{1,0},{2,1},{3,2},{0,3},{5,4},{6,5},{7,6},{4,7},{9,8},{10,9},{11,1... | collective-permute-start | bytes 786440 | tf_op jit(solution)/shard_map/ppermute | solution.py:223
  (14 other events, 110.5 us)
